TPU v7x, 32 devices: a whole 2x2x4 slice. The times are simulated.
32 devices in a mesh: leaf: 32 (over z, y, x, core).
Axes of the slice: x: 2, y: 2, z: 4, core: 2. Of those that a mesh axis runs over, the one named last changes fastest.
Arguments:
- right_sides: bfloat16 [32, 65536], P(None, 'leaf'), may hold values from -6 to 6
- point_order: int32 [32, 2048], P('leaf'), may hold values from 0 to 2047, each once within a row
- leaf_inverse: bfloat16 [65536, 2048], P('leaf'), may hold values from -0.09375 to 0.09375
- basis_in: bfloat16 [65536, 256], P('leaf'), may hold values from -0.125 to 0.125
- basis_out: bfloat16 [8192, 2048], P('leaf'), may hold values from -0.1875 to 0.1875
- leaf_up: bfloat16 [8192, 256], P('leaf'), may hold values from -0.25 to 0.25
- leaf_down: bfloat16 [8192, 256], P('leaf'), may hold values from -0.3125 to 0.3125
- node_up: bfloat16 [8192, 256], P('leaf'), may hold values from -0.25 to 0.25
- node_down: bfloat16 [8192, 256], P('leaf'), may hold values from -0.3125 to 0.3125
- node_cross: bfloat16 [16384, 256], P('leaf'), may hold values from -0.25 to 0.25
- leaf_map: int32 [32], replicated, may hold values from 0 to 31, as said below
Outputs:
- solution: float32 [32, 65536], P(None, 'leaf')
Inputs may be any that keep to these rules, and one draw needn't show every extreme that they name: `point_order`: each row is a permutation of the leaf's columns. `leaf_map`: A permutation of the tree positions that keeps every device's leaf inside the device's aligned block of 4 devices.
All inputs are finite; a program needn't handle non-finite values.
Results may differ from a plain program's by a relative error of at most 0.015.
Values may be sent and summed in bfloat16 or wider, within the bound.
No kernel may reach another device: no remote copies, remote signals or barrier semaphores. Data moves between devices by JAX's collectives and lax.ppermute only.
A program may use at most 192 MiB of HBM per device.

v0:
```python
import jax
import jax.numpy as jnp
from jax import lax
from jax.sharding import PartitionSpec as P

SPREAD = 4


def swapped(block, axis, apart):
    count = lax.axis_size(axis)
    route = []
    for low in range(count):
        high = low | 1 << apart
        if high != low and high < count:
            route += [(low, high), (high, low)]
    return lax.ppermute(block, axis, route)


def block_rise(value, self_index, depth_bits):
    collected = value[None]
    for bit_index in range(depth_bits):
        partner = swapped(collected, "leaf", bit_index)
        upper_bit = self_index >> bit_index & 1
        collected = jnp.where(
            upper_bit == 1,
            jnp.concatenate([partner, collected], 0),
            jnp.concatenate([collected, partner], 0),
        )
    return collected


def block_fall(value, self_index, depth_bits):
    collected = value[None]
    for bit_index in range(depth_bits):
        partner = swapped(collected, "leaf", bit_index)
        upper_bit = self_index >> bit_index & 1
        collected = jnp.where(
            upper_bit == 1,
            jnp.concatenate([partner, collected], 0),
            jnp.concatenate([collected, partner], 0),
        )
    return collected


def spread_node_maps(own_block, self_index, height_count):
    entries = []
    for height in range(1, height_count + 1):
        owning = self_index & (1 << height) - 1 == 1 << height - 1
        entries.append(jnp.where(owning, own_block, jnp.zeros_like(own_block)))
    stacked = jnp.stack(entries)
    for bit_index in range(height_count):
        moving = stacked[bit_index:]
        partner = swapped(moving, "leaf", bit_index)
        heights = jnp.arange(bit_index + 1, height_count + 1, dtype=jnp.int32)
        anchor = jnp.left_shift(jnp.right_shift(self_index, heights), heights) + jnp.left_shift(
            jnp.int32(1), heights - 1
        )
        taking = jnp.right_shift(jnp.bitwise_xor(self_index, anchor), bit_index) == 1
        updated = jnp.where(taking[:, None, None], partner, moving)
        stacked = jnp.concatenate([stacked[:bit_index], updated], 0)
    return stacked


def body(
    right_sides,
    point_order,
    leaf_inverse,
    basis_in,
    basis_out,
    leaf_up,
    leaf_down,
    node_up,
    node_down,
    node_cross,
    leaf_map,
):
    members = lax.axis_size("leaf")
    levels = members.bit_length() - 1
    depth_bits = SPREAD.bit_length() - 1
    self_index = lax.axis_index("leaf")
    rank_rows = leaf_up.shape[0]
    ordering = point_order[0]
    tree_rhs = jnp.take(right_sides, ordering, axis=1)
    near = jnp.dot(tree_rhs, leaf_inverse, preferred_element_type=jnp.float32)
    reduced = jnp.dot(tree_rhs, basis_in, preferred_element_type=jnp.float32).astype(jnp.bfloat16)
    slot_ids = jnp.arange(members, dtype=jnp.int32)
    source = jnp.sum(jnp.where(leaf_map == self_index, slot_ids, 0))
    position = jnp.sum(jnp.where(slot_ids == self_index, leaf_map, 0))
    collected = block_rise(reduced, self_index, depth_bits)
    node_g = lax.dynamic_index_in_dim(collected, source % SPREAD, 0, keepdims=False)
    own_block = jnp.concatenate([node_up, node_down, node_cross], 0)
    ancestry = spread_node_maps(own_block, self_index, levels)
    stored = []
    for height in range(1, levels + 1):
        if height == 1:
            child_up = leaf_up
        else:
            child_up = ancestry[height - 2, :rank_rows]
        product = jnp.dot(node_g, child_up, preferred_element_type=jnp.float32)
        payload = jnp.stack([node_g.astype(jnp.float32), product])
        partner = swapped(payload, "leaf", height - 1)
        stored.append(partner[0].astype(jnp.bfloat16))
        node_g = (product + partner[1]).astype(jnp.bfloat16)
    node_f = jnp.dot(
        node_g, ancestry[levels - 1, :rank_rows], preferred_element_type=jnp.float32
    ).astype(jnp.bfloat16)
    for height in range(levels, 0, -1):
        other_g = stored[height - 1]
        side_bit = self_index >> height - 1 & 1
        cross_rows = ancestry[height - 1, 2 * rank_rows :]
        coupling = jnp.where(side_bit == 0, cross_rows[:rank_rows], cross_rows[rank_rows:])
        if height == 1:
            child_down = leaf_down
        else:
            child_down = ancestry[height - 2, rank_rows : 2 * rank_rows]
        node_f = (
            jnp.dot(other_g, coupling, preferred_element_type=jnp.float32)
            + jnp.dot(node_f, child_down, preferred_element_type=jnp.float32)
        ).astype(jnp.bfloat16)
    collected_f = block_fall(node_f, self_index, depth_bits)
    leaf_f = lax.dynamic_index_in_dim(collected_f, position % SPREAD, 0, keepdims=False)
    answer = near + jnp.dot(leaf_f, basis_out, preferred_element_type=jnp.float32)
    return jnp.zeros_like(answer).at[:, ordering].set(answer)


def solution(mesh):
    placed = (
        P(None, "leaf"),
        P("leaf", None),
        P("leaf", None),
        P("leaf", None),
        P("leaf", None),
        P("leaf", None),
        P("leaf", None),
        P("leaf", None),
        P("leaf", None),
        P("leaf", None),
        P(),
    )
    return jax.shard_map(
        body, mesh=mesh, in_specs=placed, out_specs=P(None, "leaf"), check_vma=False
    )
```

profile of v0, /device:TPU:0, one launch (start us, length us, event | category | flops | bytes accessed | tf_op | source)
XLA Modules:
  0.0 172.8 jit_solution(11176966582685093510)
XLA Ops:
  0.0 1.3 select_dynamic-update-slice_fusion.4
  1.3 1.1 select_dynamic-update-slice_fusion.3
  2.4 1.1 select_dynamic-update-slice_fusion.2
  4.4 4.5 %collective-permute-done.3 = bf16[5,1024,256]{2,1,0:T(8,128)(2,1)S(1)} collective-permute-done((bf16[5,1024,256]{2,1,0:T(8,128)(2,1)S(1)}, bf16[5,1024,256]{2,1,0:T(8,128)(2,1)S(1)}, u32[]{:S(2)}, u32[]{:S(2)}) %collective-permute-start.3) | collective-permute-done | bytes 2621472 | tf_op jit(solution)/shard_map/ppermute | solution.py:16
  9.4 2.9 %collective-permute-start.5 = (bf16[4,1024,256]{2,1,0:T(8,128)(2,1)S(1)}, bf16[4,1024,256]{2,1,0:T(8,128)(2,1)S(1)}, u32[]{:S(2)}, u32[]{:S(2)}) collective-permute-start(bf16[4,1024,256]{2,1,0:T(8,128)(2,1)S(1)} %slice.242), channel_id=1, source_target_pairs={{0,2},{2,0},{1,3},{3,1},{4,6},{6,4},{5,7},{7,5},{8,10},{10,8},{9,1... | collective-permute-start | bytes 6291464 | tf_op jit(solution)/shard_map/ppermute | solution.py:16
  12.4 45.9 %collective-permute-done.5 = bf16[4,1024,256]{2,1,0:T(8,128)(2,1)S(1)} collective-permute-done((bf16[4,1024,256]{2,1,0:T(8,128)(2,1)S(1)}, bf16[4,1024,256]{2,1,0:T(8,128)(2,1)S(1)}, u32[]{:S(2)}, u32[]{:S(2)}) %collective-permute-start.5) | collective-permute-done | bytes 2097184 | tf_op jit(solution)/shard_map/ppermute | solution.py:16
  58.6 1.2 slice.248
  59.9 1.8 %collective-permute-start.7 = (bf16[3,1024,256]{2,1,0:T(8,128)(2,1)}, bf16[3,1024,256]{2,1,0:T(8,128)(2,1)}, u32[]{:S(2)}, u32[]{:S(2)}) collective-permute-start(bf16[3,1024,256]{2,1,0:T(8,128)(2,1)} %slice.248), channel_id=1, source_target_pairs={{0,4},{4,0},{1,5},{5,1},{2,6},{6,2},{3,7},{7,3},{8,12},{12,8},{9,1... | collective-permute-start | bytes 4718600 | tf_op jit(solution)/shard_map/ppermute | solution.py:16
  62.6 8.7 %gather_fusion = bf16[2048,32]{1,0:T(8,128)(2,1)} fusion(bf16[32,2048]{0,1:T(8,128)(2,1)} %copy.15, s32[2048]{0:T(1024)S(1)} %broadcast_clamp_fusion), kind=kCustom, calls=%fused_computation | custom fusion | bytes 270336 | tf_op jit(solution)/shard_map/jit(_take)/gather | solution.py:83
  71.4 2.0 %fusion.6 = bf16[1,32,256]{2,1,0:T(8,128)(2,1)S(1)} fusion(bf16[2048,256]{1,0:T(8,128)(2,1)} %param.14, bf16[2048,32]{1,0:T(8,128)(2,1)} %gather_fusion, pred[2048]{0:T(1024)(128)(4,1)S(1)} %compare_and_fusion), kind=kOutput, calls=%fused_computation.19 | convolution fusion | flops 33628160 | bytes 1198080 | tf_op jit(solution)/shard_map/dot_general | solution.py:85
  73.5 1.2 collective-permute-done
  74.6 1.6 collective-permute-start.1
  79.3 1.2 collective-permute-done.2
  81.5 1.1 collective-permute-start.4
  82.7 13.4 %collective-permute-done.7 = bf16[3,1024,256]{2,1,0:T(8,128)(2,1)} collective-permute-done((bf16[3,1024,256]{2,1,0:T(8,128)(2,1)}, bf16[3,1024,256]{2,1,0:T(8,128)(2,1)}, u32[]{:S(2)}, u32[]{:S(2)}) %collective-permute-start.7) | collective-permute-done | bytes 1572896 | tf_op jit(solution)/shard_map/ppermute | solution.py:16
  96.1 1.6 broadcast_select_fusion.2
  97.8 1.6 collective-permute-start.9
  99.6 1.5 collective-permute-start.6
  101.1 2.7 %collective-permute-done.6 = f32[2,32,256]{2,1,0:T(8,128)S(1)} collective-permute-done((f32[2,32,256]{2,1,0:T(8,128)S(1)}, f32[2,32,256]{2,1,0:T(8,128)S(1)}, u32[]{:S(2)}, u32[]{:S(2)}) %collective-permute-start.6) | collective-permute-done | bytes 65568 | tf_op jit(solution)/shard_map/ppermute | solution.py:16
  104.5 17.8 %collective-permute-done.9 = bf16[2,1024,256]{2,1,0:T(8,128)(2,1)S(1)} collective-permute-done((bf16[2,1024,256]{2,1,0:T(8,128)(2,1)S(1)}, bf16[2,1024,256]{2,1,0:T(8,128)(2,1)S(1)}, u32[]{:S(2)}, u32[]{:S(2)}) %collective-permute-start.9) | collective-permute-done | bytes 1048608 | tf_op jit(solution)/shard_map/ppermute | solution.py:16
  122.7 2.6 %collective-permute-start.11 = (bf16[1,1024,256]{2,1,0:T(8,128)(2,1)S(1)}, bf16[1,1024,256]{2,1,0:T(8,128)(2,1)S(1)}, u32[]{:S(2)}, u32[]{:S(2)}) collective-permute-start(bf16[1,1024,256]{2,1,0:T(8,128)(2,1)S(1)} %slice.260), channel_id=1, source_target_pairs={{0,16},{16,0},{1,17},{17,1},{2,18},{18,2},{3,19},{19,3},{4,20},{20... | collective-permute-start | bytes 1572872 | tf_op jit(solution)/shard_map/ppermute | solution.py:16
  125.4 1.1 collective-permute-start.10
  126.5 21.4 %collective-permute-done.11 = bf16[1,1024,256]{2,1,0:T(8,128)(2,1)S(1)} collective-permute-done((bf16[1,1024,256]{2,1,0:T(8,128)(2,1)S(1)}, bf16[1,1024,256]{2,1,0:T(8,128)(2,1)S(1)}, u32[]{:S(2)}, u32[]{:S(2)}) %collective-permute-start.11) | collective-permute-done | bytes 524320 | tf_op jit(solution)/shard_map/ppermute | solution.py:16
  148.8 1.3 fusion.7
  150.0 1.3 fusion.8
  151.4 1.2 fusion.9
  152.6 1.3 fusion.10
  153.9 1.2 fusion.11
  155.1 1.1 fusion.12
  156.2 1.2 collective-permute-done.12
  158.3 5.2 %fusion.15 = f32[32,2048]{1,0:T(8,128)S(1)} fusion(bf16[2048,2048]{1,0:T(8,128)(2,1)} %param.13, bf16[2048,32]{1,0:T(8,128)(2,1)} %gather_fusion, pred[2048]{0:T(1024)(128)(4,1)S(1)} %compare_and_fusion), kind=kOutput, calls=%fused_computation.37 | convolution fusion | flops 268500992 | bytes 8783872 | tf_op jit(solution)/shard_map/dot_general | solution.py:84
  165.9 5.8 %scatter_custom_fusion = f32[32,2048]{0,1:T(8,128)S(1)} fusion(s32[2048]{0:T(1024)S(1)} %bitcast.172, f32[2048,32]{1,0:T(8,128)S(1)} %copy.16, f32[]{:T(128)} %constant.31.clone.1), kind=kCustom, calls=%fused_computation.33 | custom fusion | bytes 262148 | tf_op jit(solution)/shard_map/scatter | solution.py:123
  (71 shorter events, 9.4 us)
Async XLA Ops:
  0.0 165.3 %copy-start = (bf16[256,2048]{1,0:T(8,128)(2,1)S(1)}, bf16[256,2048]{1,0:T(8,128)(2,1)}, u32[]{:S(2)}) copy-start(bf16[256,2048]{1,0:T(8,128)(2,1)} %param.15) | copy-start | bytes 3145732
  0.0 3.6 %copy-start.3 = (bf16[512,256]{1,0:T(8,128)(2,1)S(1)}, bf16[512,256]{1,0:T(8,128)(2,1)}, u32[]{:S(2)}) copy-start(bf16[512,256]{1,0:T(8,128)(2,1)} %param.20) | copy-start | bytes 786436
  0.0 3.6 %copy-start.5 = (bf16[256,256]{1,0:T(8,128)(2,1)S(1)}, bf16[256,256]{1,0:T(8,128)(2,1)}, u32[]{:S(2)}) copy-start(bf16[256,256]{1,0:T(8,128)(2,1)} %param.19) | copy-start | bytes 393220
  0.0 3.6 %copy-start.6 = (bf16[256,256]{1,0:T(8,128)(2,1)S(1)}, bf16[256,256]{1,0:T(8,128)(2,1)}, u32[]{:S(2)}) copy-start(bf16[256,256]{1,0:T(8,128)(2,1)} %param.18) | copy-start | bytes 393220
  3.8 5.1 %collective-permute-start.3 = (bf16[5,1024,256]{2,1,0:T(8,128)(2,1)S(1)}, bf16[5,1024,256]{2,1,0:T(8,128)(2,1)S(1)}, u32[]{:S(2)}, u32[]{:S(2)}) collective-permute-start(bf16[5,1024,256]{2,1,0:T(8,128)(2,1)S(1)} %select_dynamic-update-slice_fusion), channel_id=1, source_target_pairs={{0,1},{1,0},{2,3},{3,2},{4,5},{5,4},{6,7},{7,6},{8,9},{9,8},{10,11... | collective-permute-start | bytes 7864328 | tf_op jit(solution)/shard_map/ppermute | solution.py:16
  9.2 49.4 %copy-start.1 = (bf16[5,1024,256]{2,1,0:T(8,128)(2,1)}, bf16[5,1024,256]{2,1,0:T(8,128)(2,1)S(1)}, u32[]{:S(2)}) copy-start(bf16[5,1024,256]{2,1,0:T(8,128)(2,1)S(1)} %broadcast_select_fusion) | copy-start | bytes 7864324
  9.2 3.1 %copy-start.9 = (s32[1,2048]{1,0:T(1,128)S(1)}, s32[1,2048]{1,0:T(1,128)}, u32[]{:S(2)}) copy-start(s32[1,2048]{1,0:T(1,128)} %param.12) | copy-start | bytes 24580
  9.4 48.9 %collective-permute-start.5 = (bf16[4,1024,256]{2,1,0:T(8,128)(2,1)S(1)}, bf16[4,1024,256]{2,1,0:T(8,128)(2,1)S(1)}, u32[]{:S(2)}, u32[]{:S(2)}) collective-permute-start(bf16[4,1024,256]{2,1,0:T(8,128)(2,1)S(1)} %slice.242), channel_id=1, source_target_pairs={{0,2},{2,0},{1,3},{3,1},{4,6},{6,4},{5,7},{7,5},{8,10},{10,8},{9,1... | collective-permute-start | bytes 6291464 | tf_op jit(solution)/shard_map/ppermute | solution.py:16
  58.6 3.0 %copy-start.7 = (bf16[32,2048]{1,0:T(8,128)(2,1)S(1)}, bf16[32,2048]{1,0:T(8,128)(2,1)}, u32[]{:S(2)}) copy-start(bf16[32,2048]{1,0:T(8,128)(2,1)} %param.11) | copy-start | bytes 393220
  58.6 17.6 %copy-start.10 = (s32[32]{0:T(128)S(1)}, s32[32]{0:T(128)}, u32[]{:S(2)}) copy-start(s32[32]{0:T(128)} %param.21) | copy-start | bytes 388
  59.9 19.2 %copy-start.8 = (bf16[256,256]{1,0:T(8,128)(2,1)S(1)}, bf16[256,256]{1,0:T(8,128)(2,1)}, u32[]{:S(2)}) copy-start(bf16[256,256]{1,0:T(8,128)(2,1)} %param.16) | copy-start | bytes 393220
  59.9 36.2 %collective-permute-start.7 = (bf16[3,1024,256]{2,1,0:T(8,128)(2,1)}, bf16[3,1024,256]{2,1,0:T(8,128)(2,1)}, u32[]{:S(2)}, u32[]{:S(2)}) collective-permute-start(bf16[3,1024,256]{2,1,0:T(8,128)(2,1)} %slice.248), channel_id=1, source_target_pairs={{0,4},{4,0},{1,5},{5,1},{2,6},{6,2},{3,7},{7,3},{8,12},{12,8},{9,1... | collective-permute-start | bytes 4718600 | tf_op jit(solution)/shard_map/ppermute | solution.py:16
  73.4 1.2 collective-permute-start
  74.6 4.4 %collective-permute-start.1 = (bf16[2,32,256]{2,1,0:T(8,128)(2,1)S(1)}, bf16[2,32,256]{2,1,0:T(8,128)(2,1)S(1)}, u32[]{:S(2)}, u32[]{:S(2)}) collective-permute-start(bf16[2,32,256]{2,1,0:T(8,128)(2,1)S(1)} %maximum_select_fusion), channel_id=1, source_target_pairs={{0,2},{2,0},{1,3},{3,1},{4,6},{6,4},{5,7},{7,5},{8,10},{10,8},{9,1... | collective-permute-start | bytes 98312 | tf_op jit(solution)/shard_map/ppermute | solution.py:16
  79.2 1.3 collective-permute-start.2
  81.5 17.9 %collective-permute-start.4 = (f32[2,32,256]{2,1,0:T(8,128)S(1)}, f32[2,32,256]{2,1,0:T(8,128)S(1)}, u32[]{:S(2)}, u32[]{:S(2)}) collective-permute-start(f32[2,32,256]{2,1,0:T(8,128)S(1)} %pad_maximum_fusion.2), channel_id=1, source_target_pairs={{0,2},{2,0},{1,3},{3,1},{4,6},{6,4},{5,7},{7,5},{8,10},{10,8},{9,1... | collective-permute-start | bytes 196616 | tf_op jit(solution)/shard_map/ppermute | solution.py:16
  97.7 24.9 %copy-start.2 = (bf16[3,1024,256]{2,1,0:T(8,128)(2,1)}, bf16[3,1024,256]{2,1,0:T(8,128)(2,1)S(1)}, u32[]{:S(2)}) copy-start(bf16[3,1024,256]{2,1,0:T(8,128)(2,1)S(1)} %broadcast_select_fusion.2) | copy-start | bytes 4718596
  97.8 24.6 %collective-permute-start.9 = (bf16[2,1024,256]{2,1,0:T(8,128)(2,1)S(1)}, bf16[2,1024,256]{2,1,0:T(8,128)(2,1)S(1)}, u32[]{:S(2)}, u32[]{:S(2)}) collective-permute-start(bf16[2,1024,256]{2,1,0:T(8,128)(2,1)S(1)} %slice.254), channel_id=1, source_target_pairs={{0,8},{8,0},{1,9},{9,1},{2,10},{10,2},{3,11},{11,3},{4,12},{12,4},... | collective-permute-start | bytes 3145736 | tf_op jit(solution)/shard_map/ppermute | solution.py:16
  99.6 4.3 %collective-permute-start.6 = (f32[2,32,256]{2,1,0:T(8,128)S(1)}, f32[2,32,256]{2,1,0:T(8,128)S(1)}, u32[]{:S(2)}, u32[]{:S(2)}) collective-permute-start(f32[2,32,256]{2,1,0:T(8,128)S(1)} %pad_maximum_fusion.3), channel_id=1, source_target_pairs={{0,4},{4,0},{1,5},{5,1},{2,6},{6,2},{3,7},{7,3},{8,12},{12,8},{9,1... | collective-permute-start | bytes 196616 | tf_op jit(solution)/shard_map/ppermute | solution.py:16
  104.0 21.3 %collective-permute-start.8 = (f32[2,32,256]{2,1,0:T(8,128)S(1)}, f32[2,32,256]{2,1,0:T(8,128)S(1)}, u32[]{:S(2)}, u32[]{:S(2)}) collective-permute-start(f32[2,32,256]{2,1,0:T(8,128)S(1)} %pad_maximum_fusion.4), channel_id=1, source_target_pairs={{0,8},{8,0},{1,9},{9,1},{2,10},{10,2},{3,11},{11,3},{4,12},{12,4},... | collective-permute-start | bytes 196616 | tf_op jit(solution)/shard_map/ppermute | solution.py:16
  122.6 25.3 %copy-start.4 = (bf16[2,1024,256]{2,1,0:T(8,128)(2,1)}, bf16[2,1024,256]{2,1,0:T(8,128)(2,1)S(1)}, u32[]{:S(2)}) copy-start(bf16[2,1024,256]{2,1,0:T(8,128)(2,1)S(1)} %broadcast_select_fusion.3) | copy-start | bytes 3145732
  122.7 25.2 %collective-permute-start.11 = (bf16[1,1024,256]{2,1,0:T(8,128)(2,1)S(1)}, bf16[1,1024,256]{2,1,0:T(8,128)(2,1)S(1)}, u32[]{:S(2)}, u32[]{:S(2)}) collective-permute-start(bf16[1,1024,256]{2,1,0:T(8,128)(2,1)S(1)} %slice.260), channel_id=1, source_target_pairs={{0,16},{16,0},{1,17},{17,1},{2,18},{18,2},{3,19},{19,3},{4,20},{20... | collective-permute-start | bytes 1572872 | tf_op jit(solution)/shard_map/ppermute | solution.py:16
  125.4 23.4 %collective-permute-start.10 = (f32[2,32,256]{2,1,0:T(8,128)S(1)}, f32[2,32,256]{2,1,0:T(8,128)}, u32[]{:S(2)}, u32[]{:S(2)}) collective-permute-start(f32[2,32,256]{2,1,0:T(8,128)S(1)} %pad_maximum_fusion.5), channel_id=1, source_target_pairs={{0,16},{16,0},{1,17},{17,1},{2,18},{18,2},{3,19},{19,3},{4,20},{20... | collective-permute-start | bytes 196616 | tf_op jit(solution)/shard_map/ppermute | solution.py:16
  156.2 1.2 collective-permute-start.12
  157.4 7.8 %collective-permute-start.13 = (bf16[2,32,256]{2,1,0:T(8,128)(2,1)S(1)}, bf16[2,32,256]{2,1,0:T(8,128)(2,1)S(1)}, u32[]{:S(2)}, u32[]{:S(2)}) collective-permute-start(bf16[2,32,256]{2,1,0:T(8,128)(2,1)S(1)} %maximum_select_fusion.1), channel_id=1, source_target_pairs={{0,2},{2,0},{1,3},{3,1},{4,6},{6,4},{5,7},{7,5},{8,10},{10,8},{9,1... | collective-permute-start | bytes 98312 | tf_op jit(solution)/shard_map/ppermute | solution.py:16
where the time goes:
time: 173 us
  waiting for transfers between devices  109 us (63%)
  local copies, waits for them, and re-layouts  18.5 us (11%)
  matrix products  16.5 us (10%)
  starting transfers between devices  16.2 us (9%)
  other arithmetic  8 us (5%)
  between operations  4.17 us (2%)
    ppermute x14, waiting for transfers between devices, swapped(): return lax.ppermute(block, axis, route)  109 us
    ppermute x14, starting transfers between devices, swapped(): return lax.ppermute(block, axis, route)  16.2 us
    gather x1, local copies, waits for them, and re-layouts, body(): tree_rhs = jnp.take(right_sides, ordering, axis=1)  8.74 us
    scatter x2, local copies, waits for them, and re-layouts, body(): return jnp.zeros_like(answer).at[:, ordering].set(answer)  6.86 us
    dot_general x5, matrix products, body(): jnp.dot(node_f, child_down, preferred_element_type=jnp.float32)  6.3 us
    dot_general x1, matrix products, body(): near = jnp.dot(tree_rhs, leaf_inverse, preferred_element_type=jnp.float32)  5.23 us
    unnamed x4, other arithmetic  3.64 us
  transfers between devices with their start and end apart: 14, of which 9 were waited for; matrix products, arithmetic and copies ran while one was open for 13% of the time, Pallas kernels for 0%

commit v1 on v0

v1 whole, which is shorter than its diff:
```python
import functools

import jax
import jax.numpy as jnp
from jax import lax
from jax.experimental import pallas as pl
from jax.experimental.pallas import tpu as pltpu
from jax.sharding import PartitionSpec as P

SPREAD = 4
LANES = 128
BF = jnp.bfloat16
F32 = jnp.float32
VMEM = pl.BlockSpec(memory_space=pltpu.VMEM)
SMEM = pl.BlockSpec(memory_space=pltpu.SMEM)
ANY = pl.BlockSpec(memory_space=pl.ANY)
LIMIT = 32 * 2**20


def mm(a, b):
    return jnp.dot(a, b, preferred_element_type=F32)


def params():
    return pltpu.CompilerParams(vmem_limit_bytes=LIMIT)


def cost(flops, nbytes):
    return pl.CostEstimate(flops=flops, bytes_accessed=nbytes, transcendentals=0)


def swap(block, mask):
    count = lax.axis_size("leaf")
    return lax.ppermute(block, "leaf", [(i, i ^ mask) for i in range(count)])


def gather_columns(table, slots, store):
    rows, columns = table.shape
    tiles = columns // LANES
    for out_tile in range(tiles):
        slot = jnp.broadcast_to(slots(out_tile), (rows, LANES))
        low = slot & (LANES - 1)
        high = slot // LANES
        found = None
        for tile in range(tiles):
            part = jnp.take_along_axis(
                table[:, tile * LANES : (tile + 1) * LANES], low, axis=1
            )
            found = part if found is None else jnp.where(high == tile, part, found)
        store(out_tile, found)


def entry_kernel(rhs_hbm, order_hbm, basis_hbm, tree_ref, red_ref, rhs, order, basis, table, sems):
    copies = [
        pltpu.make_async_copy(rhs_hbm, rhs, sems.at[0]),
        pltpu.make_async_copy(order_hbm, order, sems.at[1]),
        pltpu.make_async_copy(basis_hbm, basis, sems.at[2]),
    ]
    for copy in copies:
        copy.start()
    copies[0].wait()
    table[...] = rhs[...].astype(F32)
    copies[1].wait()

    def store(tile, found):
        tree_ref[:, tile * LANES : (tile + 1) * LANES] = found.astype(BF)

    gather_columns(
        table, lambda tile: order[:, tile * LANES : (tile + 1) * LANES], store
    )
    copies[2].wait()
    red_ref[...] = mm(tree_ref[...], basis[...]).astype(BF)


def entry(right_sides, point_order, basis_in):
    rows, columns = right_sides.shape
    rank = basis_in.shape[1]
    return pl.pallas_call(
        entry_kernel,
        out_shape=(
            jax.ShapeDtypeStruct((rows, columns), BF),
            jax.ShapeDtypeStruct((rows, rank), BF),
        ),
        in_specs=[ANY] * 3,
        out_specs=(VMEM, VMEM),
        scratch_shapes=[
            pltpu.VMEM(right_sides.shape, BF),
            pltpu.VMEM(point_order.shape, jnp.int32),
            pltpu.VMEM(basis_in.shape, BF),
            pltpu.VMEM(right_sides.shape, F32),
            pltpu.SemaphoreType.DMA((3,)),
        ],
        compiler_params=params(),
        cost_estimate=cost(2 * rows * columns * rank, columns * rank * 2),
        name="entry",
    )(right_sides, point_order, basis_in)


def invert_kernel(order_ref, inv_ref):
    slot = order_ref[...]
    columns = slot.shape[1]
    tiles = columns // LANES
    low = slot & (LANES - 1)
    high = slot // LANES
    here = lax.broadcasted_iota(jnp.int32, (tiles, columns), 1)
    mask = lax.broadcasted_iota(jnp.int32, (tiles, columns), 0) == high
    left = jnp.concatenate(
        [
            jnp.where(mask, (here // LANES).astype(F32), 0.0),
            jnp.where(mask, (here & (LANES - 1)).astype(F32), 0.0),
        ],
        0,
    ).astype(BF)
    right = (lax.broadcasted_iota(jnp.int32, (LANES, columns), 0) == low).astype(F32).astype(BF)
    both = lax.dot_general(left, right, (((1,), (1,)), ((), ())), preferred_element_type=F32)
    inv_ref[...] = (both[:tiles] * LANES + both[tiles:]).astype(jnp.int32)


def invert(point_order):
    columns = point_order.shape[1]
    return pl.pallas_call(
        invert_kernel,
        out_shape=jax.ShapeDtypeStruct((columns // LANES, LANES), jnp.int32),
        in_specs=[VMEM],
        out_specs=VMEM,
        compiler_params=params(),
        cost_estimate=cost(2 * 32 * columns * LANES, columns * 4),
        name="invert",
    )(point_order)


def near_kernel(tree_ref, inverse_ref, near_ref):
    near_ref[...] = mm(tree_ref[...], inverse_ref[...])


def near_strip(tree, leaf_inverse, strip, strips):
    rows, columns = tree.shape
    width = columns // strips
    half = width // 2
    return pl.pallas_call(
        near_kernel,
        grid=(2,),
        out_shape=jax.ShapeDtypeStruct((rows, width), F32),
        in_specs=[
            pl.BlockSpec((rows, columns), lambda i: (0, 0)),
            pl.BlockSpec((columns, half), lambda i: (0, 2 * strip + i)),
        ],
        out_specs=pl.BlockSpec((rows, half), lambda i: (0, i)),
        compiler_params=params(),
        cost_estimate=cost(2 * rows * columns * width, columns * width * 2),
        name="near",
    )(tree, leaf_inverse)


def rise_kernel(pick, red0, red1, red2, red3, up0, up1, up2, up3, lvl_ref, g0_ref, g1_ref, near_ref, far_ref, table):
    rank = red0.shape[1]
    for m, red in enumerate((red0, red1, red2, red3)):
        table[m] = red[...]
    ups = (up0, up1, up2, up3)
    odd = pick[4] == 1
    sums = []
    for m in range(4):
        leaf = table[pick[m]]
        g0_ref[m] = leaf
        sums.append(mm(leaf, ups[m][:rank, :]))
    own = (sums[0] + sums[1]).astype(BF)
    other = (sums[2] + sums[3]).astype(BF)
    g1_ref[0] = own
    g1_ref[1] = other
    own_map = jnp.where(odd, up0[rank:, :], up1[rank:, :])
    other_map = jnp.where(odd, up2[rank:, :], up3[rank:, :])
    rows = red0.shape[0]
    g2 = (mm(own, own_map) + mm(other, other_map)).astype(BF)
    h2 = mm(g2, up2[rank:, :]).astype(BF)
    near_ref[:rows] = g2
    near_ref[rows:] = h2
    far_ref[:rows] = h2
    far_ref[rows:] = mm(h2, lvl_ref[:rank, :]).astype(BF)


def rise(pick, reds, ups, level_maps):
    rows, rank = reds[0].shape
    return pl.pallas_call(
        rise_kernel,
        out_shape=(
            jax.ShapeDtypeStruct((SPREAD, rows, rank), BF),
            jax.ShapeDtypeStruct((2, rows, rank), BF),
            jax.ShapeDtypeStruct((2 * rows, rank), BF),
            jax.ShapeDtypeStruct((2 * rows, rank), BF),
        ),
        in_specs=[SMEM] + [VMEM] * 9,
        out_specs=(VMEM,) * 4,
        scratch_shapes=[pltpu.VMEM((SPREAD, rows, rank), BF)],
        compiler_params=params(),
        cost_estimate=cost(2 * 8 * rows * rank * rank, 8 * rank * rank * 2),
        name="rise",
    )(pick, *reds, *ups, level_maps)


def pair_kernel(chain, *refs):
    mine, near, far, both, maps = refs[:5]
    following = refs[5 : 5 + chain]
    outs = refs[5 + chain :]
    rows = mine.shape[0] // 2
    rank = mine.shape[1]
    grown = (mine[rows:].astype(F32) + near[rows:].astype(F32)).astype(BF)
    outs[0][...] = (far[:rows].astype(F32) + both[:rows].astype(F32)).astype(BF)
    higher = mm(grown, maps[:rank, :]) + far[rows:].astype(F32) + both[rows:].astype(F32)
    higher = higher.astype(BF)
    if chain == 0:
        outs[1][...] = higher
        return
    sent = mm(higher, following[0][:rank, :]).astype(BF)
    outs[1][:rows] = higher
    outs[1][rows:] = sent
    if chain == 2:
        outs[2][:rows] = sent
        outs[2][rows:] = mm(sent, following[1][:rank, :]).astype(BF)


def pair(mine, near, far, both, maps, following):
    double, rank = mine.shape
    rows = double // 2
    single = jax.ShapeDtypeStruct((rows, rank), BF)
    twofold = jax.ShapeDtypeStruct((double, rank), BF)
    chain = len(following)
    shapes = {0: (single, single), 1: (single, twofold), 2: (single, twofold, twofold)}[chain]
    return pl.pallas_call(
        functools.partial(pair_kernel, chain),
        out_shape=shapes,
        in_specs=[VMEM] * (5 + chain),
        out_specs=(VMEM,) * len(shapes),
        compiler_params=params(),
        cost_estimate=cost(6 * rows * rank * rank, 6 * rank * rank),
        name="pair",
    )(mine, near, far, both, maps, *following)


def fall_kernel(count, *refs):
    top = refs[0]
    siblings = refs[1 : 1 + count]
    maps = refs[1 + count : 1 + 2 * count]
    block_down = refs[1 + 2 * count]
    out = refs[2 + 2 * count]
    rank = top.shape[1]
    value = mm(top[...], maps[count - 1][:rank, :]).astype(BF)
    for k in range(count - 1, -1, -1):
        down = block_down[...] if k == 0 else maps[k - 1][rank : 2 * rank, :]
        cross = maps[k][maps[k].shape[0] - rank :, :]
        value = (mm(siblings[k][...], cross) + mm(value, down)).astype(BF)
    out[...] = value


def fall(top, siblings, maps, block_down):
    count = len(maps)
    rows, rank = top.shape
    return pl.pallas_call(
        functools.partial(fall_kernel, count),
        out_shape=jax.ShapeDtypeStruct((rows, rank), BF),
        in_specs=[VMEM] * (2 + 2 * count),
        out_specs=VMEM,
        compiler_params=params(),
        cost_estimate=cost(12 * rows * rank * rank, 12 * rank * rank),
        name="fall",
    )(top, *siblings, *maps, block_down)


def local_kernel(pick, g0_ref, g1_ref, dn0, dn1, dn2, dn3, r1_ref, r0_ref, e1_ref, e0_ref, b2, b1, sems):
    rank = r0_ref.shape[0]
    packs = (dn0, dn1, dn2, dn3)

    def fetch(mask, row, dst, sem):
        start = pl.multiple_of(row, rank)
        for m in range(4):

            @pl.when(mask == m)
            def _():
                pltpu.make_async_copy(packs[m].at[pl.ds(start, rank), :], dst, sem).start()

    fetch(pick[5], 0, r0_ref, sems.at[0])
    fetch(pick[6], rank, r1_ref, sems.at[1])
    fetch(pick[6], (2 + pick[8]) * rank, b1, sems.at[2])
    fetch(pick[7], (2 + pick[9]) * rank, b2, sems.at[3])
    for i, dst in enumerate((r0_ref, r1_ref, b1, b2)):
        pltpu.make_async_copy(dn0.at[pl.ds(0, rank), :], dst, sems.at[i]).wait()
    e0_ref[...] = mm(g0_ref[pick[10]], b1[...])
    e1_ref[...] = mm(g1_ref[pick[11]], b2[...])


def local(pick, g0, g1, downs):
    _, rows, rank = g0.shape
    square = jax.ShapeDtypeStruct((rank, rank), BF)
    flat = jax.ShapeDtypeStruct((rows, rank), F32)
    return pl.pallas_call(
        local_kernel,
        out_shape=(square, square, flat, flat),
        in_specs=[SMEM, VMEM, VMEM] + [ANY] * 4,
        out_specs=(VMEM,) * 4,
        scratch_shapes=[
            pltpu.VMEM((rank, rank), BF),
            pltpu.VMEM((rank, rank), BF),
            pltpu.SemaphoreType.DMA((4,)),
        ],
        compiler_params=params(),
        cost_estimate=cost(4 * rows * rank * rank, 8 * rank * rank),
        name="local",
    )(pick, g0, g1, *downs)


def final_kernel(strips, f_ref, r1_ref, r0_ref, e1_ref, e0_ref, out_basis, inv_ref, *refs):
    nears = refs[:strips]
    answer, total = refs[strips:]
    f1 = (mm(f_ref[...], r1_ref[...]) + e1_ref[...]).astype(BF)
    f0 = (mm(f1, r0_ref[...]) + e0_ref[...]).astype(BF)
    width = nears[0].shape[1]
    for i in range(strips):
        span = slice(i * width, (i + 1) * width)
        total[:, span] = nears[i][...] + mm(f0, out_basis[:, span])

    def store(tile, found):
        answer[:, tile * LANES : (tile + 1) * LANES] = found

    gather_columns(total, lambda tile: inv_ref[tile : tile + 1, :], store)


def final(f2, r1, r0, e1, e0, basis_out, inverse_order, nears):
    rows, rank = f2.shape
    columns = basis_out.shape[1]
    return pl.pallas_call(
        functools.partial(final_kernel, len(nears)),
        out_shape=jax.ShapeDtypeStruct((rows, columns), F32),
        in_specs=[VMEM] * (7 + len(nears)),
        out_specs=VMEM,
        scratch_shapes=[pltpu.VMEM((rows, columns), F32)],
        compiler_params=params(),
        cost_estimate=cost(2 * rows * rank * columns, rank * columns * 2),
        name="final",
    )(f2, r1, r0, e1, e0, basis_out, inverse_order, *nears)


def body(
    right_sides,
    point_order,
    leaf_inverse,
    basis_in,
    basis_out,
    leaf_up,
    leaf_down,
    node_up,
    node_down,
    node_cross,
    leaf_map,
):
    members = lax.axis_size("leaf")
    levels = members.bit_length() - 1
    cut = SPREAD.bit_length() - 1
    me = lax.axis_index("leaf")
    rank = leaf_up.shape[1]
    offset = me & (SPREAD - 1)

    slots = jnp.arange(SPREAD, dtype=jnp.int32)
    block_map = lax.dynamic_slice(leaf_map, (me - offset,), (SPREAD,)) & (SPREAD - 1)
    wanted = slots ^ offset
    source = jnp.sum(jnp.where(block_map[None, :] == wanted[:, None], slots[None, :], 0), axis=1)
    seat = jnp.sum(jnp.where(slots == offset, block_map, 0))
    mask = seat ^ offset
    node = (seat | 1) ^ offset
    middle = offset ^ (SPREAD // 2)
    pick = jnp.concatenate(
        [
            source ^ offset,
            jnp.stack(
                [
                    offset & 1,
                    mask,
                    node,
                    middle,
                    seat & 1,
                    seat >> 1,
                    mask ^ 1,
                    1 - (mask >> 1),
                ]
            ),
        ]
    ).astype(jnp.int32)

    up_own = jnp.concatenate([leaf_up, node_up], 0)
    up_x = swap(up_own, 2)
    up_core = swap(up_own, 1)
    up_both = swap(up_x, 1)
    down_own = jnp.concatenate([leaf_down, node_down, node_cross], 0)

    level_maps = []
    for level in range(cut + 1, levels + 1):
        parts = [node_up] if level == levels else [node_up, node_down]
        first = jnp.concatenate(parts + [node_cross[:rank]], 0)
        second = jnp.concatenate(parts + [node_cross[rank:]], 0)
        half = 1 << (level - 1)
        arrived = lax.ppermute(
            first, "leaf", [(i + half, i) for i in range(0, members, 2 * half)]
        )
        held = jnp.where(me & half != 0, second, arrived)
        for bit in range(level - 2, cut - 1, -1):
            step = 1 << bit
            arrived = lax.ppermute(
                held, "leaf", [(i, i + step) for i in range(0, members, 2 * step)]
            )
            held = jnp.where(me & step != 0, arrived, held)
        level_maps.append(held)

    tree, reduced = entry(right_sides, point_order, basis_in)
    reds = [reduced] + [swap(reduced, m) for m in range(1, SPREAD)]
    strips = 4
    nears = [near_strip(tree, leaf_inverse, i, strips) for i in range(strips)]
    inverse_order = invert(point_order)

    down_x = swap(down_own, 2)
    down_core = swap(down_own, 1)
    down_both = swap(down_x, 1)

    g0, g1, near, far = rise(pick, reds, [up_own, up_core, up_x, up_both], level_maps[0])
    r1, r0, e1, e0 = local(pick, g0, g1, [down_own, down_core, down_x, down_both])
    rows = right_sides.shape[0]

    siblings = []
    bit = cut
    while bit < levels:
        low = 1 << bit
        near_in = swap(near, low)
        siblings.append(near_in[:rows])
        if bit + 1 < levels:
            far_in = swap(far, 2 * low)
            both_in = swap(far, 3 * low)
            after = bit + 2
            following = [level_maps[i - cut - 1] for i in (after, after + 1) if i < levels]
            results = pair(near, near_in, far_in, both_in, level_maps[bit + 1 - cut - 1], following)
            siblings.append(results[0])
            near = results[1]
            if len(results) == 3:
                far = results[2]
            top = near[:rows]
            bit += 2
        else:
            top = (near[rows:].astype(F32) + near_in[rows:].astype(F32)).astype(BF)
            bit += 1

    block_f = fall(top, siblings, level_maps, down_x[rank : 2 * rank])
    from_x = swap(block_f, 2)
    block_f = jnp.where(offset & 2 != 0, from_x, block_f)
    from_core = swap(block_f, 1)
    block_f = jnp.where(offset & 1 != 0, from_core, block_f)
    return final(block_f, r1, r0, e1, e0, basis_out, inverse_order, nears)


def solution(mesh):
    placed = (
        P(None, "leaf"),
        P("leaf", None),
        P("leaf", None),
        P("leaf", None),
        P("leaf", None),
        P("leaf", None),
        P("leaf", None),
        P("leaf", None),
        P("leaf", None),
        P("leaf", None),
        P(),
    )
    return jax.shard_map(
        body, mesh=mesh, in_specs=placed, out_specs=P(None, "leaf"), check_vma=False
    )
```

time: 173 us -> 70.4 us (0.41)
  waiting for transfers between devices: 109 us -> 8.73 us
  matrix products: 16.5 us -> 0 us
  Pallas kernels: 0 us -> 11.2 us
  starting transfers between devices: 16.2 us -> 23.1 us
  local copies, waits for them, and re-layouts: 18.5 us -> 16.1 us
    ppermute x14 -> x21, waiting for transfers between devices: 109 us -> 8.73 us  [the longest x15 7.83 us: swap(): return lax.ppermute(block, 'leaf', [(i, i ^ mask) for i in range(count)])]
    dot_general x14 -> x0, matrix products: 16.5 us -> none  [the longest x5 6.3 us: body(): jnp.dot(node_f, child_down, preferred_element_type=jnp.float32)]
    unnamed x23 -> x21, local copies, waits for them, and re-layouts: 1.06 us -> 13.1 us
    pallas_call x0 -> x11, Pallas kernels: none -> 11.2 us  [the longest x4 3.63 us: near_strip(): pl.pallas_call(near_kernel, grid=(2,), out_shape=jax.ShapeDtypeStruct((ro...]
    gather x1 -> x0, local copies, waits for them, and re-layouts: 8.74 us -> none  [body(): tree_rhs = jnp.take(right_sides, ordering, axis=1)]
    ppermute x14 -> x21, starting transfers between devices: 16.2 us -> 23.1 us  [the longest x3 10.5 us: body(): lax.ppermute(held, 'leaf', [(i, i + step) for i in range(0, members, 2 *...]
    scatter x2 -> x0, local copies, waits for them, and re-layouts: 6.86 us -> none  [body(): return jnp.zeros_like(answer).at[:, ordering].set(answer)]
    unnamed x4 -> x0, other arithmetic: 3.64 us -> none
  transfers between devices with their start and end apart: 14 -> 21, of which waited for: 9 -> 5; matrix products, arithmetic and copies ran while one was open for 13% -> 16% of each run, Pallas kernels for 0% -> 10%
where the time goes in v1:
time: 70.4 us; the launch traced here: 69.6 us
  starting transfers between devices  23.1 us (33%)
  local copies, waits for them, and re-layouts  16.1 us (23%)
  Pallas kernels  11.2 us (16%)
  waiting for transfers between devices  8.73 us (12%)
  other arithmetic  7.63 us (11%)
  between operations  2.94 us (4%)
    unnamed x21, local copies, waits for them, and re-layouts  13.1 us
    ppermute x3, starting transfers between devices, body(): lax.ppermute(held, 'leaf', [(i, i + step) for i in range(0, members, 2 *...  10.5 us
    ppermute x15, starting transfers between devices, swap(): return lax.ppermute(block, 'leaf', [(i, i ^ mask) for i in range(count)])  8.74 us
    ppermute x15, waiting for transfers between devices, swap(): return lax.ppermute(block, 'leaf', [(i, i ^ mask) for i in range(count)])  7.83 us
    ppermute x3, starting transfers between devices, body(): lax.ppermute(first, 'leaf', [(i + half, i) for i in range(0, members, 2 *...  3.88 us
    pallas_call x4, Pallas kernels, near_strip(): pl.pallas_call(near_kernel, grid=(2,), out_shape=jax.ShapeDtypeStruct((ro...  3.63 us
    select_n x2, other arithmetic, body(): held = jnp.where(me & half != 0, second, arrived)  3.05 us
    pallas_call x1, Pallas kernels, final(): pl.pallas_call(functools.partial(final_kernel, len(nears)), out_shape=jax...  2.57 us
  transfers between devices with their start and end apart: 21, of which 5 were waited for; matrix products, arithmetic and copies ran while one was open for 16% of the time, Pallas kernels for 10%

profile of v1, /device:TPU:0, one launch (start us, length us, event | category | flops | bytes accessed | tf_op | source)
XLA Modules:
  0.0 69.6 jit_solution(13595925988525081319)
XLA Ops:
  0.0 1.0 %fusion.2 = (bf16[256,256]{1,0:T(8,128)(2,1)S(1)}, bf16[256,256]{1,0:T(8,128)(2,1)S(1)}) fusion(bf16[512,256]{1,0:T(8,128)(2,1)} %param.20), kind=kLoop, calls=%fused_computation.25 | loop fusion | bytes 524288 | tf_op jit(solution)/shard_map/slice | solution.py:397
  1.0 1.0 %pad_maximum_fusion.2 = bf16[768,256]{1,0:T(8,128)(2,1)S(1)} fusion(bf16[256,256]{1,0:T(8,128)(2,1)S(1)} %get-tuple-element.34, bf16[256,256]{1,0:T(8,128)(2,1)} %param.19, bf16[256,256]{1,0:T(8,128)(2,1)} %param.18), kind=kLoop, calls=%fused_computation.2 | loop fusion | flops 1179648 | bytes 786432 | tf_op jit(solution)/shard_map/concatenate | solution.py:396
  2.0 1.3 %collective-permute-start.10 = (bf16[768,256]{1,0:T(8,128)(2,1)S(1)}, bf16[768,256]{1,0:T(8,128)(2,1)S(1)}, u32[]{:S(2)}, u32[]{:S(2)}) collective-permute-start(bf16[768,256]{1,0:T(8,128)(2,1)S(1)} %pad_maximum_fusion.2), channel_id=1, source_target_pairs={{8,0},{24,16}} | collective-permute-start | bytes 1179656 | tf_op jit(solution)/shard_map/ppermute | solution.py:399
  3.3 1.3 %collective-permute-start.6 = (bf16[768,256]{1,0:T(8,128)(2,1)S(1)}, bf16[768,256]{1,0:T(8,128)(2,1)S(1)}, u32[]{:S(2)}, u32[]{:S(2)}) collective-permute-start(bf16[768,256]{1,0:T(8,128)(2,1)S(1)} %pad_maximum_fusion.2), channel_id=1, source_target_pairs={{4,0},{12,8},{20,16},{28,24}} | collective-permute-start | bytes 1179656 | tf_op jit(solution)/shard_map/ppermute | solution.py:399
  4.6 1.2 %copy-done.2 = bf16[2048,256]{1,0:T(8,128)(2,1)S(1)} copy-done((bf16[2048,256]{1,0:T(8,128)(2,1)S(1)}, bf16[2048,256]{1,0:T(8,128)(2,1)}, u32[]{:S(2)}) %copy-start.2) | copy-done | bytes 1048600
  7.4 1.2 %entry.1 = (bf16[32,2048]{1,0:T(8,128)(2,1)S(1)}, bf16[32,256]{1,0:T(8,128)(2,1)S(1)}) custom-call(bf16[32,2048]{1,0:T(8,128)(2,1)S(1)} %copy-done.4, s32[1,2048]{1,0:T(1,128)S(1)} %copy-done.5, bf16[2048,256]{1,0:T(8,128)(2,1)S(1)} %copy-done.2), custom_call_target="tpu_custom_call" | custom-call | flops 33554432 | bytes 1048576 | tf_op jit(solution)/shard_map/entry/pallas_call | solution.py:78
  8.7 0.9 %constant_dynamic-update-slice_fusion.1 = bf16[512,256]{1,0:T(8,128)(2,1)S(1)} fusion(bf16[256,256]{1,0:T(8,128)(2,1)} %param.16), kind=kLoop, calls=%fused_computation.15 | loop fusion | bytes 262144
  9.6 0.9 %constant_dynamic-update-slice_fusion.up0 = bf16[512,256]{1,0:T(8,128)(2,1)S(1)} fusion(bf16[512,256]{1,0:T(8,128)(2,1)S(1)} %constant_dynamic-update-slice_fusion.1, bf16[256,256]{1,0:T(8,128)(2,1)} %param.18), kind=kLoop, calls=%fused_computation.14 | loop fusion | bytes 262144 | tf_op jit(solution)/shard_map/concatenate | solution.py:387
  10.5 1.8 %collective-permute-start.4 = (bf16[512,256]{1,0:T(8,128)(2,1)S(1)}, bf16[512,256]{1,0:T(8,128)(2,1)S(1)}, u32[]{:S(2)}, u32[]{:S(2)}) collective-permute-start(bf16[512,256]{1,0:T(8,128)(2,1)S(1)} %constant_dynamic-update-slice_fusion.up0), channel_id=1, source_target_pairs={{0,2},{1,3},{2,0},{3,1},{4,6},{5,7},{6,4},{7,5},{8,10},{9,11},{10,... | collective-permute-start | bytes 786440 | tf_op jit(solution)/shard_map/ppermute | solution.py:34
  12.3 0.9 %pad_maximum_fusion.3 = bf16[512,256]{1,0:T(8,128)(2,1)S(1)} fusion(bf16[256,256]{1,0:T(8,128)(2,1)} %param.18, bf16[256,256]{1,0:T(8,128)(2,1)S(1)} %get-tuple-element.34), kind=kLoop, calls=%fused_computation.6 | loop fusion | flops 524288 | bytes 524288 | tf_op jit(solution)/shard_map/concatenate | solution.py:396
  13.3 1.3 %collective-permute-start.13 = (bf16[512,256]{1,0:T(8,128)(2,1)S(1)}, bf16[512,256]{1,0:T(8,128)(2,1)S(1)}, u32[]{:S(2)}, u32[]{:S(2)}) collective-permute-start(bf16[512,256]{1,0:T(8,128)(2,1)S(1)} %pad_maximum_fusion.3), channel_id=1, source_target_pairs={{16,0}} | collective-permute-start | bytes 786440 | tf_op jit(solution)/shard_map/ppermute | solution.py:399
  14.6 0.9 %constant_dynamic-update-slice_fusion.4 = bf16[1024,256]{1,0:T(8,128)(2,1)S(1)} fusion(bf16[256,256]{1,0:T(8,128)(2,1)} %param.17), kind=kLoop, calls=%fused_computation.18 | loop fusion | bytes 262144
  15.5 0.9 %constant_dynamic-update-slice_fusion.3 = bf16[1024,256]{1,0:T(8,128)(2,1)S(1)} fusion(bf16[1024,256]{1,0:T(8,128)(2,1)S(1)} %constant_dynamic-update-slice_fusion.4, bf16[256,256]{1,0:T(8,128)(2,1)} %param.19), kind=kLoop, calls=%fused_computation.17 | loop fusion | bytes 262144
  16.4 1.0 %constant_dynamic-update-slice_fusion.2.dn0 = bf16[1024,256]{1,0:T(8,128)(2,1)S(1)} fusion(bf16[1024,256]{1,0:T(8,128)(2,1)S(1)} %constant_dynamic-update-slice_fusion.3, bf16[512,256]{1,0:T(8,128)(2,1)} %param.20), kind=kLoop, calls=%fused_computation.16 | loop fusion | bytes 524288 | tf_op jit(solution)/shard_map/concatenate | solution.py:391
  17.4 1.4 %fusion.1 = (s32[]{:T(128)}, s32[4]{0:T(128)S(1)}, s32[4]{0:T(128)S(1)}) fusion(s32[]{:T(128)S(6)} %and.29, s32[32]{0:T(128)} %param.21, s32[]{:T(128)S(6)} %select_n.65), kind=kLoop, calls=%fused_computation.21 | loop fusion | flops 19 | bytes 60 | tf_op jit(solution)/shard_map/reduce_sum | solution.py:365
  22.4 1.7 %fusion = bf16[512,256]{1,0:T(8,128)(2,1)} fusion(bf16[512,256]{1,0:T(8,128)(2,1)S(1)} %collective-permute-done.13, bf16[256,256]{1,0:T(8,128)(2,1)} %param.18, bf16[256,256]{1,0:T(8,128)(2,1)S(1)} %get-tuple-element.33, pred[]{:T(512)S(6)} %ne.22), kind=kLoop, calls=%fused_computation.8 | loop fusion | flops 655360 | bytes 786433 | tf_op jit(solution)/shard_map/jit(_where)/select_n | solution.py:402
  24.2 1.9 %collective-permute-done.1.red2 = bf16[32,256]{1,0:T(8,128)(2,1)S(1)} collective-permute-done((bf16[32,256]{1,0:T(8,128)(2,1)S(1)}, bf16[32,256]{1,0:T(8,128)(2,1)S(1)}, u32[]{:S(2)}, u32[]{:S(2)}) %collective-permute-start.1) | collective-permute-done | bytes 16416 | tf_op jit(solution)/shard_map/ppermute | solution.py:34
  26.3 4.5 %collective-permute-start.14 = (bf16[512,256]{1,0:T(8,128)(2,1)}, bf16[512,256]{1,0:T(8,128)(2,1)}, u32[]{:S(2)}, u32[]{:S(2)}) collective-permute-start(bf16[512,256]{1,0:T(8,128)(2,1)} %fusion), channel_id=1, source_target_pairs={{0,8},{16,24}} | collective-permute-start | bytes 786440 | tf_op jit(solution)/shard_map/ppermute | solution.py:405
  31.6 1.4 %broadcast_select_fusion = (bf16[768,256]{1,0:T(8,128)(2,1)S(1)}, bf16[768,256]{1,0:T(8,128)(2,1)S(1)}) fusion(bf16[768,256]{1,0:T(8,128)(2,1)} %copy-done.7, pred[]{:T(512)S(6)} %ne.21, bf16[256,256]{1,0:T(8,128)(2,1)S(1)} %get-tuple-element.33, bf16[256,256]{1,0:T(8,128)(2,1)} %param.19, bf16[256,256]{1,0:T(8,128)(2,1)} %param.18, ...), kind=kLoop, calls=%fused_computation.3 | loop fusion | flops 1572864 | bytes 1966082 | tf_op jit(solution)/shard_map/jit(_where)/select_n | solution.py:402
  33.0 2.1 %collective-permute-start.11 = (bf16[768,256]{1,0:T(8,128)(2,1)S(1)}, bf16[768,256]{1,0:T(8,128)(2,1)}, u32[]{:S(2)}, u32[]{:S(2)}) collective-permute-start(bf16[768,256]{1,0:T(8,128)(2,1)S(1)} %get-tuple-element.31), channel_id=1, source_target_pairs={{0,4},{8,12},{16,20},{24,28}} | collective-permute-start | bytes 1179656 | tf_op jit(solution)/shard_map/ppermute | solution.py:405
  35.1 1.1 %rise.1 = (bf16[4,32,256]{2,1,0:T(8,128)(2,1)S(1)}, bf16[2,32,256]{2,1,0:T(8,128)(2,1)S(1)}, bf16[64,256]{1,0:T(8,128)(2,1)S(1)}, bf16[64,256]{1,0:T(8,128)(2,1)S(1)}) custom-call(s32[12]{0:T(128)S(1)} %concatenate.23.pick, bf16[32,256]{1,0:T(8,128)(2,1)S(1)} %get-tuple-element.17.red0, bf16[32,256]{1,0:T(8,128)(2,1)S(1)} %collective-permute-done.red1, ...), custom_call_target="tpu_custom_call" | custom-call | flops 33554432 | bytes 1048576 | tf_op jit(solution)/shard_map/rise/pallas_call | solution.py:183
  36.3 1.0 %broadcast_select_fusion.3 = bf16[512,256]{1,0:T(8,128)(2,1)S(1)} fusion(bf16[512,256]{1,0:T(8,128)(2,1)} %collective-permute-done.14, bf16[512,256]{1,0:T(8,128)(2,1)} %fusion, pred[]{:T(512)S(6)} %ne.21), kind=kLoop, calls=%fused_computation.9 | loop fusion | flops 131072 | bytes 786433 | tf_op jit(solution)/shard_map/jit(_where)/select_n | solution.py:408
  37.3 3.9 %collective-permute-start.15 = (bf16[512,256]{1,0:T(8,128)(2,1)S(1)}, bf16[512,256]{1,0:T(8,128)(2,1)S(1)}, u32[]{:S(2)}, u32[]{:S(2)}) collective-permute-start(bf16[512,256]{1,0:T(8,128)(2,1)S(1)} %broadcast_select_fusion.3), channel_id=1, source_target_pairs={{0,4},{8,12},{16,20},{24,28}} | collective-permute-start | bytes 786440 | tf_op jit(solution)/shard_map/ppermute | solution.py:405
  41.3 2.0 %collective-permute-start.8 = (bf16[64,256]{1,0:T(8,128)(2,1)S(1)}, bf16[64,256]{1,0:T(8,128)(2,1)S(1)}, u32[]{:S(2)}, u32[]{:S(2)}) collective-permute-start(bf16[64,256]{1,0:T(8,128)(2,1)S(1)} %get-tuple-element.19), channel_id=1, source_target_pairs={{0,8},{1,9},{2,10},{3,11},{4,12},{5,13},{6,14},{7,15},{8,0},{9,1},... | collective-permute-start | bytes 98312 | tf_op jit(solution)/shard_map/ppermute | solution.py:34
  44.2 1.3 %collective-permute-done.8.refs_2_ = bf16[64,256]{1,0:T(8,128)(2,1)S(1)} collective-permute-done((bf16[64,256]{1,0:T(8,128)(2,1)S(1)}, bf16[64,256]{1,0:T(8,128)(2,1)S(1)}, u32[]{:S(2)}, u32[]{:S(2)}) %collective-permute-start.8) | collective-permute-done | bytes 32800 | tf_op jit(solution)/shard_map/ppermute | solution.py:34
  45.4 2.8 %collective-permute-done.9.refs_3_ = bf16[64,256]{1,0:T(8,128)(2,1)S(1)} collective-permute-done((bf16[64,256]{1,0:T(8,128)(2,1)S(1)}, bf16[64,256]{1,0:T(8,128)(2,1)S(1)}, u32[]{:S(2)}, u32[]{:S(2)}) %collective-permute-start.9) | collective-permute-done | bytes 32800 | tf_op jit(solution)/shard_map/ppermute | solution.py:34
  48.5 3.7 %collective-permute-start.12 = (bf16[64,256]{1,0:T(8,128)(2,1)S(1)}, bf16[64,256]{1,0:T(8,128)(2,1)S(1)}, u32[]{:S(2)}, u32[]{:S(2)}) collective-permute-start(bf16[64,256]{1,0:T(8,128)(2,1)S(1)} %get-tuple-element.20), channel_id=1, source_target_pairs={{0,16},{1,17},{2,18},{3,19},{4,20},{5,21},{6,22},{7,23},{8,24},{9,... | collective-permute-start | bytes 98312 | tf_op jit(solution)/shard_map/ppermute | solution.py:34
  52.2 1.9 %collective-permute-done.12 = bf16[64,256]{1,0:T(8,128)(2,1)S(1)} collective-permute-done((bf16[64,256]{1,0:T(8,128)(2,1)S(1)}, bf16[64,256]{1,0:T(8,128)(2,1)S(1)}, u32[]{:S(2)}, u32[]{:S(2)}) %collective-permute-start.12) | collective-permute-done | bytes 32800 | tf_op jit(solution)/shard_map/ppermute | solution.py:34
  54.6 3.4 %copy-done = bf16[2048,2048]{1,0:T(8,128)(2,1)S(1)} copy-done((bf16[2048,2048]{1,0:T(8,128)(2,1)S(1)}, bf16[2048,2048]{1,0:T(8,128)(2,1)}, u32[]{:S(2)}) %copy-start) | copy-done | bytes 8388632
  60.3 3.4 %copy-done.1 = bf16[2048,2048]{1,0:T(8,128)(2,1)S(1)} copy-done((bf16[2048,2048]{1,0:T(8,128)(2,1)S(1)}, bf16[2048,2048]{1,0:T(8,128)(2,1)}, u32[]{:S(2)}) %copy-start.1) | copy-done | bytes 8388632
  65.5 1.5 %local.1 = (bf16[256,256]{1,0:T(8,128)(2,1)S(1)}, bf16[256,256]{1,0:T(8,128)(2,1)S(1)}, f32[32,256]{1,0:T(8,128)S(1)}, f32[32,256]{1,0:T(8,128)S(1)}) custom-call(s32[12]{0:T(128)S(1)} %concatenate.23.pick, bf16[4,32,256]{2,1,0:T(8,128)(2,1)S(1)} %get-tuple-element.22.g0_ref, bf16[2,32,256]{2,1,0:T(8,128)(2,1)S(1)} %get-tuple-element.23.g1_ref, ...), custom_call_target="tpu_custom_call" | custom-call | flops 8388608 | bytes 524288 | tf_op jit(solution)/shard_map/local/pallas_call | solution.py:294
  67.1 2.6 %final.1 = f32[32,2048]{1,0:T(8,128)} custom-call(bf16[32,256]{1,0:T(8,128)(2,1)S(1)} %broadcast_select_fusion.6.f_ref, bf16[256,256]{1,0:T(8,128)(2,1)S(1)} %get-tuple-element.24.r1_ref, bf16[256,256]{1,0:T(8,128)(2,1)S(1)} %get-tuple-element.25.r0_ref, f32[32,256]{1,0:T(8,128)S(1)} %get-tuple-element.26.e1_ref, f32[32,256]{1,0:T(8,128)S(1)} %get-tuple-element.27.e0_ref, ...), custom_call_target="tpu_custom_call" | custom-call | flops 33554432 | bytes 1048576 | tf_op jit(solution)/shard_map/final/pallas_call | solution.py:329
  (62 shorter events, 9.8 us)
Async XLA Ops:
  2.0 24.3 %collective-permute-start.10 = (bf16[768,256]{1,0:T(8,128)(2,1)S(1)}, bf16[768,256]{1,0:T(8,128)(2,1)S(1)}, u32[]{:S(2)}, u32[]{:S(2)}) collective-permute-start(bf16[768,256]{1,0:T(8,128)(2,1)S(1)} %pad_maximum_fusion.2), channel_id=1, source_target_pairs={{8,0},{24,16}} | collective-permute-start | bytes 1179656 | tf_op jit(solution)/shard_map/ppermute | solution.py:399
  3.3 27.5 %collective-permute-start.6 = (bf16[768,256]{1,0:T(8,128)(2,1)S(1)}, bf16[768,256]{1,0:T(8,128)(2,1)S(1)}, u32[]{:S(2)}, u32[]{:S(2)}) collective-permute-start(bf16[768,256]{1,0:T(8,128)(2,1)S(1)} %pad_maximum_fusion.2), channel_id=1, source_target_pairs={{4,0},{12,8},{20,16},{28,24}} | collective-permute-start | bytes 1179656 | tf_op jit(solution)/shard_map/ppermute | solution.py:399
  4.6 1.2 %copy-start.2 = (bf16[2048,256]{1,0:T(8,128)(2,1)S(1)}, bf16[2048,256]{1,0:T(8,128)(2,1)}, u32[]{:S(2)}) copy-start(bf16[2048,256]{1,0:T(8,128)(2,1)} %basis_hbm.1) | copy-start | bytes 3145732
  5.8 0.9 %copy-start.4 = (bf16[32,2048]{1,0:T(8,128)(2,1)S(1)}, bf16[32,2048]{1,0:T(8,128)(2,1)}, u32[]{:S(2)}) copy-start(bf16[32,2048]{1,0:T(8,128)(2,1)} %rhs_hbm.1) | copy-start | bytes 393220
  6.7 0.7 %copy-start.5 = (s32[1,2048]{1,0:T(1,128)S(1)}, s32[1,2048]{1,0:T(1,128)}, u32[]{:S(2)}) copy-start(s32[1,2048]{1,0:T(1,128)} %order_ref.1) | copy-start | bytes 24580
  8.6 15.5 %collective-permute-start = (bf16[32,256]{1,0:T(8,128)(2,1)S(1)}, bf16[32,256]{1,0:T(8,128)(2,1)S(1)}, u32[]{:S(2)}, u32[]{:S(2)}) collective-permute-start(bf16[32,256]{1,0:T(8,128)(2,1)S(1)} %get-tuple-element.17.red0), channel_id=1, source_target_pairs={{0,1},{1,0},{2,3},{3,2},{4,5},{5,4},{6,7},{7,6},{8,9},{9,8},{10,11... | collective-permute-start | bytes 49160 | tf_op jit(solution)/shard_map/ppermute | solution.py:34
  10.5 15.7 %collective-permute-start.4 = (bf16[512,256]{1,0:T(8,128)(2,1)S(1)}, bf16[512,256]{1,0:T(8,128)(2,1)S(1)}, u32[]{:S(2)}, u32[]{:S(2)}) collective-permute-start(bf16[512,256]{1,0:T(8,128)(2,1)S(1)} %constant_dynamic-update-slice_fusion.up0), channel_id=1, source_target_pairs={{0,2},{1,3},{2,0},{3,1},{4,6},{5,7},{6,4},{7,5},{8,10},{9,11},{10,... | collective-permute-start | bytes 786440 | tf_op jit(solution)/shard_map/ppermute | solution.py:34
  13.3 9.2 %collective-permute-start.13 = (bf16[512,256]{1,0:T(8,128)(2,1)S(1)}, bf16[512,256]{1,0:T(8,128)(2,1)S(1)}, u32[]{:S(2)}, u32[]{:S(2)}) collective-permute-start(bf16[512,256]{1,0:T(8,128)(2,1)S(1)} %pad_maximum_fusion.3), channel_id=1, source_target_pairs={{16,0}} | collective-permute-start | bytes 786440 | tf_op jit(solution)/shard_map/ppermute | solution.py:399
  22.4 3.7 %collective-permute-start.1 = (bf16[32,256]{1,0:T(8,128)(2,1)S(1)}, bf16[32,256]{1,0:T(8,128)(2,1)S(1)}, u32[]{:S(2)}, u32[]{:S(2)}) collective-permute-start(bf16[32,256]{1,0:T(8,128)(2,1)S(1)} %get-tuple-element.17.red0), channel_id=1, source_target_pairs={{0,2},{1,3},{2,0},{3,1},{4,6},{5,7},{6,4},{7,5},{8,10},{9,11},{10,... | collective-permute-start | bytes 49160 | tf_op jit(solution)/shard_map/ppermute | solution.py:34
  24.1 8.8 %collective-permute-start.2 = (bf16[32,256]{1,0:T(8,128)(2,1)S(1)}, bf16[32,256]{1,0:T(8,128)(2,1)S(1)}, u32[]{:S(2)}, u32[]{:S(2)}) collective-permute-start(bf16[32,256]{1,0:T(8,128)(2,1)S(1)} %get-tuple-element.17.red0), channel_id=1, source_target_pairs={{0,3},{1,2},{2,1},{3,0},{4,7},{5,6},{6,5},{7,4},{8,11},{9,10},{10,... | collective-permute-start | bytes 49160 | tf_op jit(solution)/shard_map/ppermute | solution.py:34
  26.2 8.9 %collective-permute-start.3 = (bf16[512,256]{1,0:T(8,128)(2,1)S(1)}, bf16[512,256]{1,0:T(8,128)(2,1)S(1)}, u32[]{:S(2)}, u32[]{:S(2)}) collective-permute-start(bf16[512,256]{1,0:T(8,128)(2,1)S(1)} %constant_dynamic-update-slice_fusion.up0), channel_id=1, source_target_pairs={{0,1},{1,0},{2,3},{3,2},{4,5},{5,4},{6,7},{7,6},{8,9},{9,8},{10,11... | collective-permute-start | bytes 786440 | tf_op jit(solution)/shard_map/ppermute | solution.py:34
  26.3 15.0 %collective-permute-start.16 = (bf16[1024,256]{1,0:T(8,128)(2,1)S(1)}, bf16[1024,256]{1,0:T(8,128)(2,1)S(1)}, u32[]{:S(2)}, u32[]{:S(2)}) collective-permute-start(bf16[1024,256]{1,0:T(8,128)(2,1)S(1)} %constant_dynamic-update-slice_fusion.2.dn0), channel_id=1, source_target_pairs={{0,2},{1,3},{2,0},{3,1},{4,6},{5,7},{6,4},{7,5},{8,10},{9,11},{10,... | collective-permute-start | bytes 1572872 | tf_op jit(solution)/shard_map/ppermute | solution.py:34
  26.3 4.5 %copy-start.7 = (bf16[768,256]{1,0:T(8,128)(2,1)}, bf16[768,256]{1,0:T(8,128)(2,1)S(1)}, u32[]{:S(2)}) copy-start(bf16[768,256]{1,0:T(8,128)(2,1)S(1)} %collective-permute-done.10) | copy-start | bytes 1179652
  26.3 10.0 %collective-permute-start.14 = (bf16[512,256]{1,0:T(8,128)(2,1)}, bf16[512,256]{1,0:T(8,128)(2,1)}, u32[]{:S(2)}, u32[]{:S(2)}) collective-permute-start(bf16[512,256]{1,0:T(8,128)(2,1)} %fusion), channel_id=1, source_target_pairs={{0,8},{16,24}} | collective-permute-start | bytes 786440 | tf_op jit(solution)/shard_map/ppermute | solution.py:405
  30.8 0.8 %copy-start.8 = (bf16[768,256]{1,0:T(8,128)(2,1)}, bf16[768,256]{1,0:T(8,128)(2,1)S(1)}, u32[]{:S(2)}) copy-start(bf16[768,256]{1,0:T(8,128)(2,1)S(1)} %collective-permute-done.6) | copy-start | bytes 1179652
  31.6 3.6 %collective-permute-start.5 = (bf16[512,256]{1,0:T(8,128)(2,1)S(1)}, bf16[512,256]{1,0:T(8,128)(2,1)S(1)}, u32[]{:S(2)}, u32[]{:S(2)}) collective-permute-start(bf16[512,256]{1,0:T(8,128)(2,1)S(1)} %collective-permute-done.4.up2), channel_id=1, source_target_pairs={{0,1},{1,0},{2,3},{3,2},{4,5},{5,4},{6,7},{7,6},{8,9},{9,8},{10,11... | collective-permute-start | bytes 786440 | tf_op jit(solution)/shard_map/ppermute | solution.py:34
  33.0 11.1 %collective-permute-start.11 = (bf16[768,256]{1,0:T(8,128)(2,1)S(1)}, bf16[768,256]{1,0:T(8,128)(2,1)}, u32[]{:S(2)}, u32[]{:S(2)}) collective-permute-start(bf16[768,256]{1,0:T(8,128)(2,1)S(1)} %get-tuple-element.31), channel_id=1, source_target_pairs={{0,4},{8,12},{16,20},{24,28}} | collective-permute-start | bytes 1179656 | tf_op jit(solution)/shard_map/ppermute | solution.py:405
  36.2 7.1 %collective-permute-start.7 = (bf16[64,256]{1,0:T(8,128)(2,1)S(1)}, bf16[64,256]{1,0:T(8,128)(2,1)S(1)}, u32[]{:S(2)}, u32[]{:S(2)}) collective-permute-start(bf16[64,256]{1,0:T(8,128)(2,1)S(1)} %get-tuple-element.18.refs_0_), channel_id=1, source_target_pairs={{0,4},{1,5},{2,6},{3,7},{4,0},{5,1},{6,2},{7,3},{8,12},{9,13},{10,... | collective-permute-start | bytes 98312 | tf_op jit(solution)/shard_map/ppermute | solution.py:34
  37.3 14.9 %collective-permute-start.15 = (bf16[512,256]{1,0:T(8,128)(2,1)S(1)}, bf16[512,256]{1,0:T(8,128)(2,1)S(1)}, u32[]{:S(2)}, u32[]{:S(2)}) collective-permute-start(bf16[512,256]{1,0:T(8,128)(2,1)S(1)} %broadcast_select_fusion.3), channel_id=1, source_target_pairs={{0,4},{8,12},{16,20},{24,28}} | collective-permute-start | bytes 786440 | tf_op jit(solution)/shard_map/ppermute | solution.py:405
  41.2 24.3 %collective-permute-start.19 = (bf16[1024,256]{1,0:T(8,128)(2,1)S(1)}, bf16[1024,256]{1,0:T(8,128)(2,1)S(1)}, u32[]{:S(2)}, u32[]{:S(2)}) collective-permute-start(bf16[1024,256]{1,0:T(8,128)(2,1)S(1)} %constant_dynamic-update-slice_fusion.2.dn0), channel_id=1, source_target_pairs={{0,1},{1,0},{2,3},{3,2},{4,5},{5,4},{6,7},{7,6},{8,9},{9,8},{10,11... | collective-permute-start | bytes 1572872 | tf_op jit(solution)/shard_map/ppermute | solution.py:34
  41.3 4.1 %collective-permute-start.8 = (bf16[64,256]{1,0:T(8,128)(2,1)S(1)}, bf16[64,256]{1,0:T(8,128)(2,1)S(1)}, u32[]{:S(2)}, u32[]{:S(2)}) collective-permute-start(bf16[64,256]{1,0:T(8,128)(2,1)S(1)} %get-tuple-element.19), channel_id=1, source_target_pairs={{0,8},{1,9},{2,10},{3,11},{4,12},{5,13},{6,14},{7,15},{8,0},{9,1},... | collective-permute-start | bytes 98312 | tf_op jit(solution)/shard_map/ppermute | solution.py:34
  43.3 4.9 %collective-permute-start.9 = (bf16[64,256]{1,0:T(8,128)(2,1)S(1)}, bf16[64,256]{1,0:T(8,128)(2,1)S(1)}, u32[]{:S(2)}, u32[]{:S(2)}) collective-permute-start(bf16[64,256]{1,0:T(8,128)(2,1)S(1)} %get-tuple-element.19), channel_id=1, source_target_pairs={{0,12},{1,13},{2,14},{3,15},{4,8},{5,9},{6,10},{7,11},{8,4},{9,5},... | collective-permute-start | bytes 98312 | tf_op jit(solution)/shard_map/ppermute | solution.py:34
  44.1 21.4 %collective-permute-start.20 = (bf16[1024,256]{1,0:T(8,128)(2,1)S(1)}, bf16[1024,256]{1,0:T(8,128)(2,1)S(1)}, u32[]{:S(2)}, u32[]{:S(2)}) collective-permute-start(bf16[1024,256]{1,0:T(8,128)(2,1)S(1)} %collective-permute-done.16.dn2), channel_id=1, source_target_pairs={{0,1},{1,0},{2,3},{3,2},{4,5},{5,4},{6,7},{7,6},{8,9},{9,8},{10,11... | collective-permute-start | bytes 1572872 | tf_op jit(solution)/shard_map/ppermute | solution.py:34
  48.5 5.6 %collective-permute-start.12 = (bf16[64,256]{1,0:T(8,128)(2,1)S(1)}, bf16[64,256]{1,0:T(8,128)(2,1)S(1)}, u32[]{:S(2)}, u32[]{:S(2)}) collective-permute-start(bf16[64,256]{1,0:T(8,128)(2,1)S(1)} %get-tuple-element.20), channel_id=1, source_target_pairs={{0,16},{1,17},{2,18},{3,19},{4,20},{5,21},{6,22},{7,23},{8,24},{9,... | collective-permute-start | bytes 98312 | tf_op jit(solution)/shard_map/ppermute | solution.py:34
  54.6 4.3 %collective-permute-start.17 = (bf16[32,256]{1,0:T(8,128)(2,1)S(1)}, bf16[32,256]{1,0:T(8,128)(2,1)S(1)}, u32[]{:S(2)}, u32[]{:S(2)}) collective-permute-start(bf16[32,256]{1,0:T(8,128)(2,1)S(1)} %fall.1), channel_id=1, source_target_pairs={{0,2},{1,3},{2,0},{3,1},{4,6},{5,7},{6,4},{7,5},{8,10},{9,11},{10,... | collective-permute-start | bytes 49160 | tf_op jit(solution)/shard_map/ppermute | solution.py:34
  54.6 3.4 %copy-start = (bf16[2048,2048]{1,0:T(8,128)(2,1)S(1)}, bf16[2048,2048]{1,0:T(8,128)(2,1)}, u32[]{:S(2)}) copy-start(bf16[2048,2048]{1,0:T(8,128)(2,1)} %inverse_ref.7) | copy-start | bytes 25165828
  58.0 1.9 %copy-start.6 = (s32[1,2048]{1,0:T(1,128)S(1)}, s32[1,2048]{1,0:T(1,128)}, u32[]{:S(2)}) copy-start(s32[1,2048]{1,0:T(1,128)} %order_ref.1) | copy-start | bytes 24580
  59.0 6.5 %collective-permute-start.18 = (bf16[32,256]{1,0:T(8,128)(2,1)S(1)}, bf16[32,256]{1,0:T(8,128)(2,1)S(1)}, u32[]{:S(2)}, u32[]{:S(2)}) collective-permute-start(bf16[32,256]{1,0:T(8,128)(2,1)S(1)} %broadcast_select_fusion.5), channel_id=1, source_target_pairs={{0,1},{1,0},{2,3},{3,2},{4,5},{5,4},{6,7},{7,6},{8,9},{9,8},{10,11... | collective-permute-start | bytes 49160 | tf_op jit(solution)/shard_map/ppermute | solution.py:34
  60.3 3.4 %copy-start.1 = (bf16[2048,2048]{1,0:T(8,128)(2,1)S(1)}, bf16[2048,2048]{1,0:T(8,128)(2,1)}, u32[]{:S(2)}) copy-start(bf16[2048,2048]{1,0:T(8,128)(2,1)} %inverse_ref.7) | copy-start | bytes 25165828
  63.7 3.4 %copy-start.3 = (bf16[256,2048]{1,0:T(8,128)(2,1)S(1)}, bf16[256,2048]{1,0:T(8,128)(2,1)}, u32[]{:S(2)}) copy-start(bf16[256,2048]{1,0:T(8,128)(2,1)} %out_basis.1) | copy-start | bytes 3145732

commit v2 on v1

v2 whole, which is shorter than its diff:
```python
import functools

import jax
import jax.numpy as jnp
from jax import lax
from jax.experimental import pallas as pl
from jax.experimental.pallas import tpu as pltpu
from jax.sharding import PartitionSpec as P

SPREAD = 4
LANES = 128
BF = jnp.bfloat16
F32 = jnp.float32
VMEM = pl.BlockSpec(memory_space=pltpu.VMEM)
SMEM = pl.BlockSpec(memory_space=pltpu.SMEM)
ANY = pl.BlockSpec(memory_space=pl.ANY)
LIMIT = 32 * 2**20


def mm(a, b):
    return jnp.dot(a, b, preferred_element_type=F32)


def params():
    return pltpu.CompilerParams(vmem_limit_bytes=LIMIT)


def cost(flops, nbytes):
    return pl.CostEstimate(flops=flops, bytes_accessed=nbytes, transcendentals=0)


def swap(block, mask):
    count = lax.axis_size("leaf")
    return lax.ppermute(block, "leaf", [(i, i ^ mask) for i in range(count)])


def gather_columns(table, slots, store):
    rows, columns = table.shape
    tiles = columns // LANES
    for out_tile in range(tiles):
        slot = jnp.broadcast_to(slots(out_tile), (rows, LANES))
        low = slot & (LANES - 1)
        high = slot // LANES
        found = None
        for tile in range(tiles):
            part = jnp.take_along_axis(
                table[:, tile * LANES : (tile + 1) * LANES], low, axis=1
            )
            found = part if found is None else jnp.where(high == tile, part, found)
        store(out_tile, found)


def start_kernel(rhs_hbm, order_hbm, basis_hbm, map_hbm, leaf_down, node_up, node_down, node_cross,
                 pick, tree_ref, red_ref, down_ref, low_ref, high_ref, toplow_ref, tophigh_ref,
                 rhs, order, basis, table, seats, sems):
    rank = red_ref.shape[1]
    first = [
        pltpu.make_async_copy(rhs_hbm, rhs, sems.at[0]),
        pltpu.make_async_copy(order_hbm, order, sems.at[1]),
        pltpu.make_async_copy(map_hbm, seats, sems.at[2]),
        pltpu.make_async_copy(basis_hbm, basis, sems.at[3]),
    ]
    cross_low = node_cross.at[pl.ds(0, rank), :]
    cross_high = node_cross.at[pl.ds(rank, rank), :]
    packs = [
        (down_ref, (leaf_down, node_down, cross_low, cross_high)),
        (low_ref, (node_up, node_down, cross_low)),
        (high_ref, (node_up, node_down, cross_high)),
        (toplow_ref, (node_up, cross_low)),
        (tophigh_ref, (node_up, cross_high)),
    ]
    rest = []
    for dst, parts in packs:
        for i, part in enumerate(parts):
            rest.append(
                pltpu.make_async_copy(
                    part, dst.at[pl.ds(i * rank, rank), :], sems.at[4 + len(rest)]
                )
            )
    for copy in first + rest:
        copy.start()
    first[0].wait()
    table[...] = rhs[...].astype(F32)
    first[1].wait()

    def store(tile, found):
        tree_ref[:, tile * LANES : (tile + 1) * LANES] = found.astype(BF)

    gather_columns(
        table, lambda tile: order[:, tile * LANES : (tile + 1) * LANES], store
    )
    first[2].wait()
    me = lax.axis_index("leaf").astype(jnp.int32)
    offset = me & (SPREAD - 1)
    base = me - offset
    placed = [seats[base + slot] & (SPREAD - 1) for slot in range(SPREAD)]
    seat = placed[0]
    for slot in range(1, SPREAD):
        seat = jnp.where(offset == slot, placed[slot], seat)
    for m in range(SPREAD):
        source = jnp.int32(0)
        for slot in range(1, SPREAD):
            source = jnp.where(placed[slot] == (offset ^ m), slot, source)
        pick[m] = source ^ offset
    mask = seat ^ offset
    pick[4] = offset & 1
    pick[5] = mask
    pick[6] = (seat | 1) ^ offset
    pick[7] = offset ^ (SPREAD // 2)
    pick[8] = seat & 1
    pick[9] = seat // 2
    pick[10] = mask ^ 1
    pick[11] = 1 - mask // 2
    first[3].wait()
    red_ref[...] = mm(tree_ref[...], basis[...]).astype(BF)
    for copy in rest:
        copy.wait()


def start(right_sides, point_order, basis_in, leaf_map, leaf_down, node_up, node_down, node_cross):
    rows, columns = right_sides.shape
    rank = basis_in.shape[1]

    def block(count):
        return jax.ShapeDtypeStruct((count * rank, rank), BF)

    return pl.pallas_call(
        start_kernel,
        out_shape=(
            jax.ShapeDtypeStruct((12,), jnp.int32),
            jax.ShapeDtypeStruct((rows, columns), BF),
            jax.ShapeDtypeStruct((rows, rank), BF),
            block(4),
            block(3),
            block(3),
            block(2),
            block(2),
        ),
        in_specs=[ANY] * 8,
        out_specs=(SMEM,) + (VMEM,) * 7,
        scratch_shapes=[
            pltpu.VMEM(right_sides.shape, BF),
            pltpu.VMEM(point_order.shape, jnp.int32),
            pltpu.VMEM(basis_in.shape, BF),
            pltpu.VMEM(right_sides.shape, F32),
            pltpu.SMEM(leaf_map.shape, jnp.int32),
            pltpu.SemaphoreType.DMA((18,)),
        ],
        compiler_params=params(),
        cost_estimate=cost(2 * rows * columns * rank, columns * rank * 2),
        name="start",
    )(right_sides, point_order, basis_in, leaf_map, leaf_down, node_up, node_down, node_cross)


def invert_kernel(order_ref, inv_ref):
    slot = order_ref[...]
    columns = slot.shape[1]
    tiles = columns // LANES
    low = slot & (LANES - 1)
    high = slot // LANES
    here = lax.broadcasted_iota(jnp.int32, (tiles, columns), 1)
    mask = lax.broadcasted_iota(jnp.int32, (tiles, columns), 0) == high
    left = jnp.concatenate(
        [
            jnp.where(mask, (here // LANES).astype(F32), 0.0),
            jnp.where(mask, (here & (LANES - 1)).astype(F32), 0.0),
        ],
        0,
    ).astype(BF)
    right = (lax.broadcasted_iota(jnp.int32, (LANES, columns), 0) == low).astype(F32).astype(BF)
    both = lax.dot_general(left, right, (((1,), (1,)), ((), ())), preferred_element_type=F32)
    inv_ref[...] = (both[:tiles] * LANES + both[tiles:]).astype(jnp.int32)


def invert(point_order):
    columns = point_order.shape[1]
    return pl.pallas_call(
        invert_kernel,
        out_shape=jax.ShapeDtypeStruct((columns // LANES, LANES), jnp.int32),
        in_specs=[VMEM],
        out_specs=VMEM,
        compiler_params=params(),
        cost_estimate=cost(2 * 32 * columns * LANES, columns * 4),
        name="invert",
    )(point_order)


def near_kernel(tree_ref, inverse_ref, after, near_ref):
    near_ref[...] = mm(tree_ref[...], inverse_ref[...])


def near_strip(tree, leaf_inverse, strip, strips, after):
    rows, columns = tree.shape
    width = columns // strips
    half = width // 2
    return pl.pallas_call(
        near_kernel,
        grid=(2,),
        out_shape=jax.ShapeDtypeStruct((rows, width), F32),
        in_specs=[
            pl.BlockSpec((rows, columns), lambda i: (0, 0)),
            pl.BlockSpec((columns, half), lambda i: (0, 2 * strip + i)),
            ANY,
        ],
        out_specs=pl.BlockSpec((rows, half), lambda i: (0, i)),
        compiler_params=params(),
        cost_estimate=cost(2 * rows * columns * width, columns * width * 2),
        name="near",
    )(tree, leaf_inverse, after)


def leaf_kernel(pick, red0, red1, red2, red3, up_ref, g0_ref, out_ref, table):
    for m, red in enumerate((red0, red1, red2, red3)):
        table[m] = red[...]
    for m in range(SPREAD):
        g0_ref[m] = table[pick[m]]
    out_ref[...] = mm(g0_ref[0], up_ref[...])


def leaf_rise(pick, reds, leaf_up):
    rows, rank = reds[0].shape
    return pl.pallas_call(
        leaf_kernel,
        out_shape=(
            jax.ShapeDtypeStruct((SPREAD, rows, rank), BF),
            jax.ShapeDtypeStruct((rows, rank), F32),
        ),
        in_specs=[SMEM] + [VMEM] * 5,
        out_specs=(VMEM,) * 2,
        scratch_shapes=[pltpu.VMEM((SPREAD, rows, rank), BF)],
        compiler_params=params(),
        cost_estimate=cost(2 * rows * rank * rank, rank * rank * 2),
        name="leaf_rise",
    )(pick, *reds, leaf_up)


def node_kernel(pick, mine, other, up_own, up_other, out_ref):
    rows = mine.shape[0]
    odd = pick[4] == 1
    g1 = (mine[...] + other[...]).astype(BF)
    out_ref[:rows] = g1
    node_map = jnp.where(odd, up_own[...], up_other[...])
    out_ref[rows:] = mm(g1, node_map).astype(BF)


def node_rise(pick, mine, other, up_own, up_other):
    rows, rank = mine.shape
    return pl.pallas_call(
        node_kernel,
        out_shape=jax.ShapeDtypeStruct((2 * rows, rank), BF),
        in_specs=[SMEM] + [VMEM] * 4,
        out_specs=VMEM,
        compiler_params=params(),
        cost_estimate=cost(2 * rows * rank * rank, rank * rank * 2),
        name="node_rise",
    )(pick, mine, other, up_own, up_other)


def block_kernel(mine, other, up_ref, level_ref, after, g1_ref, near_ref, far_ref):
    rows = mine.shape[0] // 2
    rank = mine.shape[1]
    g1_ref[0] = mine[:rows]
    g1_ref[1] = other[:rows]
    g2 = (mine[rows:].astype(F32) + other[rows:].astype(F32)).astype(BF)
    h2 = mm(g2, up_ref[...]).astype(BF)
    near_ref[:rows] = g2
    near_ref[rows:] = h2
    far_ref[:rows] = h2
    far_ref[rows:] = mm(h2, level_ref[:rank, :]).astype(BF)


def block_rise(mine, other, block_up, level_maps, after):
    double, rank = mine.shape
    rows = double // 2
    return pl.pallas_call(
        block_kernel,
        out_shape=(
            jax.ShapeDtypeStruct((2, rows, rank), BF),
            jax.ShapeDtypeStruct((double, rank), BF),
            jax.ShapeDtypeStruct((double, rank), BF),
        ),
        in_specs=[VMEM] * 4 + [ANY],
        out_specs=(VMEM,) * 3,
        compiler_params=params(),
        cost_estimate=cost(4 * rows * rank * rank, 2 * rank * rank * 2),
        name="block_rise",
    )(mine, other, block_up, level_maps, after)


def pair_kernel(chain, *refs):
    mine, near, far, both, maps = refs[:5]
    following = refs[5 : 5 + chain]
    outs = refs[6 + chain :]
    rows = mine.shape[0] // 2
    rank = mine.shape[1]
    grown = (mine[rows:].astype(F32) + near[rows:].astype(F32)).astype(BF)
    outs[0][...] = (far[:rows].astype(F32) + both[:rows].astype(F32)).astype(BF)
    higher = mm(grown, maps[:rank, :]) + far[rows:].astype(F32) + both[rows:].astype(F32)
    higher = higher.astype(BF)
    if chain == 0:
        outs[1][...] = higher
        return
    sent = mm(higher, following[0][:rank, :]).astype(BF)
    outs[1][:rows] = higher
    outs[1][rows:] = sent
    if chain == 2:
        outs[2][:rows] = sent
        outs[2][rows:] = mm(sent, following[1][:rank, :]).astype(BF)


def pair(mine, near, far, both, maps, following, after):
    double, rank = mine.shape
    rows = double // 2
    single = jax.ShapeDtypeStruct((rows, rank), BF)
    twofold = jax.ShapeDtypeStruct((double, rank), BF)
    chain = len(following)
    shapes = {0: (single, single), 1: (single, twofold), 2: (single, twofold, twofold)}[chain]
    return pl.pallas_call(
        functools.partial(pair_kernel, chain),
        out_shape=shapes,
        in_specs=[VMEM] * (5 + chain) + [ANY],
        out_specs=(VMEM,) * len(shapes),
        compiler_params=params(),
        cost_estimate=cost(6 * rows * rank * rank, 6 * rank * rank),
        name="pair",
    )(mine, near, far, both, maps, *following, after)


def fall_kernel(count, *refs):
    top = refs[0]
    siblings = refs[1 : 1 + count]
    maps = refs[1 + count : 1 + 2 * count]
    cut_maps, out = refs[1 + 2 * count], refs[3 + 2 * count]
    rank = top.shape[1]
    value = mm(top[...], maps[count - 1][:rank, :]).astype(BF)
    for k in range(count - 1, -1, -1):
        down = cut_maps if k == 0 else maps[k - 1]
        cross = maps[k][maps[k].shape[0] - rank :, :]
        value = (mm(siblings[k][...], cross) + mm(value, down[rank : 2 * rank, :])).astype(BF)
    out[...] = value


def fall(top, siblings, maps, cut_maps, after):
    count = len(maps)
    rows, rank = top.shape
    return pl.pallas_call(
        functools.partial(fall_kernel, count),
        out_shape=jax.ShapeDtypeStruct((rows, rank), BF),
        in_specs=[VMEM] * (2 + 2 * count) + [ANY],
        out_specs=VMEM,
        compiler_params=params(),
        cost_estimate=cost(12 * rows * rank * rank, 12 * rank * rank),
        name="fall",
    )(top, *siblings, *maps, cut_maps, after)


def step_kernel(flag, mine, other, sibling, maps, down_pack, after, out):
    rank = mine.shape[1]
    value = jnp.where(flag[0] != 0, other[...], mine[...])
    cross = maps[2 * rank :, :]
    out[...] = (mm(sibling[...], cross) + mm(value, down_pack[rank : 2 * rank, :])).astype(BF)


def step_down(flag, mine, other, sibling, maps, down_pack, after):
    rows, rank = mine.shape
    return pl.pallas_call(
        step_kernel,
        out_shape=jax.ShapeDtypeStruct((rows, rank), BF),
        in_specs=[SMEM] + [VMEM] * 5 + [ANY],
        out_specs=VMEM,
        compiler_params=params(),
        cost_estimate=cost(4 * rows * rank * rank, 4 * rank * rank),
        name="step_down",
    )(flag, mine, other, sibling, maps, down_pack, after)


def local_kernel(pick, g0_ref, g1_ref, dn0, dn1, dn2, dn3, r1_ref, r0_ref, e1_ref, e0_ref, b2, b1, sems):
    rank = r0_ref.shape[0]
    packs = (dn0, dn1, dn2, dn3)

    def fetch(mask, row, dst, sem):
        start = pl.multiple_of(row, rank)
        for m in range(4):

            @pl.when(mask == m)
            def _():
                pltpu.make_async_copy(packs[m].at[pl.ds(start, rank), :], dst, sem).start()

    fetch(pick[5], 0, r0_ref, sems.at[0])
    fetch(pick[6], rank, r1_ref, sems.at[1])
    fetch(pick[6], (2 + pick[8]) * rank, b1, sems.at[2])
    fetch(pick[7], (2 + pick[9]) * rank, b2, sems.at[3])
    for i, dst in enumerate((r0_ref, r1_ref, b1, b2)):
        pltpu.make_async_copy(dn0.at[pl.ds(0, rank), :], dst, sems.at[i]).wait()
    e0_ref[...] = mm(g0_ref[pick[10]], b1[...])
    e1_ref[...] = mm(g1_ref[pick[11]], b2[...])


def local(pick, g0, g1, downs):
    _, rows, rank = g0.shape
    square = jax.ShapeDtypeStruct((rank, rank), BF)
    flat = jax.ShapeDtypeStruct((rows, rank), F32)
    return pl.pallas_call(
        local_kernel,
        out_shape=(square, square, flat, flat),
        in_specs=[SMEM, VMEM, VMEM] + [ANY] * 4,
        out_specs=(VMEM,) * 4,
        scratch_shapes=[
            pltpu.VMEM((rank, rank), BF),
            pltpu.VMEM((rank, rank), BF),
            pltpu.SemaphoreType.DMA((4,)),
        ],
        compiler_params=params(),
        cost_estimate=cost(4 * rows * rank * rank, 8 * rank * rank),
        name="local",
    )(pick, g0, g1, *downs)


def final_kernel(strips, pick, f_own, f_core, r1_ref, r0_ref, e1_ref, e0_ref, out_basis, inv_ref, *refs):
    nears = refs[:strips]
    answer, total = refs[strips:]
    f2 = jnp.where(pick[4] == 1, f_core[...], f_own[...])
    f1 = (mm(f2, r1_ref[...]) + e1_ref[...]).astype(BF)
    f0 = (mm(f1, r0_ref[...]) + e0_ref[...]).astype(BF)
    width = nears[0].shape[1]
    for i in range(strips):
        span = slice(i * width, (i + 1) * width)
        total[:, span] = nears[i][...] + mm(f0, out_basis[:, span])

    def store(tile, found):
        answer[:, tile * LANES : (tile + 1) * LANES] = found

    gather_columns(total, lambda tile: inv_ref[tile : tile + 1, :], store)


def final(pick, f2, f2_core, r1, r0, e1, e0, basis_out, inverse_order, nears):
    rows, rank = f2.shape
    columns = basis_out.shape[1]
    return pl.pallas_call(
        functools.partial(final_kernel, len(nears)),
        out_shape=jax.ShapeDtypeStruct((rows, columns), F32),
        in_specs=[SMEM] + [VMEM] * (8 + len(nears)),
        out_specs=VMEM,
        scratch_shapes=[pltpu.VMEM((rows, columns), F32)],
        compiler_params=params(),
        cost_estimate=cost(2 * rows * rank * columns, rank * columns * 2),
        name="final",
    )(pick, f2, f2_core, r1, r0, e1, e0, basis_out, inverse_order, *nears)


def body(
    right_sides,
    point_order,
    leaf_inverse,
    basis_in,
    basis_out,
    leaf_up,
    leaf_down,
    node_up,
    node_down,
    node_cross,
    leaf_map,
):
    members = lax.axis_size("leaf")
    levels = members.bit_length() - 1
    cut = SPREAD.bit_length() - 1
    me = lax.axis_index("leaf")
    rows = right_sides.shape[0]
    offset = me & (SPREAD - 1)

    pick, tree, reduced, down_own, low, high, top_low, top_high = start(
        right_sides, point_order, basis_in, leaf_map, leaf_down, node_up, node_down, node_cross
    )
    reds = [reduced] + [swap(reduced, m) for m in range(1, SPREAD)]
    up_core = swap(node_up, 1)
    half = SPREAD // 2
    block_up = lax.ppermute(
        node_up, "leaf", [(i + half, i) for i in range(0, members, SPREAD)]
    )

    level_maps = []
    for level in range(cut + 1, levels + 1):
        first, second = (top_low, top_high) if level == levels else (low, high)
        span = 1 << (level - 1)
        arrived = lax.ppermute(
            first, "leaf", [(i + span, i) for i in range(0, members, 2 * span)]
        )
        held = jnp.where(me & span != 0, second, arrived)
        for bit in range(level - 2, cut, -1):
            step = 1 << bit
            arrived = lax.ppermute(
                held, "leaf", [(i, i + step) for i in range(0, members, 2 * step)]
            )
            held = jnp.where(me & step != 0, arrived, held)
        level_maps.append(held)

    inverse_order = invert(point_order)
    down_x = swap(down_own, 2)
    down_core = swap(down_own, 1)
    down_both = swap(down_x, 1)

    g0, product = leaf_rise(pick, reds, leaf_up)
    node_pay = node_rise(pick, product, swap(product, 1), node_up, up_core)
    node_in = swap(node_pay, 2)
    near0 = near_strip(tree, leaf_inverse, 0, 2, node_pay)
    g1, near, far = block_rise(node_pay, node_in, block_up, level_maps[0], near0)

    siblings = []
    bit = cut
    after = near0
    while bit < levels:
        step = 1 << bit
        near_in = swap(near, step)
        siblings.append(near_in[:rows])
        if bit + 1 < levels:
            far_in = swap(far, 2 * step)
            both_in = swap(far, 3 * step)
            if bit == cut:
                near1 = near_strip(tree, leaf_inverse, 1, 2, near)
                after = near1
            following = [level_maps[i - cut - 1] for i in (bit + 2, bit + 3) if i < levels]
            results = pair(near, near_in, far_in, both_in, level_maps[bit - cut], following, after)
            siblings.append(results[0])
            near = results[1]
            if len(results) == 3:
                far = results[2]
            top = near[:rows]
            bit += 2
        else:
            top = (near[rows:].astype(F32) + near_in[rows:].astype(F32)).astype(BF)
            bit += 1

    r1, r0, e1, e0 = local(pick, g0, g1, [down_own, down_core, down_x, down_both])
    cut_f = fall(top, siblings[1:], level_maps[1:], level_maps[0], e0)
    flag = (me >> cut & 1).astype(jnp.int32)[None]
    block_f = step_down(flag, cut_f, swap(cut_f, SPREAD), siblings[0], level_maps[0], down_x, inverse_order)
    from_x = swap(block_f, 2)
    block_f = jnp.where(offset & 2 != 0, from_x, block_f)
    return final(
        pick, block_f, swap(block_f, 1), r1, r0, e1, e0, basis_out, inverse_order, [near0, near1]
    )


def solution(mesh):
    placed = (
        P(None, "leaf"),
        P("leaf", None),
        P("leaf", None),
        P("leaf", None),
        P("leaf", None),
        P("leaf", None),
        P("leaf", None),
        P("leaf", None),
        P("leaf", None),
        P("leaf", None),
        P(),
    )
    return jax.shard_map(
        body, mesh=mesh, in_specs=placed, out_specs=P(None, "leaf"), check_vma=False
    )
```

time: 70.4 us -> 76.6 us (1.088)
  waiting for transfers between devices: 8.73 us -> 29.2 us
  other arithmetic: 7.63 us -> 1.15 us
  local copies, waits for them, and re-layouts: 16.1 us -> 10.6 us
  Pallas kernels: 11.2 us -> 14 us
  between operations: 2.94 us -> 0.26 us
  starting transfers between devices: 23.1 us -> 20.9 us
    ppermute x15 -> x16, waiting for transfers between devices: 7.83 us -> 28.8 us  [swap(): return lax.ppermute(block, 'leaf', [(i, i ^ mask) for i in range(count)])]
    ppermute x3 -> x1, starting transfers between devices: 10.5 us -> 3.62 us  [body(): lax.ppermute(held, 'leaf', [(i, i + step) for i in range(0, members, 2 *...]
    pallas_call x2 -> x5, Pallas kernels: 2.32 us -> 5.84 us  [the longest x1 3.69 us: start(): pl.pallas_call(start_kernel, out_shape=(jax.ShapeDtypeStruct((12,), jnp.i...]
    ppermute x15 -> x16, starting transfers between devices: 8.74 us -> 11.9 us  [swap(): return lax.ppermute(block, 'leaf', [(i, i ^ mask) for i in range(count)])]
    unnamed x21 -> x24, local copies, waits for them, and re-layouts: 13.1 us -> 10.5 us
    concatenate x3 -> x0, local copies, waits for them, and re-layouts: 1.97 us -> none  [the longest x1 0.97 us: body(): down_own = jnp.concatenate([leaf_down, node_down, node_cross], 0)]
    select_n x3 -> x2, other arithmetic: 3.06 us -> 1.11 us  [body(): held = jnp.where(me & span != 0, second, arrived)]
    concatenate x2 -> x0, other arithmetic: 1.92 us -> none  [body(): first = jnp.concatenate(parts + [node_cross[:rank]], 0)]
  transfers between devices with their start and end apart: 21 -> 21, of which waited for: 5 -> 11; matrix products, arithmetic and copies ran while one was open for 16% -> 2% of each run, Pallas kernels for 10% -> 7%
where the time goes in v2:
time: 76.6 us; the launch traced here: 76.1 us
  waiting for transfers between devices  29.2 us (38%)
  starting transfers between devices  20.9 us (27%)
  Pallas kernels  14 us (18%)
  local copies, waits for them, and re-layouts  10.6 us (14%)
  other arithmetic  1.15 us (2%)
    ppermute x16, waiting for transfers between devices, swap(): return lax.ppermute(block, 'leaf', [(i, i ^ mask) for i in range(count)])  28.8 us
    ppermute x16, starting transfers between devices, swap(): return lax.ppermute(block, 'leaf', [(i, i ^ mask) for i in range(count)])  11.9 us
    unnamed x24, local copies, waits for them, and re-layouts  10.5 us
    ppermute x3, starting transfers between devices, body(): lax.ppermute(first, 'leaf', [(i + span, i) for i in range(0, members, 2 *...  4.14 us
    pallas_call x1, Pallas kernels, start(): pl.pallas_call(start_kernel, out_shape=(jax.ShapeDtypeStruct((12,), jnp.i...  3.69 us
    ppermute x1, starting transfers between devices, body(): lax.ppermute(held, 'leaf', [(i, i + step) for i in range(0, members, 2 *...  3.62 us
    pallas_call x1, Pallas kernels, final(): pl.pallas_call(functools.partial(final_kernel, len(nears)), out_shape=jax...  3.1 us
    pallas_call x2, Pallas kernels, near_strip(): pl.pallas_call(near_kernel, grid=(2,), out_shape=jax.ShapeDtypeStruct((ro...  2.57 us
  transfers between devices with their start and end apart: 21, of which 11 were waited for; matrix products, arithmetic and copies ran while one was open for 2% of the time, Pallas kernels for 7%

profile of v2, /device:TPU:0, one launch (start us, length us, event | category | flops | bytes accessed | tf_op | source)
XLA Modules:
  0.0 76.1 jit_solution(12536960256804849765)
XLA Ops:
  0.0 1.2 %copy-done.2 = bf16[2048,256]{1,0:T(8,128)(2,1)S(1)} copy-done((bf16[2048,256]{1,0:T(8,128)(2,1)S(1)}, bf16[2048,256]{1,0:T(8,128)(2,1)}, u32[]{:S(2)}) %copy-start.2) | copy-done | bytes 1048600
  1.2 0.9 %copy-done.4 = bf16[512,256]{1,0:T(8,128)(2,1)S(1)} copy-done((bf16[512,256]{1,0:T(8,128)(2,1)S(1)}, bf16[512,256]{1,0:T(8,128)(2,1)}, u32[]{:S(2)}) %copy-start.4) | copy-done | bytes 262168
  2.2 0.9 %copy-done.6 = bf16[32,2048]{1,0:T(8,128)(2,1)S(1)} copy-done((bf16[32,2048]{1,0:T(8,128)(2,1)S(1)}, bf16[32,2048]{1,0:T(8,128)(2,1)}, u32[]{:S(2)}) %copy-start.6) | copy-done | bytes 131096
  6.2 3.7 %start.1 = (s32[12]{0:T(128)S(1)}, bf16[32,2048]{1,0:T(8,128)(2,1)S(1)}, bf16[32,256]{1,0:T(8,128)(2,1)S(1)}, bf16[1024,256]{1,0:T(8,128)(2,1)S(1)}, bf16[768,25...) custom-call(bf16[32,2048]{1,0:T(8,128)(2,1)S(1)} %copy-done.6, ...), custom_call_target="tpu_custom_call" | custom-call | flops 33554432 | bytes 1048576 | tf_op jit(solution)/shard_map/start/pallas_call | solution.py:127
  9.9 1.3 %collective-permute-start.11 = (bf16[768,256]{1,0:T(8,128)(2,1)S(1)}, bf16[768,256]{1,0:T(8,128)(2,1)S(1)}, u32[]{:S(2)}, u32[]{:S(2)}) collective-permute-start(bf16[768,256]{1,0:T(8,128)(2,1)S(1)} %get-tuple-element.28), channel_id=1, source_target_pairs={{8,0},{24,16}} | collective-permute-start | bytes 1179656 | tf_op jit(solution)/shard_map/ppermute | solution.py:485
  11.2 1.3 %collective-permute-start.7 = (bf16[768,256]{1,0:T(8,128)(2,1)S(1)}, bf16[768,256]{1,0:T(8,128)(2,1)}, u32[]{:S(2)}, u32[]{:S(2)}) collective-permute-start(bf16[768,256]{1,0:T(8,128)(2,1)S(1)} %get-tuple-element.28), channel_id=1, source_target_pairs={{4,0},{12,8},{20,16},{28,24}} | collective-permute-start | bytes 1179656 | tf_op jit(solution)/shard_map/ppermute | solution.py:485
  12.5 2.5 %collective-permute-start.16 = (bf16[1024,256]{1,0:T(8,128)(2,1)S(1)}, bf16[1024,256]{1,0:T(8,128)(2,1)S(1)}, u32[]{:S(2)}, u32[]{:S(2)}) collective-permute-start(bf16[1024,256]{1,0:T(8,128)(2,1)S(1)} %get-tuple-element.38.dn0), channel_id=1, source_target_pairs={{0,2},{1,3},{2,0},{3,1},{4,6},{5,7},{6,4},{7,5},{8,10},{9,11},{10,... | collective-permute-start | bytes 1572872 | tf_op jit(solution)/shard_map/ppermute | solution.py:34
  15.1 11.4 %collective-permute-done.2.red3 = bf16[32,256]{1,0:T(8,128)(2,1)S(1)} collective-permute-done((bf16[32,256]{1,0:T(8,128)(2,1)S(1)}, bf16[32,256]{1,0:T(8,128)(2,1)S(1)}, u32[]{:S(2)}, u32[]{:S(2)}) %collective-permute-start.2) | collective-permute-done | bytes 16416 | tf_op jit(solution)/shard_map/ppermute | solution.py:34
  26.5 1.3 %collective-permute-start.1 = (bf16[32,256]{1,0:T(8,128)(2,1)S(1)}, bf16[32,256]{1,0:T(8,128)(2,1)S(1)}, u32[]{:S(2)}, u32[]{:S(2)}) collective-permute-start(bf16[32,256]{1,0:T(8,128)(2,1)S(1)} %get-tuple-element.25.red0), channel_id=1, source_target_pairs={{0,2},{1,3},{2,0},{3,1},{4,6},{5,7},{6,4},{7,5},{8,10},{9,11},{10,... | collective-permute-start | bytes 49160 | tf_op jit(solution)/shard_map/ppermute | solution.py:34
  27.9 2.4 %collective-permute-done.1.red2 = bf16[32,256]{1,0:T(8,128)(2,1)S(1)} collective-permute-done((bf16[32,256]{1,0:T(8,128)(2,1)S(1)}, bf16[32,256]{1,0:T(8,128)(2,1)S(1)}, u32[]{:S(2)}, u32[]{:S(2)}) %collective-permute-start.1) | collective-permute-done | bytes 16416 | tf_op jit(solution)/shard_map/ppermute | solution.py:34
  30.3 1.2 %collective-permute-done.red1 = bf16[32,256]{1,0:T(8,128)(2,1)S(1)} collective-permute-done((bf16[32,256]{1,0:T(8,128)(2,1)S(1)}, bf16[32,256]{1,0:T(8,128)(2,1)S(1)}, u32[]{:S(2)}, u32[]{:S(2)}) %collective-permute-start) | collective-permute-done | bytes 16416 | tf_op jit(solution)/shard_map/ppermute | solution.py:34
  31.5 0.9 %copy-done.5 = bf16[256,256]{1,0:T(8,128)(2,1)S(1)} copy-done((bf16[256,256]{1,0:T(8,128)(2,1)S(1)}, bf16[256,256]{1,0:T(8,128)(2,1)}, u32[]{:S(2)}) %copy-start.5) | copy-done | bytes 131096
  33.2 1.0 %collective-permute-done.3.other = f32[32,256]{1,0:T(8,128)S(1)} collective-permute-done((f32[32,256]{1,0:T(8,128)S(1)}, f32[32,256]{1,0:T(8,128)S(1)}, u32[]{:S(2)}, u32[]{:S(2)}) %collective-permute-start.3) | collective-permute-done | bytes 32800 | tf_op jit(solution)/shard_map/ppermute | solution.py:34
  34.3 1.3 %collective-permute-start.6 = (bf16[256,256]{1,0:T(8,128)(2,1)}, bf16[256,256]{1,0:T(8,128)(2,1)S(1)}, u32[]{:S(2)}, u32[]{:S(2)}) collective-permute-start(bf16[256,256]{1,0:T(8,128)(2,1)} %up_own.1), channel_id=1, source_target_pairs={{2,0},{6,4},{10,8},{14,12},{18,16},{22,20},{26,24},{30,28}} | collective-permute-start | bytes 393224 | tf_op jit(solution)/shard_map/ppermute | solution.py:477
  35.6 1.1 %node_rise.1.after.mine = bf16[64,256]{1,0:T(8,128)(2,1)S(1)} custom-call(s32[12]{0:T(128)S(1)} %get-tuple-element.24.pick, f32[32,256]{1,0:T(8,128)S(1)} %get-tuple-element.26.mine, f32[32,256]{1,0:T(8,128)S(1)} %collective-permute-done.3.other, bf16[256,256]{1,0:T(8,128)(2,1)} %up_own.1, bf16[256,256]{1,0:T(8,128)(2,1)S(1)} %collective-permute-done.4.up_other), custom_call_target="tpu_custom_call" | custom-call | flops 4194304 | bytes 131072 | tf_op jit(solution)/shard_map/node_rise/pallas_call | solution.py:248
  36.7 3.4 %copy-done = bf16[2048,2048]{1,0:T(8,128)(2,1)S(1)} copy-done((bf16[2048,2048]{1,0:T(8,128)(2,1)S(1)}, bf16[2048,2048]{1,0:T(8,128)(2,1)}, u32[]{:S(2)}) %copy-start) | copy-done | bytes 8388632
  40.1 1.3 %near.2.after.refs_0_ = f32[32,1024]{1,0:T(8,128)S(1)} custom-call(bf16[32,2048]{1,0:T(8,128)(2,1)S(1)} %get-tuple-element.29.tree_ref, bf16[2048,2048]{1,0:T(8,128)(2,1)S(1)} %copy-done, bf16[64,256]{1,0:T(8,128)(2,1)S(1)} %node_rise.1.after.mine), custom_call_target="tpu_custom_call" | custom-call | flops 134217728 | bytes 4194304 | tf_op jit(solution)/shard_map/near/pallas_call | solution.py:196
  41.4 1.6 %collective-permute-start.13 = (bf16[512,256]{1,0:T(8,128)(2,1)S(1)}, bf16[512,256]{1,0:T(8,128)(2,1)S(1)}, u32[]{:S(2)}, u32[]{:S(2)}) collective-permute-start(bf16[512,256]{1,0:T(8,128)(2,1)S(1)} %get-tuple-element.35), channel_id=1, source_target_pairs={{16,0}} | collective-permute-start | bytes 786440 | tf_op jit(solution)/shard_map/ppermute | solution.py:485
  43.0 2.0 %collective-permute-start.5 = (bf16[64,256]{1,0:T(8,128)(2,1)S(1)}, bf16[64,256]{1,0:T(8,128)(2,1)S(1)}, u32[]{:S(2)}, u32[]{:S(2)}) collective-permute-start(bf16[64,256]{1,0:T(8,128)(2,1)S(1)} %node_rise.1.after.mine), channel_id=1, source_target_pairs={{0,2},{1,3},{2,0},{3,1},{4,6},{5,7},{6,4},{7,5},{8,10},{9,11},{10,... | collective-permute-start | bytes 98312 | tf_op jit(solution)/shard_map/ppermute | solution.py:34
  44.9 1.1 %broadcast_select_fusion = (bf16[768,256]{1,0:T(8,128)(2,1)S(1)}, bf16[768,256]{1,0:T(8,128)(2,1)S(1)}) fusion(bf16[768,256]{1,0:T(8,128)(2,1)S(1)} %get-tuple-element.27, bf16[768,256]{1,0:T(8,128)(2,1)S(1)} %collective-permute-done.11, pred[]{:T(512)S(6)} %ne.15, bf16[768,256]{1,0:T(8,128)(2,1)} %collective-permute-done.7, pred[]{:T(512)S(6)} %ne.14), kind=kLoop, calls=%fused_computation | loop fusion | flops 393216 | bytes 1966082 | tf_op jit(solution)/shard_map/jit(_where)/select_n | solution.py:488
  46.0 0.9 %collective-permute-done.5.other = bf16[64,256]{1,0:T(8,128)(2,1)S(1)} collective-permute-done((bf16[64,256]{1,0:T(8,128)(2,1)S(1)}, bf16[64,256]{1,0:T(8,128)(2,1)S(1)}, u32[]{:S(2)}, u32[]{:S(2)}) %collective-permute-start.5) | collective-permute-done | bytes 32800 | tf_op jit(solution)/shard_map/ppermute | solution.py:34
  47.3 2.7 %collective-permute-start.10 = (bf16[64,256]{1,0:T(8,128)(2,1)S(1)}, bf16[64,256]{1,0:T(8,128)(2,1)S(1)}, u32[]{:S(2)}, u32[]{:S(2)}) collective-permute-start(bf16[64,256]{1,0:T(8,128)(2,1)S(1)} %get-tuple-element.31), channel_id=1, source_target_pairs={{0,12},{1,13},{2,14},{3,15},{4,8},{5,9},{6,10},{7,11},{8,4},{9,5},... | collective-permute-start | bytes 98312 | tf_op jit(solution)/shard_map/ppermute | solution.py:34
  50.9 1.2 %collective-permute-done.10.refs_3_ = bf16[64,256]{1,0:T(8,128)(2,1)S(1)} collective-permute-done((bf16[64,256]{1,0:T(8,128)(2,1)S(1)}, bf16[64,256]{1,0:T(8,128)(2,1)S(1)}, u32[]{:S(2)}, u32[]{:S(2)}) %collective-permute-start.10) | collective-permute-done | bytes 32800 | tf_op jit(solution)/shard_map/ppermute | solution.py:34
  52.1 3.6 %collective-permute-start.14 = (bf16[512,256]{1,0:T(8,128)(2,1)S(1)}, bf16[512,256]{1,0:T(8,128)(2,1)S(1)}, u32[]{:S(2)}, u32[]{:S(2)}) collective-permute-start(bf16[512,256]{1,0:T(8,128)(2,1)S(1)} %broadcast_select_fusion.2), channel_id=1, source_target_pairs={{0,8},{16,24}} | collective-permute-start | bytes 786440 | tf_op jit(solution)/shard_map/ppermute | solution.py:491
  55.7 1.3 %near.3.refs_6_.refs_1_ = f32[32,1024]{1,0:T(8,128)S(1)} custom-call(bf16[32,2048]{1,0:T(8,128)(2,1)S(1)} %get-tuple-element.29.tree_ref, bf16[2048,2048]{1,0:T(8,128)(2,1)S(1)} %copy-done.1, bf16[64,256]{1,0:T(8,128)(2,1)S(1)} %get-tuple-element.30.after.refs_0_), custom_call_target="tpu_custom_call" | custom-call | flops 134217728 | bytes 4194304 | tf_op jit(solution)/shard_map/near/pallas_call | solution.py:196
  57.3 2.6 %collective-permute-start.12 = (bf16[64,256]{1,0:T(8,128)(2,1)S(1)}, bf16[64,256]{1,0:T(8,128)(2,1)S(1)}, u32[]{:S(2)}, u32[]{:S(2)}) collective-permute-start(bf16[64,256]{1,0:T(8,128)(2,1)S(1)} %get-tuple-element.32), channel_id=1, source_target_pairs={{0,16},{1,17},{2,18},{3,19},{4,20},{5,21},{6,22},{7,23},{8,24},{9,... | collective-permute-start | bytes 98312 | tf_op jit(solution)/shard_map/ppermute | solution.py:34
  59.9 2.2 %collective-permute-done.12 = bf16[64,256]{1,0:T(8,128)(2,1)S(1)} collective-permute-done((bf16[64,256]{1,0:T(8,128)(2,1)S(1)}, bf16[64,256]{1,0:T(8,128)(2,1)S(1)}, u32[]{:S(2)}, u32[]{:S(2)}) %collective-permute-start.12) | collective-permute-done | bytes 32800 | tf_op jit(solution)/shard_map/ppermute | solution.py:34
  62.2 1.5 %local.1 = (bf16[256,256]{1,0:T(8,128)(2,1)S(1)}, bf16[256,256]{1,0:T(8,128)(2,1)S(1)}, f32[32,256]{1,0:T(8,128)S(1)}, f32[32,256]{1,0:T(8,128)S(1)}) custom-call(s32[12]{0:T(128)S(1)} %get-tuple-element.24.pick, bf16[4,32,256]{2,1,0:T(8,128)(2,1)S(1)} %get-tuple-element.36.g0_ref, bf16[2,32,256]{2,1,0:T(8,128)(2,1)S(1)} %get-tuple-element.37.g1_ref, ...), custom_call_target="tpu_custom_call" | custom-call | flops 8388608 | bytes 524288 | tf_op jit(solution)/shard_map/local/pallas_call | solution.py:403
  64.5 3.4 %collective-permute-done.18.other = bf16[32,256]{1,0:T(8,128)(2,1)S(1)} collective-permute-done((bf16[32,256]{1,0:T(8,128)(2,1)S(1)}, bf16[32,256]{1,0:T(8,128)(2,1)S(1)}, u32[]{:S(2)}, u32[]{:S(2)}) %collective-permute-start.18) | collective-permute-done | bytes 16416 | tf_op jit(solution)/shard_map/ppermute | solution.py:34
  68.1 3.7 %collective-permute-done.19 = bf16[32,256]{1,0:T(8,128)(2,1)S(1)} collective-permute-done((bf16[32,256]{1,0:T(8,128)(2,1)S(1)}, bf16[32,256]{1,0:T(8,128)(2,1)S(1)}, u32[]{:S(2)}, u32[]{:S(2)}) %collective-permute-start.19) | collective-permute-done | bytes 16416 | tf_op jit(solution)/shard_map/ppermute | solution.py:34
  71.8 1.2 %collective-permute-done.20.f_core = bf16[32,256]{1,0:T(8,128)(2,1)S(1)} collective-permute-done((bf16[32,256]{1,0:T(8,128)(2,1)S(1)}, bf16[32,256]{1,0:T(8,128)(2,1)S(1)}, u32[]{:S(2)}, u32[]{:S(2)}) %collective-permute-start.20) | collective-permute-done | bytes 16416 | tf_op jit(solution)/shard_map/ppermute | solution.py:34
  73.0 3.1 %final.1 = f32[32,2048]{1,0:T(8,128)} custom-call(s32[12]{0:T(128)S(1)} %get-tuple-element.24.pick, bf16[32,256]{1,0:T(8,128)(2,1)S(1)} %broadcast_select_fusion.4.f_own, bf16[32,256]{1,0:T(8,128)(2,1)S(1)} %collective-permute-done.20.f_core, bf16[256,256]{1,0:T(8,128)(2,1)S(1)} %get-tuple-element.40.r1_ref, bf16[256,256]{1,0:T(8,128)(2,1)S(1)} %get-tuple-element.41.r0_ref, ...), custom_call_target="tpu_custom_call" | custom-call | flops 33554432 | bytes 1048576 | tf_op jit(solution)/shard_map/final/pallas_call | solution.py:439
  (53 shorter events, 6.7 us)
Async XLA Ops:
  0.0 1.2 %copy-start.2 = (bf16[2048,256]{1,0:T(8,128)(2,1)S(1)}, bf16[2048,256]{1,0:T(8,128)(2,1)}, u32[]{:S(2)}) copy-start(bf16[2048,256]{1,0:T(8,128)(2,1)} %basis_hbm.1) | copy-start | bytes 3145732
  1.2 0.9 %copy-start.4 = (bf16[512,256]{1,0:T(8,128)(2,1)S(1)}, bf16[512,256]{1,0:T(8,128)(2,1)}, u32[]{:S(2)}) copy-start(bf16[512,256]{1,0:T(8,128)(2,1)} %node_cross.1) | copy-start | bytes 786436
  2.2 0.9 %copy-start.6 = (bf16[32,2048]{1,0:T(8,128)(2,1)S(1)}, bf16[32,2048]{1,0:T(8,128)(2,1)}, u32[]{:S(2)}) copy-start(bf16[32,2048]{1,0:T(8,128)(2,1)} %rhs_hbm.1) | copy-start | bytes 393220
  3.1 0.9 %copy-start.7 = (bf16[256,256]{1,0:T(8,128)(2,1)S(1)}, bf16[256,256]{1,0:T(8,128)(2,1)}, u32[]{:S(2)}) copy-start(bf16[256,256]{1,0:T(8,128)(2,1)} %leaf_down.1) | copy-start | bytes 393220
  4.0 0.9 %copy-start.8 = (bf16[256,256]{1,0:T(8,128)(2,1)S(1)}, bf16[256,256]{1,0:T(8,128)(2,1)}, u32[]{:S(2)}) copy-start(bf16[256,256]{1,0:T(8,128)(2,1)} %node_down.1) | copy-start | bytes 393220
  4.9 0.7 copy-start.9
  9.9 31.5 %collective-permute-start.11 = (bf16[768,256]{1,0:T(8,128)(2,1)S(1)}, bf16[768,256]{1,0:T(8,128)(2,1)S(1)}, u32[]{:S(2)}, u32[]{:S(2)}) collective-permute-start(bf16[768,256]{1,0:T(8,128)(2,1)S(1)} %get-tuple-element.28), channel_id=1, source_target_pairs={{8,0},{24,16}} | collective-permute-start | bytes 1179656 | tf_op jit(solution)/shard_map/ppermute | solution.py:485
  11.2 31.7 %collective-permute-start.7 = (bf16[768,256]{1,0:T(8,128)(2,1)S(1)}, bf16[768,256]{1,0:T(8,128)(2,1)}, u32[]{:S(2)}, u32[]{:S(2)}) collective-permute-start(bf16[768,256]{1,0:T(8,128)(2,1)S(1)} %get-tuple-element.28), channel_id=1, source_target_pairs={{4,0},{12,8},{20,16},{28,24}} | collective-permute-start | bytes 1179656 | tf_op jit(solution)/shard_map/ppermute | solution.py:485
  12.5 38.3 %collective-permute-start.16 = (bf16[1024,256]{1,0:T(8,128)(2,1)S(1)}, bf16[1024,256]{1,0:T(8,128)(2,1)S(1)}, u32[]{:S(2)}, u32[]{:S(2)}) collective-permute-start(bf16[1024,256]{1,0:T(8,128)(2,1)S(1)} %get-tuple-element.38.dn0), channel_id=1, source_target_pairs={{0,2},{1,3},{2,0},{3,1},{4,6},{5,7},{6,4},{7,5},{8,10},{9,11},{10,... | collective-permute-start | bytes 1572872 | tf_op jit(solution)/shard_map/ppermute | solution.py:34
  15.0 20.6 %collective-permute-start.4 = (bf16[256,256]{1,0:T(8,128)(2,1)}, bf16[256,256]{1,0:T(8,128)(2,1)S(1)}, u32[]{:S(2)}, u32[]{:S(2)}) collective-permute-start(bf16[256,256]{1,0:T(8,128)(2,1)} %up_own.1), channel_id=1, source_target_pairs={{0,1},{1,0},{2,3},{3,2},{4,5},{5,4},{6,7},{7,6},{8,9},{9,8},{10,11... | collective-permute-start | bytes 393224 | tf_op jit(solution)/shard_map/ppermute | solution.py:34
  15.0 11.5 %collective-permute-start.2 = (bf16[32,256]{1,0:T(8,128)(2,1)S(1)}, bf16[32,256]{1,0:T(8,128)(2,1)S(1)}, u32[]{:S(2)}, u32[]{:S(2)}) collective-permute-start(bf16[32,256]{1,0:T(8,128)(2,1)S(1)} %get-tuple-element.25.red0), channel_id=1, source_target_pairs={{0,3},{1,2},{2,1},{3,0},{4,7},{5,6},{6,5},{7,4},{8,11},{9,10},{10,... | collective-permute-start | bytes 49160 | tf_op jit(solution)/shard_map/ppermute | solution.py:34
  26.5 3.7 %collective-permute-start.1 = (bf16[32,256]{1,0:T(8,128)(2,1)S(1)}, bf16[32,256]{1,0:T(8,128)(2,1)S(1)}, u32[]{:S(2)}, u32[]{:S(2)}) collective-permute-start(bf16[32,256]{1,0:T(8,128)(2,1)S(1)} %get-tuple-element.25.red0), channel_id=1, source_target_pairs={{0,2},{1,3},{2,0},{3,1},{4,6},{5,7},{6,4},{7,5},{8,10},{9,11},{10,... | collective-permute-start | bytes 49160 | tf_op jit(solution)/shard_map/ppermute | solution.py:34
  30.3 1.2 %collective-permute-start = (bf16[32,256]{1,0:T(8,128)(2,1)S(1)}, bf16[32,256]{1,0:T(8,128)(2,1)S(1)}, u32[]{:S(2)}, u32[]{:S(2)}) collective-permute-start(bf16[32,256]{1,0:T(8,128)(2,1)S(1)} %get-tuple-element.25.red0), channel_id=1, source_target_pairs={{0,1},{1,0},{2,3},{3,2},{4,5},{5,4},{6,7},{7,6},{8,9},{9,8},{10,11... | collective-permute-start | bytes 49160 | tf_op jit(solution)/shard_map/ppermute | solution.py:34
  31.5 0.9 %copy-start.5 = (bf16[256,256]{1,0:T(8,128)(2,1)S(1)}, bf16[256,256]{1,0:T(8,128)(2,1)}, u32[]{:S(2)}) copy-start(bf16[256,256]{1,0:T(8,128)(2,1)} %up_ref.1) | copy-start | bytes 393220
  33.1 1.2 %collective-permute-start.3 = (f32[32,256]{1,0:T(8,128)S(1)}, f32[32,256]{1,0:T(8,128)S(1)}, u32[]{:S(2)}, u32[]{:S(2)}) collective-permute-start(f32[32,256]{1,0:T(8,128)S(1)} %get-tuple-element.26.mine), channel_id=1, source_target_pairs={{0,1},{1,0},{2,3},{3,2},{4,5},{5,4},{6,7},{7,6},{8,9},{9,8},{10,11... | collective-permute-start | bytes 98312 | tf_op jit(solution)/shard_map/ppermute | solution.py:34
  34.3 11.8 %collective-permute-start.6 = (bf16[256,256]{1,0:T(8,128)(2,1)}, bf16[256,256]{1,0:T(8,128)(2,1)S(1)}, u32[]{:S(2)}, u32[]{:S(2)}) collective-permute-start(bf16[256,256]{1,0:T(8,128)(2,1)} %up_own.1), channel_id=1, source_target_pairs={{2,0},{6,4},{10,8},{14,12},{18,16},{22,20},{26,24},{30,28}} | collective-permute-start | bytes 393224 | tf_op jit(solution)/shard_map/ppermute | solution.py:477
  35.6 26.6 %collective-permute-start.15 = (bf16[1024,256]{1,0:T(8,128)(2,1)S(1)}, bf16[1024,256]{1,0:T(8,128)(2,1)S(1)}, u32[]{:S(2)}, u32[]{:S(2)}) collective-permute-start(bf16[1024,256]{1,0:T(8,128)(2,1)S(1)} %get-tuple-element.38.dn0), channel_id=1, source_target_pairs={{0,1},{1,0},{2,3},{3,2},{4,5},{5,4},{6,7},{7,6},{8,9},{9,8},{10,11... | collective-permute-start | bytes 1572872 | tf_op jit(solution)/shard_map/ppermute | solution.py:34
  36.7 3.4 %copy-start = (bf16[2048,2048]{1,0:T(8,128)(2,1)S(1)}, bf16[2048,2048]{1,0:T(8,128)(2,1)}, u32[]{:S(2)}) copy-start(bf16[2048,2048]{1,0:T(8,128)(2,1)} %inverse_ref.3) | copy-start | bytes 25165828
  40.1 15.6 %copy-start.1 = (bf16[2048,2048]{1,0:T(8,128)(2,1)S(1)}, bf16[2048,2048]{1,0:T(8,128)(2,1)}, u32[]{:S(2)}) copy-start(bf16[2048,2048]{1,0:T(8,128)(2,1)} %inverse_ref.3) | copy-start | bytes 25165828
  41.4 9.4 %collective-permute-start.13 = (bf16[512,256]{1,0:T(8,128)(2,1)S(1)}, bf16[512,256]{1,0:T(8,128)(2,1)S(1)}, u32[]{:S(2)}, u32[]{:S(2)}) collective-permute-start(bf16[512,256]{1,0:T(8,128)(2,1)S(1)} %get-tuple-element.35), channel_id=1, source_target_pairs={{16,0}} | collective-permute-start | bytes 786440 | tf_op jit(solution)/shard_map/ppermute | solution.py:485
  43.0 4.0 %collective-permute-start.5 = (bf16[64,256]{1,0:T(8,128)(2,1)S(1)}, bf16[64,256]{1,0:T(8,128)(2,1)S(1)}, u32[]{:S(2)}, u32[]{:S(2)}) collective-permute-start(bf16[64,256]{1,0:T(8,128)(2,1)S(1)} %node_rise.1.after.mine), channel_id=1, source_target_pairs={{0,2},{1,3},{2,0},{3,1},{4,6},{5,7},{6,4},{7,5},{8,10},{9,11},{10,... | collective-permute-start | bytes 98312 | tf_op jit(solution)/shard_map/ppermute | solution.py:34
  44.9 19.2 %copy-start.10 = (s32[1,2048]{1,0:T(1,128)S(1)}, s32[1,2048]{1,0:T(1,128)}, u32[]{:S(2)}) copy-start(s32[1,2048]{1,0:T(1,128)} %order_ref.1) | copy-start | bytes 24580
  46.0 27.0 %copy-start.3 = (bf16[256,2048]{1,0:T(8,128)(2,1)S(1)}, bf16[256,2048]{1,0:T(8,128)(2,1)}, u32[]{:S(2)}) copy-start(bf16[256,2048]{1,0:T(8,128)(2,1)} %out_basis.1) | copy-start | bytes 3145732
  47.3 4.8 %collective-permute-start.10 = (bf16[64,256]{1,0:T(8,128)(2,1)S(1)}, bf16[64,256]{1,0:T(8,128)(2,1)S(1)}, u32[]{:S(2)}, u32[]{:S(2)}) collective-permute-start(bf16[64,256]{1,0:T(8,128)(2,1)S(1)} %get-tuple-element.31), channel_id=1, source_target_pairs={{0,12},{1,13},{2,14},{3,15},{4,8},{5,9},{6,10},{7,11},{8,4},{9,5},... | collective-permute-start | bytes 98312 | tf_op jit(solution)/shard_map/ppermute | solution.py:34
  49.9 7.1 %collective-permute-start.9 = (bf16[64,256]{1,0:T(8,128)(2,1)S(1)}, bf16[64,256]{1,0:T(8,128)(2,1)S(1)}, u32[]{:S(2)}, u32[]{:S(2)}) collective-permute-start(bf16[64,256]{1,0:T(8,128)(2,1)S(1)} %get-tuple-element.31), channel_id=1, source_target_pairs={{0,8},{1,9},{2,10},{3,11},{4,12},{5,13},{6,14},{7,15},{8,0},{9,1},... | collective-permute-start | bytes 98312 | tf_op jit(solution)/shard_map/ppermute | solution.py:34
  50.8 6.2 %collective-permute-start.8 = (bf16[64,256]{1,0:T(8,128)(2,1)S(1)}, bf16[64,256]{1,0:T(8,128)(2,1)S(1)}, u32[]{:S(2)}, u32[]{:S(2)}) collective-permute-start(bf16[64,256]{1,0:T(8,128)(2,1)S(1)} %get-tuple-element.30.after.refs_0_), channel_id=1, source_target_pairs={{0,4},{1,5},{2,6},{3,7},{4,0},{5,1},{6,2},{7,3},{8,12},{9,13},{10,... | collective-permute-start | bytes 98312 | tf_op jit(solution)/shard_map/ppermute | solution.py:34
  50.8 11.4 %collective-permute-start.17 = (bf16[1024,256]{1,0:T(8,128)(2,1)S(1)}, bf16[1024,256]{1,0:T(8,128)(2,1)S(1)}, u32[]{:S(2)}, u32[]{:S(2)}) collective-permute-start(bf16[1024,256]{1,0:T(8,128)(2,1)S(1)} %collective-permute-done.16.dn2.down_pack), channel_id=1, source_target_pairs={{0,1},{1,0},{2,3},{3,2},{4,5},{5,4},{6,7},{7,6},{8,9},{9,8},{10,11... | collective-permute-start | bytes 1572872 | tf_op jit(solution)/shard_map/ppermute | solution.py:34
  52.1 10.1 %collective-permute-start.14 = (bf16[512,256]{1,0:T(8,128)(2,1)S(1)}, bf16[512,256]{1,0:T(8,128)(2,1)S(1)}, u32[]{:S(2)}, u32[]{:S(2)}) collective-permute-start(bf16[512,256]{1,0:T(8,128)(2,1)S(1)} %broadcast_select_fusion.2), channel_id=1, source_target_pairs={{0,8},{16,24}} | collective-permute-start | bytes 786440 | tf_op jit(solution)/shard_map/ppermute | solution.py:491
  57.3 4.8 %collective-permute-start.12 = (bf16[64,256]{1,0:T(8,128)(2,1)S(1)}, bf16[64,256]{1,0:T(8,128)(2,1)S(1)}, u32[]{:S(2)}, u32[]{:S(2)}) collective-permute-start(bf16[64,256]{1,0:T(8,128)(2,1)S(1)} %get-tuple-element.32), channel_id=1, source_target_pairs={{0,16},{1,17},{2,18},{3,19},{4,20},{5,21},{6,22},{7,23},{8,24},{9,... | collective-permute-start | bytes 98312 | tf_op jit(solution)/shard_map/ppermute | solution.py:34
  64.2 3.8 %collective-permute-start.18 = (bf16[32,256]{1,0:T(8,128)(2,1)S(1)}, bf16[32,256]{1,0:T(8,128)(2,1)S(1)}, u32[]{:S(2)}, u32[]{:S(2)}) collective-permute-start(bf16[32,256]{1,0:T(8,128)(2,1)S(1)} %fall.1.mine), channel_id=1, source_target_pairs={{0,4},{1,5},{2,6},{3,7},{4,0},{5,1},{6,2},{7,3},{8,12},{9,13},{10,... | collective-permute-start | bytes 49160 | tf_op jit(solution)/shard_map/ppermute | solution.py:34
  68.1 3.7 %collective-permute-start.19 = (bf16[32,256]{1,0:T(8,128)(2,1)S(1)}, bf16[32,256]{1,0:T(8,128)(2,1)S(1)}, u32[]{:S(2)}, u32[]{:S(2)}) collective-permute-start(bf16[32,256]{1,0:T(8,128)(2,1)S(1)} %step_down.1), channel_id=1, source_target_pairs={{0,2},{1,3},{2,0},{3,1},{4,6},{5,7},{6,4},{7,5},{8,10},{9,11},{10,... | collective-permute-start | bytes 49160 | tf_op jit(solution)/shard_map/ppermute | solution.py:34
  71.8 1.2 %collective-permute-start.20 = (bf16[32,256]{1,0:T(8,128)(2,1)S(1)}, bf16[32,256]{1,0:T(8,128)(2,1)S(1)}, u32[]{:S(2)}, u32[]{:S(2)}) collective-permute-start(bf16[32,256]{1,0:T(8,128)(2,1)S(1)} %broadcast_select_fusion.4.f_own), channel_id=1, source_target_pairs={{0,1},{1,0},{2,3},{3,2},{4,5},{5,4},{6,7},{7,6},{8,9},{9,8},{10,11... | collective-permute-start | bytes 49160 | tf_op jit(solution)/shard_map/ppermute | solution.py:34
  (1 other events, 0.7 us)

commit v3 on v2

v3 whole, which is shorter than its diff:
```python
import functools

import jax
import jax.numpy as jnp
from jax import lax
from jax.experimental import pallas as pl
from jax.experimental.pallas import tpu as pltpu
from jax.sharding import PartitionSpec as P

SPREAD = 4
LANES = 128
BF = jnp.bfloat16
F32 = jnp.float32
VMEM = pl.BlockSpec(memory_space=pltpu.VMEM)
SMEM = pl.BlockSpec(memory_space=pltpu.SMEM)
ANY = pl.BlockSpec(memory_space=pl.ANY)
HBM = pl.BlockSpec(memory_space=pltpu.HBM)
LIMIT = 32 * 2**20


def mm(a, b):
    return jnp.dot(a, b, preferred_element_type=F32)


def params():
    return pltpu.CompilerParams(vmem_limit_bytes=LIMIT)


def cost(flops, nbytes):
    return pl.CostEstimate(flops=flops, bytes_accessed=nbytes, transcendentals=0)


def swap(block, mask):
    count = lax.axis_size("leaf")
    return lax.ppermute(block, "leaf", [(i, i ^ mask) for i in range(count)])


def bit_of_device(bit):
    return (lax.axis_index("leaf").astype(jnp.int32) & (1 << bit)) != 0


def gather_columns(table, slots, store):
    rows, columns = table.shape
    tiles = columns // LANES
    for out_tile in range(tiles):
        slot = jnp.broadcast_to(slots(out_tile), (rows, LANES))
        low = slot & (LANES - 1)
        high = slot // LANES
        found = None
        for tile in range(tiles):
            part = jnp.take_along_axis(
                table[:, tile * LANES : (tile + 1) * LANES], low, axis=1
            )
            found = part if found is None else jnp.where(high == tile, part, found)
        store(out_tile, found)


def start_kernel(rhs_hbm, order_hbm, basis_hbm, map_hbm, pick, tree_ref, red_ref,
                 rhs, order, basis, table, seats, sems):
    copies = [
        pltpu.make_async_copy(rhs_hbm, rhs, sems.at[0]),
        pltpu.make_async_copy(order_hbm, order, sems.at[1]),
        pltpu.make_async_copy(map_hbm, seats, sems.at[2]),
        pltpu.make_async_copy(basis_hbm, basis, sems.at[3]),
    ]
    for copy in copies:
        copy.start()
    copies[2].wait()
    me = lax.axis_index("leaf").astype(jnp.int32)
    offset = me & (SPREAD - 1)
    base = me - offset
    placed = [seats[base + slot] & (SPREAD - 1) for slot in range(SPREAD)]
    seat = placed[0]
    for slot in range(1, SPREAD):
        seat = jnp.where(offset == slot, placed[slot], seat)
    for m in range(SPREAD):
        source = jnp.int32(0)
        for slot in range(1, SPREAD):
            source = jnp.where(placed[slot] == (offset ^ m), slot, source)
        pick[m] = source ^ offset
    pick[SPREAD] = seat ^ offset
    copies[0].wait()
    table[...] = rhs[...].astype(F32)
    copies[1].wait()

    def store(tile, found):
        tree_ref[:, tile * LANES : (tile + 1) * LANES] = found.astype(BF)

    gather_columns(
        table, lambda tile: order[:, tile * LANES : (tile + 1) * LANES], store
    )
    copies[3].wait()
    red_ref[...] = mm(tree_ref[...], basis[...]).astype(BF)


def start(right_sides, point_order, basis_in, leaf_map):
    rows, columns = right_sides.shape
    rank = basis_in.shape[1]
    return pl.pallas_call(
        start_kernel,
        out_shape=(
            jax.ShapeDtypeStruct((SPREAD + 1,), jnp.int32),
            jax.ShapeDtypeStruct((rows, columns), BF),
            jax.ShapeDtypeStruct((rows, rank), BF),
        ),
        in_specs=[HBM] * 4,
        out_specs=(SMEM, VMEM, VMEM),
        scratch_shapes=[
            pltpu.VMEM(right_sides.shape, BF),
            pltpu.VMEM(point_order.shape, jnp.int32),
            pltpu.VMEM(basis_in.shape, BF),
            pltpu.VMEM(right_sides.shape, F32),
            pltpu.SMEM(leaf_map.shape, jnp.int32),
            pltpu.SemaphoreType.DMA((4,)),
        ],
        compiler_params=params(),
        cost_estimate=cost(2 * rows * columns * rank, columns * rank * 2),
        name="start",
    )(right_sides, point_order, basis_in, leaf_map)


def pack_kernel(node_up, node_down, node_cross, after, low_ref, high_ref, fulllow_ref,
                fullhigh_ref, toplow_ref, tophigh_ref, sems):
    rank = node_up.shape[1]
    cross_low = node_cross.at[pl.ds(0, rank), :]
    cross_high = node_cross.at[pl.ds(rank, rank), :]
    packs = [
        (low_ref, (node_down, cross_low)),
        (high_ref, (node_down, cross_high)),
        (fulllow_ref, (node_up, node_down, cross_low)),
        (fullhigh_ref, (node_up, node_down, cross_high)),
        (toplow_ref, (node_up, cross_low)),
        (tophigh_ref, (node_up, cross_high)),
    ]
    copies = []
    for dst, parts in packs:
        for i, part in enumerate(parts):
            copies.append(
                pltpu.make_async_copy(
                    part, dst.at[pl.ds(i * rank, rank), :], sems.at[len(copies)]
                )
            )
    for copy in copies:
        copy.start()
    for copy in copies:
        copy.wait()


def pack(node_up, node_down, node_cross, after):
    rank = node_up.shape[1]
    sizes = (2, 2, 3, 3, 2, 2)
    return pl.pallas_call(
        pack_kernel,
        out_shape=tuple(jax.ShapeDtypeStruct((n * rank, rank), BF) for n in sizes),
        in_specs=[HBM] * 3 + [ANY],
        out_specs=(VMEM,) * 6,
        scratch_shapes=[pltpu.SemaphoreType.DMA((sum(sizes),))],
        compiler_params=params(),
        cost_estimate=cost(0, 14 * rank * rank * 2),
        name="pack",
    )(node_up, node_down, node_cross, after)


def invert_kernel(order_hbm, after, inv_ref, order, sem):
    copy = pltpu.make_async_copy(order_hbm, order, sem)
    copy.start()
    copy.wait()
    slot = order[...]
    columns = slot.shape[1]
    tiles = columns // LANES
    low = slot & (LANES - 1)
    high = slot // LANES
    here = lax.broadcasted_iota(jnp.int32, (tiles, columns), 1)
    mask = lax.broadcasted_iota(jnp.int32, (tiles, columns), 0) == high
    left = jnp.concatenate(
        [
            jnp.where(mask, (here // LANES).astype(F32), 0.0),
            jnp.where(mask, (here & (LANES - 1)).astype(F32), 0.0),
        ],
        0,
    ).astype(BF)
    right = (lax.broadcasted_iota(jnp.int32, (LANES, columns), 0) == low).astype(F32).astype(BF)
    both = lax.dot_general(left, right, (((1,), (1,)), ((), ())), preferred_element_type=F32)
    inv_ref[...] = (both[:tiles] * LANES + both[tiles:]).astype(jnp.int32)


def invert(point_order, after):
    columns = point_order.shape[1]
    return pl.pallas_call(
        invert_kernel,
        out_shape=jax.ShapeDtypeStruct((columns // LANES, LANES), jnp.int32),
        in_specs=[HBM, ANY],
        out_specs=VMEM,
        scratch_shapes=[pltpu.VMEM(point_order.shape, jnp.int32), pltpu.SemaphoreType.DMA],
        compiler_params=params(),
        cost_estimate=cost(2 * 32 * columns * LANES, columns * 4),
        name="invert",
    )(point_order, after)


def near_kernel(first, tree_ref, inverse_hbm, after, near_ref, held, sems):
    chunks, _, width = held.shape
    copies = [
        pltpu.make_async_copy(
            inverse_hbm.at[:, pl.ds(first + i * width, width)], held.at[i], sems.at[i]
        )
        for i in range(chunks)
    ]
    for copy in copies:
        copy.start()
    for i, copy in enumerate(copies):
        copy.wait()
        near_ref[:, i * width : (i + 1) * width] = mm(tree_ref[...], held[i])


def near_strip(tree, leaf_inverse, strip, strips, after):
    rows, columns = tree.shape
    width = columns // strips
    chunk = 2 * LANES
    chunks = width // chunk
    return pl.pallas_call(
        functools.partial(near_kernel, strip * width),
        out_shape=jax.ShapeDtypeStruct((rows, width), F32),
        in_specs=[VMEM, HBM, ANY],
        out_specs=VMEM,
        scratch_shapes=[
            pltpu.VMEM((chunks, columns, chunk), BF),
            pltpu.SemaphoreType.DMA((chunks,)),
        ],
        compiler_params=params(),
        cost_estimate=cost(2 * rows * columns * width, columns * width * 2),
        name="near",
    )(tree, leaf_inverse, after)


def leaf_kernel(pick, red0, red1, red2, red3, up_ref, after, g0_ref, out_ref, table):
    for m, red in enumerate((red0, red1, red2, red3)):
        table[m] = red[...]
    for m in range(SPREAD):
        g0_ref[m] = table[pick[m]]
    out_ref[...] = mm(g0_ref[0], up_ref[...])


def leaf_rise(pick, reds, leaf_up, after):
    rows, rank = reds[0].shape
    return pl.pallas_call(
        leaf_kernel,
        out_shape=(
            jax.ShapeDtypeStruct((SPREAD, rows, rank), BF),
            jax.ShapeDtypeStruct((rows, rank), F32),
        ),
        in_specs=[SMEM] + [VMEM] * 5 + [ANY],
        out_specs=(VMEM,) * 2,
        scratch_shapes=[pltpu.VMEM((SPREAD, rows, rank), BF)],
        compiler_params=params(),
        cost_estimate=cost(2 * rows * rank * rank, rank * rank * 2),
        name="leaf_rise",
    )(pick, *reds, leaf_up, after)


def node_kernel(mine, other, up_own, up_other, out_ref):
    rows = mine.shape[0]
    odd = bit_of_device(0)
    g1 = (mine[...] + other[...]).astype(BF)
    out_ref[:rows] = g1
    node_map = jnp.where(odd, up_own[...], up_other[...])
    out_ref[rows:] = mm(g1, node_map).astype(BF)


def node_rise(mine, other, up_own, up_other):
    rows, rank = mine.shape
    return pl.pallas_call(
        node_kernel,
        out_shape=jax.ShapeDtypeStruct((2 * rows, rank), BF),
        in_specs=[VMEM] * 4,
        out_specs=VMEM,
        compiler_params=params(),
        cost_estimate=cost(2 * rows * rank * rank, rank * rank * 2),
        name="node_rise",
    )(mine, other, up_own, up_other)


def block_kernel(mine, other, up_ref, level_own, level_in, after, g1_ref, near_ref, far_ref):
    rows = mine.shape[0] // 2
    rank = mine.shape[1]
    g1_ref[0] = mine[:rows]
    g1_ref[1] = other[:rows]
    g2 = (mine[rows:].astype(F32) + other[rows:].astype(F32)).astype(BF)
    h2 = mm(g2, up_ref[...]).astype(BF)
    near_ref[:rows] = g2
    near_ref[rows:] = h2
    far_ref[:rows] = h2
    level_map = jnp.where(bit_of_device(SPREAD.bit_length() - 1), level_own[...], level_in[...])
    far_ref[rows:] = mm(h2, level_map).astype(BF)


def block_rise(mine, other, block_up, level_own, level_in, after):
    double, rank = mine.shape
    rows = double // 2
    return pl.pallas_call(
        block_kernel,
        out_shape=(
            jax.ShapeDtypeStruct((2, rows, rank), BF),
            jax.ShapeDtypeStruct((double, rank), BF),
            jax.ShapeDtypeStruct((double, rank), BF),
        ),
        in_specs=[VMEM] * 5 + [ANY],
        out_specs=(VMEM,) * 3,
        compiler_params=params(),
        cost_estimate=cost(4 * rows * rank * rank, 2 * rank * rank * 2),
        name="block_rise",
    )(mine, other, block_up, level_own, level_in, after)


def pair_kernel(bit, chain, *refs):
    mine, near, far, both, maps_own, maps_in = refs[:6]
    following = refs[6 : 6 + chain]
    outs = refs[7 + chain :]
    rows = mine.shape[0] // 2
    rank = mine.shape[1]
    grown = (mine[rows:].astype(F32) + near[rows:].astype(F32)).astype(BF)
    outs[0][...] = (far[:rows].astype(F32) + both[:rows].astype(F32)).astype(BF)
    maps = jnp.where(bit_of_device(bit), maps_own[:rank, :], maps_in[:rank, :])
    higher = mm(grown, maps) + far[rows:].astype(F32) + both[rows:].astype(F32)
    higher = higher.astype(BF)
    if chain == 0:
        outs[1][...] = higher
        return
    sent = mm(higher, following[0][:rank, :]).astype(BF)
    outs[1][:rows] = higher
    outs[1][rows:] = sent
    if chain == 2:
        outs[2][:rows] = sent
        outs[2][rows:] = mm(sent, following[1][:rank, :]).astype(BF)


def pair(bit, mine, near, far, both, maps_own, maps_in, following, after):
    double, rank = mine.shape
    rows = double // 2
    single = jax.ShapeDtypeStruct((rows, rank), BF)
    twofold = jax.ShapeDtypeStruct((double, rank), BF)
    chain = len(following)
    shapes = {0: (single, single), 1: (single, twofold), 2: (single, twofold, twofold)}[chain]
    return pl.pallas_call(
        functools.partial(pair_kernel, bit, chain),
        out_shape=shapes,
        in_specs=[VMEM] * (6 + chain) + [ANY],
        out_specs=(VMEM,) * len(shapes),
        compiler_params=params(),
        cost_estimate=cost(6 * rows * rank * rank, 6 * rank * rank),
        name="pair",
    )(mine, near, far, both, maps_own, maps_in, *following, after)


def fall_kernel(count, *refs):
    top = refs[0]
    siblings = refs[1 : 1 + count]
    maps = refs[1 + count : 1 + 2 * count]
    cut_maps, out = refs[1 + 2 * count], refs[3 + 2 * count]
    rank = top.shape[1]
    value = mm(top[...], maps[count - 1][:rank, :]).astype(BF)
    for k in range(count - 1, -1, -1):
        down = cut_maps[:rank, :] if k == 0 else maps[k - 1][rank : 2 * rank, :]
        cross = maps[k][maps[k].shape[0] - rank :, :]
        value = (mm(siblings[k][...], cross) + mm(value, down)).astype(BF)
    out[...] = value


def fall(top, siblings, maps, cut_maps, after):
    count = len(maps)
    rows, rank = top.shape
    return pl.pallas_call(
        functools.partial(fall_kernel, count),
        out_shape=jax.ShapeDtypeStruct((rows, rank), BF),
        in_specs=[VMEM] * (2 + 2 * count) + [ANY],
        out_specs=VMEM,
        compiler_params=params(),
        cost_estimate=cost(12 * rows * rank * rank, 12 * rank * rank),
        name="fall",
    )(top, *siblings, *maps, cut_maps, after)


def step_kernel(bit, mine, other, sibling, maps_own, maps_in, down_pack, after, out):
    rank = mine.shape[1]
    upper = bit_of_device(bit)
    value = jnp.where(upper, other[...], mine[...])
    cross = jnp.where(upper, maps_own[rank:, :], maps_in[rank:, :])
    out[...] = (mm(sibling[...], cross) + mm(value, down_pack[:rank, :])).astype(BF)


def step_down(bit, mine, other, sibling, maps_own, maps_in, down_pack, after):
    rows, rank = mine.shape
    return pl.pallas_call(
        functools.partial(step_kernel, bit),
        out_shape=jax.ShapeDtypeStruct((rows, rank), BF),
        in_specs=[VMEM] * 6 + [ANY],
        out_specs=VMEM,
        compiler_params=params(),
        cost_estimate=cost(4 * rows * rank * rank, 4 * rank * rank),
        name="step_down",
    )(mine, other, sibling, maps_own, maps_in, down_pack, after)


def local_kernel(g0_ref, g1_ref, down_ref, node_own, node_in, block_own, block_in, out_ref):
    rank = down_ref.shape[0]
    odd = bit_of_device(0)
    node = jnp.where(odd, node_own[...], node_in[...])
    cross = jnp.where(odd, block_in[rank:, :], block_own[rank:, :])
    out_ref[:rank] = mm(node[:rank, :], down_ref[...]).astype(BF)
    inner = mm(g1_ref[1], cross).astype(BF)
    out_ref[rank:] = (mm(g0_ref[1], node[rank:, :]) + mm(inner, down_ref[...])).astype(BF)


def local(g0, g1, leaf_down, node_own, node_in, block_own, block_in):
    _, rows, rank = g0.shape
    return pl.pallas_call(
        local_kernel,
        out_shape=jax.ShapeDtypeStruct((rank + rows, rank), BF),
        in_specs=[VMEM] * 7,
        out_specs=VMEM,
        compiler_params=params(),
        cost_estimate=cost(2 * (rank + 3 * rows) * rank * rank, 8 * rank * rank),
        name="local",
    )(g0, g1, leaf_down, node_own, node_in, block_own, block_in)


def final_kernel(strips, pick, f_own, f_core, l0, l1, l2, l3, out_basis, inv_ref, *refs):
    nears = refs[:strips]
    answer, total, leaf_f = refs[strips:]
    rank = f_own.shape[1]
    f2 = jnp.where(bit_of_device(0), f_core[...], f_own[...])
    for m, pack_ref in enumerate((l0, l1, l2, l3)):

        @pl.when(pick[SPREAD] == m)
        def _():
            leaf_f[...] = (mm(f2, pack_ref[:rank, :]) + pack_ref[rank:, :].astype(F32)).astype(BF)

    width = nears[0].shape[1]
    for i in range(strips):
        span = slice(i * width, (i + 1) * width)
        total[:, span] = nears[i][...] + mm(leaf_f[...], out_basis[:, span])

    def store(tile, found):
        answer[:, tile * LANES : (tile + 1) * LANES] = found

    gather_columns(total, lambda tile: inv_ref[tile : tile + 1, :], store)


def final(pick, f2, f2_core, locals_, basis_out, inverse_order, nears):
    rows, rank = f2.shape
    columns = basis_out.shape[1]
    return pl.pallas_call(
        functools.partial(final_kernel, len(nears)),
        out_shape=jax.ShapeDtypeStruct((rows, columns), F32),
        in_specs=[SMEM] + [VMEM] * (8 + len(nears)),
        out_specs=VMEM,
        scratch_shapes=[pltpu.VMEM((rows, columns), F32), pltpu.VMEM((rows, rank), BF)],
        compiler_params=params(),
        cost_estimate=cost(2 * rows * rank * columns, rank * columns * 2),
        name="final",
    )(pick, f2, f2_core, *locals_, basis_out, inverse_order, *nears)


def body(
    right_sides,
    point_order,
    leaf_inverse,
    basis_in,
    basis_out,
    leaf_up,
    leaf_down,
    node_up,
    node_down,
    node_cross,
    leaf_map,
):
    members = lax.axis_size("leaf")
    levels = members.bit_length() - 1
    cut = SPREAD.bit_length() - 1
    me = lax.axis_index("leaf")
    rows = right_sides.shape[0]
    offset = me & (SPREAD - 1)

    def to_left(block, bit):
        step = 1 << bit
        return lax.ppermute(block, "leaf", [(i + step, i) for i in range(0, members, 2 * step)])

    def to_right(block, bit, every):
        step = 1 << bit
        pairs = [(i, i + step) for i in range(0, members, every) if i & step == 0]
        return lax.ppermute(block, "leaf", pairs)

    block_up = to_left(node_up, 1)
    group_up = to_left(node_up, 2)
    node_up_in = swap(node_up, 1)

    pick, tree, reduced = start(right_sides, point_order, basis_in, leaf_map)
    reds = [reduced] + [swap(reduced, m) for m in range(1, SPREAD)]
    low, high, full_low, full_high, top_low, top_high = pack(node_up, node_down, node_cross, reduced)

    level_maps = []
    for level in range(cut + 2, levels + 1):
        first, second = (top_low, top_high) if level == levels else (full_low, full_high)
        span = 1 << (level - 1)
        held = jnp.where(me & span != 0, second, to_left(first, level - 1))
        for bit in range(level - 2, cut, -1):
            arrived = to_right(held, bit, 1 << bit)
            held = jnp.where(me & (1 << bit) != 0, arrived, held)
        level_maps.append(held)
    group_in = to_left(low, cut)
    block_in = to_left(low, 1)
    block_held = jnp.where(offset & 2 != 0, high, block_in)
    block_core = to_right(block_held, 0, 2)
    node_in = to_left(low, 0)

    g0, product = leaf_rise(pick, reds, leaf_up, low)
    node_pay = node_rise(product, swap(product, 1), node_up, node_up_in)
    pay_in = swap(node_pay, 2)
    near0 = near_strip(tree, leaf_inverse, 0, 2, node_pay)
    g1, near, far = block_rise(node_pay, pay_in, block_up, node_up, group_up, near0)

    own_local = local(g0, g1, leaf_down, high, node_in, block_held, block_core)
    local_x = swap(own_local, 2)
    locals_ = [own_local, swap(own_local, 1), local_x, swap(local_x, 1)]

    siblings = []
    bit = cut
    after = near0
    while bit < levels:
        step = 1 << bit
        near_in = swap(near, step)
        siblings.append(near_in[:rows])
        if bit + 1 < levels:
            far_in = swap(far, 2 * step)
            both_in = swap(far, 3 * step)
            if bit == cut:
                maps_own, maps_in = node_up, group_up
                near1 = near_strip(tree, leaf_inverse, 1, 2, near)
                after = near1
            else:
                maps_own = maps_in = level_maps[bit - cut - 1]
            following = [level_maps[i - cut - 2] for i in (bit + 2, bit + 3) if i < levels]
            results = pair(bit, near, near_in, far_in, both_in, maps_own, maps_in, following, after)
            siblings.append(results[0])
            near = results[1]
            if len(results) == 3:
                far = results[2]
            top = near[:rows]
            bit += 2
        else:
            top = (near[rows:].astype(F32) + near_in[rows:].astype(F32)).astype(BF)
            bit += 1

    inverse_order = invert(point_order, near1)
    cut_f = fall(top, siblings[1:], level_maps, group_in, inverse_order)
    block_f = step_down(
        cut, cut_f, swap(cut_f, SPREAD), siblings[0], high, group_in, block_held, own_local
    )
    from_x = swap(block_f, 2)
    block_f = jnp.where(offset & 2 != 0, from_x, block_f)
    return final(
        pick, block_f, swap(block_f, 1), locals_, basis_out, inverse_order, [near0, near1]
    )


def solution(mesh):
    placed = (
        P(None, "leaf"),
        P("leaf", None),
        P("leaf", None),
        P("leaf", None),
        P("leaf", None),
        P("leaf", None),
        P("leaf", None),
        P("leaf", None),
        P("leaf", None),
        P("leaf", None),
        P(),
    )
    return jax.shard_map(
        body, mesh=mesh, in_specs=placed, out_specs=P(None, "leaf"), check_vma=False
    )
```

time: 76.6 us -> 75.9 us (level)
  waiting for transfers between devices: 29.2 us -> 20.4 us
  starting transfers between devices: 20.9 us -> 27.6 us
  Pallas kernels: 14 us -> 17.2 us
  other arithmetic: 1.15 us -> 0.17 us
  local copies, waits for them, and re-layouts: 10.6 us -> 9.64 us
    ppermute x16, waiting for transfers between devices: 28.8 us -> 14.1 us  [swap(): return lax.ppermute(block, 'leaf', [(i, i ^ mask) for i in range(count)])]
    ppermute x5 -> x9, waiting for transfers between devices: 0.47 us -> 6.22 us  [the longest x7 4.39 us: to_left(): lax.ppermute(block, 'leaf', [(i + step, i) for i in range(0, members, 2 *...]
    ppermute x5 -> x9, starting transfers between devices: 9.04 us -> 14.3 us  [the longest x7 9.16 us: to_left(): lax.ppermute(block, 'leaf', [(i + step, i) for i in range(0, members, 2 *...]
    pallas_call x6 -> x7, Pallas kernels: 8.18 us -> 10.6 us  [the longest x2 4.41 us: near_strip(): pl.pallas_call(functools.partial(near_kernel, strip * width), out_shape=j...]
    ppermute x16, starting transfers between devices: 11.9 us -> 13.3 us  [swap(): return lax.ppermute(block, 'leaf', [(i, i ^ mask) for i in range(count)])]
    select_n x3 -> x4, other arithmetic: 1.14 us -> 0.15 us  [the longest x2 0.09 us: body(): held = jnp.where(me & span != 0, second, to_left(first, level - 1))]
    pallas_call x1, Pallas kernels: 0.26 us -> 1.18 us  [block_rise(): pl.pallas_call(block_kernel, out_shape=(jax.ShapeDtypeStruct((2, rows, ra...]
    unnamed x24, local copies, waits for them, and re-layouts: 10.5 us -> 9.63 us
  transfers between devices with their start and end apart: 21 -> 25, of which waited for: 11 -> 7; matrix products, arithmetic and copies ran while one was open for 2% -> 0% of each run, Pallas kernels for 7% -> 13%
where the time goes in v3:
time: 75.9 us; the launch traced here: 75.4 us
  starting transfers between devices  27.6 us (36%)
  waiting for transfers between devices  20.4 us (27%)
  Pallas kernels  17.2 us (23%)
  local copies, waits for them, and re-layouts  9.64 us (13%)
    ppermute x16, waiting for transfers between devices, swap(): return lax.ppermute(block, 'leaf', [(i, i ^ mask) for i in range(count)])  14.1 us
    ppermute x16, starting transfers between devices, swap(): return lax.ppermute(block, 'leaf', [(i, i ^ mask) for i in range(count)])  13.3 us
    unnamed x24, local copies, waits for them, and re-layouts  9.63 us
    ppermute x7, starting transfers between devices, to_left(): lax.ppermute(block, 'leaf', [(i + step, i) for i in range(0, members, 2 *...  9.16 us
    ppermute x2, starting transfers between devices, to_right(): return lax.ppermute(block, 'leaf', pairs)  5.15 us
    pallas_call x2, Pallas kernels, near_strip(): pl.pallas_call(functools.partial(near_kernel, strip * width), out_shape=j...  4.41 us
    ppermute x7, waiting for transfers between devices, to_left(): lax.ppermute(block, 'leaf', [(i + step, i) for i in range(0, members, 2 *...  4.39 us
    pallas_call x1, Pallas kernels, final(): pl.pallas_call(functools.partial(final_kernel, len(nears)), out_shape=jax...  2.91 us
  transfers between devices with their start and end apart: 25, of which 7 were waited for; matrix products, arithmetic and copies ran while one was open for 0% of the time, Pallas kernels for 13%

profile of v3, /device:TPU:0, one launch (start us, length us, event | category | flops | bytes accessed | tf_op | source)
XLA Modules:
  0.0 75.4 jit_solution(16010724735570387307)
XLA Ops:
  0.0 1.2 %copy-done.3 = bf16[2048,256]{1,0:T(8,128)(2,1)S(1)} copy-done((bf16[2048,256]{1,0:T(8,128)(2,1)S(1)}, bf16[2048,256]{1,0:T(8,128)(2,1)}, u32[]{:S(2)}) %copy-start.3) | copy-done | bytes 1048600
  3.5 2.0 %start.1 = (s32[5]{0:T(128)S(1)}, bf16[32,2048]{1,0:T(8,128)(2,1)S(1)}, bf16[32,256]{1,0:T(8,128)(2,1)S(1)}) custom-call(bf16[32,2048]{1,0:T(8,128)(2,1)S(1)} %copy-done.5, s32[1,2048]{1,0:T(1,128)S(1)} %copy-done.9, bf16[2048,256]{1,0:T(8,128)(2,1)S(1)} %copy-done.3, s32[32]{0:T(128)S(1)} %copy-done.11), custom_call_target="tpu_custom_call" | custom-call | flops 33554432 | bytes 1048576 | tf_op jit(solution)/shard_map/start/pallas_call | solution.py:99
  5.5 0.9 %copy-done.4 = bf16[512,256]{1,0:T(8,128)(2,1)S(1)} copy-done((bf16[512,256]{1,0:T(8,128)(2,1)S(1)}, bf16[512,256]{1,0:T(8,128)(2,1)}, u32[]{:S(2)}) %copy-start.4) | copy-done | bytes 262168
  7.4 2.6 %pack.1 = (bf16[512,256]{1,0:T(8,128)(2,1)S(1)}, bf16[512,256]{1,0:T(8,128)(2,1)S(1)}, bf16[768,256]{1,0:T(8,128)(2,1)S(1)}, bf16[768,256]{1,0:T(8,128)(2,1)S(1)...) custom-call(bf16[256,256]{1,0:T(8,128)(2,1)} %refs_4_.1, bf16[256,256]{1,0:T(8,128)(2,1)S(1)} %copy-done.6, ...), custom_call_target="tpu_custom_call" | custom-call | bytes 1835008 | tf_op jit(solution)/shard_map/pack/pallas_call | solution.py:152
  9.9 1.3 %collective-permute-start.17 = (bf16[512,256]{1,0:T(8,128)(2,1)S(1)}, bf16[512,256]{1,0:T(8,128)(2,1)S(1)}, u32[]{:S(2)}, u32[]{:S(2)}) collective-permute-start(bf16[512,256]{1,0:T(8,128)(2,1)S(1)} %get-tuple-element.23.after), channel_id=1, source_target_pairs={{2,0},{6,4},{10,8},{14,12},{18,16},{22,20},{26,24},{30,28}} | collective-permute-start | bytes 786440 | tf_op jit(solution)/shard_map/ppermute | solution.py:486
  11.3 3.0 %collective-permute-start.1 = (bf16[32,256]{1,0:T(8,128)(2,1)S(1)}, bf16[32,256]{1,0:T(8,128)(2,1)S(1)}, u32[]{:S(2)}, u32[]{:S(2)}) collective-permute-start(bf16[32,256]{1,0:T(8,128)(2,1)S(1)} %get-tuple-element.22.after.red0), channel_id=1, source_target_pairs={{0,2},{1,3},{2,0},{3,1},{4,6},{5,7},{6,4},{7,5},{8,10},{9,11},{10,... | collective-permute-start | bytes 49160 | tf_op jit(solution)/shard_map/ppermute | solution.py:35
  14.6 4.4 %collective-permute-done.1.red2 = bf16[32,256]{1,0:T(8,128)(2,1)S(1)} collective-permute-done((bf16[32,256]{1,0:T(8,128)(2,1)S(1)}, bf16[32,256]{1,0:T(8,128)(2,1)S(1)}, u32[]{:S(2)}, u32[]{:S(2)}) %collective-permute-start.1) | collective-permute-done | bytes 16416 | tf_op jit(solution)/shard_map/ppermute | solution.py:35
  20.7 1.3 %collective-permute-start.11 = (bf16[768,256]{1,0:T(8,128)(2,1)S(1)}, bf16[768,256]{1,0:T(8,128)(2,1)S(1)}, u32[]{:S(2)}, u32[]{:S(2)}) collective-permute-start(bf16[768,256]{1,0:T(8,128)(2,1)S(1)} %get-tuple-element.29), channel_id=1, source_target_pairs={{8,0},{24,16}} | collective-permute-start | bytes 1179656 | tf_op jit(solution)/shard_map/ppermute | solution.py:486
  22.0 1.3 %collective-permute-start.6 = (bf16[256,256]{1,0:T(8,128)(2,1)}, bf16[256,256]{1,0:T(8,128)(2,1)S(1)}, u32[]{:S(2)}, u32[]{:S(2)}) collective-permute-start(bf16[256,256]{1,0:T(8,128)(2,1)} %refs_4_.1), channel_id=1, source_target_pairs={{2,0},{6,4},{10,8},{14,12},{18,16},{22,20},{26,24},{30,28}} | collective-permute-start | bytes 393224 | tf_op jit(solution)/shard_map/ppermute | solution.py:486
  23.3 1.3 %collective-permute-start.7 = (bf16[256,256]{1,0:T(8,128)(2,1)}, bf16[256,256]{1,0:T(8,128)(2,1)S(1)}, u32[]{:S(2)}, u32[]{:S(2)}) collective-permute-start(bf16[256,256]{1,0:T(8,128)(2,1)} %refs_4_.1), channel_id=1, source_target_pairs={{4,0},{12,8},{20,16},{28,24}} | collective-permute-start | bytes 393224 | tf_op jit(solution)/shard_map/ppermute | solution.py:486
  24.6 1.1 %node_rise.1.after.mine = bf16[64,256]{1,0:T(8,128)(2,1)S(1)} custom-call(f32[32,256]{1,0:T(8,128)S(1)} %get-tuple-element.24.mine, f32[32,256]{1,0:T(8,128)S(1)} %collective-permute-done.3.other, bf16[256,256]{1,0:T(8,128)(2,1)} %refs_4_.1, bf16[256,256]{1,0:T(8,128)(2,1)S(1)} %collective-permute-done.4.up_other), custom_call_target="tpu_custom_call" | custom-call | flops 4194304 | bytes 131072 | tf_op jit(solution)/shard_map/node_rise/pallas_call | solution.py:272
  25.6 2.0 %collective-permute-start.5 = (bf16[64,256]{1,0:T(8,128)(2,1)S(1)}, bf16[64,256]{1,0:T(8,128)(2,1)S(1)}, u32[]{:S(2)}, u32[]{:S(2)}) collective-permute-start(bf16[64,256]{1,0:T(8,128)(2,1)S(1)} %node_rise.1.after.mine), channel_id=1, source_target_pairs={{0,2},{1,3},{2,0},{3,1},{4,6},{5,7},{6,4},{7,5},{8,10},{9,11},{10,... | collective-permute-start | bytes 98312 | tf_op jit(solution)/shard_map/ppermute | solution.py:35
  27.7 3.4 %copy-done = bf16[2048,2048]{1,0:T(8,128)(2,1)S(1)} copy-done((bf16[2048,2048]{1,0:T(8,128)(2,1)S(1)}, bf16[2048,2048]{1,0:T(8,128)(2,1)}, u32[]{:S(2)}) %copy-start) | copy-done | bytes 8388632
  31.1 2.2 %near.2.after.refs_0_ = f32[32,1024]{1,0:T(8,128)S(1)} custom-call(bf16[32,2048]{1,0:T(8,128)(2,1)S(1)} %get-tuple-element.25.tree_ref, bf16[2048,2048]{1,0:T(8,128)(2,1)S(1)} %copy-done, bf16[64,256]{1,0:T(8,128)(2,1)S(1)} %node_rise.1.after.mine), custom_call_target="tpu_custom_call" | custom-call | flops 134217728 | bytes 4194304 | tf_op jit(solution)/shard_map/near/pallas_call | solution.py:221
  33.3 1.4 %collective-permute-start.18 = (bf16[512,256]{1,0:T(8,128)(2,1)S(1)}, bf16[512,256]{1,0:T(8,128)(2,1)S(1)}, u32[]{:S(2)}, u32[]{:S(2)}) collective-permute-start(bf16[512,256]{1,0:T(8,128)(2,1)S(1)} %get-tuple-element.23.after), channel_id=1, source_target_pairs={{1,0},{3,2},{5,4},{7,6},{9,8},{11,10},{13,12},{15,14},{17,16},{19,... | collective-permute-start | bytes 786440 | tf_op jit(solution)/shard_map/ppermute | solution.py:486
  34.8 1.3 %collective-permute-start.13 = (bf16[512,256]{1,0:T(8,128)(2,1)S(1)}, bf16[512,256]{1,0:T(8,128)(2,1)S(1)}, u32[]{:S(2)}, u32[]{:S(2)}) collective-permute-start(bf16[512,256]{1,0:T(8,128)(2,1)S(1)} %get-tuple-element.33), channel_id=1, source_target_pairs={{16,0}} | collective-permute-start | bytes 786440 | tf_op jit(solution)/shard_map/ppermute | solution.py:486
  36.1 1.2 %block_rise.1 = (bf16[2,32,256]{2,1,0:T(8,128)(2,1)S(1)}, bf16[64,256]{1,0:T(8,128)(2,1)S(1)}, bf16[64,256]{1,0:T(8,128)(2,1)S(1)}) custom-call(bf16[64,256]{1,0:T(8,128)(2,1)S(1)} %node_rise.1.after.mine, bf16[64,256]{1,0:T(8,128)(2,1)S(1)} %collective-permute-done.5.other, bf16[256,256]{1,0:T(8,128)(2,1)S(1)} %collective-permute-done.6.up_ref, ...), custom_call_target="tpu_custom_call" | custom-call | flops 8388608 | bytes 262144 | tf_op jit(solution)/shard_map/block_rise/pallas_call | solution.py:300
  37.2 1.5 %collective-permute-start.8 = (bf16[64,256]{1,0:T(8,128)(2,1)S(1)}, bf16[64,256]{1,0:T(8,128)(2,1)S(1)}, u32[]{:S(2)}, u32[]{:S(2)}) collective-permute-start(bf16[64,256]{1,0:T(8,128)(2,1)S(1)} %get-tuple-element.26.after.refs_0_), channel_id=1, source_target_pairs={{0,4},{1,5},{2,6},{3,7},{4,0},{5,1},{6,2},{7,3},{8,12},{9,13},{10,... | collective-permute-start | bytes 98312 | tf_op jit(solution)/shard_map/ppermute | solution.py:35
  38.7 2.2 %near.3.refs_7_.after.refs_1_ = f32[32,1024]{1,0:T(8,128)S(1)} custom-call(bf16[32,2048]{1,0:T(8,128)(2,1)S(1)} %get-tuple-element.25.tree_ref, bf16[2048,2048]{1,0:T(8,128)(2,1)S(1)} %copy-done.1, bf16[64,256]{1,0:T(8,128)(2,1)S(1)} %get-tuple-element.26.after.refs_0_), custom_call_target="tpu_custom_call" | custom-call | flops 134217728 | bytes 4194304 | tf_op jit(solution)/shard_map/near/pallas_call | solution.py:221
  41.0 1.6 %collective-permute-start.9 = (bf16[64,256]{1,0:T(8,128)(2,1)S(1)}, bf16[64,256]{1,0:T(8,128)(2,1)S(1)}, u32[]{:S(2)}, u32[]{:S(2)}) collective-permute-start(bf16[64,256]{1,0:T(8,128)(2,1)S(1)} %get-tuple-element.27), channel_id=1, source_target_pairs={{0,8},{1,9},{2,10},{3,11},{4,12},{5,13},{6,14},{7,15},{8,0},{9,1},... | collective-permute-start | bytes 98312 | tf_op jit(solution)/shard_map/ppermute | solution.py:35
  43.4 2.5 %collective-permute-start.19 = (bf16[512,256]{1,0:T(8,128)(2,1)S(1)}, bf16[512,256]{1,0:T(8,128)(2,1)S(1)}, u32[]{:S(2)}, u32[]{:S(2)}) collective-permute-start(bf16[512,256]{1,0:T(8,128)(2,1)S(1)} %broadcast_select_fusion.1.block_own.down_pack), channel_id=1, source_target_pairs={{0,1},{2,3},{4,5},{6,7},{8,9},{10,11},{12,13},{14,15},{16,17},{18,... | collective-permute-start | bytes 786440 | tf_op jit(solution)/shard_map/ppermute | solution.py:491
  45.9 1.6 %collective-permute-done.10.refs_3_ = bf16[64,256]{1,0:T(8,128)(2,1)S(1)} collective-permute-done((bf16[64,256]{1,0:T(8,128)(2,1)S(1)}, bf16[64,256]{1,0:T(8,128)(2,1)S(1)}, u32[]{:S(2)}, u32[]{:S(2)}) %collective-permute-start.10) | collective-permute-done | bytes 32800 | tf_op jit(solution)/shard_map/ppermute | solution.py:35
  47.5 1.2 %pair.1 = (bf16[32,256]{1,0:T(8,128)(2,1)S(1)}, bf16[64,256]{1,0:T(8,128)(2,1)S(1)}) custom-call(bf16[64,256]{1,0:T(8,128)(2,1)S(1)} %get-tuple-element.26.after.refs_0_, bf16[64,256]{1,0:T(8,128)(2,1)S(1)} %collective-permute-done.8.refs_1_, bf16[64,256]{1,0:T(8,128)(2,1)S(1)} %collective-permute-done.9.refs_2_, ...), custom_call_target="tpu_custom_call" | custom-call | flops 12582912 | bytes 393216 | tf_op jit(solution)/shard_map/pair/pallas_call | solution.py:344
  48.7 3.4 %collective-permute-start.12 = (bf16[64,256]{1,0:T(8,128)(2,1)S(1)}, bf16[64,256]{1,0:T(8,128)(2,1)S(1)}, u32[]{:S(2)}, u32[]{:S(2)}) collective-permute-start(bf16[64,256]{1,0:T(8,128)(2,1)S(1)} %get-tuple-element.30), channel_id=1, source_target_pairs={{0,16},{1,17},{2,18},{3,19},{4,20},{5,21},{6,22},{7,23},{8,24},{9,... | collective-permute-start | bytes 98312 | tf_op jit(solution)/shard_map/ppermute | solution.py:35
  52.2 2.6 %collective-permute-start.14 = (bf16[512,256]{1,0:T(8,128)(2,1)S(1)}, bf16[512,256]{1,0:T(8,128)(2,1)S(1)}, u32[]{:S(2)}, u32[]{:S(2)}) collective-permute-start(bf16[512,256]{1,0:T(8,128)(2,1)S(1)} %broadcast_select_fusion.2), channel_id=1, source_target_pairs={{0,8},{16,24}} | collective-permute-start | bytes 786440 | tf_op jit(solution)/shard_map/ppermute | solution.py:491
  54.8 1.3 %collective-permute-start.15 = (bf16[512,256]{1,0:T(8,128)(2,1)S(1)}, bf16[512,256]{1,0:T(8,128)(2,1)S(1)}, u32[]{:S(2)}, u32[]{:S(2)}) collective-permute-start(bf16[512,256]{1,0:T(8,128)(2,1)S(1)} %get-tuple-element.23.after), channel_id=1, source_target_pairs={{4,0},{12,8},{20,16},{28,24}} | collective-permute-start | bytes 786440 | tf_op jit(solution)/shard_map/ppermute | solution.py:486
  56.9 1.8 %collective-permute-done.14 = bf16[512,256]{1,0:T(8,128)(2,1)S(1)} collective-permute-done((bf16[512,256]{1,0:T(8,128)(2,1)S(1)}, bf16[512,256]{1,0:T(8,128)(2,1)S(1)}, u32[]{:S(2)}, u32[]{:S(2)}) %collective-permute-start.14) | collective-permute-done | bytes 262176 | tf_op jit(solution)/shard_map/ppermute | solution.py:491
  58.7 4.4 %collective-permute-done.15.refs_5_.maps_in = bf16[512,256]{1,0:T(8,128)(2,1)S(1)} collective-permute-done((bf16[512,256]{1,0:T(8,128)(2,1)S(1)}, bf16[512,256]{1,0:T(8,128)(2,1)S(1)}, u32[]{:S(2)}, u32[]{:S(2)}) %collective-permute-start.15) | collective-permute-done | bytes 262176 | tf_op jit(solution)/shard_map/ppermute | solution.py:486
  63.5 3.7 %collective-permute-done.16.other = bf16[32,256]{1,0:T(8,128)(2,1)S(1)} collective-permute-done((bf16[32,256]{1,0:T(8,128)(2,1)S(1)}, bf16[32,256]{1,0:T(8,128)(2,1)S(1)}, u32[]{:S(2)}, u32[]{:S(2)}) %collective-permute-start.16) | collective-permute-done | bytes 16416 | tf_op jit(solution)/shard_map/ppermute | solution.py:35
  68.1 3.1 %collective-permute-done.20 = bf16[32,256]{1,0:T(8,128)(2,1)S(1)} collective-permute-done((bf16[32,256]{1,0:T(8,128)(2,1)S(1)}, bf16[32,256]{1,0:T(8,128)(2,1)S(1)}, u32[]{:S(2)}, u32[]{:S(2)}) %collective-permute-start.20) | collective-permute-done | bytes 16416 | tf_op jit(solution)/shard_map/ppermute | solution.py:35
  71.3 1.2 %collective-permute-done.21.f_core = bf16[32,256]{1,0:T(8,128)(2,1)S(1)} collective-permute-done((bf16[32,256]{1,0:T(8,128)(2,1)S(1)}, bf16[32,256]{1,0:T(8,128)(2,1)S(1)}, u32[]{:S(2)}, u32[]{:S(2)}) %collective-permute-start.21) | collective-permute-done | bytes 16416 | tf_op jit(solution)/shard_map/ppermute | solution.py:35
  72.5 2.9 %final.1 = f32[32,2048]{1,0:T(8,128)} custom-call(s32[5]{0:T(128)S(1)} %get-tuple-element.21.pick, bf16[32,256]{1,0:T(8,128)(2,1)S(1)} %broadcast_select_fusion.4.f_own, bf16[32,256]{1,0:T(8,128)(2,1)S(1)} %collective-permute-done.21.f_core, bf16[288,256]{1,0:T(8,128)(2,1)S(1)} %local.1.after.l0, bf16[288,256]{1,0:T(8,128)(2,1)S(1)} %collective-permute-done.22.l1, ...), custom_call_target="tpu_custom_call" | custom-call | flops 33554432 | bytes 1048576 | tf_op jit(solution)/shard_map/final/pallas_call | solution.py:452
  (63 shorter events, 7.9 us)
Async XLA Ops:
  0.0 1.2 %copy-start.3 = (bf16[2048,256]{1,0:T(8,128)(2,1)S(1)}, bf16[2048,256]{1,0:T(8,128)(2,1)}, u32[]{:S(2)}) copy-start(bf16[2048,256]{1,0:T(8,128)(2,1)} %basis_hbm.1) | copy-start | bytes 3145732
  5.5 1.0 %copy-start.4 = (bf16[512,256]{1,0:T(8,128)(2,1)S(1)}, bf16[512,256]{1,0:T(8,128)(2,1)}, u32[]{:S(2)}) copy-start(bf16[512,256]{1,0:T(8,128)(2,1)} %node_cross.1) | copy-start | bytes 786436
  9.9 31.0 %collective-permute-start.17 = (bf16[512,256]{1,0:T(8,128)(2,1)S(1)}, bf16[512,256]{1,0:T(8,128)(2,1)S(1)}, u32[]{:S(2)}, u32[]{:S(2)}) collective-permute-start(bf16[512,256]{1,0:T(8,128)(2,1)S(1)} %get-tuple-element.23.after), channel_id=1, source_target_pairs={{2,0},{6,4},{10,8},{14,12},{18,16},{22,20},{26,24},{30,28}} | collective-permute-start | bytes 786440 | tf_op jit(solution)/shard_map/ppermute | solution.py:486
  11.2 3.3 %collective-permute-start = (bf16[32,256]{1,0:T(8,128)(2,1)S(1)}, bf16[32,256]{1,0:T(8,128)(2,1)S(1)}, u32[]{:S(2)}, u32[]{:S(2)}) collective-permute-start(bf16[32,256]{1,0:T(8,128)(2,1)S(1)} %get-tuple-element.22.after.red0), channel_id=1, source_target_pairs={{0,1},{1,0},{2,3},{3,2},{4,5},{5,4},{6,7},{7,6},{8,9},{9,8},{10,11... | collective-permute-start | bytes 49160 | tf_op jit(solution)/shard_map/ppermute | solution.py:35
  11.3 7.6 %collective-permute-start.1 = (bf16[32,256]{1,0:T(8,128)(2,1)S(1)}, bf16[32,256]{1,0:T(8,128)(2,1)S(1)}, u32[]{:S(2)}, u32[]{:S(2)}) collective-permute-start(bf16[32,256]{1,0:T(8,128)(2,1)S(1)} %get-tuple-element.22.after.red0), channel_id=1, source_target_pairs={{0,2},{1,3},{2,0},{3,1},{4,6},{5,7},{6,4},{7,5},{8,10},{9,11},{10,... | collective-permute-start | bytes 49160 | tf_op jit(solution)/shard_map/ppermute | solution.py:35
  14.3 4.6 %collective-permute-start.2 = (bf16[32,256]{1,0:T(8,128)(2,1)S(1)}, bf16[32,256]{1,0:T(8,128)(2,1)S(1)}, u32[]{:S(2)}, u32[]{:S(2)}) collective-permute-start(bf16[32,256]{1,0:T(8,128)(2,1)S(1)} %get-tuple-element.22.after.red0), channel_id=1, source_target_pairs={{0,3},{1,2},{2,1},{3,0},{4,7},{5,6},{6,5},{7,4},{8,11},{9,10},{10,... | collective-permute-start | bytes 49160 | tf_op jit(solution)/shard_map/ppermute | solution.py:35
  14.4 10.2 %collective-permute-start.4 = (bf16[256,256]{1,0:T(8,128)(2,1)}, bf16[256,256]{1,0:T(8,128)(2,1)S(1)}, u32[]{:S(2)}, u32[]{:S(2)}) collective-permute-start(bf16[256,256]{1,0:T(8,128)(2,1)} %refs_4_.1), channel_id=1, source_target_pairs={{0,1},{1,0},{2,3},{3,2},{4,5},{5,4},{6,7},{7,6},{8,9},{9,8},{10,11... | collective-permute-start | bytes 393224 | tf_op jit(solution)/shard_map/ppermute | solution.py:35
  20.6 2.7 %collective-permute-start.3 = (f32[32,256]{1,0:T(8,128)S(1)}, f32[32,256]{1,0:T(8,128)S(1)}, u32[]{:S(2)}, u32[]{:S(2)}) collective-permute-start(f32[32,256]{1,0:T(8,128)S(1)} %get-tuple-element.24.mine), channel_id=1, source_target_pairs={{0,1},{1,0},{2,3},{3,2},{4,5},{5,4},{6,7},{7,6},{8,9},{9,8},{10,11... | collective-permute-start | bytes 98312 | tf_op jit(solution)/shard_map/ppermute | solution.py:35
  20.7 22.0 %collective-permute-start.11 = (bf16[768,256]{1,0:T(8,128)(2,1)S(1)}, bf16[768,256]{1,0:T(8,128)(2,1)S(1)}, u32[]{:S(2)}, u32[]{:S(2)}) collective-permute-start(bf16[768,256]{1,0:T(8,128)(2,1)S(1)} %get-tuple-element.29), channel_id=1, source_target_pairs={{8,0},{24,16}} | collective-permute-start | bytes 1179656 | tf_op jit(solution)/shard_map/ppermute | solution.py:486
  22.0 11.3 %collective-permute-start.6 = (bf16[256,256]{1,0:T(8,128)(2,1)}, bf16[256,256]{1,0:T(8,128)(2,1)S(1)}, u32[]{:S(2)}, u32[]{:S(2)}) collective-permute-start(bf16[256,256]{1,0:T(8,128)(2,1)} %refs_4_.1), channel_id=1, source_target_pairs={{2,0},{6,4},{10,8},{14,12},{18,16},{22,20},{26,24},{30,28}} | collective-permute-start | bytes 393224 | tf_op jit(solution)/shard_map/ppermute | solution.py:486
  23.3 11.5 %collective-permute-start.7 = (bf16[256,256]{1,0:T(8,128)(2,1)}, bf16[256,256]{1,0:T(8,128)(2,1)S(1)}, u32[]{:S(2)}, u32[]{:S(2)}) collective-permute-start(bf16[256,256]{1,0:T(8,128)(2,1)} %refs_4_.1), channel_id=1, source_target_pairs={{4,0},{12,8},{20,16},{28,24}} | collective-permute-start | bytes 393224 | tf_op jit(solution)/shard_map/ppermute | solution.py:486
  25.6 10.4 %collective-permute-start.5 = (bf16[64,256]{1,0:T(8,128)(2,1)S(1)}, bf16[64,256]{1,0:T(8,128)(2,1)S(1)}, u32[]{:S(2)}, u32[]{:S(2)}) collective-permute-start(bf16[64,256]{1,0:T(8,128)(2,1)S(1)} %node_rise.1.after.mine), channel_id=1, source_target_pairs={{0,2},{1,3},{2,0},{3,1},{4,6},{5,7},{6,4},{7,5},{8,10},{9,11},{10,... | collective-permute-start | bytes 98312 | tf_op jit(solution)/shard_map/ppermute | solution.py:35
  27.7 3.4 %copy-start = (bf16[2048,2048]{1,0:T(8,128)(2,1)S(1)}, bf16[2048,2048]{1,0:T(8,128)(2,1)}, u32[]{:S(2)}) copy-start(bf16[2048,2048]{1,0:T(8,128)(2,1)} %inverse_hbm.3) | copy-start | bytes 25165828
  31.1 7.7 %copy-start.1 = (bf16[2048,2048]{1,0:T(8,128)(2,1)S(1)}, bf16[2048,2048]{1,0:T(8,128)(2,1)}, u32[]{:S(2)}) copy-start(bf16[2048,2048]{1,0:T(8,128)(2,1)} %inverse_hbm.3) | copy-start | bytes 25165828
  33.3 22.9 %copy-start.10 = (s32[1,2048]{1,0:T(1,128)S(1)}, s32[1,2048]{1,0:T(1,128)}, u32[]{:S(2)}) copy-start(s32[1,2048]{1,0:T(1,128)} %order_hbm.3) | copy-start | bytes 24580
  33.3 23.2 %copy-start.8 = (bf16[256,256]{1,0:T(8,128)(2,1)S(1)}, bf16[256,256]{1,0:T(8,128)(2,1)}, u32[]{:S(2)}) copy-start(bf16[256,256]{1,0:T(8,128)(2,1)} %down_ref.1) | copy-start | bytes 393220
  33.3 23.2 %collective-permute-start.18 = (bf16[512,256]{1,0:T(8,128)(2,1)S(1)}, bf16[512,256]{1,0:T(8,128)(2,1)S(1)}, u32[]{:S(2)}, u32[]{:S(2)}) collective-permute-start(bf16[512,256]{1,0:T(8,128)(2,1)S(1)} %get-tuple-element.23.after), channel_id=1, source_target_pairs={{1,0},{3,2},{5,4},{7,6},{9,8},{11,10},{13,12},{15,14},{17,16},{19,... | collective-permute-start | bytes 786440 | tf_op jit(solution)/shard_map/ppermute | solution.py:486
  34.8 17.4 %collective-permute-start.13 = (bf16[512,256]{1,0:T(8,128)(2,1)S(1)}, bf16[512,256]{1,0:T(8,128)(2,1)S(1)}, u32[]{:S(2)}, u32[]{:S(2)}) collective-permute-start(bf16[512,256]{1,0:T(8,128)(2,1)S(1)} %get-tuple-element.33), channel_id=1, source_target_pairs={{16,0}} | collective-permute-start | bytes 786440 | tf_op jit(solution)/shard_map/ppermute | solution.py:486
  37.2 35.2 %copy-start.2 = (bf16[256,2048]{1,0:T(8,128)(2,1)S(1)}, bf16[256,2048]{1,0:T(8,128)(2,1)}, u32[]{:S(2)}) copy-start(bf16[256,2048]{1,0:T(8,128)(2,1)} %out_basis.1) | copy-start | bytes 3145732
  37.2 6.1 %collective-permute-start.8 = (bf16[64,256]{1,0:T(8,128)(2,1)S(1)}, bf16[64,256]{1,0:T(8,128)(2,1)S(1)}, u32[]{:S(2)}, u32[]{:S(2)}) collective-permute-start(bf16[64,256]{1,0:T(8,128)(2,1)S(1)} %get-tuple-element.26.after.refs_0_), channel_id=1, source_target_pairs={{0,4},{1,5},{2,6},{3,7},{4,0},{5,1},{6,2},{7,3},{8,12},{9,13},{10,... | collective-permute-start | bytes 98312 | tf_op jit(solution)/shard_map/ppermute | solution.py:35
  41.0 4.9 %collective-permute-start.9 = (bf16[64,256]{1,0:T(8,128)(2,1)S(1)}, bf16[64,256]{1,0:T(8,128)(2,1)S(1)}, u32[]{:S(2)}, u32[]{:S(2)}) collective-permute-start(bf16[64,256]{1,0:T(8,128)(2,1)S(1)} %get-tuple-element.27), channel_id=1, source_target_pairs={{0,8},{1,9},{2,10},{3,11},{4,12},{5,13},{6,14},{7,15},{8,0},{9,1},... | collective-permute-start | bytes 98312 | tf_op jit(solution)/shard_map/ppermute | solution.py:35
  42.6 4.9 %collective-permute-start.10 = (bf16[64,256]{1,0:T(8,128)(2,1)S(1)}, bf16[64,256]{1,0:T(8,128)(2,1)S(1)}, u32[]{:S(2)}, u32[]{:S(2)}) collective-permute-start(bf16[64,256]{1,0:T(8,128)(2,1)S(1)} %get-tuple-element.27), channel_id=1, source_target_pairs={{0,12},{1,13},{2,14},{3,15},{4,8},{5,9},{6,10},{7,11},{8,4},{9,5},... | collective-permute-start | bytes 98312 | tf_op jit(solution)/shard_map/ppermute | solution.py:35
  43.4 13.1 %collective-permute-start.19 = (bf16[512,256]{1,0:T(8,128)(2,1)S(1)}, bf16[512,256]{1,0:T(8,128)(2,1)S(1)}, u32[]{:S(2)}, u32[]{:S(2)}) collective-permute-start(bf16[512,256]{1,0:T(8,128)(2,1)S(1)} %broadcast_select_fusion.1.block_own.down_pack), channel_id=1, source_target_pairs={{0,1},{2,3},{4,5},{6,7},{8,9},{10,11},{12,13},{14,15},{16,17},{18,... | collective-permute-start | bytes 786440 | tf_op jit(solution)/shard_map/ppermute | solution.py:491
  48.7 7.8 %collective-permute-start.12 = (bf16[64,256]{1,0:T(8,128)(2,1)S(1)}, bf16[64,256]{1,0:T(8,128)(2,1)S(1)}, u32[]{:S(2)}, u32[]{:S(2)}) collective-permute-start(bf16[64,256]{1,0:T(8,128)(2,1)S(1)} %get-tuple-element.30), channel_id=1, source_target_pairs={{0,16},{1,17},{2,18},{3,19},{4,20},{5,21},{6,22},{7,23},{8,24},{9,... | collective-permute-start | bytes 98312 | tf_op jit(solution)/shard_map/ppermute | solution.py:35
  52.2 6.5 %collective-permute-start.14 = (bf16[512,256]{1,0:T(8,128)(2,1)S(1)}, bf16[512,256]{1,0:T(8,128)(2,1)S(1)}, u32[]{:S(2)}, u32[]{:S(2)}) collective-permute-start(bf16[512,256]{1,0:T(8,128)(2,1)S(1)} %broadcast_select_fusion.2), channel_id=1, source_target_pairs={{0,8},{16,24}} | collective-permute-start | bytes 786440 | tf_op jit(solution)/shard_map/ppermute | solution.py:491
  54.8 8.3 %collective-permute-start.15 = (bf16[512,256]{1,0:T(8,128)(2,1)S(1)}, bf16[512,256]{1,0:T(8,128)(2,1)S(1)}, u32[]{:S(2)}, u32[]{:S(2)}) collective-permute-start(bf16[512,256]{1,0:T(8,128)(2,1)S(1)} %get-tuple-element.23.after), channel_id=1, source_target_pairs={{4,0},{12,8},{20,16},{28,24}} | collective-permute-start | bytes 786440 | tf_op jit(solution)/shard_map/ppermute | solution.py:486
  56.9 10.8 %collective-permute-start.23 = (bf16[288,256]{1,0:T(8,128)(2,1)S(1)}, bf16[288,256]{1,0:T(8,128)(2,1)S(1)}, u32[]{:S(2)}, u32[]{:S(2)}) collective-permute-start(bf16[288,256]{1,0:T(8,128)(2,1)S(1)} %local.1.after.l0), channel_id=1, source_target_pairs={{0,2},{1,3},{2,0},{3,1},{4,6},{5,7},{6,4},{7,5},{8,10},{9,11},{10,... | collective-permute-start | bytes 442376 | tf_op jit(solution)/shard_map/ppermute | solution.py:35
  63.5 3.8 %collective-permute-start.16 = (bf16[32,256]{1,0:T(8,128)(2,1)S(1)}, bf16[32,256]{1,0:T(8,128)(2,1)S(1)}, u32[]{:S(2)}, u32[]{:S(2)}) collective-permute-start(bf16[32,256]{1,0:T(8,128)(2,1)S(1)} %fall.1.mine), channel_id=1, source_target_pairs={{0,4},{1,5},{2,6},{3,7},{4,0},{5,1},{6,2},{7,3},{8,12},{9,13},{10,... | collective-permute-start | bytes 49160 | tf_op jit(solution)/shard_map/ppermute | solution.py:35
  67.4 3.8 %collective-permute-start.20 = (bf16[32,256]{1,0:T(8,128)(2,1)S(1)}, bf16[32,256]{1,0:T(8,128)(2,1)S(1)}, u32[]{:S(2)}, u32[]{:S(2)}) collective-permute-start(bf16[32,256]{1,0:T(8,128)(2,1)S(1)} %step_down.1), channel_id=1, source_target_pairs={{0,2},{1,3},{2,0},{3,1},{4,6},{5,7},{6,4},{7,5},{8,10},{9,11},{10,... | collective-permute-start | bytes 49160 | tf_op jit(solution)/shard_map/ppermute | solution.py:35
  67.5 4.9 %collective-permute-start.22 = (bf16[288,256]{1,0:T(8,128)(2,1)S(1)}, bf16[288,256]{1,0:T(8,128)(2,1)S(1)}, u32[]{:S(2)}, u32[]{:S(2)}) collective-permute-start(bf16[288,256]{1,0:T(8,128)(2,1)S(1)} %local.1.after.l0), channel_id=1, source_target_pairs={{0,1},{1,0},{2,3},{3,2},{4,5},{5,4},{6,7},{7,6},{8,9},{9,8},{10,11... | collective-permute-start | bytes 442376 | tf_op jit(solution)/shard_map/ppermute | solution.py:35
  67.6 4.8 %collective-permute-start.24 = (bf16[288,256]{1,0:T(8,128)(2,1)S(1)}, bf16[288,256]{1,0:T(8,128)(2,1)S(1)}, u32[]{:S(2)}, u32[]{:S(2)}) collective-permute-start(bf16[288,256]{1,0:T(8,128)(2,1)S(1)} %collective-permute-done.23.l2), channel_id=1, source_target_pairs={{0,1},{1,0},{2,3},{3,2},{4,5},{5,4},{6,7},{7,6},{8,9},{9,8},{10,11... | collective-permute-start | bytes 442376 | tf_op jit(solution)/shard_map/ppermute | solution.py:35
  71.3 1.2 %collective-permute-start.21 = (bf16[32,256]{1,0:T(8,128)(2,1)S(1)}, bf16[32,256]{1,0:T(8,128)(2,1)S(1)}, u32[]{:S(2)}, u32[]{:S(2)}) collective-permute-start(bf16[32,256]{1,0:T(8,128)(2,1)S(1)} %broadcast_select_fusion.4.f_own), channel_id=1, source_target_pairs={{0,1},{1,0},{2,3},{3,2},{4,5},{5,4},{6,7},{7,6},{8,9},{9,8},{10,11... | collective-permute-start | bytes 49160 | tf_op jit(solution)/shard_map/ppermute | solution.py:35
  (5 other events, 4.1 us)

commit v4 on v3

v4 whole, which is shorter than its diff:
```python
import functools

import jax
import jax.numpy as jnp
from jax import lax
from jax.experimental import pallas as pl
from jax.experimental.pallas import tpu as pltpu
from jax.sharding import PartitionSpec as P

SPREAD = 4
LANES = 128
BF = jnp.bfloat16
F32 = jnp.float32
VMEM = pl.BlockSpec(memory_space=pltpu.VMEM)
SMEM = pl.BlockSpec(memory_space=pltpu.SMEM)
ANY = pl.BlockSpec(memory_space=pl.ANY)
HBM = pl.BlockSpec(memory_space=pltpu.HBM)
LIMIT = 32 * 2**20


def mm(a, b):
    return jnp.dot(a, b, preferred_element_type=F32)


def params():
    return pltpu.CompilerParams(vmem_limit_bytes=LIMIT)


def in_hbm(*arrays):
    return [pltpu.with_memory_space_constraint(array, pltpu.HBM) for array in arrays]


def took(micros):
    return pl.CostEstimate(flops=0, bytes_accessed=int(micros * 3e6), transcendentals=0)


def swap(block, mask):
    count = lax.axis_size("leaf")
    return lax.ppermute(block, "leaf", [(i, i ^ mask) for i in range(count)])


def bit_of_device(bit):
    return (lax.axis_index("leaf").astype(jnp.int32) & (1 << bit)) != 0


def held(bit, own, arrived, begin, size):
    rows = slice(begin, begin + size)
    if own is arrived:
        return own[rows, :]
    return jnp.where(bit_of_device(bit), own[rows, :], arrived[rows, :])


def gather_columns(table, slots, store):
    rows, columns = table.shape
    tiles = columns // LANES
    for out_tile in range(tiles):
        slot = jnp.broadcast_to(slots(out_tile), (rows, LANES))
        low = slot & (LANES - 1)
        high = slot // LANES
        found = None
        for tile in range(tiles):
            part = jnp.take_along_axis(
                table[:, tile * LANES : (tile + 1) * LANES], low, axis=1
            )
            found = part if found is None else jnp.where(high == tile, part, found)
        store(out_tile, found)


def start_kernel(rhs_hbm, order_hbm, basis_hbm, map_hbm, leaf_up, leaf_down, node_up, node_down, node_cross,
                 pick, tree_ref, red_ref, low_ref, high_ref, toplow_ref, tophigh_ref, up_ref, down_ref,
                 rhs, order, basis, table, seats, sems):
    rank = red_ref.shape[1]
    cross_low = node_cross.at[pl.ds(0, rank), :]
    cross_high = node_cross.at[pl.ds(rank, rank), :]
    copies = [
        pltpu.make_async_copy(rhs_hbm, rhs, sems.at[0]),
        pltpu.make_async_copy(order_hbm, order, sems.at[1]),
        pltpu.make_async_copy(map_hbm, seats, sems.at[2]),
        pltpu.make_async_copy(basis_hbm, basis, sems.at[3]),
    ]
    packs = (
        (low_ref, (node_up, node_down, cross_low)),
        (high_ref, (node_up, node_down, cross_high)),
        (toplow_ref, (node_up, cross_low)),
        (tophigh_ref, (node_up, cross_high)),
        (up_ref, (leaf_up,)),
        (down_ref, (leaf_down,)),
    )
    for dst, parts in packs:
        for i, part in enumerate(parts):
            copies.append(
                pltpu.make_async_copy(
                    part, dst.at[pl.ds(i * rank, rank), :], sems.at[len(copies)]
                )
            )
    for copy in copies:
        copy.start()
    copies[2].wait()
    me = lax.axis_index("leaf").astype(jnp.int32)
    offset = me & (SPREAD - 1)
    base = me - offset
    placed = [seats[base + slot] & (SPREAD - 1) for slot in range(SPREAD)]
    seat = placed[0]
    for slot in range(1, SPREAD):
        seat = jnp.where(offset == slot, placed[slot], seat)
    for m in range(SPREAD):
        source = jnp.int32(0)
        for slot in range(1, SPREAD):
            source = jnp.where(placed[slot] == (offset ^ m), slot, source)
        pick[m] = source ^ offset
    pick[SPREAD] = seat ^ offset
    copies[0].wait()
    table[...] = rhs[...].astype(F32)
    copies[1].wait()

    def store(tile, found):
        tree_ref[:, tile * LANES : (tile + 1) * LANES] = found.astype(BF)

    gather_columns(
        table, lambda tile: order[:, tile * LANES : (tile + 1) * LANES], store
    )
    copies[3].wait()
    red_ref[...] = mm(tree_ref[...], basis[...]).astype(BF)
    for copy in copies[4:]:
        copy.wait()


def start(right_sides, point_order, basis_in, leaf_map, *matrices):
    rows, columns = right_sides.shape
    rank = basis_in.shape[1]

    def block(count):
        return jax.ShapeDtypeStruct((count * rank, rank), BF)

    return pl.pallas_call(
        start_kernel,
        out_shape=(
            jax.ShapeDtypeStruct((SPREAD + 1,), jnp.int32),
            jax.ShapeDtypeStruct((rows, columns), BF),
            jax.ShapeDtypeStruct((rows, rank), BF),
            block(3),
            block(3),
            block(2),
            block(2),
            block(1),
            block(1),
        ),
        in_specs=[HBM] * 9,
        out_specs=(SMEM,) + (VMEM,) * 8,
        scratch_shapes=[
            pltpu.VMEM(right_sides.shape, BF),
            pltpu.VMEM(point_order.shape, jnp.int32),
            pltpu.VMEM(basis_in.shape, BF),
            pltpu.VMEM(right_sides.shape, F32),
            pltpu.SMEM(leaf_map.shape, jnp.int32),
            pltpu.SemaphoreType.DMA((16,)),
        ],
        compiler_params=params(),
        cost_estimate=took(2.7),
        name="start",
    )(*in_hbm(right_sides, point_order, basis_in, leaf_map, *matrices))


def invert_kernel(order_hbm, after, inv_ref, order, sem):
    copy = pltpu.make_async_copy(order_hbm, order, sem)
    copy.start()
    copy.wait()
    slot = order[...]
    columns = slot.shape[1]
    tiles = columns // LANES
    low = slot & (LANES - 1)
    high = slot // LANES
    here = lax.broadcasted_iota(jnp.int32, (tiles, columns), 1)
    mask = lax.broadcasted_iota(jnp.int32, (tiles, columns), 0) == high
    left = jnp.concatenate(
        [
            jnp.where(mask, (here // LANES).astype(F32), 0.0),
            jnp.where(mask, (here & (LANES - 1)).astype(F32), 0.0),
        ],
        0,
    ).astype(BF)
    right = (lax.broadcasted_iota(jnp.int32, (LANES, columns), 0) == low).astype(F32).astype(BF)
    both = lax.dot_general(left, right, (((1,), (1,)), ((), ())), preferred_element_type=F32)
    inv_ref[...] = (both[:tiles] * LANES + both[tiles:]).astype(jnp.int32)


def invert(point_order, after):
    columns = point_order.shape[1]
    return pl.pallas_call(
        invert_kernel,
        out_shape=jax.ShapeDtypeStruct((columns // LANES, LANES), jnp.int32),
        in_specs=[HBM, ANY],
        out_specs=VMEM,
        scratch_shapes=[pltpu.VMEM(point_order.shape, jnp.int32), pltpu.SemaphoreType.DMA],
        compiler_params=params(),
        cost_estimate=took(1.0),
        name="invert",
    )(*in_hbm(point_order), after)


def near_kernel(first, tree_ref, inverse_hbm, after, near_ref, held, sems):
    chunks, _, width = held.shape
    copies = [
        pltpu.make_async_copy(
            inverse_hbm.at[:, pl.ds(first + i * width, width)], held.at[i], sems.at[i]
        )
        for i in range(chunks)
    ]
    for copy in copies:
        copy.start()
    for i, copy in enumerate(copies):
        copy.wait()
        near_ref[:, i * width : (i + 1) * width] = mm(tree_ref[...], held[i])


def near_strip(tree, leaf_inverse, strip, strips, after):
    rows, columns = tree.shape
    width = columns // strips
    chunk = 2 * LANES
    chunks = width // chunk
    return pl.pallas_call(
        functools.partial(near_kernel, strip * width),
        out_shape=jax.ShapeDtypeStruct((rows, width), F32),
        in_specs=[VMEM, HBM, ANY],
        out_specs=VMEM,
        scratch_shapes=[
            pltpu.VMEM((chunks, columns, chunk), BF),
            pltpu.SemaphoreType.DMA((chunks,)),
        ],
        compiler_params=params(),
        cost_estimate=took(5.6 / strips),
        name="near",
    )(tree, *in_hbm(leaf_inverse), after)


def join_kernel(mine, other, after, out_ref):
    rows = mine.shape[0]
    out_ref[:rows] = mine[...]
    out_ref[rows:] = other[...]


def join(mine, other, after):
    rows, rank = mine.shape
    return pl.pallas_call(
        join_kernel,
        out_shape=jax.ShapeDtypeStruct((2 * rows, rank), BF),
        in_specs=[VMEM] * 2 + [ANY],
        out_specs=VMEM,
        compiler_params=params(),
        cost_estimate=took(0.1),
        name="join",
    )(mine, other, after)


def leaf_kernel(pick, pair_own, pair_x, up_ref, after, g0_ref, out_ref, table):
    rows = out_ref.shape[0]
    for m in range(SPREAD):
        pair = pair_own if m < 2 else pair_x
        table[m] = pair[m % 2 * rows : (m % 2 + 1) * rows]
    for m in range(SPREAD):
        g0_ref[m] = table[pick[m]]
    out_ref[...] = mm(g0_ref[0], up_ref[...])


def leaf_rise(pick, pair_own, pair_x, leaf_up, after):
    double, rank = pair_own.shape
    rows = double // 2
    return pl.pallas_call(
        leaf_kernel,
        out_shape=(
            jax.ShapeDtypeStruct((SPREAD, rows, rank), BF),
            jax.ShapeDtypeStruct((rows, rank), F32),
        ),
        in_specs=[SMEM] + [VMEM] * 3 + [ANY],
        out_specs=(VMEM,) * 2,
        scratch_shapes=[pltpu.VMEM((SPREAD, rows, rank), BF)],
        compiler_params=params(),
        cost_estimate=took(0.4),
        name="leaf_rise",
    )(pick, pair_own, pair_x, leaf_up, after)


def node_kernel(mine, other, maps_own, maps_in, after, out_ref):
    rows, rank = mine.shape
    g1 = (mine[...] + other[...]).astype(BF)
    out_ref[:rows] = g1
    out_ref[rows:] = mm(g1, held(0, maps_own, maps_in, 0, rank)).astype(BF)


def node_rise(mine, other, maps, after):
    rows, rank = mine.shape
    return pl.pallas_call(
        node_kernel,
        out_shape=jax.ShapeDtypeStruct((2 * rows, rank), BF),
        in_specs=[VMEM] * 4 + [ANY],
        out_specs=VMEM,
        compiler_params=params(),
        cost_estimate=took(0.2),
        name="node_rise",
    )(mine, other, *maps, after)


def level_kernel(bit, mine, other, maps_own, maps_in, after, sibling_ref, out_ref):
    rows = mine.shape[0] // 2
    rank = mine.shape[1]
    sibling_ref[...] = other[:rows]
    grown = (mine[rows:].astype(F32) + other[rows:].astype(F32)).astype(BF)
    out_ref[:rows] = grown
    out_ref[rows:] = mm(grown, held(bit, maps_own, maps_in, 0, rank)).astype(BF)


def level_rise(bit, mine, other, maps, after):
    double, rank = mine.shape
    return pl.pallas_call(
        functools.partial(level_kernel, bit),
        out_shape=(
            jax.ShapeDtypeStruct((double // 2, rank), BF),
            jax.ShapeDtypeStruct((double, rank), BF),
        ),
        in_specs=[VMEM] * 4 + [ANY],
        out_specs=(VMEM,) * 2,
        compiler_params=params(),
        cost_estimate=took(0.25),
        name="level_rise",
    )(mine, other, *maps, after)


def fall_kernel(low_bit, count, *refs):
    mine, other = refs[:2]
    siblings = refs[2 : 1 + count]
    owns = refs[1 + count : 2 + 2 * count]
    arrivals = refs[2 + 2 * count : 3 + 3 * count]
    out = refs[4 + 3 * count]
    rows = mine.shape[0] // 2
    rank = mine.shape[1]
    top = (mine[rows:].astype(F32) + other[rows:].astype(F32)).astype(BF)

    def part(k, begin):
        return held(low_bit + min(k, 1), owns[k], arrivals[k], begin, rank)

    value = mm(top, part(count, 0)).astype(BF)
    for k in range(count, 0, -1):
        sibling = other[:rows] if k == count else siblings[k - 1][...]
        cross = part(k, owns[k].shape[0] - rank)
        value = (mm(sibling, cross) + mm(value, part(k - 1, rank))).astype(BF)
    out[...] = value


def fall(low_bit, mine, other, siblings, maps, after):
    count = len(maps) - 1
    double, rank = mine.shape
    return pl.pallas_call(
        functools.partial(fall_kernel, low_bit, count),
        out_shape=jax.ShapeDtypeStruct((double // 2, rank), BF),
        in_specs=[VMEM] * (3 + 3 * count) + [ANY],
        out_specs=VMEM,
        compiler_params=params(),
        cost_estimate=took(0.45),
        name="fall",
    )(mine, other, *siblings, *[m[0] for m in maps], *[m[1] for m in maps], after)


def step_kernel(bit, mine, other, sibling, maps_own, maps_in, block_own, block_in, after, out):
    rank = mine.shape[1]
    value = jnp.where(bit_of_device(bit), other[...], mine[...])
    cross = held(bit, maps_own, maps_in, 2 * rank, rank)
    down = held(bit - 1, block_own, block_in, rank, rank)
    out[...] = (mm(sibling[...], cross) + mm(value, down)).astype(BF)


def step_down(bit, mine, other, sibling, maps, block_maps, after):
    rows, rank = mine.shape
    return pl.pallas_call(
        functools.partial(step_kernel, bit),
        out_shape=jax.ShapeDtypeStruct((rows, rank), BF),
        in_specs=[VMEM] * 7 + [ANY],
        out_specs=VMEM,
        compiler_params=params(),
        cost_estimate=took(0.2),
        name="step_down",
    )(mine, other, sibling, *maps, *block_maps, after)


def local_kernel(g0_ref, node_pay, node_own, node_in, block_own, block_in, cross_in, down_ref, after, out_ref):
    rank = down_ref.shape[0]
    rows = node_pay.shape[0] // 2
    cross = held(1, block_own, block_in, 2 * rank, rank)
    cross = jnp.where(bit_of_device(0), cross_in[...], cross)
    inner = mm(node_pay[:rows], cross).astype(BF)
    out_ref[:rank] = mm(held(0, node_own, node_in, rank, rank), down_ref[...]).astype(BF)
    nearest = held(0, node_own, node_in, 2 * rank, rank)
    out_ref[rank:] = (mm(g0_ref[1], nearest) + mm(inner, down_ref[...])).astype(BF)


def local(g0, node_pay, node_maps, block_maps, block_cross, leaf_down, after):
    _, rows, rank = g0.shape
    return pl.pallas_call(
        local_kernel,
        out_shape=jax.ShapeDtypeStruct((rank + rows, rank), BF),
        in_specs=[VMEM] * 8 + [ANY],
        out_specs=VMEM,
        compiler_params=params(),
        cost_estimate=took(0.6),
        name="local",
    )(g0, node_pay, *node_maps, *block_maps, block_cross, leaf_down, after)


def choose_kernel(bit, upper, lower, after, out_ref):
    out_ref[...] = held(bit, upper, lower, 0, out_ref.shape[0])


def choose(bit, upper, lower, after):
    return pl.pallas_call(
        functools.partial(choose_kernel, bit),
        out_shape=jax.ShapeDtypeStruct(upper.shape, BF),
        in_specs=[VMEM] * 2 + [ANY],
        out_specs=VMEM,
        compiler_params=params(),
        cost_estimate=took(0.2),
        name="choose",
    )(upper, lower, after)


def final_kernel(strips, pick, f_own, f_core, l0, l1, l2, l3, out_basis, inv_ref, *refs):
    nears = refs[:strips]
    answer, total, leaf_f = refs[strips:]
    rank = f_own.shape[1]
    f2 = jnp.where(bit_of_device(0), f_core[...], f_own[...])
    for m, pack_ref in enumerate((l0, l1, l2, l3)):

        @pl.when(pick[SPREAD] == m)
        def _():
            leaf_f[...] = (mm(f2, pack_ref[:rank, :]) + pack_ref[rank:, :].astype(F32)).astype(BF)

    width = nears[0].shape[1]
    for i in range(strips):
        span = slice(i * width, (i + 1) * width)
        total[:, span] = nears[i][...] + mm(leaf_f[...], out_basis[:, span])

    def store(tile, found):
        answer[:, tile * LANES : (tile + 1) * LANES] = found

    gather_columns(total, lambda tile: inv_ref[tile : tile + 1, :], store)


def final(pick, f2, f2_core, locals_, basis_out, inverse_order, nears):
    rows, rank = f2.shape
    columns = basis_out.shape[1]
    return pl.pallas_call(
        functools.partial(final_kernel, len(nears)),
        out_shape=jax.ShapeDtypeStruct((rows, columns), F32),
        in_specs=[SMEM] + [VMEM] * (8 + len(nears)),
        out_specs=VMEM,
        scratch_shapes=[pltpu.VMEM((rows, columns), F32), pltpu.VMEM((rows, rank), BF)],
        compiler_params=params(),
        cost_estimate=took(2.9),
        name="final",
    )(pick, f2, f2_core, *locals_, basis_out, inverse_order, *nears)


def body(
    right_sides,
    point_order,
    leaf_inverse,
    basis_in,
    basis_out,
    leaf_up,
    leaf_down,
    node_up,
    node_down,
    node_cross,
    leaf_map,
):
    members = lax.axis_size("leaf")
    levels = members.bit_length() - 1
    cut = SPREAD.bit_length() - 1
    me = lax.axis_index("leaf")
    rank = leaf_up.shape[1]
    offset = me & (SPREAD - 1)

    def to_left(block, bit):
        step = 1 << bit
        return lax.ppermute(block, "leaf", [(i + step, i) for i in range(0, members, 2 * step)])

    def to_right(block, bit, every):
        step = 1 << bit
        pairs = [(i, i + step) for i in range(0, members, every) if i & step == 0]
        return lax.ppermute(block, "leaf", pairs)

    pick, tree, reduced, low, high, top_low, top_high, up_map, down_map = start(
        right_sides, point_order, basis_in, leaf_map, leaf_up, leaf_down, node_up, node_down, node_cross
    )
    node_maps = (high, to_left(low, 0))
    block_maps = (high, to_left(low, 1))
    held_maps = []
    for level in range(cut + 1, levels + 1):
        first, second = (top_low, top_high) if level == levels else (low, high)
        held_maps.append((second, to_left(first, level - 1)))

    pair = join(reduced, swap(reduced, 1), reduced)
    g0, product = leaf_rise(pick, pair, swap(pair, 2), up_map, pair)
    pay = node_rise(product, swap(product, 1), node_maps, product)
    node_in = swap(pay, 2)
    siblings = []
    near0 = near1 = None
    for bit in range(1, levels - 1):
        arrived = node_in if bit == 1 else swap(pay, 1 << bit)
        after = pay
        if bit == 2:
            near0 = after = near_strip(tree, leaf_inverse, 0, 2, pay)
            block_cross = choose(1, high[2 * rank :], block_maps[1][2 * rank :], pay)
            block_cross = to_right(block_cross, 0, 2)
        if bit == cut + 1:
            for level in range(cut + 3, levels + 1):
                own, passed = held_maps[level - cut - 1]
                now = choose(level - 1, own, passed, pay)
                for step in range(level - 2, cut, -1):
                    passed = to_right(now, step, 1 << step)
                    if step > cut + 1:
                        now = choose(step, passed, now, pay)
                held_maps[level - cut - 1] = (passed, now)
        if bit == 3:
            own_local = after = local(
                g0, node_in, node_maps, block_maps, block_cross, down_map, pay
            )
        maps = block_maps if bit == 1 else held_maps[bit - cut]
        sibling, pay = level_rise(min(bit, cut + 1), pay, arrived, maps, after)
        siblings.append(sibling)

    local_x = swap(own_local, 2)
    locals_ = [own_local, swap(own_local, 1), local_x, swap(local_x, 1)]
    near1 = near_strip(tree, leaf_inverse, 1, 2, pay)

    cut_f = fall(cut, pay, swap(pay, 1 << (levels - 1)), siblings[2:], held_maps, near1)
    inverse_order = invert(point_order, cut_f)
    block_f = step_down(
        cut, cut_f, swap(cut_f, SPREAD), siblings[1], held_maps[0], block_maps, inverse_order
    )
    from_x = swap(block_f, 2)
    block_f = jnp.where(offset & 2 != 0, from_x, block_f)
    return final(
        pick, block_f, swap(block_f, 1), locals_, basis_out, inverse_order, [near0, near1]
    )


def solution(mesh):
    placed = (
        P(None, "leaf"),
        P("leaf", None),
        P("leaf", None),
        P("leaf", None),
        P("leaf", None),
        P("leaf", None),
        P("leaf", None),
        P("leaf", None),
        P("leaf", None),
        P("leaf", None),
        P(),
    )
    return jax.shard_map(
        body, mesh=mesh, in_specs=placed, out_specs=P(None, "leaf"), check_vma=False
    )
```

time: 75.9 us -> 57.3 us (0.75)
  local copies, waits for them, and re-layouts: 9.64 us -> 0.03 us
  starting transfers between devices: 27.6 us -> 21.8 us
  Pallas kernels: 17.2 us -> 14.9 us
    unnamed x24 -> x2, local copies, waits for them, and re-layouts: 9.63 us -> 0.01 us
    ppermute x16 -> x13, waiting for transfers between devices: 14.1 us -> 19 us  [swap(): return lax.ppermute(block, 'leaf', [(i, i ^ mask) for i in range(count)])]
    ppermute x7 -> x5, waiting for transfers between devices: 4.39 us -> 0.01 us  [to_left(): lax.ppermute(block, 'leaf', [(i + step, i) for i in range(0, members, 2 *...]
    pallas_call x4 -> x7, Pallas kernels: 5.35 us -> 1.44 us  [the longest x3 0.93 us: level_rise(): pl.pallas_call(functools.partial(level_kernel, bit), out_shape=(jax.Shape...]
    ppermute x16 -> x13, starting transfers between devices: 13.3 us -> 10.3 us  [swap(): return lax.ppermute(block, 'leaf', [(i, i ^ mask) for i in range(count)])]
    ppermute x7 -> x5, starting transfers between devices: 9.16 us -> 6.45 us  [to_left(): lax.ppermute(block, 'leaf', [(i + step, i) for i in range(0, members, 2 *...]
    pallas_call x2, Pallas kernels: 4.41 us -> 5.65 us  [near_strip(): pl.pallas_call(functools.partial(near_kernel, strip * width), out_shape=j...]
    pallas_call x1, Pallas kernels: 1.06 us -> 0.15 us  [node_rise(): pl.pallas_call(node_kernel, out_shape=jax.ShapeDtypeStruct((2 * rows, ran...]
  transfers between devices with their start and end apart: 25 -> 20, of which waited for: 7 -> 9; matrix products, arithmetic and copies ran while one was open for 0% -> 0% of each run, Pallas kernels for 13% -> 17%
where the time goes in v4:
time: 57.3 us; the launch traced here: 57 us
  starting transfers between devices  21.8 us (38%)
  waiting for transfers between devices  20 us (35%)
  Pallas kernels  14.9 us (26%)
    ppermute x13, waiting for transfers between devices, swap(): return lax.ppermute(block, 'leaf', [(i, i ^ mask) for i in range(count)])  19 us
    ppermute x13, starting transfers between devices, swap(): return lax.ppermute(block, 'leaf', [(i, i ^ mask) for i in range(count)])  10.3 us
    ppermute x5, starting transfers between devices, to_left(): lax.ppermute(block, 'leaf', [(i + step, i) for i in range(0, members, 2 *...  6.45 us
    pallas_call x2, Pallas kernels, near_strip(): pl.pallas_call(functools.partial(near_kernel, strip * width), out_shape=j...  5.65 us
    ppermute x2, starting transfers between devices, to_right(): return lax.ppermute(block, 'leaf', pairs)  5.09 us
    pallas_call x1, Pallas kernels, final(): pl.pallas_call(functools.partial(final_kernel, len(nears)), out_shape=jax...  2.9 us
    pallas_call x1, Pallas kernels, start(): pl.pallas_call(start_kernel, out_shape=(jax.ShapeDtypeStruct((SPREAD + 1,...  2.62 us
  transfers between devices with their start and end apart: 20, of which 9 were waited for; matrix products, arithmetic and copies ran while one was open for 0% of the time, Pallas kernels for 17%

profile of v4, /device:TPU:0, one launch (start us, length us, event | category | flops | bytes accessed | tf_op | source)
XLA Modules:
  0.0 57.0 jit_solution(12905023152117657659)
XLA Ops:
  0.0 2.6 %start.1 = (s32[5]{0:T(128)S(1)}, bf16[32,2048]{1,0:T(8,128)(2,1)S(1)}, bf16[32,256]{1,0:T(8,128)(2,1)S(1)}, bf16[768,256]{1,0:T(8,128)(2,1)S(1)}, bf16[768,256]...) custom-call(bf16[32,2048]{1,0:T(8,128)(2,1)} %rhs_hbm.1, ...), custom_call_target="tpu_custom_call" | custom-call | bytes 8100000 | tf_op jit(solution)/shard_map/start/pallas_call | solution.py:135
  2.6 1.3 %collective-permute-start.3 = (bf16[768,256]{1,0:T(8,128)(2,1)S(1)}, bf16[768,256]{1,0:T(8,128)(2,1)S(1)}, u32[]{:S(2)}, u32[]{:S(2)}) collective-permute-start(bf16[768,256]{1,0:T(8,128)(2,1)S(1)} %get-tuple-element.26), channel_id=1, source_target_pairs={{1,0},{3,2},{5,4},{7,6},{9,8},{11,10},{13,12},{15,14},{17,16},{19,... | collective-permute-start | bytes 1179656 | tf_op jit(solution)/shard_map/ppermute | solution.py:483
  3.9 1.3 %collective-permute-start.5 = (bf16[768,256]{1,0:T(8,128)(2,1)S(1)}, bf16[768,256]{1,0:T(8,128)(2,1)S(1)}, u32[]{:S(2)}, u32[]{:S(2)}) collective-permute-start(bf16[768,256]{1,0:T(8,128)(2,1)S(1)} %get-tuple-element.26), channel_id=1, source_target_pairs={{2,0},{6,4},{10,8},{14,12},{18,16},{22,20},{26,24},{30,28}} | collective-permute-start | bytes 1179656 | tf_op jit(solution)/shard_map/ppermute | solution.py:483
  5.2 1.3 %collective-permute-start.7 = (bf16[768,256]{1,0:T(8,128)(2,1)S(1)}, bf16[768,256]{1,0:T(8,128)(2,1)S(1)}, u32[]{:S(2)}, u32[]{:S(2)}) collective-permute-start(bf16[768,256]{1,0:T(8,128)(2,1)S(1)} %get-tuple-element.26), channel_id=1, source_target_pairs={{4,0},{12,8},{20,16},{28,24}} | collective-permute-start | bytes 1179656 | tf_op jit(solution)/shard_map/ppermute | solution.py:483
  6.5 1.3 %collective-permute-start.12 = (bf16[512,256]{1,0:T(8,128)(2,1)S(1)}, bf16[512,256]{1,0:T(8,128)(2,1)S(1)}, u32[]{:S(2)}, u32[]{:S(2)}) collective-permute-start(bf16[512,256]{1,0:T(8,128)(2,1)S(1)} %get-tuple-element.35), channel_id=1, source_target_pairs={{16,0}} | collective-permute-start | bytes 786440 | tf_op jit(solution)/shard_map/ppermute | solution.py:483
  7.9 1.2 %collective-permute-done.other = bf16[32,256]{1,0:T(8,128)(2,1)S(1)} collective-permute-done((bf16[32,256]{1,0:T(8,128)(2,1)S(1)}, bf16[32,256]{1,0:T(8,128)(2,1)S(1)}, u32[]{:S(2)}, u32[]{:S(2)}) %collective-permute-start) | collective-permute-done | bytes 16416 | tf_op jit(solution)/shard_map/ppermute | solution.py:39
  9.1 1.9 %collective-permute-start.1 = (bf16[64,256]{1,0:T(8,128)(2,1)S(1)}, bf16[64,256]{1,0:T(8,128)(2,1)S(1)}, u32[]{:S(2)}, u32[]{:S(2)}) collective-permute-start(bf16[64,256]{1,0:T(8,128)(2,1)S(1)} %join.1.pair_own.after), channel_id=1, source_target_pairs={{0,2},{1,3},{2,0},{3,1},{4,6},{5,7},{6,4},{7,5},{8,10},{9,11},{10,... | collective-permute-start | bytes 98312 | tf_op jit(solution)/shard_map/ppermute | solution.py:39
  11.0 3.6 %collective-permute-done.1.pair_x = bf16[64,256]{1,0:T(8,128)(2,1)S(1)} collective-permute-done((bf16[64,256]{1,0:T(8,128)(2,1)S(1)}, bf16[64,256]{1,0:T(8,128)(2,1)S(1)}, u32[]{:S(2)}, u32[]{:S(2)}) %collective-permute-start.1) | collective-permute-done | bytes 32800 | tf_op jit(solution)/shard_map/ppermute | solution.py:39
  14.6 0.7 %leaf_rise.1 = (bf16[4,32,256]{2,1,0:T(8,128)(2,1)S(1)}, f32[32,256]{1,0:T(8,128)S(1)}) custom-call(s32[5]{0:T(128)S(1)} %get-tuple-element.21.pick, bf16[64,256]{1,0:T(8,128)(2,1)S(1)} %join.1.pair_own.after, bf16[64,256]{1,0:T(8,128)(2,1)S(1)} %collective-permute-done.1.pair_x, bf16[256,256]{1,0:T(8,128)(2,1)S(1)} %get-tuple-element.23.up_ref, ...), custom_call_target="tpu_custom_call" | custom-call | bytes 1200000 | tf_op jit(solution)/shard_map/leaf_rise/pallas_call | solution.py:268
  15.3 1.2 %collective-permute-done.2.other = f32[32,256]{1,0:T(8,128)S(1)} collective-permute-done((f32[32,256]{1,0:T(8,128)S(1)}, f32[32,256]{1,0:T(8,128)S(1)}, u32[]{:S(2)}, u32[]{:S(2)}) %collective-permute-start.2) | collective-permute-done | bytes 32800 | tf_op jit(solution)/shard_map/ppermute | solution.py:39
  16.5 1.3 %collective-permute-start.9 = (bf16[768,256]{1,0:T(8,128)(2,1)S(1)}, bf16[768,256]{1,0:T(8,128)(2,1)S(1)}, u32[]{:S(2)}, u32[]{:S(2)}) collective-permute-start(bf16[768,256]{1,0:T(8,128)(2,1)S(1)} %get-tuple-element.26), channel_id=1, source_target_pairs={{8,0},{24,16}} | collective-permute-start | bytes 1179656 | tf_op jit(solution)/shard_map/ppermute | solution.py:483
  18.0 3.9 %collective-permute-done.4.other.node_pay = bf16[64,256]{1,0:T(8,128)(2,1)S(1)} collective-permute-done((bf16[64,256]{1,0:T(8,128)(2,1)S(1)}, bf16[64,256]{1,0:T(8,128)(2,1)S(1)}, u32[]{:S(2)}, u32[]{:S(2)}) %collective-permute-start.4) | collective-permute-done | bytes 32800 | tf_op jit(solution)/shard_map/ppermute | solution.py:39
  21.9 0.6 %level_rise.3 = (bf16[32,256]{1,0:T(8,128)(2,1)}, bf16[64,256]{1,0:T(8,128)(2,1)S(1)}) custom-call(bf16[64,256]{1,0:T(8,128)(2,1)S(1)} %node_rise.1.mine.after, bf16[64,256]{1,0:T(8,128)(2,1)S(1)} %collective-permute-done.4.other.node_pay, bf16[768,256]{1,0:T(8,128)(2,1)S(1)} %get-tuple-element.25.maps_own.node_own.block_own.refs_3_.refs_4_, ...), custom_call_target="tpu_custom_call" | custom-call | bytes 750000 | tf_op jit(solution)/shard_map/level_rise/pallas_call | solution.py:314
  22.5 2.1 %collective-permute-start.6 = (bf16[64,256]{1,0:T(8,128)(2,1)S(1)}, bf16[64,256]{1,0:T(8,128)(2,1)S(1)}, u32[]{:S(2)}, u32[]{:S(2)}) collective-permute-start(bf16[64,256]{1,0:T(8,128)(2,1)S(1)} %get-tuple-element.27.after.mine), channel_id=1, source_target_pairs={{0,4},{1,5},{2,6},{3,7},{4,0},{5,1},{6,2},{7,3},{8,12},{9,13},{10,... | collective-permute-start | bytes 98312 | tf_op jit(solution)/shard_map/ppermute | solution.py:39
  24.6 2.8 %near.2.after.refs_0_ = f32[32,1024]{1,0:T(8,128)S(1)} custom-call(bf16[32,2048]{1,0:T(8,128)(2,1)S(1)} %get-tuple-element.28.tree_ref, bf16[2048,2048]{1,0:T(8,128)(2,1)} %inverse_hbm.3, bf16[64,256]{1,0:T(8,128)(2,1)S(1)} %get-tuple-element.27.after.mine), custom_call_target="tpu_custom_call" | custom-call | bytes 8400000 | tf_op jit(solution)/shard_map/near/pallas_call | solution.py:221
  27.4 0.2 level_rise.4
  27.6 3.8 %collective-permute-start.13 = (bf16[512,256]{1,0:T(8,128)(2,1)S(1)}, bf16[512,256]{1,0:T(8,128)(2,1)S(1)}, u32[]{:S(2)}, u32[]{:S(2)}) collective-permute-start(bf16[512,256]{1,0:T(8,128)(2,1)S(1)} %choose.3.refs_8_), channel_id=1, source_target_pairs={{0,8},{16,24}} | collective-permute-start | bytes 786440 | tf_op jit(solution)/shard_map/ppermute | solution.py:488
  31.5 1.3 %collective-permute-start.10 = (bf16[256,256]{1,0:T(8,128)(2,1)S(1)}, bf16[256,256]{1,0:T(8,128)(2,1)S(1)}, u32[]{:S(2)}, u32[]{:S(2)}) collective-permute-start(bf16[256,256]{1,0:T(8,128)(2,1)S(1)} %choose.2), channel_id=1, source_target_pairs={{0,1},{2,3},{4,5},{6,7},{8,9},{10,11},{12,13},{14,15},{16,17},{18,... | collective-permute-start | bytes 393224 | tf_op jit(solution)/shard_map/ppermute | solution.py:488
  32.8 1.0 %collective-permute-done.10.cross_in = bf16[256,256]{1,0:T(8,128)(2,1)S(1)} collective-permute-done((bf16[256,256]{1,0:T(8,128)(2,1)S(1)}, bf16[256,256]{1,0:T(8,128)(2,1)S(1)}, u32[]{:S(2)}, u32[]{:S(2)}) %collective-permute-start.10) | collective-permute-done | bytes 131104 | tf_op jit(solution)/shard_map/ppermute | solution.py:488
  33.8 0.3 local.1.after.l0
  34.2 3.9 %collective-permute-done.8.other = bf16[64,256]{1,0:T(8,128)(2,1)S(1)} collective-permute-done((bf16[64,256]{1,0:T(8,128)(2,1)S(1)}, bf16[64,256]{1,0:T(8,128)(2,1)S(1)}, u32[]{:S(2)}, u32[]{:S(2)}) %collective-permute-start.8) | collective-permute-done | bytes 32800 | tf_op jit(solution)/shard_map/ppermute | solution.py:39
  38.2 3.7 %collective-permute-start.11 = (bf16[64,256]{1,0:T(8,128)(2,1)S(1)}, bf16[64,256]{1,0:T(8,128)(2,1)S(1)}, u32[]{:S(2)}, u32[]{:S(2)}) collective-permute-start(bf16[64,256]{1,0:T(8,128)(2,1)S(1)} %get-tuple-element.32.after.refs_0_), channel_id=1, source_target_pairs={{0,16},{1,17},{2,18},{3,19},{4,20},{5,21},{6,22},{7,23},{8,24},{9,... | collective-permute-start | bytes 98312 | tf_op jit(solution)/shard_map/ppermute | solution.py:39
  41.9 2.8 %near.3.refs_9_.refs_1_ = f32[32,1024]{1,0:T(8,128)S(1)} custom-call(bf16[32,2048]{1,0:T(8,128)(2,1)S(1)} %get-tuple-element.28.tree_ref, bf16[2048,2048]{1,0:T(8,128)(2,1)} %inverse_hbm.3, bf16[64,256]{1,0:T(8,128)(2,1)S(1)} %get-tuple-element.32.after.refs_0_), custom_call_target="tpu_custom_call" | custom-call | bytes 8400000 | tf_op jit(solution)/shard_map/near/pallas_call | solution.py:221
  44.8 0.5 fall.1.after.mine
  45.2 1.0 %invert.1.after.inv_ref = s32[16,128]{1,0:T(8,128)S(1)} custom-call(s32[1,2048]{1,0:T(1,128)} %order_hbm.3, bf16[32,256]{1,0:T(8,128)(2,1)S(1)} %fall.1.after.mine), custom_call_target="tpu_custom_call" | custom-call | bytes 3000000 | tf_op jit(solution)/shard_map/invert/pallas_call | solution.py:189
  46.2 2.7 %collective-permute-done.14.other = bf16[32,256]{1,0:T(8,128)(2,1)S(1)} collective-permute-done((bf16[32,256]{1,0:T(8,128)(2,1)S(1)}, bf16[32,256]{1,0:T(8,128)(2,1)S(1)}, u32[]{:S(2)}, u32[]{:S(2)}) %collective-permute-start.14) | collective-permute-done | bytes 16416 | tf_op jit(solution)/shard_map/ppermute | solution.py:39
  49.0 0.2 step_down.1
  49.1 2.0 %collective-permute-start.15 = (bf16[32,256]{1,0:T(8,128)(2,1)S(1)}, bf16[32,256]{1,0:T(8,128)(2,1)S(1)}, u32[]{:S(2)}, u32[]{:S(2)}) collective-permute-start(bf16[32,256]{1,0:T(8,128)(2,1)S(1)} %step_down.1), channel_id=1, source_target_pairs={{0,2},{1,3},{2,0},{3,1},{4,6},{5,7},{6,4},{7,5},{8,10},{9,11},{10,... | collective-permute-start | bytes 49160 | tf_op jit(solution)/shard_map/ppermute | solution.py:39
  51.1 0.5 collective-permute-start.19
  51.6 1.3 %collective-permute-done.15 = bf16[32,256]{1,0:T(8,128)(2,1)S(1)} collective-permute-done((bf16[32,256]{1,0:T(8,128)(2,1)S(1)}, bf16[32,256]{1,0:T(8,128)(2,1)S(1)}, u32[]{:S(2)}, u32[]{:S(2)}) %collective-permute-start.15) | collective-permute-done | bytes 16416 | tf_op jit(solution)/shard_map/ppermute | solution.py:39
  52.9 1.2 %collective-permute-done.16.f_core = bf16[32,256]{1,0:T(8,128)(2,1)S(1)} collective-permute-done((bf16[32,256]{1,0:T(8,128)(2,1)S(1)}, bf16[32,256]{1,0:T(8,128)(2,1)S(1)}, u32[]{:S(2)}, u32[]{:S(2)}) %collective-permute-start.16) | collective-permute-done | bytes 16416 | tf_op jit(solution)/shard_map/ppermute | solution.py:39
  54.1 2.9 %final.1 = f32[32,2048]{1,0:T(8,128)} custom-call(s32[5]{0:T(128)S(1)} %get-tuple-element.21.pick, bf16[32,256]{1,0:T(8,128)(2,1)S(1)} %broadcast_select_fusion.f_own, bf16[32,256]{1,0:T(8,128)(2,1)S(1)} %collective-permute-done.16.f_core, bf16[288,256]{1,0:T(8,128)(2,1)S(1)} %local.1.after.l0, bf16[288,256]{1,0:T(8,128)(2,1)S(1)} %collective-permute-done.17.l1, ...), custom_call_target="tpu_custom_call" | custom-call | bytes 8700000 | tf_op jit(solution)/shard_map/final/pallas_call | solution.py:449
  (29 shorter events, 0.6 us)
Async XLA Ops:
  2.6 15.2 %collective-permute-start.3 = (bf16[768,256]{1,0:T(8,128)(2,1)S(1)}, bf16[768,256]{1,0:T(8,128)(2,1)S(1)}, u32[]{:S(2)}, u32[]{:S(2)}) collective-permute-start(bf16[768,256]{1,0:T(8,128)(2,1)S(1)} %get-tuple-element.26), channel_id=1, source_target_pairs={{1,0},{3,2},{5,4},{7,6},{9,8},{11,10},{13,12},{15,14},{17,16},{19,... | collective-permute-start | bytes 1179656 | tf_op jit(solution)/shard_map/ppermute | solution.py:483
  3.9 14.0 %collective-permute-start.5 = (bf16[768,256]{1,0:T(8,128)(2,1)S(1)}, bf16[768,256]{1,0:T(8,128)(2,1)S(1)}, u32[]{:S(2)}, u32[]{:S(2)}) collective-permute-start(bf16[768,256]{1,0:T(8,128)(2,1)S(1)} %get-tuple-element.26), channel_id=1, source_target_pairs={{2,0},{6,4},{10,8},{14,12},{18,16},{22,20},{26,24},{30,28}} | collective-permute-start | bytes 1179656 | tf_op jit(solution)/shard_map/ppermute | solution.py:483
  5.2 22.2 %collective-permute-start.7 = (bf16[768,256]{1,0:T(8,128)(2,1)S(1)}, bf16[768,256]{1,0:T(8,128)(2,1)S(1)}, u32[]{:S(2)}, u32[]{:S(2)}) collective-permute-start(bf16[768,256]{1,0:T(8,128)(2,1)S(1)} %get-tuple-element.26), channel_id=1, source_target_pairs={{4,0},{12,8},{20,16},{28,24}} | collective-permute-start | bytes 1179656 | tf_op jit(solution)/shard_map/ppermute | solution.py:483
  6.5 21.0 %collective-permute-start.12 = (bf16[512,256]{1,0:T(8,128)(2,1)S(1)}, bf16[512,256]{1,0:T(8,128)(2,1)S(1)}, u32[]{:S(2)}, u32[]{:S(2)}) collective-permute-start(bf16[512,256]{1,0:T(8,128)(2,1)S(1)} %get-tuple-element.35), channel_id=1, source_target_pairs={{16,0}} | collective-permute-start | bytes 786440 | tf_op jit(solution)/shard_map/ppermute | solution.py:483
  7.8 1.2 %collective-permute-start = (bf16[32,256]{1,0:T(8,128)(2,1)S(1)}, bf16[32,256]{1,0:T(8,128)(2,1)S(1)}, u32[]{:S(2)}, u32[]{:S(2)}) collective-permute-start(bf16[32,256]{1,0:T(8,128)(2,1)S(1)} %get-tuple-element.22.mine.after), channel_id=1, source_target_pairs={{0,1},{1,0},{2,3},{3,2},{4,5},{5,4},{6,7},{7,6},{8,9},{9,8},{10,11... | collective-permute-start | bytes 49160 | tf_op jit(solution)/shard_map/ppermute | solution.py:39
  9.1 5.5 %collective-permute-start.1 = (bf16[64,256]{1,0:T(8,128)(2,1)S(1)}, bf16[64,256]{1,0:T(8,128)(2,1)S(1)}, u32[]{:S(2)}, u32[]{:S(2)}) collective-permute-start(bf16[64,256]{1,0:T(8,128)(2,1)S(1)} %join.1.pair_own.after), channel_id=1, source_target_pairs={{0,2},{1,3},{2,0},{3,1},{4,6},{5,7},{6,4},{7,5},{8,10},{9,11},{10,... | collective-permute-start | bytes 98312 | tf_op jit(solution)/shard_map/ppermute | solution.py:39
  15.3 1.2 %collective-permute-start.2 = (f32[32,256]{1,0:T(8,128)S(1)}, f32[32,256]{1,0:T(8,128)S(1)}, u32[]{:S(2)}, u32[]{:S(2)}) collective-permute-start(f32[32,256]{1,0:T(8,128)S(1)} %get-tuple-element.24.mine.after), channel_id=1, source_target_pairs={{0,1},{1,0},{2,3},{3,2},{4,5},{5,4},{6,7},{7,6},{8,9},{9,8},{10,11... | collective-permute-start | bytes 98312 | tf_op jit(solution)/shard_map/ppermute | solution.py:39
  16.5 17.7 %collective-permute-start.9 = (bf16[768,256]{1,0:T(8,128)(2,1)S(1)}, bf16[768,256]{1,0:T(8,128)(2,1)S(1)}, u32[]{:S(2)}, u32[]{:S(2)}) collective-permute-start(bf16[768,256]{1,0:T(8,128)(2,1)S(1)} %get-tuple-element.26), channel_id=1, source_target_pairs={{8,0},{24,16}} | collective-permute-start | bytes 1179656 | tf_op jit(solution)/shard_map/ppermute | solution.py:483
  17.9 3.9 %collective-permute-start.4 = (bf16[64,256]{1,0:T(8,128)(2,1)S(1)}, bf16[64,256]{1,0:T(8,128)(2,1)S(1)}, u32[]{:S(2)}, u32[]{:S(2)}) collective-permute-start(bf16[64,256]{1,0:T(8,128)(2,1)S(1)} %node_rise.1.mine.after), channel_id=1, source_target_pairs={{0,2},{1,3},{2,0},{3,1},{4,6},{5,7},{6,4},{7,5},{8,10},{9,11},{10,... | collective-permute-start | bytes 98312 | tf_op jit(solution)/shard_map/ppermute | solution.py:39
  22.5 4.9 %collective-permute-start.6 = (bf16[64,256]{1,0:T(8,128)(2,1)S(1)}, bf16[64,256]{1,0:T(8,128)(2,1)S(1)}, u32[]{:S(2)}, u32[]{:S(2)}) collective-permute-start(bf16[64,256]{1,0:T(8,128)(2,1)S(1)} %get-tuple-element.27.after.mine), channel_id=1, source_target_pairs={{0,4},{1,5},{2,6},{3,7},{4,0},{5,1},{6,2},{7,3},{8,12},{9,13},{10,... | collective-permute-start | bytes 98312 | tf_op jit(solution)/shard_map/ppermute | solution.py:39
  27.6 26.4 %copy-start = (bf16[256,2048]{1,0:T(8,128)(2,1)S(1)}, bf16[256,2048]{1,0:T(8,128)(2,1)}, u32[]{:S(2)}) copy-start(bf16[256,2048]{1,0:T(8,128)(2,1)} %out_basis.1) | copy-start | bytes 3145732
  27.6 17.1 %collective-permute-start.13 = (bf16[512,256]{1,0:T(8,128)(2,1)S(1)}, bf16[512,256]{1,0:T(8,128)(2,1)S(1)}, u32[]{:S(2)}, u32[]{:S(2)}) collective-permute-start(bf16[512,256]{1,0:T(8,128)(2,1)S(1)} %choose.3.refs_8_), channel_id=1, source_target_pairs={{0,8},{16,24}} | collective-permute-start | bytes 786440 | tf_op jit(solution)/shard_map/ppermute | solution.py:488
  31.5 2.3 %collective-permute-start.10 = (bf16[256,256]{1,0:T(8,128)(2,1)S(1)}, bf16[256,256]{1,0:T(8,128)(2,1)S(1)}, u32[]{:S(2)}, u32[]{:S(2)}) collective-permute-start(bf16[256,256]{1,0:T(8,128)(2,1)S(1)} %choose.2), channel_id=1, source_target_pairs={{0,1},{2,3},{4,5},{6,7},{8,9},{10,11},{12,13},{14,15},{16,17},{18,... | collective-permute-start | bytes 393224 | tf_op jit(solution)/shard_map/ppermute | solution.py:488
  34.1 17.0 %collective-permute-start.18 = (bf16[288,256]{1,0:T(8,128)(2,1)S(1)}, bf16[288,256]{1,0:T(8,128)(2,1)S(1)}, u32[]{:S(2)}, u32[]{:S(2)}) collective-permute-start(bf16[288,256]{1,0:T(8,128)(2,1)S(1)} %local.1.after.l0), channel_id=1, source_target_pairs={{0,2},{1,3},{2,0},{3,1},{4,6},{5,7},{6,4},{7,5},{8,10},{9,11},{10,... | collective-permute-start | bytes 442376 | tf_op jit(solution)/shard_map/ppermute | solution.py:39
  34.1 4.0 %collective-permute-start.8 = (bf16[64,256]{1,0:T(8,128)(2,1)S(1)}, bf16[64,256]{1,0:T(8,128)(2,1)S(1)}, u32[]{:S(2)}, u32[]{:S(2)}) collective-permute-start(bf16[64,256]{1,0:T(8,128)(2,1)S(1)} %get-tuple-element.29.after.mine), channel_id=1, source_target_pairs={{0,8},{1,9},{2,10},{3,11},{4,12},{5,13},{6,14},{7,15},{8,0},{9,1},... | collective-permute-start | bytes 98312 | tf_op jit(solution)/shard_map/ppermute | solution.py:39
  38.2 6.5 %collective-permute-start.11 = (bf16[64,256]{1,0:T(8,128)(2,1)S(1)}, bf16[64,256]{1,0:T(8,128)(2,1)S(1)}, u32[]{:S(2)}, u32[]{:S(2)}) collective-permute-start(bf16[64,256]{1,0:T(8,128)(2,1)S(1)} %get-tuple-element.32.after.refs_0_), channel_id=1, source_target_pairs={{0,16},{1,17},{2,18},{3,19},{4,20},{5,21},{6,22},{7,23},{8,24},{9,... | collective-permute-start | bytes 98312 | tf_op jit(solution)/shard_map/ppermute | solution.py:39
  45.2 3.8 %collective-permute-start.14 = (bf16[32,256]{1,0:T(8,128)(2,1)S(1)}, bf16[32,256]{1,0:T(8,128)(2,1)S(1)}, u32[]{:S(2)}, u32[]{:S(2)}) collective-permute-start(bf16[32,256]{1,0:T(8,128)(2,1)S(1)} %fall.1.after.mine), channel_id=1, source_target_pairs={{0,4},{1,5},{2,6},{3,7},{4,0},{5,1},{6,2},{7,3},{8,12},{9,13},{10,... | collective-permute-start | bytes 49160 | tf_op jit(solution)/shard_map/ppermute | solution.py:39
  49.1 3.7 %collective-permute-start.15 = (bf16[32,256]{1,0:T(8,128)(2,1)S(1)}, bf16[32,256]{1,0:T(8,128)(2,1)S(1)}, u32[]{:S(2)}, u32[]{:S(2)}) collective-permute-start(bf16[32,256]{1,0:T(8,128)(2,1)S(1)} %step_down.1), channel_id=1, source_target_pairs={{0,2},{1,3},{2,0},{3,1},{4,6},{5,7},{6,4},{7,5},{8,10},{9,11},{10,... | collective-permute-start | bytes 49160 | tf_op jit(solution)/shard_map/ppermute | solution.py:39
  51.1 1.8 %collective-permute-start.17 = (bf16[288,256]{1,0:T(8,128)(2,1)S(1)}, bf16[288,256]{1,0:T(8,128)(2,1)S(1)}, u32[]{:S(2)}, u32[]{:S(2)}) collective-permute-start(bf16[288,256]{1,0:T(8,128)(2,1)S(1)} %local.1.after.l0), channel_id=1, source_target_pairs={{0,1},{1,0},{2,3},{3,2},{4,5},{5,4},{6,7},{7,6},{8,9},{9,8},{10,11... | collective-permute-start | bytes 442376 | tf_op jit(solution)/shard_map/ppermute | solution.py:39
  51.1 3.0 %collective-permute-start.19 = (bf16[288,256]{1,0:T(8,128)(2,1)S(1)}, bf16[288,256]{1,0:T(8,128)(2,1)S(1)}, u32[]{:S(2)}, u32[]{:S(2)}) collective-permute-start(bf16[288,256]{1,0:T(8,128)(2,1)S(1)} %collective-permute-done.18.l2), channel_id=1, source_target_pairs={{0,1},{1,0},{2,3},{3,2},{4,5},{5,4},{6,7},{7,6},{8,9},{9,8},{10,11... | collective-permute-start | bytes 442376 | tf_op jit(solution)/shard_map/ppermute | solution.py:39
  52.9 1.2 %collective-permute-start.16 = (bf16[32,256]{1,0:T(8,128)(2,1)S(1)}, bf16[32,256]{1,0:T(8,128)(2,1)S(1)}, u32[]{:S(2)}, u32[]{:S(2)}) collective-permute-start(bf16[32,256]{1,0:T(8,128)(2,1)S(1)} %broadcast_select_fusion.f_own), channel_id=1, source_target_pairs={{0,1},{1,0},{2,3},{3,2},{4,5},{5,4},{6,7},{7,6},{8,9},{9,8},{10,11... | collective-permute-start | bytes 49160 | tf_op jit(solution)/shard_map/ppermute | solution.py:39

commit v5 on v4

--- a/solution.py
+++ b/solution.py
@@ -12,7 +12,6 @@
 BF = jnp.bfloat16
 F32 = jnp.float32
 VMEM = pl.BlockSpec(memory_space=pltpu.VMEM)
-SMEM = pl.BlockSpec(memory_space=pltpu.SMEM)
 ANY = pl.BlockSpec(memory_space=pl.ANY)
 HBM = pl.BlockSpec(memory_space=pltpu.HBM)
 LIMIT = 32 * 2**20
@@ -41,6 +40,14 @@
 
 def bit_of_device(bit):
     return (lax.axis_index("leaf").astype(jnp.int32) & (1 << bit)) != 0
+
+
+def picked(number, choices):
+    number = number[:, :1]
+    result = choices[0]
+    for m in range(1, len(choices)):
+        result = jnp.where(number == m, choices[m], result)
+    return result
 
 
 def held(bit, own, arrived, begin, size):
@@ -107,8 +114,8 @@
         source = jnp.int32(0)
         for slot in range(1, SPREAD):
             source = jnp.where(placed[slot] == (offset ^ m), slot, source)
-        pick[m] = source ^ offset
-    pick[SPREAD] = seat ^ offset
+        pick[m : m + 1, :] = jnp.full((1, LANES), source ^ offset, jnp.int32)
+    pick[SPREAD : SPREAD + 1, :] = jnp.full((1, LANES), seat ^ offset, jnp.int32)
     copies[0].wait()
     table[...] = rhs[...].astype(F32)
     copies[1].wait()
@@ -135,7 +142,7 @@
     return pl.pallas_call(
         start_kernel,
         out_shape=(
-            jax.ShapeDtypeStruct((SPREAD + 1,), jnp.int32),
+            jax.ShapeDtypeStruct((2 * SPREAD, LANES), jnp.int32),
             jax.ShapeDtypeStruct((rows, columns), BF),
             jax.ShapeDtypeStruct((rows, rank), BF),
             block(3),
@@ -146,7 +153,7 @@
             block(1),
         ),
         in_specs=[HBM] * 9,
-        out_specs=(SMEM,) + (VMEM,) * 8,
+        out_specs=(VMEM,) * 9,
         scratch_shapes=[
             pltpu.VMEM(right_sides.shape, BF),
             pltpu.VMEM(point_order.shape, jnp.int32),
@@ -252,13 +259,13 @@
     )(mine, other, after)
 
 
-def leaf_kernel(pick, pair_own, pair_x, up_ref, after, g0_ref, out_ref, table):
+def leaf_kernel(pick, pair_own, pair_x, up_ref, after, g0_ref, out_ref):
     rows = out_ref.shape[0]
+    table = [
+        pair[m * rows : (m + 1) * rows, :].astype(F32) for pair in (pair_own, pair_x) for m in (0, 1)
+    ]
     for m in range(SPREAD):
-        pair = pair_own if m < 2 else pair_x
-        table[m] = pair[m % 2 * rows : (m % 2 + 1) * rows]
-    for m in range(SPREAD):
-        g0_ref[m] = table[pick[m]]
+        g0_ref[m] = picked(pick[m : m + 1, :], table).astype(BF)
     out_ref[...] = mm(g0_ref[0], up_ref[...])
 
 
@@ -271,9 +278,8 @@
             jax.ShapeDtypeStruct((SPREAD, rows, rank), BF),
             jax.ShapeDtypeStruct((rows, rank), F32),
         ),
-        in_specs=[SMEM] + [VMEM] * 3 + [ANY],
+        in_specs=[VMEM] * 4 + [ANY],
         out_specs=(VMEM,) * 2,
-        scratch_shapes=[pltpu.VMEM((SPREAD, rows, rank), BF)],
         compiler_params=params(),
         cost_estimate=took(0.4),
         name="leaf_rise",
@@ -300,10 +306,9 @@
     )(mine, other, *maps, after)
 
 
-def level_kernel(bit, mine, other, maps_own, maps_in, after, sibling_ref, out_ref):
+def level_kernel(bit, mine, other, maps_own, maps_in, after, out_ref):
     rows = mine.shape[0] // 2
     rank = mine.shape[1]
-    sibling_ref[...] = other[:rows]
     grown = (mine[rows:].astype(F32) + other[rows:].astype(F32)).astype(BF)
     out_ref[:rows] = grown
     out_ref[rows:] = mm(grown, held(bit, maps_own, maps_in, 0, rank)).astype(BF)
@@ -313,12 +318,9 @@
     double, rank = mine.shape
     return pl.pallas_call(
         functools.partial(level_kernel, bit),
-        out_shape=(
-            jax.ShapeDtypeStruct((double // 2, rank), BF),
-            jax.ShapeDtypeStruct((double, rank), BF),
-        ),
+        out_shape=jax.ShapeDtypeStruct((double, rank), BF),
         in_specs=[VMEM] * 4 + [ANY],
-        out_specs=(VMEM,) * 2,
+        out_specs=VMEM,
         compiler_params=params(),
         cost_estimate=took(0.25),
         name="level_rise",
@@ -340,7 +342,7 @@
 
     value = mm(top, part(count, 0)).astype(BF)
     for k in range(count, 0, -1):
-        sibling = other[:rows] if k == count else siblings[k - 1][...]
+        sibling = other[:rows] if k == count else siblings[k - 1][:rows]
         cross = part(k, owns[k].shape[0] - rank)
         value = (mm(sibling, cross) + mm(value, part(k - 1, rank))).astype(BF)
     out[...] = value
@@ -365,7 +367,7 @@
     value = jnp.where(bit_of_device(bit), other[...], mine[...])
     cross = held(bit, maps_own, maps_in, 2 * rank, rank)
     down = held(bit - 1, block_own, block_in, rank, rank)
-    out[...] = (mm(sibling[...], cross) + mm(value, down)).astype(BF)
+    out[...] = (mm(sibling[: mine.shape[0]], cross) + mm(value, down)).astype(BF)
 
 
 def step_down(bit, mine, other, sibling, maps, block_maps, after):
@@ -409,6 +411,22 @@
     out_ref[...] = held(bit, upper, lower, 0, out_ref.shape[0])
 
 
+def pass_kernel(block, after, out_ref):
+    out_ref[...] = block[...]
+
+
+def pass_on(block, after):
+    return pl.pallas_call(
+        pass_kernel,
+        out_shape=jax.ShapeDtypeStruct(block.shape, block.dtype),
+        in_specs=[VMEM, ANY],
+        out_specs=VMEM,
+        compiler_params=params(),
+        cost_estimate=took(0.2),
+        name="pass_on",
+    )(block, after)
+
+
 def choose(bit, upper, lower, after):
     return pl.pallas_call(
         functools.partial(choose_kernel, bit),
@@ -423,24 +441,34 @@
 
 def final_kernel(strips, pick, f_own, f_core, l0, l1, l2, l3, out_basis, inv_ref, *refs):
     nears = refs[:strips]
-    answer, total, leaf_f = refs[strips:]
+    answer_hbm, total, answer, sems = refs[strips:]
     rank = f_own.shape[1]
     f2 = jnp.where(bit_of_device(0), f_core[...], f_own[...])
-    for m, pack_ref in enumerate((l0, l1, l2, l3)):
-
-        @pl.when(pick[SPREAD] == m)
-        def _():
-            leaf_f[...] = (mm(f2, pack_ref[:rank, :]) + pack_ref[rank:, :].astype(F32)).astype(BF)
-
+    values = [
+        mm(f2, pack_ref[:rank, :]) + pack_ref[rank:, :].astype(F32) for pack_ref in (l0, l1, l2, l3)
+    ]
+    leaf_f = picked(pick[SPREAD : SPREAD + 1, :], values).astype(BF)
     width = nears[0].shape[1]
     for i in range(strips):
         span = slice(i * width, (i + 1) * width)
-        total[:, span] = nears[i][...] + mm(leaf_f[...], out_basis[:, span])
+        total[:, span] = nears[i][...] + mm(leaf_f, out_basis[:, span])
+
+    copies = []
 
     def store(tile, found):
         answer[:, tile * LANES : (tile + 1) * LANES] = found
+        if tile % 4 == 3:
+            span = pl.ds((tile - 3) * LANES, 4 * LANES)
+            copies.append(
+                pltpu.make_async_copy(
+                    answer.at[:, span], answer_hbm.at[:, span], sems.at[len(copies)]
+                )
+            )
+            copies[-1].start()
 
     gather_columns(total, lambda tile: inv_ref[tile : tile + 1, :], store)
+    for copy in copies:
+        copy.wait()
 
 
 def final(pick, f2, f2_core, locals_, basis_out, inverse_order, nears):
@@ -449,9 +477,13 @@
     return pl.pallas_call(
         functools.partial(final_kernel, len(nears)),
         out_shape=jax.ShapeDtypeStruct((rows, columns), F32),
-        in_specs=[SMEM] + [VMEM] * (8 + len(nears)),
-        out_specs=VMEM,
-        scratch_shapes=[pltpu.VMEM((rows, columns), F32), pltpu.VMEM((rows, rank), BF)],
+        in_specs=[VMEM] * (9 + len(nears)),
+        out_specs=ANY,
+        scratch_shapes=[
+            pltpu.VMEM((rows, columns), F32),
+            pltpu.VMEM((rows, columns), F32),
+            pltpu.SemaphoreType.DMA((columns // (4 * LANES),)),
+        ],
         compiler_params=params(),
         cost_estimate=took(2.9),
         name="final",
@@ -478,68 +510,78 @@
     rank = leaf_up.shape[1]
     offset = me & (SPREAD - 1)
 
+    def cycle(bit):
+        step = 1 << bit
+        pairs = []
+        for i in range(0, members, 2):
+            if i & step == 0:
+                pairs += [(i + step, i), (i, i | 1), (i | 1, (i + step) | 1), ((i + step) | 1, i + step)]
+        return pairs
+
     def to_left(block, bit):
-        step = 1 << bit
-        return lax.ppermute(block, "leaf", [(i + step, i) for i in range(0, members, 2 * step)])
-
-    def to_right(block, bit, every):
-        step = 1 << bit
-        pairs = [(i, i + step) for i in range(0, members, every) if i & step == 0]
-        return lax.ppermute(block, "leaf", pairs)
+        if bit == 0:
+            return swap(block, 1)
+        return lax.ppermute(block, "leaf", cycle(bit))
+
+    def to_right(block, bit):
+        if bit == 0:
+            return swap(block, 1)
+        return lax.ppermute(block, "leaf", [(j, i) for i, j in cycle(bit)])
 
     pick, tree, reduced, low, high, top_low, top_high, up_map, down_map = start(
         right_sides, point_order, basis_in, leaf_map, leaf_up, leaf_down, node_up, node_down, node_cross
     )
     node_maps = (high, to_left(low, 0))
-    block_maps = (high, to_left(low, 1))
-    held_maps = []
-    for level in range(cut + 1, levels + 1):
+
+    pair = join(reduced, swap(reduced, 1), reduced)
+    gate = pass_on(low, pair)
+    block_maps = (high, to_left(gate, 1))
+    g0, product = leaf_rise(pick, pair, swap(pair, 2), up_map, gate)
+    gate = pass_on(low, product)
+    held_maps = [(high, to_left(gate, cut))]
+    pay = node_rise(product, swap(product, 1), node_maps, gate)
+    for level in range(levels, cut + 1, -1):
         first, second = (top_low, top_high) if level == levels else (low, high)
-        held_maps.append((second, to_left(first, level - 1)))
-
-    pair = join(reduced, swap(reduced, 1), reduced)
-    g0, product = leaf_rise(pick, pair, swap(pair, 2), up_map, pair)
-    pay = node_rise(product, swap(product, 1), node_maps, product)
-    node_in = swap(pay, 2)
-    siblings = []
-    near0 = near1 = None
+        gate = pass_on(first, pay)
+        held_maps.insert(1, (second, to_left(gate, level - 1)))
+    strips = 4
+    nears = []
+    arrivals = []
     for bit in range(1, levels - 1):
-        arrived = node_in if bit == 1 else swap(pay, 1 << bit)
-        after = pay
-        if bit == 2:
-            near0 = after = near_strip(tree, leaf_inverse, 0, 2, pay)
-            block_cross = choose(1, high[2 * rank :], block_maps[1][2 * rank :], pay)
-            block_cross = to_right(block_cross, 0, 2)
+        arrivals.append(swap(pay, 1 << bit))
+        if bit <= cut:
+            after = near_strip(tree, leaf_inverse, len(nears), strips, pay)
+            nears.append(after)
         if bit == cut + 1:
+            after = pay
             for level in range(cut + 3, levels + 1):
                 own, passed = held_maps[level - cut - 1]
-                now = choose(level - 1, own, passed, pay)
+                now = after = choose(level - 1, own, passed, pay)
                 for step in range(level - 2, cut, -1):
-                    passed = to_right(now, step, 1 << step)
+                    passed = to_right(now, step)
                     if step > cut + 1:
                         now = choose(step, passed, now, pay)
                 held_maps[level - cut - 1] = (passed, now)
-        if bit == 3:
-            own_local = after = local(
-                g0, node_in, node_maps, block_maps, block_cross, down_map, pay
-            )
         maps = block_maps if bit == 1 else held_maps[bit - cut]
-        sibling, pay = level_rise(min(bit, cut + 1), pay, arrived, maps, after)
-        siblings.append(sibling)
-
+        pay = level_rise(min(bit, cut + 1), pay, arrivals[-1], maps, after)
+        if bit == cut:
+            block_cross = choose(1, high[2 * rank :], block_maps[1][2 * rank :], pay)
+            block_cross = to_right(block_cross, 0)
+
+    own_local = local(g0, arrivals[0], node_maps, block_maps, block_cross, down_map, pay)
     local_x = swap(own_local, 2)
-    locals_ = [own_local, swap(own_local, 1), local_x, swap(local_x, 1)]
-    near1 = near_strip(tree, leaf_inverse, 1, 2, pay)
-
-    cut_f = fall(cut, pay, swap(pay, 1 << (levels - 1)), siblings[2:], held_maps, near1)
-    inverse_order = invert(point_order, cut_f)
+    nears.append(near_strip(tree, leaf_inverse, 2, strips, own_local))
+
+    cut_f = fall(cut, pay, swap(pay, 1 << (levels - 1)), arrivals[2:], held_maps, nears[2])
+    nears.append(near_strip(tree, leaf_inverse, 3, strips, cut_f))
     block_f = step_down(
-        cut, cut_f, swap(cut_f, SPREAD), siblings[1], held_maps[0], block_maps, inverse_order
+        cut, cut_f, swap(cut_f, SPREAD), arrivals[1], held_maps[0], block_maps, nears[3]
     )
-    from_x = swap(block_f, 2)
-    block_f = jnp.where(offset & 2 != 0, from_x, block_f)
+    inverse_order = invert(point_order, block_f)
+    locals_ = [own_local, swap(own_local, 1), local_x, swap(pass_on(local_x, block_f), 1)]
+    block_f = choose(1, swap(block_f, 2), block_f, inverse_order)
     return final(
-        pick, block_f, swap(block_f, 1), locals_, basis_out, inverse_order, [near0, near1]
+        pick, block_f, swap(block_f, 1), locals_, basis_out, inverse_order, nears
     )
 
 

time: 57.3 us -> 46.6 us (0.81)
  waiting for transfers between devices: 20 us -> 13.5 us
  starting transfers between devices: 21.8 us -> 17.3 us
    ppermute x7 -> x5, starting transfers between devices: 11.5 us -> 3.45 us  [the longest x4 3.1 us: to_left(): return lax.ppermute(block, 'leaf', cycle(bit))]
    ppermute x13 -> x15, waiting for transfers between devices: 19 us -> 13.5 us  [swap(): return lax.ppermute(block, 'leaf', [(i, i ^ mask) for i in range(count)])]
    ppermute x13 -> x15, starting transfers between devices: 10.3 us -> 13.8 us  [swap(): return lax.ppermute(block, 'leaf', [(i, i ^ mask) for i in range(count)])]
    pallas_call x2 -> x4, Pallas kernels: 5.65 us -> 8.09 us  [near_strip(): pl.pallas_call(functools.partial(near_kernel, strip * width), out_shape=j...]
    ppermute x7 -> x5, waiting for transfers between devices: 0.98 us -> 0.01 us  [the longest x4 0.01 us: to_left(): return lax.ppermute(block, 'leaf', cycle(bit))]
    pallas_call x4 -> x9, Pallas kernels: 3.55 us -> 2.59 us  [the longest x1 2.03 us: start(): pl.pallas_call(start_kernel, out_shape=(jax.ShapeDtypeStruct((2 * SPREAD,...]
  transfers between devices with their start and end apart: 20 -> 20, of which waited for: 9 -> 10; matrix products, arithmetic and copies ran while one was open for 0% -> 0% of each run, Pallas kernels for 17% -> 24%
where the time goes in v5:
time: 46.6 us; the launch traced here: 46.4 us
  starting transfers between devices  17.3 us (37%)
  Pallas kernels  15.4 us (33%)
  waiting for transfers between devices  13.5 us (29%)
    ppermute x15, starting transfers between devices, swap(): return lax.ppermute(block, 'leaf', [(i, i ^ mask) for i in range(count)])  13.8 us
    ppermute x15, waiting for transfers between devices, swap(): return lax.ppermute(block, 'leaf', [(i, i ^ mask) for i in range(count)])  13.5 us
    pallas_call x4, Pallas kernels, near_strip(): pl.pallas_call(functools.partial(near_kernel, strip * width), out_shape=j...  8.09 us
    ppermute x4, starting transfers between devices, to_left(): return lax.ppermute(block, 'leaf', cycle(bit))  3.1 us
    pallas_call x1, Pallas kernels, final(): pl.pallas_call(functools.partial(final_kernel, len(nears)), out_shape=jax...  2.43 us
    pallas_call x1, Pallas kernels, start(): pl.pallas_call(start_kernel, out_shape=(jax.ShapeDtypeStruct((2 * SPREAD,...  2.03 us
    pallas_call x1, Pallas kernels, invert(): pl.pallas_call(invert_kernel, out_shape=jax.ShapeDtypeStruct((columns //...  1 us
  transfers between devices with their start and end apart: 20, of which 10 were waited for; matrix products, arithmetic and copies ran while one was open for 0% of the time, Pallas kernels for 24%

profile of v5, /device:TPU:0, one launch (start us, length us, event | category | flops | bytes accessed | tf_op | source)
XLA Modules:
  0.0 46.4 jit_solution(2649809329138201785)
XLA Ops:
  0.0 2.0 %start.1 = (s32[8,128]{1,0:T(8,128)S(1)}, bf16[32,2048]{1,0:T(8,128)(2,1)S(1)}, bf16[32,256]{1,0:T(8,128)(2,1)S(1)}, bf16[768,256]{1,0:T(8,128)(2,1)S(1)}, bf16[...) custom-call(bf16[32,2048]{1,0:T(8,128)(2,1)} %rhs_hbm.1, ...), custom_call_target="tpu_custom_call" | custom-call | bytes 8100000 | tf_op jit(solution)/shard_map/start/pallas_call | solution.py:142
  2.0 0.5 %collective-permute-start.3 = (bf16[768,256]{1,0:T(8,128)(2,1)S(1)}, bf16[768,256]{1,0:T(8,128)(2,1)S(1)}, u32[]{:S(2)}, u32[]{:S(2)}) collective-permute-start(bf16[768,256]{1,0:T(8,128)(2,1)S(1)} %get-tuple-element.19.block), channel_id=1, source_target_pairs={{0,1},{1,0},{2,3},{3,2},{4,5},{5,4},{6,7},{7,6},{8,9},{9,8},{10,11... | collective-permute-start | bytes 1179656 | tf_op jit(solution)/shard_map/ppermute | solution.py:38
  2.6 1.3 %collective-permute-done.other = bf16[32,256]{1,0:T(8,128)(2,1)S(1)} collective-permute-done((bf16[32,256]{1,0:T(8,128)(2,1)S(1)}, bf16[32,256]{1,0:T(8,128)(2,1)S(1)}, u32[]{:S(2)}, u32[]{:S(2)}) %collective-permute-start) | collective-permute-done | bytes 16416 | tf_op jit(solution)/shard_map/ppermute | solution.py:38
  3.9 2.9 %collective-permute-start.1 = (bf16[64,256]{1,0:T(8,128)(2,1)S(1)}, bf16[64,256]{1,0:T(8,128)(2,1)S(1)}, u32[]{:S(2)}, u32[]{:S(2)}) collective-permute-start(bf16[64,256]{1,0:T(8,128)(2,1)S(1)} %join.1.after.pair_own), channel_id=1, source_target_pairs={{0,2},{1,3},{2,0},{3,1},{4,6},{5,7},{6,4},{7,5},{8,10},{9,11},{10,... | collective-permute-start | bytes 98312 | tf_op jit(solution)/shard_map/ppermute | solution.py:38
  6.8 1.8 %collective-permute-done.1.pair_x = bf16[64,256]{1,0:T(8,128)(2,1)S(1)} collective-permute-done((bf16[64,256]{1,0:T(8,128)(2,1)S(1)}, bf16[64,256]{1,0:T(8,128)(2,1)S(1)}, u32[]{:S(2)}, u32[]{:S(2)}) %collective-permute-start.1) | collective-permute-done | bytes 32800 | tf_op jit(solution)/shard_map/ppermute | solution.py:38
  8.7 0.2 leaf_rise.1
  8.9 0.7 %collective-permute-start.2 = (f32[32,256]{1,0:T(8,128)S(1)}, f32[32,256]{1,0:T(8,128)S(1)}, u32[]{:S(2)}, u32[]{:S(2)}) collective-permute-start(f32[32,256]{1,0:T(8,128)S(1)} %get-tuple-element.20.after.mine), channel_id=1, source_target_pairs={{0,1},{1,0},{2,3},{3,2},{4,5},{5,4},{6,7},{7,6},{8,9},{9,8},{10,11... | collective-permute-start | bytes 98312 | tf_op jit(solution)/shard_map/ppermute | solution.py:38
  9.6 0.9 %collective-permute-done.2.other = f32[32,256]{1,0:T(8,128)S(1)} collective-permute-done((f32[32,256]{1,0:T(8,128)S(1)}, f32[32,256]{1,0:T(8,128)S(1)}, u32[]{:S(2)}, u32[]{:S(2)}) %collective-permute-start.2) | collective-permute-done | bytes 32800 | tf_op jit(solution)/shard_map/ppermute | solution.py:38
  10.7 0.4 collective-permute-start.10
  11.1 2.6 %collective-permute-start.9 = (bf16[768,256]{1,0:T(8,128)(2,1)S(1)}, bf16[768,256]{1,0:T(8,128)(2,1)S(1)}, u32[]{:S(2)}, u32[]{:S(2)}) collective-permute-start(bf16[768,256]{1,0:T(8,128)(2,1)S(1)} %pass_on.7), channel_id=1, source_target_pairs={{8,0},{0,1},{1,9},{9,8},{10,2},{2,3},{3,11},{11,10},{12,4},{4,5},{... | collective-permute-start | bytes 1179656 | tf_op jit(solution)/shard_map/ppermute | solution.py:524
  13.8 1.8 %collective-permute-start.4 = (bf16[64,256]{1,0:T(8,128)(2,1)S(1)}, bf16[64,256]{1,0:T(8,128)(2,1)S(1)}, u32[]{:S(2)}, u32[]{:S(2)}) collective-permute-start(bf16[64,256]{1,0:T(8,128)(2,1)S(1)} %node_rise.1.after.mine), channel_id=1, source_target_pairs={{0,2},{1,3},{2,0},{3,1},{4,6},{5,7},{6,4},{7,5},{8,10},{9,11},{10,... | collective-permute-start | bytes 98312 | tf_op jit(solution)/shard_map/ppermute | solution.py:38
  15.6 2.0 %near.4.after.refs_0_ = f32[32,512]{1,0:T(8,128)S(1)} custom-call(bf16[32,2048]{1,0:T(8,128)(2,1)S(1)} %get-tuple-element.22.tree_ref, bf16[2048,2048]{1,0:T(8,128)(2,1)} %inverse_hbm.7, bf16[64,256]{1,0:T(8,128)(2,1)S(1)} %node_rise.1.after.mine), custom_call_target="tpu_custom_call" | custom-call | bytes 4200000 | tf_op jit(solution)/shard_map/near/pallas_call | solution.py:228
  17.9 1.7 %collective-permute-start.6 = (bf16[64,256]{1,0:T(8,128)(2,1)S(1)}, bf16[64,256]{1,0:T(8,128)(2,1)S(1)}, u32[]{:S(2)}, u32[]{:S(2)}) collective-permute-start(bf16[64,256]{1,0:T(8,128)(2,1)S(1)} %level_rise.3.after.mine), channel_id=1, source_target_pairs={{0,4},{1,5},{2,6},{3,7},{4,0},{5,1},{6,2},{7,3},{8,12},{9,13},{10,... | collective-permute-start | bytes 98312 | tf_op jit(solution)/shard_map/ppermute | solution.py:38
  19.5 2.0 %near.5.after.refs_1_ = f32[32,512]{1,0:T(8,128)S(1)} custom-call(bf16[32,2048]{1,0:T(8,128)(2,1)S(1)} %get-tuple-element.22.tree_ref, bf16[2048,2048]{1,0:T(8,128)(2,1)} %inverse_hbm.7, bf16[64,256]{1,0:T(8,128)(2,1)S(1)} %level_rise.3.after.mine), custom_call_target="tpu_custom_call" | custom-call | bytes 4200000 | tf_op jit(solution)/shard_map/near/pallas_call | solution.py:228
  21.6 0.5 %collective-permute-done.6.other.sibling = bf16[64,256]{1,0:T(8,128)(2,1)S(1)} collective-permute-done((bf16[64,256]{1,0:T(8,128)(2,1)S(1)}, bf16[64,256]{1,0:T(8,128)(2,1)S(1)}, u32[]{:S(2)}, u32[]{:S(2)}) %collective-permute-start.6) | collective-permute-done | bytes 32800 | tf_op jit(solution)/shard_map/ppermute | solution.py:38
  22.3 0.2 collective-permute-start.13
  22.6 0.3 collective-permute-start.12
  23.0 4.5 %collective-permute-done.8.other.refs_2_ = bf16[64,256]{1,0:T(8,128)(2,1)S(1)} collective-permute-done((bf16[64,256]{1,0:T(8,128)(2,1)S(1)}, bf16[64,256]{1,0:T(8,128)(2,1)S(1)}, u32[]{:S(2)}, u32[]{:S(2)}) %collective-permute-start.8) | collective-permute-done | bytes 32800 | tf_op jit(solution)/shard_map/ppermute | solution.py:38
  27.7 0.3 local.1.after.l0
  28.0 1.3 %collective-permute-start.18 = (bf16[288,256]{1,0:T(8,128)(2,1)S(1)}, bf16[288,256]{1,0:T(8,128)(2,1)S(1)}, u32[]{:S(2)}, u32[]{:S(2)}) collective-permute-start(bf16[288,256]{1,0:T(8,128)(2,1)S(1)} %local.1.after.l0), channel_id=1, source_target_pairs={{0,2},{1,3},{2,0},{3,1},{4,6},{5,7},{6,4},{7,5},{8,10},{9,11},{10,... | collective-permute-start | bytes 442376 | tf_op jit(solution)/shard_map/ppermute | solution.py:38
  29.3 1.8 %collective-permute-start.11 = (bf16[64,256]{1,0:T(8,128)(2,1)S(1)}, bf16[64,256]{1,0:T(8,128)(2,1)S(1)}, u32[]{:S(2)}, u32[]{:S(2)}) collective-permute-start(bf16[64,256]{1,0:T(8,128)(2,1)S(1)} %level_rise.5.after.refs_0_), channel_id=1, source_target_pairs={{0,16},{1,17},{2,18},{3,19},{4,20},{5,21},{6,22},{7,23},{8,24},{9,... | collective-permute-start | bytes 98312 | tf_op jit(solution)/shard_map/ppermute | solution.py:38
  31.1 2.0 %near.6.refs_9_.refs_2_ = f32[32,512]{1,0:T(8,128)S(1)} custom-call(bf16[32,2048]{1,0:T(8,128)(2,1)S(1)} %get-tuple-element.22.tree_ref, bf16[2048,2048]{1,0:T(8,128)(2,1)} %inverse_hbm.7, bf16[288,256]{1,0:T(8,128)(2,1)S(1)} %local.1.after.l0), custom_call_target="tpu_custom_call" | custom-call | bytes 4200000 | tf_op jit(solution)/shard_map/near/pallas_call | solution.py:228
  33.2 1.0 %collective-permute-done.11.refs_1_ = bf16[64,256]{1,0:T(8,128)(2,1)S(1)} collective-permute-done((bf16[64,256]{1,0:T(8,128)(2,1)S(1)}, bf16[64,256]{1,0:T(8,128)(2,1)S(1)}, u32[]{:S(2)}, u32[]{:S(2)}) %collective-permute-start.11) | collective-permute-done | bytes 32800 | tf_op jit(solution)/shard_map/ppermute | solution.py:38
  34.1 0.4 fall.1.after.mine
  34.6 1.6 %collective-permute-start.14 = (bf16[32,256]{1,0:T(8,128)(2,1)S(1)}, bf16[32,256]{1,0:T(8,128)(2,1)S(1)}, u32[]{:S(2)}, u32[]{:S(2)}) collective-permute-start(bf16[32,256]{1,0:T(8,128)(2,1)S(1)} %fall.1.after.mine), channel_id=1, source_target_pairs={{0,4},{1,5},{2,6},{3,7},{4,0},{5,1},{6,2},{7,3},{8,12},{9,13},{10,... | collective-permute-start | bytes 49160 | tf_op jit(solution)/shard_map/ppermute | solution.py:38
  36.2 2.0 %near.7.after.refs_3_ = f32[32,512]{1,0:T(8,128)S(1)} custom-call(bf16[32,2048]{1,0:T(8,128)(2,1)S(1)} %get-tuple-element.22.tree_ref, bf16[2048,2048]{1,0:T(8,128)(2,1)} %inverse_hbm.7, bf16[32,256]{1,0:T(8,128)(2,1)S(1)} %fall.1.after.mine), custom_call_target="tpu_custom_call" | custom-call | bytes 4200000 | tf_op jit(solution)/shard_map/near/pallas_call | solution.py:228
  38.5 0.5 %collective-permute-start.19 = (bf16[288,256]{1,0:T(8,128)(2,1)S(1)}, bf16[288,256]{1,0:T(8,128)(2,1)S(1)}, u32[]{:S(2)}, u32[]{:S(2)}) collective-permute-start(bf16[288,256]{1,0:T(8,128)(2,1)S(1)} %pass_on.9), channel_id=1, source_target_pairs={{0,1},{1,0},{2,3},{3,2},{4,5},{5,4},{6,7},{7,6},{8,9},{9,8},{10,11... | collective-permute-start | bytes 442376 | tf_op jit(solution)/shard_map/ppermute | solution.py:38
  39.0 0.6 %collective-permute-start.15 = (bf16[32,256]{1,0:T(8,128)(2,1)S(1)}, bf16[32,256]{1,0:T(8,128)(2,1)S(1)}, u32[]{:S(2)}, u32[]{:S(2)}) collective-permute-start(bf16[32,256]{1,0:T(8,128)(2,1)S(1)} %step_down.1.after.lower), channel_id=1, source_target_pairs={{0,2},{1,3},{2,0},{3,1},{4,6},{5,7},{6,4},{7,5},{8,10},{9,11},{10,... | collective-permute-start | bytes 49160 | tf_op jit(solution)/shard_map/ppermute | solution.py:38
  39.6 1.0 %invert.1.after.inv_ref = s32[16,128]{1,0:T(8,128)S(1)} custom-call(s32[1,2048]{1,0:T(1,128)} %order_hbm.3, bf16[32,256]{1,0:T(8,128)(2,1)S(1)} %step_down.1.after.lower), custom_call_target="tpu_custom_call" | custom-call | bytes 3000000 | tf_op jit(solution)/shard_map/invert/pallas_call | solution.py:196
  40.6 2.1 %collective-permute-done.15.upper = bf16[32,256]{1,0:T(8,128)(2,1)S(1)} collective-permute-done((bf16[32,256]{1,0:T(8,128)(2,1)S(1)}, bf16[32,256]{1,0:T(8,128)(2,1)S(1)}, u32[]{:S(2)}, u32[]{:S(2)}) %collective-permute-start.15) | collective-permute-done | bytes 16416 | tf_op jit(solution)/shard_map/ppermute | solution.py:38
  42.8 1.2 %collective-permute-done.16.f_core = bf16[32,256]{1,0:T(8,128)(2,1)S(1)} collective-permute-done((bf16[32,256]{1,0:T(8,128)(2,1)S(1)}, bf16[32,256]{1,0:T(8,128)(2,1)S(1)}, u32[]{:S(2)}, u32[]{:S(2)}) %collective-permute-start.16) | collective-permute-done | bytes 16416 | tf_op jit(solution)/shard_map/ppermute | solution.py:38
  43.9 2.4 %final.1 = f32[32,2048]{1,0:T(8,128)} custom-call(s32[8,128]{1,0:T(8,128)S(1)} %get-tuple-element.16.pick, bf16[32,256]{1,0:T(8,128)(2,1)S(1)} %choose.5.f_own, bf16[32,256]{1,0:T(8,128)(2,1)S(1)} %collective-permute-done.16.f_core, bf16[288,256]{1,0:T(8,128)(2,1)S(1)} %local.1.after.l0, bf16[288,256]{1,0:T(8,128)(2,1)S(1)} %collective-permute-done.17.l1, ...), custom_call_target="tpu_custom_call" | custom-call | bytes 8700000 | tf_op jit(solution)/shard_map/final/pallas_call | solution.py:477
  (36 shorter events, 1.3 us)
Async XLA Ops:
  2.0 8.5 %collective-permute-start.3 = (bf16[768,256]{1,0:T(8,128)(2,1)S(1)}, bf16[768,256]{1,0:T(8,128)(2,1)S(1)}, u32[]{:S(2)}, u32[]{:S(2)}) collective-permute-start(bf16[768,256]{1,0:T(8,128)(2,1)S(1)} %get-tuple-element.19.block), channel_id=1, source_target_pairs={{0,1},{1,0},{2,3},{3,2},{4,5},{5,4},{6,7},{7,6},{8,9},{9,8},{10,11... | collective-permute-start | bytes 1179656 | tf_op jit(solution)/shard_map/ppermute | solution.py:38
  2.6 1.4 %collective-permute-start = (bf16[32,256]{1,0:T(8,128)(2,1)S(1)}, bf16[32,256]{1,0:T(8,128)(2,1)S(1)}, u32[]{:S(2)}, u32[]{:S(2)}) collective-permute-start(bf16[32,256]{1,0:T(8,128)(2,1)S(1)} %get-tuple-element.17.mine.after), channel_id=1, source_target_pairs={{0,1},{1,0},{2,3},{3,2},{4,5},{5,4},{6,7},{7,6},{8,9},{9,8},{10,11... | collective-permute-start | bytes 49160 | tf_op jit(solution)/shard_map/ppermute | solution.py:38
  3.9 4.8 %collective-permute-start.1 = (bf16[64,256]{1,0:T(8,128)(2,1)S(1)}, bf16[64,256]{1,0:T(8,128)(2,1)S(1)}, u32[]{:S(2)}, u32[]{:S(2)}) collective-permute-start(bf16[64,256]{1,0:T(8,128)(2,1)S(1)} %join.1.after.pair_own), channel_id=1, source_target_pairs={{0,2},{1,3},{2,0},{3,1},{4,6},{5,7},{6,4},{7,5},{8,10},{9,11},{10,... | collective-permute-start | bytes 98312 | tf_op jit(solution)/shard_map/ppermute | solution.py:38
  6.8 10.8 %collective-permute-start.5 = (bf16[768,256]{1,0:T(8,128)(2,1)S(1)}, bf16[768,256]{1,0:T(8,128)(2,1)S(1)}, u32[]{:S(2)}, u32[]{:S(2)}) collective-permute-start(bf16[768,256]{1,0:T(8,128)(2,1)S(1)} %pass_on.5.after), channel_id=1, source_target_pairs={{2,0},{0,1},{1,3},{3,2},{6,4},{4,5},{5,7},{7,6},{10,8},{8,9},{9,11... | collective-permute-start | bytes 1179656 | tf_op jit(solution)/shard_map/ppermute | solution.py:524
  8.9 12.7 %collective-permute-start.7 = (bf16[768,256]{1,0:T(8,128)(2,1)S(1)}, bf16[768,256]{1,0:T(8,128)(2,1)S(1)}, u32[]{:S(2)}, u32[]{:S(2)}) collective-permute-start(bf16[768,256]{1,0:T(8,128)(2,1)S(1)} %pass_on.6.after), channel_id=1, source_target_pairs={{4,0},{0,1},{1,5},{5,4},{6,2},{2,3},{3,7},{7,6},{12,8},{8,9},{9,13... | collective-permute-start | bytes 1179656 | tf_op jit(solution)/shard_map/ppermute | solution.py:524
  8.9 1.6 %collective-permute-start.2 = (f32[32,256]{1,0:T(8,128)S(1)}, f32[32,256]{1,0:T(8,128)S(1)}, u32[]{:S(2)}, u32[]{:S(2)}) collective-permute-start(f32[32,256]{1,0:T(8,128)S(1)} %get-tuple-element.20.after.mine), channel_id=1, source_target_pairs={{0,1},{1,0},{2,3},{3,2},{4,5},{5,4},{6,7},{7,6},{8,9},{9,8},{10,11... | collective-permute-start | bytes 98312 | tf_op jit(solution)/shard_map/ppermute | solution.py:38
  10.7 11.8 %collective-permute-start.10 = (bf16[512,256]{1,0:T(8,128)(2,1)S(1)}, bf16[512,256]{1,0:T(8,128)(2,1)S(1)}, u32[]{:S(2)}, u32[]{:S(2)}) collective-permute-start(bf16[512,256]{1,0:T(8,128)(2,1)S(1)} %pass_on.8), channel_id=1, source_target_pairs={{16,0},{0,1},{1,17},{17,16},{18,2},{2,3},{3,19},{19,18},{20,4},{4,... | collective-permute-start | bytes 786440 | tf_op jit(solution)/shard_map/ppermute | solution.py:524
  11.1 16.4 %collective-permute-start.9 = (bf16[768,256]{1,0:T(8,128)(2,1)S(1)}, bf16[768,256]{1,0:T(8,128)(2,1)S(1)}, u32[]{:S(2)}, u32[]{:S(2)}) collective-permute-start(bf16[768,256]{1,0:T(8,128)(2,1)S(1)} %pass_on.7), channel_id=1, source_target_pairs={{8,0},{0,1},{1,9},{9,8},{10,2},{2,3},{3,11},{11,10},{12,4},{4,5},{... | collective-permute-start | bytes 1179656 | tf_op jit(solution)/shard_map/ppermute | solution.py:524
  13.8 3.9 %collective-permute-start.4 = (bf16[64,256]{1,0:T(8,128)(2,1)S(1)}, bf16[64,256]{1,0:T(8,128)(2,1)S(1)}, u32[]{:S(2)}, u32[]{:S(2)}) collective-permute-start(bf16[64,256]{1,0:T(8,128)(2,1)S(1)} %node_rise.1.after.mine), channel_id=1, source_target_pairs={{0,2},{1,3},{2,0},{3,1},{4,6},{5,7},{6,4},{7,5},{8,10},{9,11},{10,... | collective-permute-start | bytes 98312 | tf_op jit(solution)/shard_map/ppermute | solution.py:38
  17.9 4.3 %collective-permute-start.6 = (bf16[64,256]{1,0:T(8,128)(2,1)S(1)}, bf16[64,256]{1,0:T(8,128)(2,1)S(1)}, u32[]{:S(2)}, u32[]{:S(2)}) collective-permute-start(bf16[64,256]{1,0:T(8,128)(2,1)S(1)} %level_rise.3.after.mine), channel_id=1, source_target_pairs={{0,4},{1,5},{2,6},{3,7},{4,0},{5,1},{6,2},{7,3},{8,12},{9,13},{10,... | collective-permute-start | bytes 98312 | tf_op jit(solution)/shard_map/ppermute | solution.py:38
  22.3 5.4 %collective-permute-start.13 = (bf16[256,256]{1,0:T(8,128)(2,1)S(1)}, bf16[256,256]{1,0:T(8,128)(2,1)S(1)}, u32[]{:S(2)}, u32[]{:S(2)}) collective-permute-start(bf16[256,256]{1,0:T(8,128)(2,1)S(1)} %choose.4), channel_id=1, source_target_pairs={{0,1},{1,0},{2,3},{3,2},{4,5},{5,4},{6,7},{7,6},{8,9},{9,8},{10,11... | collective-permute-start | bytes 393224 | tf_op jit(solution)/shard_map/ppermute | solution.py:38
  22.6 11.5 %collective-permute-start.12 = (bf16[512,256]{1,0:T(8,128)(2,1)S(1)}, bf16[512,256]{1,0:T(8,128)(2,1)S(1)}, u32[]{:S(2)}, u32[]{:S(2)}) collective-permute-start(bf16[512,256]{1,0:T(8,128)(2,1)S(1)} %choose.3.after.refs_8_), channel_id=1, source_target_pairs={{0,8},{1,0},{9,1},{8,9},{2,10},{3,2},{11,3},{10,11},{4,12},{5,4},{... | collective-permute-start | bytes 786440 | tf_op jit(solution)/shard_map/ppermute | solution.py:529
  22.9 4.6 %collective-permute-start.8 = (bf16[64,256]{1,0:T(8,128)(2,1)S(1)}, bf16[64,256]{1,0:T(8,128)(2,1)S(1)}, u32[]{:S(2)}, u32[]{:S(2)}) collective-permute-start(bf16[64,256]{1,0:T(8,128)(2,1)S(1)} %level_rise.4.after.mine), channel_id=1, source_target_pairs={{0,8},{1,9},{2,10},{3,11},{4,12},{5,13},{6,14},{7,15},{8,0},{9,1},... | collective-permute-start | bytes 98312 | tf_op jit(solution)/shard_map/ppermute | solution.py:38
  28.0 10.5 %collective-permute-start.18 = (bf16[288,256]{1,0:T(8,128)(2,1)S(1)}, bf16[288,256]{1,0:T(8,128)(2,1)S(1)}, u32[]{:S(2)}, u32[]{:S(2)}) collective-permute-start(bf16[288,256]{1,0:T(8,128)(2,1)S(1)} %local.1.after.l0), channel_id=1, source_target_pairs={{0,2},{1,3},{2,0},{3,1},{4,6},{5,7},{6,4},{7,5},{8,10},{9,11},{10,... | collective-permute-start | bytes 442376 | tf_op jit(solution)/shard_map/ppermute | solution.py:38
  29.3 4.8 %collective-permute-start.11 = (bf16[64,256]{1,0:T(8,128)(2,1)S(1)}, bf16[64,256]{1,0:T(8,128)(2,1)S(1)}, u32[]{:S(2)}, u32[]{:S(2)}) collective-permute-start(bf16[64,256]{1,0:T(8,128)(2,1)S(1)} %level_rise.5.after.refs_0_), channel_id=1, source_target_pairs={{0,16},{1,17},{2,18},{3,19},{4,20},{5,21},{6,22},{7,23},{8,24},{9,... | collective-permute-start | bytes 98312 | tf_op jit(solution)/shard_map/ppermute | solution.py:38
  33.1 10.8 %copy-start = (bf16[256,2048]{1,0:T(8,128)(2,1)S(1)}, bf16[256,2048]{1,0:T(8,128)(2,1)}, u32[]{:S(2)}) copy-start(bf16[256,2048]{1,0:T(8,128)(2,1)} %out_basis.1) | copy-start | bytes 3145732
  34.6 3.8 %collective-permute-start.14 = (bf16[32,256]{1,0:T(8,128)(2,1)S(1)}, bf16[32,256]{1,0:T(8,128)(2,1)S(1)}, u32[]{:S(2)}, u32[]{:S(2)}) collective-permute-start(bf16[32,256]{1,0:T(8,128)(2,1)S(1)} %fall.1.after.mine), channel_id=1, source_target_pairs={{0,4},{1,5},{2,6},{3,7},{4,0},{5,1},{6,2},{7,3},{8,12},{9,13},{10,... | collective-permute-start | bytes 49160 | tf_op jit(solution)/shard_map/ppermute | solution.py:38
  36.2 6.6 %collective-permute-start.17 = (bf16[288,256]{1,0:T(8,128)(2,1)S(1)}, bf16[288,256]{1,0:T(8,128)(2,1)S(1)}, u32[]{:S(2)}, u32[]{:S(2)}) collective-permute-start(bf16[288,256]{1,0:T(8,128)(2,1)S(1)} %local.1.after.l0), channel_id=1, source_target_pairs={{0,1},{1,0},{2,3},{3,2},{4,5},{5,4},{6,7},{7,6},{8,9},{9,8},{10,11... | collective-permute-start | bytes 442376 | tf_op jit(solution)/shard_map/ppermute | solution.py:38
  38.5 5.4 %collective-permute-start.19 = (bf16[288,256]{1,0:T(8,128)(2,1)S(1)}, bf16[288,256]{1,0:T(8,128)(2,1)S(1)}, u32[]{:S(2)}, u32[]{:S(2)}) collective-permute-start(bf16[288,256]{1,0:T(8,128)(2,1)S(1)} %pass_on.9), channel_id=1, source_target_pairs={{0,1},{1,0},{2,3},{3,2},{4,5},{5,4},{6,7},{7,6},{8,9},{9,8},{10,11... | collective-permute-start | bytes 442376 | tf_op jit(solution)/shard_map/ppermute | solution.py:38
  39.0 3.7 %collective-permute-start.15 = (bf16[32,256]{1,0:T(8,128)(2,1)S(1)}, bf16[32,256]{1,0:T(8,128)(2,1)S(1)}, u32[]{:S(2)}, u32[]{:S(2)}) collective-permute-start(bf16[32,256]{1,0:T(8,128)(2,1)S(1)} %step_down.1.after.lower), channel_id=1, source_target_pairs={{0,2},{1,3},{2,0},{3,1},{4,6},{5,7},{6,4},{7,5},{8,10},{9,11},{10,... | collective-permute-start | bytes 49160 | tf_op jit(solution)/shard_map/ppermute | solution.py:38
  42.7 1.2 %collective-permute-start.16 = (bf16[32,256]{1,0:T(8,128)(2,1)S(1)}, bf16[32,256]{1,0:T(8,128)(2,1)S(1)}, u32[]{:S(2)}, u32[]{:S(2)}) collective-permute-start(bf16[32,256]{1,0:T(8,128)(2,1)S(1)} %choose.5.f_own), channel_id=1, source_target_pairs={{0,1},{1,0},{2,3},{3,2},{4,5},{5,4},{6,7},{7,6},{8,9},{9,8},{10,11... | collective-permute-start | bytes 49160 | tf_op jit(solution)/shard_map/ppermute | solution.py:38

commit v6 on v5

--- a/solution.py
+++ b/solution.py
@@ -439,20 +439,41 @@
     )(upper, lower, after)
 
 
-def final_kernel(strips, pick, f_own, f_core, l0, l1, l2, l3, out_basis, inv_ref, *refs):
+def fold_kernel(strips, pick, l0, l1, l2, l3, out_basis, after, *refs):
     nears = refs[:strips]
-    answer_hbm, total, answer, sems = refs[strips:]
-    rank = f_own.shape[1]
-    f2 = jnp.where(bit_of_device(0), f_core[...], f_own[...])
-    values = [
-        mm(f2, pack_ref[:rank, :]) + pack_ref[rank:, :].astype(F32) for pack_ref in (l0, l1, l2, l3)
-    ]
-    leaf_f = picked(pick[SPREAD : SPREAD + 1, :], values).astype(BF)
+    map_ref, base_ref = refs[strips:]
+    rank = out_basis.shape[0]
+    packs = (l0, l1, l2, l3)
+    number = pick[SPREAD : SPREAD + 1, :]
+    chosen = picked(number, [ref[:rank, :].astype(F32) for ref in packs]).astype(BF)
+    inner = picked(number, [ref[rank:, :].astype(F32) for ref in packs]).astype(BF)
+    map_ref[...] = mm(chosen, out_basis[...]).astype(BF)
     width = nears[0].shape[1]
     for i in range(strips):
         span = slice(i * width, (i + 1) * width)
-        total[:, span] = nears[i][...] + mm(leaf_f, out_basis[:, span])
-
+        base_ref[:, span] = nears[i][...] + mm(inner, out_basis[:, span])
+
+
+def fold(pick, locals_, basis_out, nears, after):
+    rank, columns = basis_out.shape
+    rows = nears[0].shape[0]
+    return pl.pallas_call(
+        functools.partial(fold_kernel, len(nears)),
+        out_shape=(
+            jax.ShapeDtypeStruct((rank, columns), BF),
+            jax.ShapeDtypeStruct((rows, columns), F32),
+        ),
+        in_specs=[VMEM] * 6 + [ANY] + [VMEM] * len(nears),
+        out_specs=(VMEM,) * 2,
+        compiler_params=params(),
+        cost_estimate=took(1.0),
+        name="fold",
+    )(pick, *locals_, basis_out, after, *nears)
+
+
+def final_kernel(f_own, f_core, map_ref, base_ref, inv_ref, answer_hbm, total, answer, sems):
+    f2 = jnp.where(bit_of_device(0), f_core[...], f_own[...])
+    total[...] = base_ref[...] + mm(f2, map_ref[...])
     copies = []
 
     def store(tile, found):
@@ -471,13 +492,12 @@
         copy.wait()
 
 
-def final(pick, f2, f2_core, locals_, basis_out, inverse_order, nears):
-    rows, rank = f2.shape
-    columns = basis_out.shape[1]
-    return pl.pallas_call(
-        functools.partial(final_kernel, len(nears)),
+def final(f2, f2_core, leaf_map, base, inverse_order):
+    rows, columns = base.shape
+    return pl.pallas_call(
+        final_kernel,
         out_shape=jax.ShapeDtypeStruct((rows, columns), F32),
-        in_specs=[VMEM] * (9 + len(nears)),
+        in_specs=[VMEM] * 5,
         out_specs=ANY,
         scratch_shapes=[
             pltpu.VMEM((rows, columns), F32),
@@ -485,9 +505,9 @@
             pltpu.SemaphoreType.DMA((columns // (4 * LANES),)),
         ],
         compiler_params=params(),
-        cost_estimate=took(2.9),
+        cost_estimate=took(1.8),
         name="final",
-    )(pick, f2, f2_core, *locals_, basis_out, inverse_order, *nears)
+    )(f2, f2_core, leaf_map, base, inverse_order)
 
 
 def body(
@@ -531,58 +551,71 @@
     pick, tree, reduced, low, high, top_low, top_high, up_map, down_map = start(
         right_sides, point_order, basis_in, leaf_map, leaf_up, leaf_down, node_up, node_down, node_cross
     )
-    node_maps = (high, to_left(low, 0))
+
+    held_maps = {}
+
+    def release(level, after):
+        first, second = (top_low, top_high) if level == levels else (low, high)
+        gate = pass_on(first, after)
+        held_maps[level] = (second, to_left(gate, level - 1))
+        return gate
+
+    def spread(level, after):
+        own, passed = held_maps[level]
+        now = choose(level - 1, own, passed, after)
+        for step in range(level - 2, cut, -1):
+            passed = to_right(now, step)
+            if step > cut + 1:
+                now = choose(step, passed, now, after)
+        held_maps[level] = (passed, now)
 
     pair = join(reduced, swap(reduced, 1), reduced)
-    gate = pass_on(low, pair)
-    block_maps = (high, to_left(gate, 1))
+    gate = release(cut, pair)
+    node_maps = (high, swap(gate, 1))
+    for level in [levels]:
+        release(level, pair)
     g0, product = leaf_rise(pick, pair, swap(pair, 2), up_map, gate)
-    gate = pass_on(low, product)
-    held_maps = [(high, to_left(gate, cut))]
+    gate = release(cut + 1, product)
+    for level in range(cut + 2, levels):
+        release(level, product)
     pay = node_rise(product, swap(product, 1), node_maps, gate)
-    for level in range(levels, cut + 1, -1):
-        first, second = (top_low, top_high) if level == levels else (low, high)
-        gate = pass_on(first, pay)
-        held_maps.insert(1, (second, to_left(gate, level - 1)))
+    for level in []:
+        release(level, pay)
     strips = 4
     nears = []
     arrivals = []
     for bit in range(1, levels - 1):
         arrivals.append(swap(pay, 1 << bit))
+        after = pay
         if bit <= cut:
             after = near_strip(tree, leaf_inverse, len(nears), strips, pay)
             nears.append(after)
+        if bit == cut:
+            for level in range(cut + 3, levels + 1):
+                spread(level, pay)
         if bit == cut + 1:
-            after = pay
-            for level in range(cut + 3, levels + 1):
-                own, passed = held_maps[level - cut - 1]
-                now = after = choose(level - 1, own, passed, pay)
-                for step in range(level - 2, cut, -1):
-                    passed = to_right(now, step)
-                    if step > cut + 1:
-                        now = choose(step, passed, now, pay)
-                held_maps[level - cut - 1] = (passed, now)
-        maps = block_maps if bit == 1 else held_maps[bit - cut]
-        pay = level_rise(min(bit, cut + 1), pay, arrivals[-1], maps, after)
+            pass
+        pay = level_rise(min(bit, cut + 1), pay, arrivals[-1], held_maps[bit + 1], after)
         if bit == cut:
-            block_cross = choose(1, high[2 * rank :], block_maps[1][2 * rank :], pay)
+            own, passed = held_maps[cut]
+            block_cross = choose(1, own[2 * rank :], passed[2 * rank :], pay)
             block_cross = to_right(block_cross, 0)
 
-    own_local = local(g0, arrivals[0], node_maps, block_maps, block_cross, down_map, pay)
+    own_local = local(g0, arrivals[0], node_maps, held_maps[cut], block_cross, down_map, pay)
     local_x = swap(own_local, 2)
-    nears.append(near_strip(tree, leaf_inverse, 2, strips, own_local))
-
-    cut_f = fall(cut, pay, swap(pay, 1 << (levels - 1)), arrivals[2:], held_maps, nears[2])
+    nears.append(near_strip(tree, leaf_inverse, 2, strips, pay))
+
+    maps = [held_maps[level] for level in range(cut + 1, levels + 1)]
+    cut_f = fall(cut, pay, swap(pay, 1 << (levels - 1)), arrivals[2:], maps, nears[2])
     nears.append(near_strip(tree, leaf_inverse, 3, strips, cut_f))
     block_f = step_down(
-        cut, cut_f, swap(cut_f, SPREAD), arrivals[1], held_maps[0], block_maps, nears[3]
+        cut, cut_f, swap(cut_f, SPREAD), arrivals[1], maps[0], held_maps[cut], nears[3]
     )
     inverse_order = invert(point_order, block_f)
     locals_ = [own_local, swap(own_local, 1), local_x, swap(pass_on(local_x, block_f), 1)]
-    block_f = choose(1, swap(block_f, 2), block_f, inverse_order)
-    return final(
-        pick, block_f, swap(block_f, 1), locals_, basis_out, inverse_order, nears
-    )
+    composed, base = fold(pick, locals_, basis_out, nears, inverse_order)
+    block_f = choose(1, swap(block_f, 2), block_f, base)
+    return final(block_f, swap(block_f, 1), composed, base, inverse_order)
 
 
 def solution(mesh):

time: 46.6 us -> 44.7 us (0.959)
  waiting for transfers between devices: 13.5 us -> 9.79 us
  starting transfers between devices: 17.3 us -> 18.7 us
    ppermute x15, waiting for transfers between devices: 13.5 us -> 9.77 us  [swap(): return lax.ppermute(block, 'leaf', [(i, i ^ mask) for i in range(count)])]
    ppermute x15, starting transfers between devices: 13.8 us -> 16.3 us  [swap(): return lax.ppermute(block, 'leaf', [(i, i ^ mask) for i in range(count)])]
    ppermute x4, starting transfers between devices: 3.1 us -> 1.83 us  [to_left(): return lax.ppermute(block, 'leaf', cycle(bit))]
    pallas_call x1 -> x2, Pallas kernels: 2.43 us -> 2.77 us  [the longest x1 2.16 us: final(): pl.pallas_call(final_kernel, out_shape=jax.ShapeDtypeStruct((rows, column...]
  transfers between devices with their start and end apart: 20 -> 20, of which waited for: 10 -> 9; matrix products, arithmetic and copies ran while one was open for 0% -> 0% of each run, Pallas kernels for 24% -> 26%
where the time goes in v6:
time: 44.7 us; the launch traced here: 44.4 us
  starting transfers between devices  18.7 us (42%)
  Pallas kernels  15.7 us (35%)
  waiting for transfers between devices  9.79 us (22%)
    ppermute x15, starting transfers between devices, swap(): return lax.ppermute(block, 'leaf', [(i, i ^ mask) for i in range(count)])  16.3 us
    ppermute x15, waiting for transfers between devices, swap(): return lax.ppermute(block, 'leaf', [(i, i ^ mask) for i in range(count)])  9.77 us
    pallas_call x4, Pallas kernels, near_strip(): pl.pallas_call(functools.partial(near_kernel, strip * width), out_shape=j...  8.09 us
    pallas_call x1, Pallas kernels, final(): pl.pallas_call(final_kernel, out_shape=jax.ShapeDtypeStruct((rows, column...  2.16 us
    pallas_call x1, Pallas kernels, start(): pl.pallas_call(start_kernel, out_shape=(jax.ShapeDtypeStruct((2 * SPREAD,...  2.03 us
    ppermute x4, starting transfers between devices, to_left(): return lax.ppermute(block, 'leaf', cycle(bit))  1.83 us
    pallas_call x1, Pallas kernels, invert(): pl.pallas_call(invert_kernel, out_shape=jax.ShapeDtypeStruct((columns //...  1 us
  transfers between devices with their start and end apart: 20, of which 9 were waited for; matrix products, arithmetic and copies ran while one was open for 0% of the time, Pallas kernels for 26%

profile of v6, /device:TPU:0, one launch (start us, length us, event | category | flops | bytes accessed | tf_op | source)
XLA Modules:
  0.0 44.4 jit_solution(5796382935918055871)
XLA Ops:
  0.0 2.0 %start.1 = (s32[8,128]{1,0:T(8,128)S(1)}, bf16[32,2048]{1,0:T(8,128)(2,1)S(1)}, bf16[32,256]{1,0:T(8,128)(2,1)S(1)}, bf16[768,256]{1,0:T(8,128)(2,1)S(1)}, bf16[...) custom-call(bf16[32,2048]{1,0:T(8,128)(2,1)} %rhs_hbm.1, ...), custom_call_target="tpu_custom_call" | custom-call | bytes 8100000 | tf_op jit(solution)/shard_map/start/pallas_call | solution.py:142
  2.0 0.5 %collective-permute-start = (bf16[32,256]{1,0:T(8,128)(2,1)S(1)}, bf16[32,256]{1,0:T(8,128)(2,1)S(1)}, u32[]{:S(2)}, u32[]{:S(2)}) collective-permute-start(bf16[32,256]{1,0:T(8,128)(2,1)S(1)} %get-tuple-element.19.mine.after), channel_id=1, source_target_pairs={{0,1},{1,0},{2,3},{3,2},{4,5},{5,4},{6,7},{7,6},{8,9},{9,8},{10,11... | collective-permute-start | bytes 49160 | tf_op jit(solution)/shard_map/ppermute | solution.py:38
  2.6 0.8 %collective-permute-done.other = bf16[32,256]{1,0:T(8,128)(2,1)S(1)} collective-permute-done((bf16[32,256]{1,0:T(8,128)(2,1)S(1)}, bf16[32,256]{1,0:T(8,128)(2,1)S(1)}, u32[]{:S(2)}, u32[]{:S(2)}) %collective-permute-start) | collective-permute-done | bytes 16416 | tf_op jit(solution)/shard_map/ppermute | solution.py:38
  3.4 0.4 collective-permute-start.3
  3.8 2.7 %collective-permute-start.1 = (bf16[64,256]{1,0:T(8,128)(2,1)S(1)}, bf16[64,256]{1,0:T(8,128)(2,1)S(1)}, u32[]{:S(2)}, u32[]{:S(2)}) collective-permute-start(bf16[64,256]{1,0:T(8,128)(2,1)S(1)} %join.1.after.pair_own), channel_id=1, source_target_pairs={{0,2},{1,3},{2,0},{3,1},{4,6},{5,7},{6,4},{7,5},{8,10},{9,11},{10,... | collective-permute-start | bytes 98312 | tf_op jit(solution)/shard_map/ppermute | solution.py:38
  6.6 1.8 %collective-permute-done.1.pair_x = bf16[64,256]{1,0:T(8,128)(2,1)S(1)} collective-permute-done((bf16[64,256]{1,0:T(8,128)(2,1)S(1)}, bf16[64,256]{1,0:T(8,128)(2,1)S(1)}, u32[]{:S(2)}, u32[]{:S(2)}) %collective-permute-start.1) | collective-permute-done | bytes 32800 | tf_op jit(solution)/shard_map/ppermute | solution.py:38
  8.6 0.9 %collective-permute-start.2 = (f32[32,256]{1,0:T(8,128)S(1)}, f32[32,256]{1,0:T(8,128)S(1)}, u32[]{:S(2)}, u32[]{:S(2)}) collective-permute-start(f32[32,256]{1,0:T(8,128)S(1)} %get-tuple-element.22.after.mine), channel_id=1, source_target_pairs={{0,1},{1,0},{2,3},{3,2},{4,5},{5,4},{6,7},{7,6},{8,9},{9,8},{10,11... | collective-permute-start | bytes 98312 | tf_op jit(solution)/shard_map/ppermute | solution.py:38
  9.7 0.8 %collective-permute-done.2.other = f32[32,256]{1,0:T(8,128)S(1)} collective-permute-done((f32[32,256]{1,0:T(8,128)S(1)}, f32[32,256]{1,0:T(8,128)S(1)}, u32[]{:S(2)}, u32[]{:S(2)}) %collective-permute-start.2) | collective-permute-done | bytes 32800 | tf_op jit(solution)/shard_map/ppermute | solution.py:38
  10.4 1.7 %collective-permute-start.9 = (bf16[768,256]{1,0:T(8,128)(2,1)S(1)}, bf16[768,256]{1,0:T(8,128)(2,1)S(1)}, u32[]{:S(2)}, u32[]{:S(2)}) collective-permute-start(bf16[768,256]{1,0:T(8,128)(2,1)S(1)} %pass_on.5.after), channel_id=1, source_target_pairs={{8,0},{0,1},{1,9},{9,8},{10,2},{2,3},{3,11},{11,10},{12,4},{4,5},{... | collective-permute-start | bytes 1179656 | tf_op jit(solution)/shard_map/ppermute | solution.py:544
  12.3 1.8 %collective-permute-start.4 = (bf16[64,256]{1,0:T(8,128)(2,1)S(1)}, bf16[64,256]{1,0:T(8,128)(2,1)S(1)}, u32[]{:S(2)}, u32[]{:S(2)}) collective-permute-start(bf16[64,256]{1,0:T(8,128)(2,1)S(1)} %node_rise.1.after.mine), channel_id=1, source_target_pairs={{0,2},{1,3},{2,0},{3,1},{4,6},{5,7},{6,4},{7,5},{8,10},{9,11},{10,... | collective-permute-start | bytes 98312 | tf_op jit(solution)/shard_map/ppermute | solution.py:38
  14.1 2.0 %near.4.after.refs_0_ = f32[32,512]{1,0:T(8,128)S(1)} custom-call(bf16[32,2048]{1,0:T(8,128)(2,1)S(1)} %get-tuple-element.24.tree_ref, bf16[2048,2048]{1,0:T(8,128)(2,1)} %inverse_hbm.7, bf16[64,256]{1,0:T(8,128)(2,1)S(1)} %node_rise.1.after.mine), custom_call_target="tpu_custom_call" | custom-call | bytes 4200000 | tf_op jit(solution)/shard_map/near/pallas_call | solution.py:228
  16.3 2.0 %collective-permute-start.6 = (bf16[64,256]{1,0:T(8,128)(2,1)S(1)}, bf16[64,256]{1,0:T(8,128)(2,1)S(1)}, u32[]{:S(2)}, u32[]{:S(2)}) collective-permute-start(bf16[64,256]{1,0:T(8,128)(2,1)S(1)} %level_rise.3.after.mine), channel_id=1, source_target_pairs={{0,4},{1,5},{2,6},{3,7},{4,0},{5,1},{6,2},{7,3},{8,12},{9,13},{10,... | collective-permute-start | bytes 98312 | tf_op jit(solution)/shard_map/ppermute | solution.py:38
  18.3 2.0 %near.5.after.refs_1_ = f32[32,512]{1,0:T(8,128)S(1)} custom-call(bf16[32,2048]{1,0:T(8,128)(2,1)S(1)} %get-tuple-element.24.tree_ref, bf16[2048,2048]{1,0:T(8,128)(2,1)} %inverse_hbm.7, bf16[64,256]{1,0:T(8,128)(2,1)S(1)} %level_rise.3.after.mine), custom_call_target="tpu_custom_call" | custom-call | bytes 4200000 | tf_op jit(solution)/shard_map/near/pallas_call | solution.py:228
  20.4 0.5 %collective-permute-start.12 = (bf16[512,256]{1,0:T(8,128)(2,1)S(1)}, bf16[512,256]{1,0:T(8,128)(2,1)S(1)}, u32[]{:S(2)}, u32[]{:S(2)}) collective-permute-start(bf16[512,256]{1,0:T(8,128)(2,1)S(1)} %choose.3.refs_8_), channel_id=1, source_target_pairs={{0,8},{1,0},{9,1},{8,9},{2,10},{3,2},{11,3},{10,11},{4,12},{5,4},{... | collective-permute-start | bytes 786440 | tf_op jit(solution)/shard_map/ppermute | solution.py:549
  21.1 0.3 collective-permute-start.15
  21.4 1.7 %collective-permute-start.8 = (bf16[64,256]{1,0:T(8,128)(2,1)S(1)}, bf16[64,256]{1,0:T(8,128)(2,1)S(1)}, u32[]{:S(2)}, u32[]{:S(2)}) collective-permute-start(bf16[64,256]{1,0:T(8,128)(2,1)S(1)} %level_rise.4.mine.after), channel_id=1, source_target_pairs={{0,8},{1,9},{2,10},{3,11},{4,12},{5,13},{6,14},{7,15},{8,0},{9,1},... | collective-permute-start | bytes 98312 | tf_op jit(solution)/shard_map/ppermute | solution.py:38
  23.1 2.6 %collective-permute-done.8.other.refs_2_ = bf16[64,256]{1,0:T(8,128)(2,1)S(1)} collective-permute-done((bf16[64,256]{1,0:T(8,128)(2,1)S(1)}, bf16[64,256]{1,0:T(8,128)(2,1)S(1)}, u32[]{:S(2)}, u32[]{:S(2)}) %collective-permute-start.8) | collective-permute-done | bytes 32800 | tf_op jit(solution)/shard_map/ppermute | solution.py:38
  25.9 0.3 local.1.l0
  26.2 1.7 %collective-permute-start.17 = (bf16[288,256]{1,0:T(8,128)(2,1)S(1)}, bf16[288,256]{1,0:T(8,128)(2,1)S(1)}, u32[]{:S(2)}, u32[]{:S(2)}) collective-permute-start(bf16[288,256]{1,0:T(8,128)(2,1)S(1)} %local.1.l0), channel_id=1, source_target_pairs={{0,2},{1,3},{2,0},{3,1},{4,6},{5,7},{6,4},{7,5},{8,10},{9,11},{10,... | collective-permute-start | bytes 442376 | tf_op jit(solution)/shard_map/ppermute | solution.py:38
  27.9 2.4 %collective-permute-start.10 = (bf16[64,256]{1,0:T(8,128)(2,1)S(1)}, bf16[64,256]{1,0:T(8,128)(2,1)S(1)}, u32[]{:S(2)}, u32[]{:S(2)}) collective-permute-start(bf16[64,256]{1,0:T(8,128)(2,1)S(1)} %level_rise.5.after.refs_0_), channel_id=1, source_target_pairs={{0,16},{1,17},{2,18},{3,19},{4,20},{5,21},{6,22},{7,23},{8,24},{9,... | collective-permute-start | bytes 98312 | tf_op jit(solution)/shard_map/ppermute | solution.py:38
  30.3 2.0 %near.6.refs_9_.refs_2_ = f32[32,512]{1,0:T(8,128)S(1)} custom-call(bf16[32,2048]{1,0:T(8,128)(2,1)S(1)} %get-tuple-element.24.tree_ref, bf16[2048,2048]{1,0:T(8,128)(2,1)} %inverse_hbm.7, bf16[64,256]{1,0:T(8,128)(2,1)S(1)} %level_rise.5.after.refs_0_), custom_call_target="tpu_custom_call" | custom-call | bytes 4200000 | tf_op jit(solution)/shard_map/near/pallas_call | solution.py:228
  32.3 0.4 collective-permute-done.10.refs_1_
  32.8 0.4 %fall.1.after.mine = bf16[32,256]{1,0:T(8,128)(2,1)S(1)} custom-call(bf16[64,256]{1,0:T(8,128)(2,1)S(1)} %level_rise.5.after.refs_0_, bf16[64,256]{1,0:T(8,128)(2,1)S(1)} %collective-permute-done.10.refs_1_, bf16[64,256]{1,0:T(8,128)(2,1)S(1)} %collective-permute-done.8.other.refs_2_, ...), custom_call_target="tpu_custom_call" | custom-call | bytes 1350000 | tf_op jit(solution)/shard_map/fall/pallas_call | solution.py:354
  33.2 1.2 %collective-permute-start.13 = (bf16[32,256]{1,0:T(8,128)(2,1)S(1)}, bf16[32,256]{1,0:T(8,128)(2,1)S(1)}, u32[]{:S(2)}, u32[]{:S(2)}) collective-permute-start(bf16[32,256]{1,0:T(8,128)(2,1)S(1)} %fall.1.after.mine), channel_id=1, source_target_pairs={{0,4},{1,5},{2,6},{3,7},{4,0},{5,1},{6,2},{7,3},{8,12},{9,13},{10,... | collective-permute-start | bytes 49160 | tf_op jit(solution)/shard_map/ppermute | solution.py:38
  34.4 2.0 %near.7.after.refs_3_ = f32[32,512]{1,0:T(8,128)S(1)} custom-call(bf16[32,2048]{1,0:T(8,128)(2,1)S(1)} %get-tuple-element.24.tree_ref, bf16[2048,2048]{1,0:T(8,128)(2,1)} %inverse_hbm.7, bf16[32,256]{1,0:T(8,128)(2,1)S(1)} %fall.1.after.mine), custom_call_target="tpu_custom_call" | custom-call | bytes 4200000 | tf_op jit(solution)/shard_map/near/pallas_call | solution.py:228
  36.5 0.5 %collective-permute-done.13.other = bf16[32,256]{1,0:T(8,128)(2,1)S(1)} collective-permute-done((bf16[32,256]{1,0:T(8,128)(2,1)S(1)}, bf16[32,256]{1,0:T(8,128)(2,1)S(1)}, u32[]{:S(2)}, u32[]{:S(2)}) %collective-permute-start.13) | collective-permute-done | bytes 16416 | tf_op jit(solution)/shard_map/ppermute | solution.py:38
  37.2 0.6 %collective-permute-start.14 = (bf16[32,256]{1,0:T(8,128)(2,1)S(1)}, bf16[32,256]{1,0:T(8,128)(2,1)S(1)}, u32[]{:S(2)}, u32[]{:S(2)}) collective-permute-start(bf16[32,256]{1,0:T(8,128)(2,1)S(1)} %step_down.1.after.lower), channel_id=1, source_target_pairs={{0,2},{1,3},{2,0},{3,1},{4,6},{5,7},{6,4},{7,5},{8,10},{9,11},{10,... | collective-permute-start | bytes 49160 | tf_op jit(solution)/shard_map/ppermute | solution.py:38
  37.8 1.0 %invert.1.after.inv_ref = s32[16,128]{1,0:T(8,128)S(1)} custom-call(s32[1,2048]{1,0:T(1,128)} %order_hbm.3, bf16[32,256]{1,0:T(8,128)(2,1)S(1)} %step_down.1.after.lower), custom_call_target="tpu_custom_call" | custom-call | bytes 3000000 | tf_op jit(solution)/shard_map/invert/pallas_call | solution.py:196
  38.9 0.6 %fold.1 = (bf16[256,2048]{1,0:T(8,128)(2,1)S(1)}, f32[32,2048]{1,0:T(8,128)S(1)}) custom-call(s32[8,128]{1,0:T(8,128)S(1)} %get-tuple-element.18.pick, bf16[288,256]{1,0:T(8,128)(2,1)S(1)} %local.1.l0, bf16[288,256]{1,0:T(8,128)(2,1)S(1)} %collective-permute-done.16.l1, bf16[288,256]{1,0:T(8,128)(2,1)S(1)} %collective-permute-done.17.block.l2, ...), custom_call_target="tpu_custom_call" | custom-call | bytes 3000000 | tf_op jit(solution)/shard_map/fold/pallas_call | solution.py:460
  39.5 1.6 %collective-permute-done.14.upper = bf16[32,256]{1,0:T(8,128)(2,1)S(1)} collective-permute-done((bf16[32,256]{1,0:T(8,128)(2,1)S(1)}, bf16[32,256]{1,0:T(8,128)(2,1)S(1)}, u32[]{:S(2)}, u32[]{:S(2)}) %collective-permute-start.14) | collective-permute-done | bytes 16416 | tf_op jit(solution)/shard_map/ppermute | solution.py:38
  41.1 1.2 %collective-permute-done.19.f_core = bf16[32,256]{1,0:T(8,128)(2,1)S(1)} collective-permute-done((bf16[32,256]{1,0:T(8,128)(2,1)S(1)}, bf16[32,256]{1,0:T(8,128)(2,1)S(1)}, u32[]{:S(2)}, u32[]{:S(2)}) %collective-permute-start.19) | collective-permute-done | bytes 16416 | tf_op jit(solution)/shard_map/ppermute | solution.py:38
  42.2 2.2 %final.1 = f32[32,2048]{1,0:T(8,128)} custom-call(bf16[32,256]{1,0:T(8,128)(2,1)S(1)} %choose.5.f_own, bf16[32,256]{1,0:T(8,128)(2,1)S(1)} %collective-permute-done.19.f_core, bf16[256,2048]{1,0:T(8,128)(2,1)S(1)} %get-tuple-element.30.map_ref, f32[32,2048]{1,0:T(8,128)S(1)} %get-tuple-element.29.after.base_ref, s32[16,128]{1,0:T(8,128)S(1)} %invert.1.after.inv_ref), custom_call_target="tpu_custom_call" | custom-call | bytes 5400000 | tf_op jit(solution)/shard_map/final/pallas_call | solution.py:497
  (36 shorter events, 1.4 us)
Async XLA Ops:
  2.0 1.4 %collective-permute-start = (bf16[32,256]{1,0:T(8,128)(2,1)S(1)}, bf16[32,256]{1,0:T(8,128)(2,1)S(1)}, u32[]{:S(2)}, u32[]{:S(2)}) collective-permute-start(bf16[32,256]{1,0:T(8,128)(2,1)S(1)} %get-tuple-element.19.mine.after), channel_id=1, source_target_pairs={{0,1},{1,0},{2,3},{3,2},{4,5},{5,4},{6,7},{7,6},{8,9},{9,8},{10,11... | collective-permute-start | bytes 49160 | tf_op jit(solution)/shard_map/ppermute | solution.py:38
  3.4 8.7 %collective-permute-start.3 = (bf16[768,256]{1,0:T(8,128)(2,1)S(1)}, bf16[768,256]{1,0:T(8,128)(2,1)S(1)}, u32[]{:S(2)}, u32[]{:S(2)}) collective-permute-start(bf16[768,256]{1,0:T(8,128)(2,1)S(1)} %pass_on.4.after), channel_id=1, source_target_pairs={{0,1},{1,0},{2,3},{3,2},{4,5},{5,4},{6,7},{7,6},{8,9},{9,8},{10,11... | collective-permute-start | bytes 1179656 | tf_op jit(solution)/shard_map/ppermute | solution.py:38
  3.8 4.5 %collective-permute-start.1 = (bf16[64,256]{1,0:T(8,128)(2,1)S(1)}, bf16[64,256]{1,0:T(8,128)(2,1)S(1)}, u32[]{:S(2)}, u32[]{:S(2)}) collective-permute-start(bf16[64,256]{1,0:T(8,128)(2,1)S(1)} %join.1.after.pair_own), channel_id=1, source_target_pairs={{0,2},{1,3},{2,0},{3,1},{4,6},{5,7},{6,4},{7,5},{8,10},{9,11},{10,... | collective-permute-start | bytes 98312 | tf_op jit(solution)/shard_map/ppermute | solution.py:38
  6.5 9.6 %collective-permute-start.5 = (bf16[768,256]{1,0:T(8,128)(2,1)S(1)}, bf16[768,256]{1,0:T(8,128)(2,1)S(1)}, u32[]{:S(2)}, u32[]{:S(2)}) collective-permute-start(bf16[768,256]{1,0:T(8,128)(2,1)S(1)} %pass_on.4.after), channel_id=1, source_target_pairs={{2,0},{0,1},{1,3},{3,2},{6,4},{4,5},{5,7},{7,6},{10,8},{8,9},{9,11... | collective-permute-start | bytes 1179656 | tf_op jit(solution)/shard_map/ppermute | solution.py:544
  8.6 12.4 %collective-permute-start.7 = (bf16[768,256]{1,0:T(8,128)(2,1)S(1)}, bf16[768,256]{1,0:T(8,128)(2,1)S(1)}, u32[]{:S(2)}, u32[]{:S(2)}) collective-permute-start(bf16[768,256]{1,0:T(8,128)(2,1)S(1)} %pass_on.5.after), channel_id=1, source_target_pairs={{4,0},{0,1},{1,5},{5,4},{6,2},{2,3},{3,7},{7,6},{12,8},{8,9},{9,13... | collective-permute-start | bytes 1179656 | tf_op jit(solution)/shard_map/ppermute | solution.py:544
  8.6 1.8 %collective-permute-start.2 = (f32[32,256]{1,0:T(8,128)S(1)}, f32[32,256]{1,0:T(8,128)S(1)}, u32[]{:S(2)}, u32[]{:S(2)}) collective-permute-start(f32[32,256]{1,0:T(8,128)S(1)} %get-tuple-element.22.after.mine), channel_id=1, source_target_pairs={{0,1},{1,0},{2,3},{3,2},{4,5},{5,4},{6,7},{7,6},{8,9},{9,8},{10,11... | collective-permute-start | bytes 98312 | tf_op jit(solution)/shard_map/ppermute | solution.py:38
  9.6 10.8 %collective-permute-start.11 = (bf16[512,256]{1,0:T(8,128)(2,1)S(1)}, bf16[512,256]{1,0:T(8,128)(2,1)S(1)}, u32[]{:S(2)}, u32[]{:S(2)}) collective-permute-start(bf16[512,256]{1,0:T(8,128)(2,1)S(1)} %pass_on.6), channel_id=1, source_target_pairs={{16,0},{0,1},{1,17},{17,16},{18,2},{2,3},{3,19},{19,18},{20,4},{4,... | collective-permute-start | bytes 786440 | tf_op jit(solution)/shard_map/ppermute | solution.py:544
  10.4 12.7 %collective-permute-start.9 = (bf16[768,256]{1,0:T(8,128)(2,1)S(1)}, bf16[768,256]{1,0:T(8,128)(2,1)S(1)}, u32[]{:S(2)}, u32[]{:S(2)}) collective-permute-start(bf16[768,256]{1,0:T(8,128)(2,1)S(1)} %pass_on.5.after), channel_id=1, source_target_pairs={{8,0},{0,1},{1,9},{9,8},{10,2},{2,3},{3,11},{11,10},{12,4},{4,5},{... | collective-permute-start | bytes 1179656 | tf_op jit(solution)/shard_map/ppermute | solution.py:544
  12.3 3.9 %collective-permute-start.4 = (bf16[64,256]{1,0:T(8,128)(2,1)S(1)}, bf16[64,256]{1,0:T(8,128)(2,1)S(1)}, u32[]{:S(2)}, u32[]{:S(2)}) collective-permute-start(bf16[64,256]{1,0:T(8,128)(2,1)S(1)} %node_rise.1.after.mine), channel_id=1, source_target_pairs={{0,2},{1,3},{2,0},{3,1},{4,6},{5,7},{6,4},{7,5},{8,10},{9,11},{10,... | collective-permute-start | bytes 98312 | tf_op jit(solution)/shard_map/ppermute | solution.py:38
  16.3 4.6 %collective-permute-start.6 = (bf16[64,256]{1,0:T(8,128)(2,1)S(1)}, bf16[64,256]{1,0:T(8,128)(2,1)S(1)}, u32[]{:S(2)}, u32[]{:S(2)}) collective-permute-start(bf16[64,256]{1,0:T(8,128)(2,1)S(1)} %level_rise.3.after.mine), channel_id=1, source_target_pairs={{0,4},{1,5},{2,6},{3,7},{4,0},{5,1},{6,2},{7,3},{8,12},{9,13},{10,... | collective-permute-start | bytes 98312 | tf_op jit(solution)/shard_map/ppermute | solution.py:38
  20.4 12.4 %collective-permute-start.12 = (bf16[512,256]{1,0:T(8,128)(2,1)S(1)}, bf16[512,256]{1,0:T(8,128)(2,1)S(1)}, u32[]{:S(2)}, u32[]{:S(2)}) collective-permute-start(bf16[512,256]{1,0:T(8,128)(2,1)S(1)} %choose.3.refs_8_), channel_id=1, source_target_pairs={{0,8},{1,0},{9,1},{8,9},{2,10},{3,2},{11,3},{10,11},{4,12},{5,4},{... | collective-permute-start | bytes 786440 | tf_op jit(solution)/shard_map/ppermute | solution.py:549
  21.1 4.7 %collective-permute-start.15 = (bf16[256,256]{1,0:T(8,128)(2,1)S(1)}, bf16[256,256]{1,0:T(8,128)(2,1)S(1)}, u32[]{:S(2)}, u32[]{:S(2)}) collective-permute-start(bf16[256,256]{1,0:T(8,128)(2,1)S(1)} %choose.4), channel_id=1, source_target_pairs={{0,1},{1,0},{2,3},{3,2},{4,5},{5,4},{6,7},{7,6},{8,9},{9,8},{10,11... | collective-permute-start | bytes 393224 | tf_op jit(solution)/shard_map/ppermute | solution.py:38
  21.4 4.3 %collective-permute-start.8 = (bf16[64,256]{1,0:T(8,128)(2,1)S(1)}, bf16[64,256]{1,0:T(8,128)(2,1)S(1)}, u32[]{:S(2)}, u32[]{:S(2)}) collective-permute-start(bf16[64,256]{1,0:T(8,128)(2,1)S(1)} %level_rise.4.mine.after), channel_id=1, source_target_pairs={{0,8},{1,9},{2,10},{3,11},{4,12},{5,13},{6,14},{7,15},{8,0},{9,1},... | collective-permute-start | bytes 98312 | tf_op jit(solution)/shard_map/ppermute | solution.py:38
  26.2 10.9 %collective-permute-start.17 = (bf16[288,256]{1,0:T(8,128)(2,1)S(1)}, bf16[288,256]{1,0:T(8,128)(2,1)S(1)}, u32[]{:S(2)}, u32[]{:S(2)}) collective-permute-start(bf16[288,256]{1,0:T(8,128)(2,1)S(1)} %local.1.l0), channel_id=1, source_target_pairs={{0,2},{1,3},{2,0},{3,1},{4,6},{5,7},{6,4},{7,5},{8,10},{9,11},{10,... | collective-permute-start | bytes 442376 | tf_op jit(solution)/shard_map/ppermute | solution.py:38
  27.9 4.9 %collective-permute-start.10 = (bf16[64,256]{1,0:T(8,128)(2,1)S(1)}, bf16[64,256]{1,0:T(8,128)(2,1)S(1)}, u32[]{:S(2)}, u32[]{:S(2)}) collective-permute-start(bf16[64,256]{1,0:T(8,128)(2,1)S(1)} %level_rise.5.after.refs_0_), channel_id=1, source_target_pairs={{0,16},{1,17},{2,18},{3,19},{4,20},{5,21},{6,22},{7,23},{8,24},{9,... | collective-permute-start | bytes 98312 | tf_op jit(solution)/shard_map/ppermute | solution.py:38
  32.3 6.5 %copy-start = (bf16[256,2048]{1,0:T(8,128)(2,1)S(1)}, bf16[256,2048]{1,0:T(8,128)(2,1)}, u32[]{:S(2)}) copy-start(bf16[256,2048]{1,0:T(8,128)(2,1)} %out_basis.1) | copy-start | bytes 3145732
  33.2 3.8 %collective-permute-start.13 = (bf16[32,256]{1,0:T(8,128)(2,1)S(1)}, bf16[32,256]{1,0:T(8,128)(2,1)S(1)}, u32[]{:S(2)}, u32[]{:S(2)}) collective-permute-start(bf16[32,256]{1,0:T(8,128)(2,1)S(1)} %fall.1.after.mine), channel_id=1, source_target_pairs={{0,4},{1,5},{2,6},{3,7},{4,0},{5,1},{6,2},{7,3},{8,12},{9,13},{10,... | collective-permute-start | bytes 49160 | tf_op jit(solution)/shard_map/ppermute | solution.py:38
  34.4 4.4 %collective-permute-start.16 = (bf16[288,256]{1,0:T(8,128)(2,1)S(1)}, bf16[288,256]{1,0:T(8,128)(2,1)S(1)}, u32[]{:S(2)}, u32[]{:S(2)}) collective-permute-start(bf16[288,256]{1,0:T(8,128)(2,1)S(1)} %local.1.l0), channel_id=1, source_target_pairs={{0,1},{1,0},{2,3},{3,2},{4,5},{5,4},{6,7},{7,6},{8,9},{9,8},{10,11... | collective-permute-start | bytes 442376 | tf_op jit(solution)/shard_map/ppermute | solution.py:38
  37.2 1.7 %collective-permute-start.18 = (bf16[288,256]{1,0:T(8,128)(2,1)S(1)}, bf16[288,256]{1,0:T(8,128)(2,1)S(1)}, u32[]{:S(2)}, u32[]{:S(2)}) collective-permute-start(bf16[288,256]{1,0:T(8,128)(2,1)S(1)} %pass_on.7), channel_id=1, source_target_pairs={{0,1},{1,0},{2,3},{3,2},{4,5},{5,4},{6,7},{7,6},{8,9},{9,8},{10,11... | collective-permute-start | bytes 442376 | tf_op jit(solution)/shard_map/ppermute | solution.py:38
  37.2 3.8 %collective-permute-start.14 = (bf16[32,256]{1,0:T(8,128)(2,1)S(1)}, bf16[32,256]{1,0:T(8,128)(2,1)S(1)}, u32[]{:S(2)}, u32[]{:S(2)}) collective-permute-start(bf16[32,256]{1,0:T(8,128)(2,1)S(1)} %step_down.1.after.lower), channel_id=1, source_target_pairs={{0,2},{1,3},{2,0},{3,1},{4,6},{5,7},{6,4},{7,5},{8,10},{9,11},{10,... | collective-permute-start | bytes 49160 | tf_op jit(solution)/shard_map/ppermute | solution.py:38
  41.0 1.2 %collective-permute-start.19 = (bf16[32,256]{1,0:T(8,128)(2,1)S(1)}, bf16[32,256]{1,0:T(8,128)(2,1)S(1)}, u32[]{:S(2)}, u32[]{:S(2)}) collective-permute-start(bf16[32,256]{1,0:T(8,128)(2,1)S(1)} %choose.5.f_own), channel_id=1, source_target_pairs={{0,1},{1,0},{2,3},{3,2},{4,5},{5,4},{6,7},{7,6},{8,9},{9,8},{10,11... | collective-permute-start | bytes 49160 | tf_op jit(solution)/shard_map/ppermute | solution.py:38

commit v7 on v6

--- a/solution.py
+++ b/solution.py
@@ -587,7 +587,7 @@
     for bit in range(1, levels - 1):
         arrivals.append(swap(pay, 1 << bit))
         after = pay
-        if bit <= cut:
+        if bit in (1, cut + 1):
             after = near_strip(tree, leaf_inverse, len(nears), strips, pay)
             nears.append(after)
         if bit == cut:

time: 44.7 us -> 44.2 us (0.989)
  starting transfers between devices: 18.7 us -> 16.7 us
  waiting for transfers between devices: 9.79 us -> 11.3 us
    ppermute x4, waiting for transfers between devices: 0.01 us -> 1.56 us  [to_left(): return lax.ppermute(block, 'leaf', cycle(bit))]
    ppermute x15, starting transfers between devices: 16.3 us -> 14.8 us  [swap(): return lax.ppermute(block, 'leaf', [(i, i ^ mask) for i in range(count)])]
    ppermute x1, starting transfers between devices: 0.52 us -> 0.07 us  [to_right(): return lax.ppermute(block, 'leaf', [(j, i) for i, j in cycle(bit)])]
  transfers between devices with their start and end apart: 20 -> 20, of which waited for: 9 -> 10; matrix products, arithmetic and copies ran while one was open for 0% -> 0% of each run, Pallas kernels for 26% -> 26%
where the time goes in v7:
time: 44.2 us; the launch traced here: 43.9 us
  starting transfers between devices  16.7 us (38%)
  Pallas kernels  15.7 us (36%)
  waiting for transfers between devices  11.3 us (26%)
    ppermute x15, starting transfers between devices, swap(): return lax.ppermute(block, 'leaf', [(i, i ^ mask) for i in range(count)])  14.8 us
    ppermute x15, waiting for transfers between devices, swap(): return lax.ppermute(block, 'leaf', [(i, i ^ mask) for i in range(count)])  9.73 us
    pallas_call x4, Pallas kernels, near_strip(): pl.pallas_call(functools.partial(near_kernel, strip * width), out_shape=j...  8.08 us
    pallas_call x1, Pallas kernels, final(): pl.pallas_call(final_kernel, out_shape=jax.ShapeDtypeStruct((rows, column...  2.16 us
    pallas_call x1, Pallas kernels, start(): pl.pallas_call(start_kernel, out_shape=(jax.ShapeDtypeStruct((2 * SPREAD,...  2.03 us
    ppermute x4, starting transfers between devices, to_left(): return lax.ppermute(block, 'leaf', cycle(bit))  1.83 us
    ppermute x4, waiting for transfers between devices, to_left(): return lax.ppermute(block, 'leaf', cycle(bit))  1.56 us
    pallas_call x1, Pallas kernels, invert(): pl.pallas_call(invert_kernel, out_shape=jax.ShapeDtypeStruct((columns //...  1 us
  transfers between devices with their start and end apart: 20, of which 10 were waited for; matrix products, arithmetic and copies ran while one was open for 0% of the time, Pallas kernels for 26%

profile of v7, /device:TPU:0, one launch (start us, length us, event | category | flops | bytes accessed | tf_op | source)
XLA Modules:
  0.0 43.9 jit_solution(15707418163419137820)
XLA Ops:
  0.0 2.0 %start.1 = (s32[8,128]{1,0:T(8,128)S(1)}, bf16[32,2048]{1,0:T(8,128)(2,1)S(1)}, bf16[32,256]{1,0:T(8,128)(2,1)S(1)}, bf16[768,256]{1,0:T(8,128)(2,1)S(1)}, bf16[...) custom-call(bf16[32,2048]{1,0:T(8,128)(2,1)} %rhs_hbm.1, ...), custom_call_target="tpu_custom_call" | custom-call | bytes 8100000 | tf_op jit(solution)/shard_map/start/pallas_call | solution.py:142
  2.0 0.5 %collective-permute-start = (bf16[32,256]{1,0:T(8,128)(2,1)S(1)}, bf16[32,256]{1,0:T(8,128)(2,1)S(1)}, u32[]{:S(2)}, u32[]{:S(2)}) collective-permute-start(bf16[32,256]{1,0:T(8,128)(2,1)S(1)} %get-tuple-element.19.mine.after), channel_id=1, source_target_pairs={{0,1},{1,0},{2,3},{3,2},{4,5},{5,4},{6,7},{7,6},{8,9},{9,8},{10,11... | collective-permute-start | bytes 49160 | tf_op jit(solution)/shard_map/ppermute | solution.py:38
  2.6 0.8 %collective-permute-done.other = bf16[32,256]{1,0:T(8,128)(2,1)S(1)} collective-permute-done((bf16[32,256]{1,0:T(8,128)(2,1)S(1)}, bf16[32,256]{1,0:T(8,128)(2,1)S(1)}, u32[]{:S(2)}, u32[]{:S(2)}) %collective-permute-start) | collective-permute-done | bytes 16416 | tf_op jit(solution)/shard_map/ppermute | solution.py:38
  3.4 0.4 collective-permute-start.3
  3.8 2.7 %collective-permute-start.1 = (bf16[64,256]{1,0:T(8,128)(2,1)S(1)}, bf16[64,256]{1,0:T(8,128)(2,1)S(1)}, u32[]{:S(2)}, u32[]{:S(2)}) collective-permute-start(bf16[64,256]{1,0:T(8,128)(2,1)S(1)} %join.1.after.pair_own), channel_id=1, source_target_pairs={{0,2},{1,3},{2,0},{3,1},{4,6},{5,7},{6,4},{7,5},{8,10},{9,11},{10,... | collective-permute-start | bytes 98312 | tf_op jit(solution)/shard_map/ppermute | solution.py:38
  6.6 1.8 %collective-permute-done.1.pair_x = bf16[64,256]{1,0:T(8,128)(2,1)S(1)} collective-permute-done((bf16[64,256]{1,0:T(8,128)(2,1)S(1)}, bf16[64,256]{1,0:T(8,128)(2,1)S(1)}, u32[]{:S(2)}, u32[]{:S(2)}) %collective-permute-start.1) | collective-permute-done | bytes 32800 | tf_op jit(solution)/shard_map/ppermute | solution.py:38
  8.6 0.9 %collective-permute-start.2 = (f32[32,256]{1,0:T(8,128)S(1)}, f32[32,256]{1,0:T(8,128)S(1)}, u32[]{:S(2)}, u32[]{:S(2)}) collective-permute-start(f32[32,256]{1,0:T(8,128)S(1)} %get-tuple-element.22.after.mine), channel_id=1, source_target_pairs={{0,1},{1,0},{2,3},{3,2},{4,5},{5,4},{6,7},{7,6},{8,9},{9,8},{10,11... | collective-permute-start | bytes 98312 | tf_op jit(solution)/shard_map/ppermute | solution.py:38
  9.7 0.8 %collective-permute-done.2.other = f32[32,256]{1,0:T(8,128)S(1)} collective-permute-done((f32[32,256]{1,0:T(8,128)S(1)}, f32[32,256]{1,0:T(8,128)S(1)}, u32[]{:S(2)}, u32[]{:S(2)}) %collective-permute-start.2) | collective-permute-done | bytes 32800 | tf_op jit(solution)/shard_map/ppermute | solution.py:38
  10.4 1.7 %collective-permute-start.9 = (bf16[768,256]{1,0:T(8,128)(2,1)S(1)}, bf16[768,256]{1,0:T(8,128)(2,1)S(1)}, u32[]{:S(2)}, u32[]{:S(2)}) collective-permute-start(bf16[768,256]{1,0:T(8,128)(2,1)S(1)} %pass_on.5.after), channel_id=1, source_target_pairs={{8,0},{0,1},{1,9},{9,8},{10,2},{2,3},{3,11},{11,10},{12,4},{4,5},{... | collective-permute-start | bytes 1179656 | tf_op jit(solution)/shard_map/ppermute | solution.py:544
  12.3 1.8 %collective-permute-start.4 = (bf16[64,256]{1,0:T(8,128)(2,1)S(1)}, bf16[64,256]{1,0:T(8,128)(2,1)S(1)}, u32[]{:S(2)}, u32[]{:S(2)}) collective-permute-start(bf16[64,256]{1,0:T(8,128)(2,1)S(1)} %node_rise.1.after.mine), channel_id=1, source_target_pairs={{0,2},{1,3},{2,0},{3,1},{4,6},{5,7},{6,4},{7,5},{8,10},{9,11},{10,... | collective-permute-start | bytes 98312 | tf_op jit(solution)/shard_map/ppermute | solution.py:38
  14.1 2.0 %near.4.after.refs_0_ = f32[32,512]{1,0:T(8,128)S(1)} custom-call(bf16[32,2048]{1,0:T(8,128)(2,1)S(1)} %get-tuple-element.24.tree_ref, bf16[2048,2048]{1,0:T(8,128)(2,1)} %inverse_hbm.7, bf16[64,256]{1,0:T(8,128)(2,1)S(1)} %node_rise.1.after.mine), custom_call_target="tpu_custom_call" | custom-call | bytes 4200000 | tf_op jit(solution)/shard_map/near/pallas_call | solution.py:228
  16.3 2.0 %collective-permute-start.6 = (bf16[64,256]{1,0:T(8,128)(2,1)S(1)}, bf16[64,256]{1,0:T(8,128)(2,1)S(1)}, u32[]{:S(2)}, u32[]{:S(2)}) collective-permute-start(bf16[64,256]{1,0:T(8,128)(2,1)S(1)} %level_rise.3.mine.after), channel_id=1, source_target_pairs={{0,4},{1,5},{2,6},{3,7},{4,0},{5,1},{6,2},{7,3},{8,12},{9,13},{10,... | collective-permute-start | bytes 98312 | tf_op jit(solution)/shard_map/ppermute | solution.py:38
  18.3 1.5 %collective-permute-done.11.lower = bf16[512,256]{1,0:T(8,128)(2,1)S(1)} collective-permute-done((bf16[512,256]{1,0:T(8,128)(2,1)S(1)}, bf16[512,256]{1,0:T(8,128)(2,1)S(1)}, u32[]{:S(2)}, u32[]{:S(2)}) %collective-permute-start.11) | collective-permute-done | bytes 262176 | tf_op jit(solution)/shard_map/ppermute | solution.py:544
  20.0 0.4 %collective-permute-done.6.other.sibling = bf16[64,256]{1,0:T(8,128)(2,1)S(1)} collective-permute-done((bf16[64,256]{1,0:T(8,128)(2,1)S(1)}, bf16[64,256]{1,0:T(8,128)(2,1)S(1)}, u32[]{:S(2)}, u32[]{:S(2)}) %collective-permute-start.6) | collective-permute-done | bytes 32800 | tf_op jit(solution)/shard_map/ppermute | solution.py:38
  20.6 0.4 collective-permute-start.15
  21.0 0.3 collective-permute-start.8
  21.3 2.0 %near.5.after.refs_1_ = f32[32,512]{1,0:T(8,128)S(1)} custom-call(bf16[32,2048]{1,0:T(8,128)(2,1)S(1)} %get-tuple-element.24.tree_ref, bf16[2048,2048]{1,0:T(8,128)(2,1)} %inverse_hbm.7, bf16[64,256]{1,0:T(8,128)(2,1)S(1)} %level_rise.4.after.mine), custom_call_target="tpu_custom_call" | custom-call | bytes 4200000 | tf_op jit(solution)/shard_map/near/pallas_call | solution.py:228
  23.4 1.8 %collective-permute-done.8.other.refs_2_ = bf16[64,256]{1,0:T(8,128)(2,1)S(1)} collective-permute-done((bf16[64,256]{1,0:T(8,128)(2,1)S(1)}, bf16[64,256]{1,0:T(8,128)(2,1)S(1)}, u32[]{:S(2)}, u32[]{:S(2)}) %collective-permute-start.8) | collective-permute-done | bytes 32800 | tf_op jit(solution)/shard_map/ppermute | solution.py:38
  25.7 1.3 %collective-permute-start.17 = (bf16[288,256]{1,0:T(8,128)(2,1)S(1)}, bf16[288,256]{1,0:T(8,128)(2,1)S(1)}, u32[]{:S(2)}, u32[]{:S(2)}) collective-permute-start(bf16[288,256]{1,0:T(8,128)(2,1)S(1)} %local.1.l0), channel_id=1, source_target_pairs={{0,2},{1,3},{2,0},{3,1},{4,6},{5,7},{6,4},{7,5},{8,10},{9,11},{10,... | collective-permute-start | bytes 442376 | tf_op jit(solution)/shard_map/ppermute | solution.py:38
  27.0 1.6 %collective-permute-start.10 = (bf16[64,256]{1,0:T(8,128)(2,1)S(1)}, bf16[64,256]{1,0:T(8,128)(2,1)S(1)}, u32[]{:S(2)}, u32[]{:S(2)}) collective-permute-start(bf16[64,256]{1,0:T(8,128)(2,1)S(1)} %level_rise.5.after.refs_0_), channel_id=1, source_target_pairs={{0,16},{1,17},{2,18},{3,19},{4,20},{5,21},{6,22},{7,23},{8,24},{9,... | collective-permute-start | bytes 98312 | tf_op jit(solution)/shard_map/ppermute | solution.py:38
  28.6 2.0 %near.6.refs_9_.refs_2_ = f32[32,512]{1,0:T(8,128)S(1)} custom-call(bf16[32,2048]{1,0:T(8,128)(2,1)S(1)} %get-tuple-element.24.tree_ref, bf16[2048,2048]{1,0:T(8,128)(2,1)} %inverse_hbm.7, bf16[64,256]{1,0:T(8,128)(2,1)S(1)} %level_rise.5.after.refs_0_), custom_call_target="tpu_custom_call" | custom-call | bytes 4200000 | tf_op jit(solution)/shard_map/near/pallas_call | solution.py:228
  30.6 1.2 %collective-permute-done.10.refs_1_ = bf16[64,256]{1,0:T(8,128)(2,1)S(1)} collective-permute-done((bf16[64,256]{1,0:T(8,128)(2,1)S(1)}, bf16[64,256]{1,0:T(8,128)(2,1)S(1)}, u32[]{:S(2)}, u32[]{:S(2)}) %collective-permute-start.10) | collective-permute-done | bytes 32800 | tf_op jit(solution)/shard_map/ppermute | solution.py:38
  31.8 0.4 %fall.1.after.mine = bf16[32,256]{1,0:T(8,128)(2,1)S(1)} custom-call(bf16[64,256]{1,0:T(8,128)(2,1)S(1)} %level_rise.5.after.refs_0_, bf16[64,256]{1,0:T(8,128)(2,1)S(1)} %collective-permute-done.10.refs_1_, bf16[64,256]{1,0:T(8,128)(2,1)S(1)} %collective-permute-done.8.other.refs_2_, ...), custom_call_target="tpu_custom_call" | custom-call | bytes 1350000 | tf_op jit(solution)/shard_map/fall/pallas_call | solution.py:354
  32.3 1.8 %collective-permute-start.13 = (bf16[32,256]{1,0:T(8,128)(2,1)S(1)}, bf16[32,256]{1,0:T(8,128)(2,1)S(1)}, u32[]{:S(2)}, u32[]{:S(2)}) collective-permute-start(bf16[32,256]{1,0:T(8,128)(2,1)S(1)} %fall.1.after.mine), channel_id=1, source_target_pairs={{0,4},{1,5},{2,6},{3,7},{4,0},{5,1},{6,2},{7,3},{8,12},{9,13},{10,... | collective-permute-start | bytes 49160 | tf_op jit(solution)/shard_map/ppermute | solution.py:38
  34.0 2.0 %near.7.after.refs_3_ = f32[32,512]{1,0:T(8,128)S(1)} custom-call(bf16[32,2048]{1,0:T(8,128)(2,1)S(1)} %get-tuple-element.24.tree_ref, bf16[2048,2048]{1,0:T(8,128)(2,1)} %inverse_hbm.7, bf16[32,256]{1,0:T(8,128)(2,1)S(1)} %fall.1.after.mine), custom_call_target="tpu_custom_call" | custom-call | bytes 4200000 | tf_op jit(solution)/shard_map/near/pallas_call | solution.py:228
  36.3 0.6 %collective-permute-start.18 = (bf16[288,256]{1,0:T(8,128)(2,1)S(1)}, bf16[288,256]{1,0:T(8,128)(2,1)S(1)}, u32[]{:S(2)}, u32[]{:S(2)}) collective-permute-start(bf16[288,256]{1,0:T(8,128)(2,1)S(1)} %pass_on.7), channel_id=1, source_target_pairs={{0,1},{1,0},{2,3},{3,2},{4,5},{5,4},{6,7},{7,6},{8,9},{9,8},{10,11... | collective-permute-start | bytes 442376 | tf_op jit(solution)/shard_map/ppermute | solution.py:38
  36.8 0.5 %collective-permute-start.14 = (bf16[32,256]{1,0:T(8,128)(2,1)S(1)}, bf16[32,256]{1,0:T(8,128)(2,1)S(1)}, u32[]{:S(2)}, u32[]{:S(2)}) collective-permute-start(bf16[32,256]{1,0:T(8,128)(2,1)S(1)} %step_down.1.after.lower), channel_id=1, source_target_pairs={{0,2},{1,3},{2,0},{3,1},{4,6},{5,7},{6,4},{7,5},{8,10},{9,11},{10,... | collective-permute-start | bytes 49160 | tf_op jit(solution)/shard_map/ppermute | solution.py:38
  37.4 1.0 %invert.1.after.inv_ref = s32[16,128]{1,0:T(8,128)S(1)} custom-call(s32[1,2048]{1,0:T(1,128)} %order_hbm.3, bf16[32,256]{1,0:T(8,128)(2,1)S(1)} %step_down.1.after.lower), custom_call_target="tpu_custom_call" | custom-call | bytes 3000000 | tf_op jit(solution)/shard_map/invert/pallas_call | solution.py:196
  38.4 0.6 %fold.1 = (bf16[256,2048]{1,0:T(8,128)(2,1)S(1)}, f32[32,2048]{1,0:T(8,128)S(1)}) custom-call(s32[8,128]{1,0:T(8,128)S(1)} %get-tuple-element.18.pick, bf16[288,256]{1,0:T(8,128)(2,1)S(1)} %local.1.l0, bf16[288,256]{1,0:T(8,128)(2,1)S(1)} %collective-permute-done.16.l1, bf16[288,256]{1,0:T(8,128)(2,1)S(1)} %collective-permute-done.17.block.l2, ...), custom_call_target="tpu_custom_call" | custom-call | bytes 3000000 | tf_op jit(solution)/shard_map/fold/pallas_call | solution.py:460
  39.0 1.5 %collective-permute-done.14.upper = bf16[32,256]{1,0:T(8,128)(2,1)S(1)} collective-permute-done((bf16[32,256]{1,0:T(8,128)(2,1)S(1)}, bf16[32,256]{1,0:T(8,128)(2,1)S(1)}, u32[]{:S(2)}, u32[]{:S(2)}) %collective-permute-start.14) | collective-permute-done | bytes 16416 | tf_op jit(solution)/shard_map/ppermute | solution.py:38
  40.6 1.2 %collective-permute-done.19.f_core = bf16[32,256]{1,0:T(8,128)(2,1)S(1)} collective-permute-done((bf16[32,256]{1,0:T(8,128)(2,1)S(1)}, bf16[32,256]{1,0:T(8,128)(2,1)S(1)}, u32[]{:S(2)}, u32[]{:S(2)}) %collective-permute-start.19) | collective-permute-done | bytes 16416 | tf_op jit(solution)/shard_map/ppermute | solution.py:38
  41.8 2.2 %final.1 = f32[32,2048]{1,0:T(8,128)} custom-call(bf16[32,256]{1,0:T(8,128)(2,1)S(1)} %choose.5.f_own, bf16[32,256]{1,0:T(8,128)(2,1)S(1)} %collective-permute-done.19.f_core, bf16[256,2048]{1,0:T(8,128)(2,1)S(1)} %get-tuple-element.30.map_ref, f32[32,2048]{1,0:T(8,128)S(1)} %get-tuple-element.29.after.base_ref, s32[16,128]{1,0:T(8,128)S(1)} %invert.1.after.inv_ref), custom_call_target="tpu_custom_call" | custom-call | bytes 5400000 | tf_op jit(solution)/shard_map/final/pallas_call | solution.py:497
  (36 shorter events, 1.7 us)
Async XLA Ops:
  2.0 1.4 %collective-permute-start = (bf16[32,256]{1,0:T(8,128)(2,1)S(1)}, bf16[32,256]{1,0:T(8,128)(2,1)S(1)}, u32[]{:S(2)}, u32[]{:S(2)}) collective-permute-start(bf16[32,256]{1,0:T(8,128)(2,1)S(1)} %get-tuple-element.19.mine.after), channel_id=1, source_target_pairs={{0,1},{1,0},{2,3},{3,2},{4,5},{5,4},{6,7},{7,6},{8,9},{9,8},{10,11... | collective-permute-start | bytes 49160 | tf_op jit(solution)/shard_map/ppermute | solution.py:38
  3.4 8.7 %collective-permute-start.3 = (bf16[768,256]{1,0:T(8,128)(2,1)S(1)}, bf16[768,256]{1,0:T(8,128)(2,1)S(1)}, u32[]{:S(2)}, u32[]{:S(2)}) collective-permute-start(bf16[768,256]{1,0:T(8,128)(2,1)S(1)} %pass_on.4.after), channel_id=1, source_target_pairs={{0,1},{1,0},{2,3},{3,2},{4,5},{5,4},{6,7},{7,6},{8,9},{9,8},{10,11... | collective-permute-start | bytes 1179656 | tf_op jit(solution)/shard_map/ppermute | solution.py:38
  3.8 4.5 %collective-permute-start.1 = (bf16[64,256]{1,0:T(8,128)(2,1)S(1)}, bf16[64,256]{1,0:T(8,128)(2,1)S(1)}, u32[]{:S(2)}, u32[]{:S(2)}) collective-permute-start(bf16[64,256]{1,0:T(8,128)(2,1)S(1)} %join.1.after.pair_own), channel_id=1, source_target_pairs={{0,2},{1,3},{2,0},{3,1},{4,6},{5,7},{6,4},{7,5},{8,10},{9,11},{10,... | collective-permute-start | bytes 98312 | tf_op jit(solution)/shard_map/ppermute | solution.py:38
  6.5 9.6 %collective-permute-start.5 = (bf16[768,256]{1,0:T(8,128)(2,1)S(1)}, bf16[768,256]{1,0:T(8,128)(2,1)S(1)}, u32[]{:S(2)}, u32[]{:S(2)}) collective-permute-start(bf16[768,256]{1,0:T(8,128)(2,1)S(1)} %pass_on.4.after), channel_id=1, source_target_pairs={{2,0},{0,1},{1,3},{3,2},{6,4},{4,5},{5,7},{7,6},{10,8},{8,9},{9,11... | collective-permute-start | bytes 1179656 | tf_op jit(solution)/shard_map/ppermute | solution.py:544
  8.6 11.4 %collective-permute-start.7 = (bf16[768,256]{1,0:T(8,128)(2,1)S(1)}, bf16[768,256]{1,0:T(8,128)(2,1)S(1)}, u32[]{:S(2)}, u32[]{:S(2)}) collective-permute-start(bf16[768,256]{1,0:T(8,128)(2,1)S(1)} %pass_on.5.after), channel_id=1, source_target_pairs={{4,0},{0,1},{1,5},{5,4},{6,2},{2,3},{3,7},{7,6},{12,8},{8,9},{9,13... | collective-permute-start | bytes 1179656 | tf_op jit(solution)/shard_map/ppermute | solution.py:544
  8.6 1.8 %collective-permute-start.2 = (f32[32,256]{1,0:T(8,128)S(1)}, f32[32,256]{1,0:T(8,128)S(1)}, u32[]{:S(2)}, u32[]{:S(2)}) collective-permute-start(f32[32,256]{1,0:T(8,128)S(1)} %get-tuple-element.22.after.mine), channel_id=1, source_target_pairs={{0,1},{1,0},{2,3},{3,2},{4,5},{5,4},{6,7},{7,6},{8,9},{9,8},{10,11... | collective-permute-start | bytes 98312 | tf_op jit(solution)/shard_map/ppermute | solution.py:38
  9.6 10.3 %collective-permute-start.11 = (bf16[512,256]{1,0:T(8,128)(2,1)S(1)}, bf16[512,256]{1,0:T(8,128)(2,1)S(1)}, u32[]{:S(2)}, u32[]{:S(2)}) collective-permute-start(bf16[512,256]{1,0:T(8,128)(2,1)S(1)} %pass_on.6), channel_id=1, source_target_pairs={{16,0},{0,1},{1,17},{17,16},{18,2},{2,3},{3,19},{19,18},{20,4},{4,... | collective-permute-start | bytes 786440 | tf_op jit(solution)/shard_map/ppermute | solution.py:544
  10.4 12.9 %collective-permute-start.9 = (bf16[768,256]{1,0:T(8,128)(2,1)S(1)}, bf16[768,256]{1,0:T(8,128)(2,1)S(1)}, u32[]{:S(2)}, u32[]{:S(2)}) collective-permute-start(bf16[768,256]{1,0:T(8,128)(2,1)S(1)} %pass_on.5.after), channel_id=1, source_target_pairs={{8,0},{0,1},{1,9},{9,8},{10,2},{2,3},{3,11},{11,10},{12,4},{4,5},{... | collective-permute-start | bytes 1179656 | tf_op jit(solution)/shard_map/ppermute | solution.py:544
  12.3 3.9 %collective-permute-start.4 = (bf16[64,256]{1,0:T(8,128)(2,1)S(1)}, bf16[64,256]{1,0:T(8,128)(2,1)S(1)}, u32[]{:S(2)}, u32[]{:S(2)}) collective-permute-start(bf16[64,256]{1,0:T(8,128)(2,1)S(1)} %node_rise.1.after.mine), channel_id=1, source_target_pairs={{0,2},{1,3},{2,0},{3,1},{4,6},{5,7},{6,4},{7,5},{8,10},{9,11},{10,... | collective-permute-start | bytes 98312 | tf_op jit(solution)/shard_map/ppermute | solution.py:38
  16.3 4.1 %collective-permute-start.6 = (bf16[64,256]{1,0:T(8,128)(2,1)S(1)}, bf16[64,256]{1,0:T(8,128)(2,1)S(1)}, u32[]{:S(2)}, u32[]{:S(2)}) collective-permute-start(bf16[64,256]{1,0:T(8,128)(2,1)S(1)} %level_rise.3.mine.after), channel_id=1, source_target_pairs={{0,4},{1,5},{2,6},{3,7},{4,0},{5,1},{6,2},{7,3},{8,12},{9,13},{10,... | collective-permute-start | bytes 98312 | tf_op jit(solution)/shard_map/ppermute | solution.py:38
  19.9 11.9 %collective-permute-start.12 = (bf16[512,256]{1,0:T(8,128)(2,1)S(1)}, bf16[512,256]{1,0:T(8,128)(2,1)S(1)}, u32[]{:S(2)}, u32[]{:S(2)}) collective-permute-start(bf16[512,256]{1,0:T(8,128)(2,1)S(1)} %choose.3.refs_8_), channel_id=1, source_target_pairs={{0,8},{1,0},{9,1},{8,9},{2,10},{3,2},{11,3},{10,11},{4,12},{5,4},{... | collective-permute-start | bytes 786440 | tf_op jit(solution)/shard_map/ppermute | solution.py:549
  20.6 4.7 %collective-permute-start.15 = (bf16[256,256]{1,0:T(8,128)(2,1)S(1)}, bf16[256,256]{1,0:T(8,128)(2,1)S(1)}, u32[]{:S(2)}, u32[]{:S(2)}) collective-permute-start(bf16[256,256]{1,0:T(8,128)(2,1)S(1)} %choose.4), channel_id=1, source_target_pairs={{0,1},{1,0},{2,3},{3,2},{4,5},{5,4},{6,7},{7,6},{8,9},{9,8},{10,11... | collective-permute-start | bytes 393224 | tf_op jit(solution)/shard_map/ppermute | solution.py:38
  21.0 4.2 %collective-permute-start.8 = (bf16[64,256]{1,0:T(8,128)(2,1)S(1)}, bf16[64,256]{1,0:T(8,128)(2,1)S(1)}, u32[]{:S(2)}, u32[]{:S(2)}) collective-permute-start(bf16[64,256]{1,0:T(8,128)(2,1)S(1)} %level_rise.4.after.mine), channel_id=1, source_target_pairs={{0,8},{1,9},{2,10},{3,11},{4,12},{5,13},{6,14},{7,15},{8,0},{9,1},... | collective-permute-start | bytes 98312 | tf_op jit(solution)/shard_map/ppermute | solution.py:38
  25.7 10.6 %collective-permute-start.17 = (bf16[288,256]{1,0:T(8,128)(2,1)S(1)}, bf16[288,256]{1,0:T(8,128)(2,1)S(1)}, u32[]{:S(2)}, u32[]{:S(2)}) collective-permute-start(bf16[288,256]{1,0:T(8,128)(2,1)S(1)} %local.1.l0), channel_id=1, source_target_pairs={{0,2},{1,3},{2,0},{3,1},{4,6},{5,7},{6,4},{7,5},{8,10},{9,11},{10,... | collective-permute-start | bytes 442376 | tf_op jit(solution)/shard_map/ppermute | solution.py:38
  27.0 4.8 %collective-permute-start.10 = (bf16[64,256]{1,0:T(8,128)(2,1)S(1)}, bf16[64,256]{1,0:T(8,128)(2,1)S(1)}, u32[]{:S(2)}, u32[]{:S(2)}) collective-permute-start(bf16[64,256]{1,0:T(8,128)(2,1)S(1)} %level_rise.5.after.refs_0_), channel_id=1, source_target_pairs={{0,16},{1,17},{2,18},{3,19},{4,20},{5,21},{6,22},{7,23},{8,24},{9,... | collective-permute-start | bytes 98312 | tf_op jit(solution)/shard_map/ppermute | solution.py:38
  30.6 7.8 %copy-start = (bf16[256,2048]{1,0:T(8,128)(2,1)S(1)}, bf16[256,2048]{1,0:T(8,128)(2,1)}, u32[]{:S(2)}) copy-start(bf16[256,2048]{1,0:T(8,128)(2,1)} %out_basis.1) | copy-start | bytes 3145732
  32.3 3.8 %collective-permute-start.13 = (bf16[32,256]{1,0:T(8,128)(2,1)S(1)}, bf16[32,256]{1,0:T(8,128)(2,1)S(1)}, u32[]{:S(2)}, u32[]{:S(2)}) collective-permute-start(bf16[32,256]{1,0:T(8,128)(2,1)S(1)} %fall.1.after.mine), channel_id=1, source_target_pairs={{0,4},{1,5},{2,6},{3,7},{4,0},{5,1},{6,2},{7,3},{8,12},{9,13},{10,... | collective-permute-start | bytes 49160 | tf_op jit(solution)/shard_map/ppermute | solution.py:38
  34.0 4.4 %collective-permute-start.16 = (bf16[288,256]{1,0:T(8,128)(2,1)S(1)}, bf16[288,256]{1,0:T(8,128)(2,1)S(1)}, u32[]{:S(2)}, u32[]{:S(2)}) collective-permute-start(bf16[288,256]{1,0:T(8,128)(2,1)S(1)} %local.1.l0), channel_id=1, source_target_pairs={{0,1},{1,0},{2,3},{3,2},{4,5},{5,4},{6,7},{7,6},{8,9},{9,8},{10,11... | collective-permute-start | bytes 442376 | tf_op jit(solution)/shard_map/ppermute | solution.py:38
  36.3 2.1 %collective-permute-start.18 = (bf16[288,256]{1,0:T(8,128)(2,1)S(1)}, bf16[288,256]{1,0:T(8,128)(2,1)S(1)}, u32[]{:S(2)}, u32[]{:S(2)}) collective-permute-start(bf16[288,256]{1,0:T(8,128)(2,1)S(1)} %pass_on.7), channel_id=1, source_target_pairs={{0,1},{1,0},{2,3},{3,2},{4,5},{5,4},{6,7},{7,6},{8,9},{9,8},{10,11... | collective-permute-start | bytes 442376 | tf_op jit(solution)/shard_map/ppermute | solution.py:38
  36.8 3.7 %collective-permute-start.14 = (bf16[32,256]{1,0:T(8,128)(2,1)S(1)}, bf16[32,256]{1,0:T(8,128)(2,1)S(1)}, u32[]{:S(2)}, u32[]{:S(2)}) collective-permute-start(bf16[32,256]{1,0:T(8,128)(2,1)S(1)} %step_down.1.after.lower), channel_id=1, source_target_pairs={{0,2},{1,3},{2,0},{3,1},{4,6},{5,7},{6,4},{7,5},{8,10},{9,11},{10,... | collective-permute-start | bytes 49160 | tf_op jit(solution)/shard_map/ppermute | solution.py:38
  40.6 1.2 %collective-permute-start.19 = (bf16[32,256]{1,0:T(8,128)(2,1)S(1)}, bf16[32,256]{1,0:T(8,128)(2,1)S(1)}, u32[]{:S(2)}, u32[]{:S(2)}) collective-permute-start(bf16[32,256]{1,0:T(8,128)(2,1)S(1)} %choose.5.f_own), channel_id=1, source_target_pairs={{0,1},{1,0},{2,3},{3,2},{4,5},{5,4},{6,7},{7,6},{8,9},{9,8},{10,11... | collective-permute-start | bytes 49160 | tf_op jit(solution)/shard_map/ppermute | solution.py:38

commit v8 on v7

--- a/solution.py
+++ b/solution.py
@@ -471,8 +471,11 @@
     )(pick, *locals_, basis_out, after, *nears)
 
 
-def final_kernel(f_own, f_core, map_ref, base_ref, inv_ref, answer_hbm, total, answer, sems):
-    f2 = jnp.where(bit_of_device(0), f_core[...], f_own[...])
+def final_kernel(f_own, f_core, f_x, f_both, map_ref, base_ref, inv_ref, answer_hbm, total, answer, sems):
+    odd = bit_of_device(0)
+    left = jnp.where(odd, f_core[...], f_own[...])
+    right = jnp.where(odd, f_both[...], f_x[...])
+    f2 = jnp.where(bit_of_device(1), right, left)
     total[...] = base_ref[...] + mm(f2, map_ref[...])
     copies = []
 
@@ -492,12 +495,12 @@
         copy.wait()
 
 
-def final(f2, f2_core, leaf_map, base, inverse_order):
+def final(values, leaf_map, base, inverse_order):
     rows, columns = base.shape
     return pl.pallas_call(
         final_kernel,
         out_shape=jax.ShapeDtypeStruct((rows, columns), F32),
-        in_specs=[VMEM] * 5,
+        in_specs=[VMEM] * 7,
         out_specs=ANY,
         scratch_shapes=[
             pltpu.VMEM((rows, columns), F32),
@@ -507,7 +510,7 @@
         compiler_params=params(),
         cost_estimate=took(1.8),
         name="final",
-    )(f2, f2_core, leaf_map, base, inverse_order)
+    )(*values, leaf_map, base, inverse_order)
 
 
 def body(
@@ -614,8 +617,8 @@
     inverse_order = invert(point_order, block_f)
     locals_ = [own_local, swap(own_local, 1), local_x, swap(pass_on(local_x, block_f), 1)]
     composed, base = fold(pick, locals_, basis_out, nears, inverse_order)
-    block_f = choose(1, swap(block_f, 2), block_f, base)
-    return final(block_f, swap(block_f, 1), composed, base, inverse_order)
+    values = [block_f] + [swap(block_f, m) for m in range(1, SPREAD)]
+    return final(values, composed, base, inverse_order)
 
 
 def solution(mesh):

time: 44.2 us -> 43.3 us (0.980)
  waiting for transfers between devices: 11.3 us -> 9.07 us
  starting transfers between devices: 16.7 us -> 18 us
    ppermute x15 -> x16, waiting for transfers between devices: 9.73 us -> 7.51 us  [swap(): return lax.ppermute(block, 'leaf', [(i, i ^ mask) for i in range(count)])]
    ppermute x15 -> x16, starting transfers between devices: 14.8 us -> 16.1 us  [swap(): return lax.ppermute(block, 'leaf', [(i, i ^ mask) for i in range(count)])]
  transfers between devices with their start and end apart: 20 -> 21, of which waited for: 10 -> 10; matrix products, arithmetic and copies ran while one was open for 0% -> 0% of each run, Pallas kernels for 26% -> 27%
where the time goes in v8:
time: 43.3 us; the launch traced here: 43 us
  starting transfers between devices  18 us (42%)
  Pallas kernels  15.7 us (36%)
  waiting for transfers between devices  9.07 us (21%)
    ppermute x16, starting transfers between devices, swap(): return lax.ppermute(block, 'leaf', [(i, i ^ mask) for i in range(count)])  16.1 us
    pallas_call x4, Pallas kernels, near_strip(): pl.pallas_call(functools.partial(near_kernel, strip * width), out_shape=j...  8.08 us
    ppermute x16, waiting for transfers between devices, swap(): return lax.ppermute(block, 'leaf', [(i, i ^ mask) for i in range(count)])  7.51 us
    pallas_call x1, Pallas kernels, final(): pl.pallas_call(final_kernel, out_shape=jax.ShapeDtypeStruct((rows, column...  2.16 us
    pallas_call x1, Pallas kernels, start(): pl.pallas_call(start_kernel, out_shape=(jax.ShapeDtypeStruct((2 * SPREAD,...  2.03 us
    ppermute x4, starting transfers between devices, to_left(): return lax.ppermute(block, 'leaf', cycle(bit))  1.83 us
    ppermute x4, waiting for transfers between devices, to_left(): return lax.ppermute(block, 'leaf', cycle(bit))  1.56 us
    pallas_call x1, Pallas kernels, invert(): pl.pallas_call(invert_kernel, out_shape=jax.ShapeDtypeStruct((columns //...  1 us
  transfers between devices with their start and end apart: 21, of which 10 were waited for; matrix products, arithmetic and copies ran while one was open for 0% of the time, Pallas kernels for 27%

profile of v8, /device:TPU:0, one launch (start us, length us, event | category | flops | bytes accessed | tf_op | source)
XLA Modules:
  0.0 43.0 jit_solution(1091096547839999290)
XLA Ops:
  0.0 2.0 %start.1 = (s32[8,128]{1,0:T(8,128)S(1)}, bf16[32,2048]{1,0:T(8,128)(2,1)S(1)}, bf16[32,256]{1,0:T(8,128)(2,1)S(1)}, bf16[768,256]{1,0:T(8,128)(2,1)S(1)}, bf16[...) custom-call(bf16[32,2048]{1,0:T(8,128)(2,1)} %rhs_hbm.1, ...), custom_call_target="tpu_custom_call" | custom-call | bytes 8100000 | tf_op jit(solution)/shard_map/start/pallas_call | solution.py:142
  2.0 0.5 %collective-permute-start = (bf16[32,256]{1,0:T(8,128)(2,1)S(1)}, bf16[32,256]{1,0:T(8,128)(2,1)S(1)}, u32[]{:S(2)}, u32[]{:S(2)}) collective-permute-start(bf16[32,256]{1,0:T(8,128)(2,1)S(1)} %get-tuple-element.19.mine.after), channel_id=1, source_target_pairs={{0,1},{1,0},{2,3},{3,2},{4,5},{5,4},{6,7},{7,6},{8,9},{9,8},{10,11... | collective-permute-start | bytes 49160 | tf_op jit(solution)/shard_map/ppermute | solution.py:38
  2.6 0.8 %collective-permute-done.other = bf16[32,256]{1,0:T(8,128)(2,1)S(1)} collective-permute-done((bf16[32,256]{1,0:T(8,128)(2,1)S(1)}, bf16[32,256]{1,0:T(8,128)(2,1)S(1)}, u32[]{:S(2)}, u32[]{:S(2)}) %collective-permute-start) | collective-permute-done | bytes 16416 | tf_op jit(solution)/shard_map/ppermute | solution.py:38
  3.4 0.4 collective-permute-start.3
  3.8 2.7 %collective-permute-start.1 = (bf16[64,256]{1,0:T(8,128)(2,1)S(1)}, bf16[64,256]{1,0:T(8,128)(2,1)S(1)}, u32[]{:S(2)}, u32[]{:S(2)}) collective-permute-start(bf16[64,256]{1,0:T(8,128)(2,1)S(1)} %join.1.after.pair_own), channel_id=1, source_target_pairs={{0,2},{1,3},{2,0},{3,1},{4,6},{5,7},{6,4},{7,5},{8,10},{9,11},{10,... | collective-permute-start | bytes 98312 | tf_op jit(solution)/shard_map/ppermute | solution.py:38
  6.6 1.8 %collective-permute-done.1.pair_x = bf16[64,256]{1,0:T(8,128)(2,1)S(1)} collective-permute-done((bf16[64,256]{1,0:T(8,128)(2,1)S(1)}, bf16[64,256]{1,0:T(8,128)(2,1)S(1)}, u32[]{:S(2)}, u32[]{:S(2)}) %collective-permute-start.1) | collective-permute-done | bytes 32800 | tf_op jit(solution)/shard_map/ppermute | solution.py:38
  8.6 0.9 %collective-permute-start.2 = (f32[32,256]{1,0:T(8,128)S(1)}, f32[32,256]{1,0:T(8,128)S(1)}, u32[]{:S(2)}, u32[]{:S(2)}) collective-permute-start(f32[32,256]{1,0:T(8,128)S(1)} %get-tuple-element.22.after.mine), channel_id=1, source_target_pairs={{0,1},{1,0},{2,3},{3,2},{4,5},{5,4},{6,7},{7,6},{8,9},{9,8},{10,11... | collective-permute-start | bytes 98312 | tf_op jit(solution)/shard_map/ppermute | solution.py:38
  9.7 0.8 %collective-permute-done.2.other = f32[32,256]{1,0:T(8,128)S(1)} collective-permute-done((f32[32,256]{1,0:T(8,128)S(1)}, f32[32,256]{1,0:T(8,128)S(1)}, u32[]{:S(2)}, u32[]{:S(2)}) %collective-permute-start.2) | collective-permute-done | bytes 32800 | tf_op jit(solution)/shard_map/ppermute | solution.py:38
  10.4 1.7 %collective-permute-start.9 = (bf16[768,256]{1,0:T(8,128)(2,1)S(1)}, bf16[768,256]{1,0:T(8,128)(2,1)S(1)}, u32[]{:S(2)}, u32[]{:S(2)}) collective-permute-start(bf16[768,256]{1,0:T(8,128)(2,1)S(1)} %pass_on.5.after), channel_id=1, source_target_pairs={{8,0},{0,1},{1,9},{9,8},{10,2},{2,3},{3,11},{11,10},{12,4},{4,5},{... | collective-permute-start | bytes 1179656 | tf_op jit(solution)/shard_map/ppermute | solution.py:547
  12.3 1.8 %collective-permute-start.4 = (bf16[64,256]{1,0:T(8,128)(2,1)S(1)}, bf16[64,256]{1,0:T(8,128)(2,1)S(1)}, u32[]{:S(2)}, u32[]{:S(2)}) collective-permute-start(bf16[64,256]{1,0:T(8,128)(2,1)S(1)} %node_rise.1.after.mine), channel_id=1, source_target_pairs={{0,2},{1,3},{2,0},{3,1},{4,6},{5,7},{6,4},{7,5},{8,10},{9,11},{10,... | collective-permute-start | bytes 98312 | tf_op jit(solution)/shard_map/ppermute | solution.py:38
  14.1 2.0 %near.4.after.refs_0_ = f32[32,512]{1,0:T(8,128)S(1)} custom-call(bf16[32,2048]{1,0:T(8,128)(2,1)S(1)} %get-tuple-element.24.tree_ref, bf16[2048,2048]{1,0:T(8,128)(2,1)} %inverse_hbm.7, bf16[64,256]{1,0:T(8,128)(2,1)S(1)} %node_rise.1.after.mine), custom_call_target="tpu_custom_call" | custom-call | bytes 4200000 | tf_op jit(solution)/shard_map/near/pallas_call | solution.py:228
  16.3 2.0 %collective-permute-start.6 = (bf16[64,256]{1,0:T(8,128)(2,1)S(1)}, bf16[64,256]{1,0:T(8,128)(2,1)S(1)}, u32[]{:S(2)}, u32[]{:S(2)}) collective-permute-start(bf16[64,256]{1,0:T(8,128)(2,1)S(1)} %level_rise.3.mine.after), channel_id=1, source_target_pairs={{0,4},{1,5},{2,6},{3,7},{4,0},{5,1},{6,2},{7,3},{8,12},{9,13},{10,... | collective-permute-start | bytes 98312 | tf_op jit(solution)/shard_map/ppermute | solution.py:38
  18.3 1.5 %collective-permute-done.11.lower = bf16[512,256]{1,0:T(8,128)(2,1)S(1)} collective-permute-done((bf16[512,256]{1,0:T(8,128)(2,1)S(1)}, bf16[512,256]{1,0:T(8,128)(2,1)S(1)}, u32[]{:S(2)}, u32[]{:S(2)}) %collective-permute-start.11) | collective-permute-done | bytes 262176 | tf_op jit(solution)/shard_map/ppermute | solution.py:547
  20.0 0.4 %collective-permute-done.6.other.sibling = bf16[64,256]{1,0:T(8,128)(2,1)S(1)} collective-permute-done((bf16[64,256]{1,0:T(8,128)(2,1)S(1)}, bf16[64,256]{1,0:T(8,128)(2,1)S(1)}, u32[]{:S(2)}, u32[]{:S(2)}) %collective-permute-start.6) | collective-permute-done | bytes 32800 | tf_op jit(solution)/shard_map/ppermute | solution.py:38
  20.6 0.4 collective-permute-start.17
  21.0 0.3 collective-permute-start.8
  21.3 2.0 %near.5.after.refs_1_ = f32[32,512]{1,0:T(8,128)S(1)} custom-call(bf16[32,2048]{1,0:T(8,128)(2,1)S(1)} %get-tuple-element.24.tree_ref, bf16[2048,2048]{1,0:T(8,128)(2,1)} %inverse_hbm.7, bf16[64,256]{1,0:T(8,128)(2,1)S(1)} %level_rise.4.after.mine), custom_call_target="tpu_custom_call" | custom-call | bytes 4200000 | tf_op jit(solution)/shard_map/near/pallas_call | solution.py:228
  23.4 1.8 %collective-permute-done.8.other.refs_2_ = bf16[64,256]{1,0:T(8,128)(2,1)S(1)} collective-permute-done((bf16[64,256]{1,0:T(8,128)(2,1)S(1)}, bf16[64,256]{1,0:T(8,128)(2,1)S(1)}, u32[]{:S(2)}, u32[]{:S(2)}) %collective-permute-start.8) | collective-permute-done | bytes 32800 | tf_op jit(solution)/shard_map/ppermute | solution.py:38
  25.7 1.3 %collective-permute-start.19 = (bf16[288,256]{1,0:T(8,128)(2,1)S(1)}, bf16[288,256]{1,0:T(8,128)(2,1)S(1)}, u32[]{:S(2)}, u32[]{:S(2)}) collective-permute-start(bf16[288,256]{1,0:T(8,128)(2,1)S(1)} %local.1.l0), channel_id=1, source_target_pairs={{0,2},{1,3},{2,0},{3,1},{4,6},{5,7},{6,4},{7,5},{8,10},{9,11},{10,... | collective-permute-start | bytes 442376 | tf_op jit(solution)/shard_map/ppermute | solution.py:38
  27.0 1.6 %collective-permute-start.10 = (bf16[64,256]{1,0:T(8,128)(2,1)S(1)}, bf16[64,256]{1,0:T(8,128)(2,1)S(1)}, u32[]{:S(2)}, u32[]{:S(2)}) collective-permute-start(bf16[64,256]{1,0:T(8,128)(2,1)S(1)} %level_rise.5.after.refs_0_), channel_id=1, source_target_pairs={{0,16},{1,17},{2,18},{3,19},{4,20},{5,21},{6,22},{7,23},{8,24},{9,... | collective-permute-start | bytes 98312 | tf_op jit(solution)/shard_map/ppermute | solution.py:38
  28.6 2.0 %near.6.refs_9_.refs_2_ = f32[32,512]{1,0:T(8,128)S(1)} custom-call(bf16[32,2048]{1,0:T(8,128)(2,1)S(1)} %get-tuple-element.24.tree_ref, bf16[2048,2048]{1,0:T(8,128)(2,1)} %inverse_hbm.7, bf16[64,256]{1,0:T(8,128)(2,1)S(1)} %level_rise.5.after.refs_0_), custom_call_target="tpu_custom_call" | custom-call | bytes 4200000 | tf_op jit(solution)/shard_map/near/pallas_call | solution.py:228
  30.6 1.2 %collective-permute-done.10.refs_1_ = bf16[64,256]{1,0:T(8,128)(2,1)S(1)} collective-permute-done((bf16[64,256]{1,0:T(8,128)(2,1)S(1)}, bf16[64,256]{1,0:T(8,128)(2,1)S(1)}, u32[]{:S(2)}, u32[]{:S(2)}) %collective-permute-start.10) | collective-permute-done | bytes 32800 | tf_op jit(solution)/shard_map/ppermute | solution.py:38
  31.8 0.4 %fall.1.after.mine = bf16[32,256]{1,0:T(8,128)(2,1)S(1)} custom-call(bf16[64,256]{1,0:T(8,128)(2,1)S(1)} %level_rise.5.after.refs_0_, bf16[64,256]{1,0:T(8,128)(2,1)S(1)} %collective-permute-done.10.refs_1_, bf16[64,256]{1,0:T(8,128)(2,1)S(1)} %collective-permute-done.8.other.refs_2_, ...), custom_call_target="tpu_custom_call" | custom-call | bytes 1350000 | tf_op jit(solution)/shard_map/fall/pallas_call | solution.py:354
  32.3 1.8 %collective-permute-start.13 = (bf16[32,256]{1,0:T(8,128)(2,1)S(1)}, bf16[32,256]{1,0:T(8,128)(2,1)S(1)}, u32[]{:S(2)}, u32[]{:S(2)}) collective-permute-start(bf16[32,256]{1,0:T(8,128)(2,1)S(1)} %fall.1.after.mine), channel_id=1, source_target_pairs={{0,4},{1,5},{2,6},{3,7},{4,0},{5,1},{6,2},{7,3},{8,12},{9,13},{10,... | collective-permute-start | bytes 49160 | tf_op jit(solution)/shard_map/ppermute | solution.py:38
  34.0 2.0 %near.7.after.refs_3_ = f32[32,512]{1,0:T(8,128)S(1)} custom-call(bf16[32,2048]{1,0:T(8,128)(2,1)S(1)} %get-tuple-element.24.tree_ref, bf16[2048,2048]{1,0:T(8,128)(2,1)} %inverse_hbm.7, bf16[32,256]{1,0:T(8,128)(2,1)S(1)} %fall.1.after.mine), custom_call_target="tpu_custom_call" | custom-call | bytes 4200000 | tf_op jit(solution)/shard_map/near/pallas_call | solution.py:228
  36.3 0.6 %collective-permute-start.20 = (bf16[288,256]{1,0:T(8,128)(2,1)S(1)}, bf16[288,256]{1,0:T(8,128)(2,1)S(1)}, u32[]{:S(2)}, u32[]{:S(2)}) collective-permute-start(bf16[288,256]{1,0:T(8,128)(2,1)S(1)} %pass_on.7), channel_id=1, source_target_pairs={{0,1},{1,0},{2,3},{3,2},{4,5},{5,4},{6,7},{7,6},{8,9},{9,8},{10,11... | collective-permute-start | bytes 442376 | tf_op jit(solution)/shard_map/ppermute | solution.py:38
  36.9 0.6 %collective-permute-start.15 = (bf16[32,256]{1,0:T(8,128)(2,1)S(1)}, bf16[32,256]{1,0:T(8,128)(2,1)S(1)}, u32[]{:S(2)}, u32[]{:S(2)}) collective-permute-start(bf16[32,256]{1,0:T(8,128)(2,1)S(1)} %step_down.1.after.f_own), channel_id=1, source_target_pairs={{0,2},{1,3},{2,0},{3,1},{4,6},{5,7},{6,4},{7,5},{8,10},{9,11},{10,... | collective-permute-start | bytes 49160 | tf_op jit(solution)/shard_map/ppermute | solution.py:38
  37.5 1.2 %collective-permute-start.16 = (bf16[32,256]{1,0:T(8,128)(2,1)S(1)}, bf16[32,256]{1,0:T(8,128)(2,1)S(1)}, u32[]{:S(2)}, u32[]{:S(2)}) collective-permute-start(bf16[32,256]{1,0:T(8,128)(2,1)S(1)} %step_down.1.after.f_own), channel_id=1, source_target_pairs={{0,3},{1,2},{2,1},{3,0},{4,7},{5,6},{6,5},{7,4},{8,11},{9,10},{10,... | collective-permute-start | bytes 49160 | tf_op jit(solution)/shard_map/ppermute | solution.py:38
  38.7 1.0 %invert.1.after.inv_ref = s32[16,128]{1,0:T(8,128)S(1)} custom-call(s32[1,2048]{1,0:T(1,128)} %order_hbm.3, bf16[32,256]{1,0:T(8,128)(2,1)S(1)} %step_down.1.after.f_own), custom_call_target="tpu_custom_call" | custom-call | bytes 3000000 | tf_op jit(solution)/shard_map/invert/pallas_call | solution.py:196
  39.7 0.6 %fold.1 = (bf16[256,2048]{1,0:T(8,128)(2,1)S(1)}, f32[32,2048]{1,0:T(8,128)S(1)}) custom-call(s32[8,128]{1,0:T(8,128)S(1)} %get-tuple-element.18.pick, bf16[288,256]{1,0:T(8,128)(2,1)S(1)} %local.1.l0, bf16[288,256]{1,0:T(8,128)(2,1)S(1)} %collective-permute-done.18.l1, bf16[288,256]{1,0:T(8,128)(2,1)S(1)} %collective-permute-done.19.block.l2, ...), custom_call_target="tpu_custom_call" | custom-call | bytes 3000000 | tf_op jit(solution)/shard_map/fold/pallas_call | solution.py:460
  40.4 0.4 collective-permute-done.15.f_x
  40.9 2.2 %final.1 = f32[32,2048]{1,0:T(8,128)} custom-call(bf16[32,256]{1,0:T(8,128)(2,1)S(1)} %step_down.1.after.f_own, bf16[32,256]{1,0:T(8,128)(2,1)S(1)} %collective-permute-done.14.f_core, bf16[32,256]{1,0:T(8,128)(2,1)S(1)} %collective-permute-done.15.f_x, bf16[32,256]{1,0:T(8,128)(2,1)S(1)} %collective-permute-done.16.f_both, ...), custom_call_target="tpu_custom_call" | custom-call | bytes 5400000 | tf_op jit(solution)/shard_map/final/pallas_call | solution.py:500
  (37 shorter events, 1.9 us)
Async XLA Ops:
  2.0 1.4 %collective-permute-start = (bf16[32,256]{1,0:T(8,128)(2,1)S(1)}, bf16[32,256]{1,0:T(8,128)(2,1)S(1)}, u32[]{:S(2)}, u32[]{:S(2)}) collective-permute-start(bf16[32,256]{1,0:T(8,128)(2,1)S(1)} %get-tuple-element.19.mine.after), channel_id=1, source_target_pairs={{0,1},{1,0},{2,3},{3,2},{4,5},{5,4},{6,7},{7,6},{8,9},{9,8},{10,11... | collective-permute-start | bytes 49160 | tf_op jit(solution)/shard_map/ppermute | solution.py:38
  3.4 8.7 %collective-permute-start.3 = (bf16[768,256]{1,0:T(8,128)(2,1)S(1)}, bf16[768,256]{1,0:T(8,128)(2,1)S(1)}, u32[]{:S(2)}, u32[]{:S(2)}) collective-permute-start(bf16[768,256]{1,0:T(8,128)(2,1)S(1)} %pass_on.4.after), channel_id=1, source_target_pairs={{0,1},{1,0},{2,3},{3,2},{4,5},{5,4},{6,7},{7,6},{8,9},{9,8},{10,11... | collective-permute-start | bytes 1179656 | tf_op jit(solution)/shard_map/ppermute | solution.py:38
  3.8 4.5 %collective-permute-start.1 = (bf16[64,256]{1,0:T(8,128)(2,1)S(1)}, bf16[64,256]{1,0:T(8,128)(2,1)S(1)}, u32[]{:S(2)}, u32[]{:S(2)}) collective-permute-start(bf16[64,256]{1,0:T(8,128)(2,1)S(1)} %join.1.after.pair_own), channel_id=1, source_target_pairs={{0,2},{1,3},{2,0},{3,1},{4,6},{5,7},{6,4},{7,5},{8,10},{9,11},{10,... | collective-permute-start | bytes 98312 | tf_op jit(solution)/shard_map/ppermute | solution.py:38
  6.5 9.6 %collective-permute-start.5 = (bf16[768,256]{1,0:T(8,128)(2,1)S(1)}, bf16[768,256]{1,0:T(8,128)(2,1)S(1)}, u32[]{:S(2)}, u32[]{:S(2)}) collective-permute-start(bf16[768,256]{1,0:T(8,128)(2,1)S(1)} %pass_on.4.after), channel_id=1, source_target_pairs={{2,0},{0,1},{1,3},{3,2},{6,4},{4,5},{5,7},{7,6},{10,8},{8,9},{9,11... | collective-permute-start | bytes 1179656 | tf_op jit(solution)/shard_map/ppermute | solution.py:547
  8.6 11.4 %collective-permute-start.7 = (bf16[768,256]{1,0:T(8,128)(2,1)S(1)}, bf16[768,256]{1,0:T(8,128)(2,1)S(1)}, u32[]{:S(2)}, u32[]{:S(2)}) collective-permute-start(bf16[768,256]{1,0:T(8,128)(2,1)S(1)} %pass_on.5.after), channel_id=1, source_target_pairs={{4,0},{0,1},{1,5},{5,4},{6,2},{2,3},{3,7},{7,6},{12,8},{8,9},{9,13... | collective-permute-start | bytes 1179656 | tf_op jit(solution)/shard_map/ppermute | solution.py:547
  8.6 1.8 %collective-permute-start.2 = (f32[32,256]{1,0:T(8,128)S(1)}, f32[32,256]{1,0:T(8,128)S(1)}, u32[]{:S(2)}, u32[]{:S(2)}) collective-permute-start(f32[32,256]{1,0:T(8,128)S(1)} %get-tuple-element.22.after.mine), channel_id=1, source_target_pairs={{0,1},{1,0},{2,3},{3,2},{4,5},{5,4},{6,7},{7,6},{8,9},{9,8},{10,11... | collective-permute-start | bytes 98312 | tf_op jit(solution)/shard_map/ppermute | solution.py:38
  9.6 10.3 %collective-permute-start.11 = (bf16[512,256]{1,0:T(8,128)(2,1)S(1)}, bf16[512,256]{1,0:T(8,128)(2,1)S(1)}, u32[]{:S(2)}, u32[]{:S(2)}) collective-permute-start(bf16[512,256]{1,0:T(8,128)(2,1)S(1)} %pass_on.6), channel_id=1, source_target_pairs={{16,0},{0,1},{1,17},{17,16},{18,2},{2,3},{3,19},{19,18},{20,4},{4,... | collective-permute-start | bytes 786440 | tf_op jit(solution)/shard_map/ppermute | solution.py:547
  10.4 12.9 %collective-permute-start.9 = (bf16[768,256]{1,0:T(8,128)(2,1)S(1)}, bf16[768,256]{1,0:T(8,128)(2,1)S(1)}, u32[]{:S(2)}, u32[]{:S(2)}) collective-permute-start(bf16[768,256]{1,0:T(8,128)(2,1)S(1)} %pass_on.5.after), channel_id=1, source_target_pairs={{8,0},{0,1},{1,9},{9,8},{10,2},{2,3},{3,11},{11,10},{12,4},{4,5},{... | collective-permute-start | bytes 1179656 | tf_op jit(solution)/shard_map/ppermute | solution.py:547
  12.3 3.9 %collective-permute-start.4 = (bf16[64,256]{1,0:T(8,128)(2,1)S(1)}, bf16[64,256]{1,0:T(8,128)(2,1)S(1)}, u32[]{:S(2)}, u32[]{:S(2)}) collective-permute-start(bf16[64,256]{1,0:T(8,128)(2,1)S(1)} %node_rise.1.after.mine), channel_id=1, source_target_pairs={{0,2},{1,3},{2,0},{3,1},{4,6},{5,7},{6,4},{7,5},{8,10},{9,11},{10,... | collective-permute-start | bytes 98312 | tf_op jit(solution)/shard_map/ppermute | solution.py:38
  16.3 4.1 %collective-permute-start.6 = (bf16[64,256]{1,0:T(8,128)(2,1)S(1)}, bf16[64,256]{1,0:T(8,128)(2,1)S(1)}, u32[]{:S(2)}, u32[]{:S(2)}) collective-permute-start(bf16[64,256]{1,0:T(8,128)(2,1)S(1)} %level_rise.3.mine.after), channel_id=1, source_target_pairs={{0,4},{1,5},{2,6},{3,7},{4,0},{5,1},{6,2},{7,3},{8,12},{9,13},{10,... | collective-permute-start | bytes 98312 | tf_op jit(solution)/shard_map/ppermute | solution.py:38
  19.9 11.9 %collective-permute-start.12 = (bf16[512,256]{1,0:T(8,128)(2,1)S(1)}, bf16[512,256]{1,0:T(8,128)(2,1)S(1)}, u32[]{:S(2)}, u32[]{:S(2)}) collective-permute-start(bf16[512,256]{1,0:T(8,128)(2,1)S(1)} %choose.2.refs_8_), channel_id=1, source_target_pairs={{0,8},{1,0},{9,1},{8,9},{2,10},{3,2},{11,3},{10,11},{4,12},{5,4},{... | collective-permute-start | bytes 786440 | tf_op jit(solution)/shard_map/ppermute | solution.py:552
  20.6 4.7 %collective-permute-start.17 = (bf16[256,256]{1,0:T(8,128)(2,1)S(1)}, bf16[256,256]{1,0:T(8,128)(2,1)S(1)}, u32[]{:S(2)}, u32[]{:S(2)}) collective-permute-start(bf16[256,256]{1,0:T(8,128)(2,1)S(1)} %choose.3), channel_id=1, source_target_pairs={{0,1},{1,0},{2,3},{3,2},{4,5},{5,4},{6,7},{7,6},{8,9},{9,8},{10,11... | collective-permute-start | bytes 393224 | tf_op jit(solution)/shard_map/ppermute | solution.py:38
  21.0 4.2 %collective-permute-start.8 = (bf16[64,256]{1,0:T(8,128)(2,1)S(1)}, bf16[64,256]{1,0:T(8,128)(2,1)S(1)}, u32[]{:S(2)}, u32[]{:S(2)}) collective-permute-start(bf16[64,256]{1,0:T(8,128)(2,1)S(1)} %level_rise.4.after.mine), channel_id=1, source_target_pairs={{0,8},{1,9},{2,10},{3,11},{4,12},{5,13},{6,14},{7,15},{8,0},{9,1},... | collective-permute-start | bytes 98312 | tf_op jit(solution)/shard_map/ppermute | solution.py:38
  25.7 10.6 %collective-permute-start.19 = (bf16[288,256]{1,0:T(8,128)(2,1)S(1)}, bf16[288,256]{1,0:T(8,128)(2,1)S(1)}, u32[]{:S(2)}, u32[]{:S(2)}) collective-permute-start(bf16[288,256]{1,0:T(8,128)(2,1)S(1)} %local.1.l0), channel_id=1, source_target_pairs={{0,2},{1,3},{2,0},{3,1},{4,6},{5,7},{6,4},{7,5},{8,10},{9,11},{10,... | collective-permute-start | bytes 442376 | tf_op jit(solution)/shard_map/ppermute | solution.py:38
  27.0 4.8 %collective-permute-start.10 = (bf16[64,256]{1,0:T(8,128)(2,1)S(1)}, bf16[64,256]{1,0:T(8,128)(2,1)S(1)}, u32[]{:S(2)}, u32[]{:S(2)}) collective-permute-start(bf16[64,256]{1,0:T(8,128)(2,1)S(1)} %level_rise.5.after.refs_0_), channel_id=1, source_target_pairs={{0,16},{1,17},{2,18},{3,19},{4,20},{5,21},{6,22},{7,23},{8,24},{9,... | collective-permute-start | bytes 98312 | tf_op jit(solution)/shard_map/ppermute | solution.py:38
  30.6 9.1 %copy-start = (bf16[256,2048]{1,0:T(8,128)(2,1)S(1)}, bf16[256,2048]{1,0:T(8,128)(2,1)}, u32[]{:S(2)}) copy-start(bf16[256,2048]{1,0:T(8,128)(2,1)} %out_basis.1) | copy-start | bytes 3145732
  32.3 3.8 %collective-permute-start.13 = (bf16[32,256]{1,0:T(8,128)(2,1)S(1)}, bf16[32,256]{1,0:T(8,128)(2,1)S(1)}, u32[]{:S(2)}, u32[]{:S(2)}) collective-permute-start(bf16[32,256]{1,0:T(8,128)(2,1)S(1)} %fall.1.after.mine), channel_id=1, source_target_pairs={{0,4},{1,5},{2,6},{3,7},{4,0},{5,1},{6,2},{7,3},{8,12},{9,13},{10,... | collective-permute-start | bytes 49160 | tf_op jit(solution)/shard_map/ppermute | solution.py:38
  34.0 5.7 %collective-permute-start.18 = (bf16[288,256]{1,0:T(8,128)(2,1)S(1)}, bf16[288,256]{1,0:T(8,128)(2,1)S(1)}, u32[]{:S(2)}, u32[]{:S(2)}) collective-permute-start(bf16[288,256]{1,0:T(8,128)(2,1)S(1)} %local.1.l0), channel_id=1, source_target_pairs={{0,1},{1,0},{2,3},{3,2},{4,5},{5,4},{6,7},{7,6},{8,9},{9,8},{10,11... | collective-permute-start | bytes 442376 | tf_op jit(solution)/shard_map/ppermute | solution.py:38
  36.3 3.5 %collective-permute-start.20 = (bf16[288,256]{1,0:T(8,128)(2,1)S(1)}, bf16[288,256]{1,0:T(8,128)(2,1)S(1)}, u32[]{:S(2)}, u32[]{:S(2)}) collective-permute-start(bf16[288,256]{1,0:T(8,128)(2,1)S(1)} %pass_on.7), channel_id=1, source_target_pairs={{0,1},{1,0},{2,3},{3,2},{4,5},{5,4},{6,7},{7,6},{8,9},{9,8},{10,11... | collective-permute-start | bytes 442376 | tf_op jit(solution)/shard_map/ppermute | solution.py:38
  36.8 3.5 %collective-permute-start.14 = (bf16[32,256]{1,0:T(8,128)(2,1)S(1)}, bf16[32,256]{1,0:T(8,128)(2,1)S(1)}, u32[]{:S(2)}, u32[]{:S(2)}) collective-permute-start(bf16[32,256]{1,0:T(8,128)(2,1)S(1)} %step_down.1.after.f_own), channel_id=1, source_target_pairs={{0,1},{1,0},{2,3},{3,2},{4,5},{5,4},{6,7},{7,6},{8,9},{9,8},{10,11... | collective-permute-start | bytes 49160 | tf_op jit(solution)/shard_map/ppermute | solution.py:38
  36.9 3.9 %collective-permute-start.15 = (bf16[32,256]{1,0:T(8,128)(2,1)S(1)}, bf16[32,256]{1,0:T(8,128)(2,1)S(1)}, u32[]{:S(2)}, u32[]{:S(2)}) collective-permute-start(bf16[32,256]{1,0:T(8,128)(2,1)S(1)} %step_down.1.after.f_own), channel_id=1, source_target_pairs={{0,2},{1,3},{2,0},{3,1},{4,6},{5,7},{6,4},{7,5},{8,10},{9,11},{10,... | collective-permute-start | bytes 49160 | tf_op jit(solution)/shard_map/ppermute | solution.py:38
  37.5 3.3 %collective-permute-start.16 = (bf16[32,256]{1,0:T(8,128)(2,1)S(1)}, bf16[32,256]{1,0:T(8,128)(2,1)S(1)}, u32[]{:S(2)}, u32[]{:S(2)}) collective-permute-start(bf16[32,256]{1,0:T(8,128)(2,1)S(1)} %step_down.1.after.f_own), channel_id=1, source_target_pairs={{0,3},{1,2},{2,1},{3,0},{4,7},{5,6},{6,5},{7,4},{8,11},{9,10},{10,... | collective-permute-start | bytes 49160 | tf_op jit(solution)/shard_map/ppermute | solution.py:38
